TPU v7x, 128 devices: a whole 4x4x4 slice. The times are simulated.
128 devices in a mesh: row: 8 (over x_lo, y), col: 16 (over z, x_hi, core).
Axes of the slice: x: 4 (x_hi: 2, x_lo: 2; x = x_hi * 2 + x_lo), y: 4, z: 4, core: 2. Of those that a mesh axis runs over, the one named last changes fastest.
Arguments:
- features: bfloat16 [65536, 1024], P(('row', 'col')), may hold values from -6 to 6
- walk_counts: int32 [8, 16, 64, 128, 128], P('row', 'col'), may hold values from 0 to 15
- tile_rows: int32 [8, 16, 64], P('row', 'col'), may hold values from 0 to 63
- tile_cols: int32 [8, 16, 64], P('row', 'col'), may hold values from 0 to 31
- live_tiles: int32 [8, 16], P('row', 'col'), may hold values from 8 to 64, as said below
- neigh_weight: bfloat16 [1024, 1024], replicated, may hold values from -0.1875 to 0.1875
- neigh_bias: float32 [1024], replicated, may hold values from -3 to 3
- combine_weight: bfloat16 [2048, 1024], replicated, may hold values from -0.125 to 0.125
- combine_bias: float32 [1024], replicated, may hold values from -3 to 3
Outputs:
- embeddings: float32 [65536, 1024], P(('row', 'col'))
Inputs may be any that keep to these rules, and one draw needn't show every extreme that they name: Slots from live_tiles on are unused; some device has all 64 slots used in every draw.
All inputs are finite; a program needn't handle non-finite values.
Results may differ from a plain program's by a relative error of at most 0.0055.
Values may be sent and summed in bfloat16 or wider, within the bound.
No kernel may reach another device: no remote copies, remote signals or barrier semaphores. Data moves between devices by JAX's collectives and lax.ppermute only.
A program may use at most 320 MiB of HBM per device.

v0:
```python
import jax
import jax.numpy as jnp
from jax import lax
from jax.sharding import PartitionSpec as P


def band_terms(blocks, counts, rows, cols, live, band_blk):
    slots = counts.shape[0]
    tile = counts.shape[1]
    panel_blk = blocks.shape[0]
    width = blocks.shape[2]
    group = min(slots, 32)
    flat_blocks = blocks.reshape(panel_blk, tile * width)
    start_state = (
        jnp.zeros((band_blk, tile, width), jnp.float32),
        jnp.zeros((band_blk, tile), jnp.float32),
    )

    def step(turn, state):
        first = turn * group
        part_counts = lax.dynamic_slice_in_dim(counts, first, group, 0)
        used = first + jnp.arange(group, dtype=jnp.int32) < live
        weights = jnp.where(used[:, None, None], part_counts, 0).astype(jnp.bfloat16)
        source = lax.dynamic_slice_in_dim(cols, first, group, 0)
        target = lax.dynamic_slice_in_dim(rows, first, group, 0)
        pick_source = (source[:, None] == jnp.arange(panel_blk, dtype=jnp.int32)[None, :]).astype(
            jnp.bfloat16
        )
        pieces = (
            jnp.dot(pick_source, flat_blocks, preferred_element_type=jnp.float32)
            .astype(jnp.bfloat16)
            .reshape(group, tile, width)
        )
        terms = jnp.einsum("sij,sjf->sif", weights, pieces, preferred_element_type=jnp.float32)
        upper = terms.astype(jnp.bfloat16)
        lower = (terms - upper.astype(jnp.float32)).astype(jnp.bfloat16)
        place = target[:, None] == jnp.arange(band_blk, dtype=jnp.int32)[None, :]
        place_low = place.astype(jnp.bfloat16)
        added = jnp.einsum("sb,sif->bif", place_low, upper, preferred_element_type=jnp.float32)
        added = added + jnp.einsum(
            "sb,sif->bif", place_low, lower, preferred_element_type=jnp.float32
        )
        row_sums = jnp.sum(weights.astype(jnp.float32), axis=2)
        degree_add = jnp.dot(place.astype(jnp.float32).T, row_sums, precision=lax.Precision.HIGHEST)
        return (state[0] + added, state[1] + degree_add)

    turns = slots // group
    return lax.fori_loop(0, turns, step, start_state)


def local(
    features,
    walk_counts,
    tile_rows,
    tile_cols,
    live_tiles,
    neigh_weight,
    neigh_bias,
    combine_weight,
    combine_bias,
):
    node_dev = features.shape[0]
    width = features.shape[1]
    tile = walk_counts.shape[3]
    band_blk = lax.axis_size("col") * node_dev // tile
    messages = jax.nn.relu(
        jnp.dot(features, neigh_weight, preferred_element_type=jnp.float32) + neigh_bias
    ).astype(jnp.bfloat16)
    panel_rows = lax.all_gather(messages, "row", axis=0, tiled=True)
    self_part = jnp.dot(features, combine_weight[:width], preferred_element_type=jnp.float32)
    blocks = panel_rows.reshape(panel_rows.shape[0] // tile, tile, width)
    counts = walk_counts[0, 0]
    rows = tile_rows[0, 0]
    cols = tile_cols[0, 0]
    live = live_tiles[0, 0]
    sums_band, degree_band = band_terms(blocks, counts, rows, cols, live, band_blk)
    pooled, degree = (
        lax.psum_scatter(sums_band, "col", scatter_dimension=0, tiled=True),
        lax.psum_scatter(degree_band, "col", scatter_dimension=0, tiled=True),
    )
    neighbours = (pooled / (1.0 + degree)[..., None]).reshape(node_dev, width).astype(jnp.bfloat16)
    hidden = self_part + jnp.dot(
        neighbours, combine_weight[width:], preferred_element_type=jnp.float32
    )
    hidden = jax.nn.relu(hidden + combine_bias)
    return hidden / jnp.sqrt(jnp.mean(hidden * hidden, axis=1, keepdims=True) + 1e-06)


def solution(mesh):
    return jax.shard_map(
        local,
        mesh=mesh,
        in_specs=(
            P(("row", "col"), None),
            P("row", "col", None, None, None),
            P("row", "col", None),
            P("row", "col", None),
            P("row", "col"),
            P(),
            P(),
            P(),
            P(),
        ),
        out_specs=P(("row", "col"), None),
        check_vma=False,
    )
```

profile of v0, /device:TPU:3, one launch (start us, length us, event | category | flops | bytes accessed | tf_op | source)
XLA Modules:
  0.0 594.1 jit_solution(14999323854629997217)
XLA Ops:
  6.5 0.0 copy-start
  6.5 0.0 all-gather.2.cloned.1.call-start
  6.5 1.6 copy-done
  8.1 3.5 maximum_convert_fusion
  11.6 0.0 all-gather.2.cloned.1.call-update
  11.6 0.0 reduce-scatter.2.cloned.1.call-start
  11.7 0.0 copy-start.6
  11.7 0.0 copy-start.7
  11.7 93.4 %all-gather.2.cloned.1.call-done = bf16[4096,1024]{1,0:T(8,128)(2,1)} async-done(((bf16[512,1024]{1,0:T(8,128)(2,1)}), bf16[4096,1024]{1,0:T(8,128)(2,1)}) %all-gather.2.cloned.1.call-update) | async-done | bytes 8388624 | tf_op jit(solution)/shard_map/all_gather | solution.py:69
  105.1 8.9 %reshape_reshape.3 = bf16[32,131072]{1,0:T(8,128)(2,1)} reshape(bf16[4096,1024]{1,0:T(8,128)(2,1)} %all-gather.2.cloned.1.call-done) | data formatting | bytes 16777216 | tf_op jit(solution)/shard_map/reshape;reshape | solution.py:13
  114.0 0.0 copy-done.6
  114.0 189.5 %while.16 = (s32[]{:T(128)}, f32[64,128,1024]{2,0,1:T(8,128)}, f32[64,128]{1,0:T(8,128)S(1)}, s32[64]{0:T(128)S(1)}, s32[]{:T(128)}, /*index=5*/s32[64,128,128]{...) while((s32[]{:T(128)}, f32[64,128,1024]{2,0,1:T(8,128)}, ...), condition=%wide.region_2.3_spmd.clone, body=%wide.region_0.2_spmd.clone.sunk | while | flops 2468367360 | bytes 230786864 | solution.py:48
  114.0 0.7 add_compare_fusion.2
  114.7 0.1 dynamic_slice.37
  114.8 0.1 dynamic_slice.36
  114.8 2.3 convert_reduce_fusion.2
  117.1 0.3 convolution_add_fusion.2
  117.4 9.0 %convolution_convert_fusion.2 = bf16[32,131072]{1,0:T(8,128)(2,1)} fusion(bf16[32,131072]{1,0:T(8,128)(2,1)} %get-tuple-element.278, s32[32]{0:T(128)S(1)} %dynamic_slice.36), kind=kOutput, calls=%fused_computation.clone.1 | convolution fusion | flops 272630784 | bytes 16777344 | tf_op jit(solution)/shard_map/while/body/eval_jaxpr/dot_general | solution.py:30
  126.4 11.5 %copy.29 = bf16[4,8,128,1024]{3,2,1,0:T(8,128)(2,1)} copy(bf16[4,8,128,1024]{3,1,2,0:T(8,128)(2,1)} %bitcast.33) | data formatting | bytes 16777216 | tf_op jit(solution)/shard_map/while
  137.9 0.0 copy-done.2
  137.9 10.6 %subtract_convert_fusion.2 = (bf16[32,128,1024]{2,1,0:T(8,128)(2,1)}, bf16[32,128,1024]{2,1,0:T(8,128)(2,1)}) fusion(bf16[32,128,1024]{2,1,0:T(8,128)(2,1)} %bitcast.34, s32[64,128,128]{2,1,0:T(8,128)S(1)} %copy-done.2, s32[]{:T(128)S(6)} %select_n.30, pred[32]{0:T(512)(128)(4,1)S(1)} %add_compare_fusion.2), kind=kOutput, calls=%fused_computation.2.clone.1 | convolution fusion | flops 1091567616 | bytes 27263492 | tf_op jit(solution)/shard_map/while/body/eval_jaxpr/sij,sjf->sif/dot_general | solution.py:34
  148.4 27.2 %fusion.39 = f32[64,128,1024]{2,0,1:T(8,128)} fusion(bf16[32,128,1024]{2,1,0:T(8,128)(2,1)} %get-tuple-element.245, s32[32]{0:T(128)S(1)} %dynamic_slice.37), kind=kOutput, calls=%fused_computation.4.clone.1 | convolution fusion | flops 536872960 | bytes 41943168 | tf_op jit(solution)/shard_map/while/body/eval_jaxpr/sb,sif->bif/dot_general | solution.py:39
  175.6 30.1 %select_add_fusion.2 = f32[64,128,1024]{2,0,1:T(8,128)} fusion(f32[64,128,1024]{2,0,1:T(8,128)} %get-tuple-element.260, f32[64,128,1024]{2,0,1:T(8,128)} %fusion.39, pred[]{:T(512)S(6)} %compare.3, bf16[32,128,1024]{2,1,0:T(8,128)(2,1)} %get-tuple-element.246, s32[32]{0:T(128)S(1)} %dynamic_slice.37), kind=kOutput, calls=%fused_computation.1.clone.1 | convolution fusion | flops 562038784 | bytes 109052032 | tf_op jit(solution)/shard_map/while/body/eval_jaxpr/sb,sif->bif/dot_general | solution.py:40
  205.7 0.7 add_compare_fusion.2
  206.4 0.1 dynamic_slice.37
  206.5 0.1 dynamic_slice.36
  206.5 2.3 convert_reduce_fusion.2
  208.8 0.3 convolution_add_fusion.2
  209.1 9.0 %convolution_convert_fusion.2 = bf16[32,131072]{1,0:T(8,128)(2,1)} fusion(bf16[32,131072]{1,0:T(8,128)(2,1)} %get-tuple-element.278, s32[32]{0:T(128)S(1)} %dynamic_slice.36), kind=kOutput, calls=%fused_computation.clone.1 | convolution fusion | flops 272630784 | bytes 16777344 | tf_op jit(solution)/shard_map/while/body/eval_jaxpr/dot_general | solution.py:30
  218.1 11.5 %copy.29 = bf16[4,8,128,1024]{3,2,1,0:T(8,128)(2,1)} copy(bf16[4,8,128,1024]{3,1,2,0:T(8,128)(2,1)} %bitcast.33) | data formatting | bytes 16777216 | tf_op jit(solution)/shard_map/while
  229.6 0.0 copy-done.2
  229.6 10.6 %subtract_convert_fusion.2 = (bf16[32,128,1024]{2,1,0:T(8,128)(2,1)}, bf16[32,128,1024]{2,1,0:T(8,128)(2,1)}) fusion(bf16[32,128,1024]{2,1,0:T(8,128)(2,1)} %bitcast.34, s32[64,128,128]{2,1,0:T(8,128)S(1)} %copy-done.2, s32[]{:T(128)S(6)} %select_n.30, pred[32]{0:T(512)(128)(4,1)S(1)} %add_compare_fusion.2), kind=kOutput, calls=%fused_computation.2.clone.1 | convolution fusion | flops 1091567616 | bytes 27263492 | tf_op jit(solution)/shard_map/while/body/eval_jaxpr/sij,sjf->sif/dot_general | solution.py:34
  240.1 27.2 %fusion.39 = f32[64,128,1024]{2,0,1:T(8,128)} fusion(bf16[32,128,1024]{2,1,0:T(8,128)(2,1)} %get-tuple-element.245, s32[32]{0:T(128)S(1)} %dynamic_slice.37), kind=kOutput, calls=%fused_computation.4.clone.1 | convolution fusion | flops 536872960 | bytes 41943168 | tf_op jit(solution)/shard_map/while/body/eval_jaxpr/sb,sif->bif/dot_general | solution.py:39
  267.3 36.2 %select_add_fusion.2 = f32[64,128,1024]{2,0,1:T(8,128)} fusion(f32[64,128,1024]{2,0,1:T(8,128)} %get-tuple-element.260, f32[64,128,1024]{2,0,1:T(8,128)} %fusion.39, pred[]{:T(512)S(6)} %compare.3, bf16[32,128,1024]{2,1,0:T(8,128)(2,1)} %get-tuple-element.246, s32[32]{0:T(128)S(1)} %dynamic_slice.37), kind=kOutput, calls=%fused_computation.1.clone.1 | convolution fusion | flops 562038784 | bytes 109052032 | tf_op jit(solution)/shard_map/while/body/eval_jaxpr/sb,sif->bif/dot_general | solution.py:40
  303.5 31.7 %copy.18 = f32[64,128,1024]{2,1,0:T(8,128)} copy(f32[64,128,1024]{2,0,1:T(8,128)} %get-tuple-element.145) | data formatting | bytes 67108864 | tf_op jit(solution)/shard_map/while | solution.py:48
  335.2 0.0 reduce-scatter.2.cloned.1.call-update
  335.3 0.6 copy-done.8
  335.9 0.6 dynamic-slice
  337.1 63.8 %all-reduce = f32[64,128]{1,0:T(8,128)S(1)} all-reduce(f32[64,128]{1,0:T(8,128)S(1)} %get-tuple-element.146), channel_id=3, replica_groups=mesh['row'=8,'col'=16] {'col'}, use_global_device_ids=true, to_apply=%region_4.5.clone | all-reduce | flops 8192 | bytes 65536
  400.9 178.2 %reduce-scatter.2.cloned.1.call-done = f32[4,128,1024]{2,1,0:T(8,128)} async-done(((f32[64,128,1024]{2,1,0:T(8,128)}), f32[4,128,1024]{2,1,0:T(8,128)}) %reduce-scatter.2.cloned.1.call-update) | async-done | bytes 2097168 | tf_op jit(solution)/shard_map/reduce_scatter | solution.py:78
  579.2 1.9 divide_convert_fusion
  581.1 0.0 copy-start.3
  581.1 0.0 copy-start.4
  581.1 0.0 copy-start.5
  581.1 3.0 fusion.11
  584.1 0.1 copy-done.4
  584.2 1.5 multiply_reduce_fusion
  585.6 1.6 broadcast_divide_fusion
  (12 shorter events, 0.0 us)
Async XLA Ops:
  6.5 1.6 copy-start
  6.5 98.6 %all-gather.2.cloned.1.call-start = ((), (), s32[]{:S(2)}) async-start(), calls=%async_computation.1 | async-start | bytes 9437184 | tf_op jit(solution)/shard_map/all_gather | solution.py:69
  11.6 567.6 %reduce-scatter.2.cloned.1.call-start = ((), (), s32[]{:S(2)}) async-start(), calls=%async_computation.2 | async-start | bytes 35651584 | tf_op jit(solution)/shard_map/reduce_scatter | solution.py:78
  11.7 102.3 %copy-start.6 = (s32[1,1,64]{2,1,0:T(1,128)S(1)}, s32[1,1,64]{2,1,0:T(1,128)}, u32[]{:S(2)}) copy-start(s32[1,1,64]{2,1,0:T(1,128)} %param.13) | copy-start | bytes 772
  11.7 102.3 %copy-start.7 = (s32[1,1,64]{2,1,0:T(1,128)S(1)}, s32[1,1,64]{2,1,0:T(1,128)}, u32[]{:S(2)}) copy-start(s32[1,1,64]{2,1,0:T(1,128)} %param.14) | copy-start | bytes 772
  126.4 11.5 %copy-start.2 = (s32[64,128,128]{2,1,0:T(8,128)S(1)}, s32[64,128,128]{2,1,0:T(8,128)}, u32[]{:S(2)}) copy-start(s32[64,128,128]{2,1,0:T(8,128)} %get-tuple-element.276) | copy-start | bytes 12582916 | tf_op jit(solution)/shard_map/while
  218.1 11.5 %copy-start.2 = (s32[64,128,128]{2,1,0:T(8,128)S(1)}, s32[64,128,128]{2,1,0:T(8,128)}, u32[]{:S(2)}) copy-start(s32[64,128,128]{2,1,0:T(8,128)} %get-tuple-element.276) | copy-start | bytes 12582916 | tf_op jit(solution)/shard_map/while
  335.2 0.7 copy-start.8
  581.1 3.0 copy-start.3
  581.1 3.1 copy-start.4
  581.1 3.1 copy-start.5
  584.2 3.0 copy-start.1
Sparse Core Ops, SparseCore 0:
  11.7 93.3 all-gather.1
  335.4 243.7 reduce-scatter.1
where the time goes:
time: 598 us; the launch traced here: 594 us
  waiting for transfers between devices  272 us (45%)
  matrix products  168 us (28%)
  local copies, waits for them, and re-layouts  66.9 us (11%)
  blocking collectives  63.8 us (11%)
  between operations  14.1 us (2%)
  other arithmetic  9.3 us (2%)
    reduce_scatter x1, waiting for transfers between devices, local(): lax.psum_scatter(sums_band, 'col', scatter_dimension=0, tiled=True)  178 us
    all_gather x1, waiting for transfers between devices, local(): panel_rows = lax.all_gather(messages, 'row', axis=0, tiled=True)  93.4 us
    dot_general x2, matrix products, step(): jnp.einsum('sb,sif->bif', place_low, lower, preferred_element_type=jnp.fl...  66.3 us
    unnamed x1, blocking collectives  63.8 us
    dot_general x2, matrix products, step(): jnp.einsum('sb,sif->bif', place_low, upper, preferred_element_type=jnp.fl...  54.4 us
    while x1, local copies, waits for them, and re-layouts, band_terms(): return lax.fori_loop(0, turns, step, start_state)  31.7 us
    while x6, local copies, waits for them, and re-layouts  23 us
    dot_general x2, matrix products, step(): jnp.einsum('sij,sjf->sif', weights, pieces, preferred_element_type=jnp.fl...  21.1 us
  transfers between devices with their start and end apart: 2, of which 2 were waited for; matrix products, arithmetic and copies ran while one was open for 0% of the time, Pallas kernels for 0%

commit v1 on v0

v1 whole, which is shorter than its diff:
```python
import jax
import jax.numpy as jnp
from jax import lax
from jax.experimental import pallas as pl
from jax.experimental.pallas import tpu as pltpu
from jax.sharding import Mesh, PartitionSpec as P

AXES = ("x_lo", "y", "z", "x_hi", "core")
SIZES = (2, 4, 4, 2, 2)
CHUNKS = 4
GROUP = 8


def shift(x, axis, step):
    n = lax.axis_size(axis)
    return lax.ppermute(x, axis, [(i, (i + step) % n) for i in range(n)])


def swap_low(x):
    return lax.ppermute(x, "z", [(i, i ^ 1) for i in range(4)])


def swap_far(x):
    return lax.ppermute(x, "z", [(i, 3 - i) for i in range(4)])


def gather_pieces(own):
    def along_y(piece):
        left = shift(piece, "y", 1)
        right = shift(piece, "y", -1)
        far0 = shift(left[0], "y", 1)
        far1 = shift(right[1], "y", -1)
        return [piece, right, far0, far1, left]

    other = shift(own, "x_lo", 1)
    return along_y(own) + along_y(other)


def tile_kernel(
    src_ref,
    dst_ref,
    live_ref,
    c_own,
    c_other,
    p0,
    p1,
    p2a,
    p2b,
    p3,
    q0,
    q1,
    q2a,
    q2b,
    q3,
    send_a,
    keep_a,
    send_b,
    keep_b,
    panel,
    acc,
    sems,
):
    plan = []
    for dx, group in enumerate(((p0, p1, p2a, p2b, p3), (q0, q1, q2a, q2b, q3))):
        base = dx * 32
        plan += [
            (group[0], base, 8),
            (group[1], base + 8, 8),
            (group[2], base + 16, 4),
            (group[3], base + 20, 4),
            (group[4], base + 24, 8),
        ]
    copies = []
    for n, (ref, at, size) in enumerate(plan):
        copies.append(pltpu.make_async_copy(ref, panel.at[pl.ds(at, size)], sems.at[n]))
        copies[-1].start()

    @pl.loop(0, 64)
    def _(i):
        acc[i] = jnp.zeros(acc.shape[1:], jnp.float32)

    for copy in copies:
        copy.wait()

    slots = c_own.shape[0]
    for q, counts in enumerate((c_own, c_other)):

        def body(g, carry, q=q, counts=counts):
            terms = []
            for i in range(GROUP):
                s = g * GROUP + i
                terms.append(
                    jnp.dot(
                        counts[s],
                        panel[src_ref[q * slots + s]],
                        preferred_element_type=jnp.float32,
                    )
                )
            for i in range(GROUP):
                at = dst_ref[q * slots + g * GROUP + i]
                acc[at] = acc[at] + terms[i]
            return carry

        lax.fori_loop(0, (live_ref[q] + GROUP - 1) // GROUP, body, 0)

    for first, out in ((0, send_a), (16, keep_a), (32, send_b), (48, keep_b)):

        @pl.loop(0, 16)
        def _(i, first=first, out=out):
            out[i] = acc[first + i].astype(out.dtype)


def tile_sums(src, dst, live, c_own, c_other, pieces):
    tile, w = pieces[0].shape[-2:]
    flat = [p.reshape(-1, tile, w) for p in pieces]
    any_spec = pl.BlockSpec(memory_space=pl.ANY)
    vmem = pl.BlockSpec(memory_space=pltpu.VMEM)
    smem = pl.BlockSpec(memory_space=pltpu.SMEM)
    slots = c_own.shape[0]
    out = lambda dt: jax.ShapeDtypeStruct((16, tile, w), dt)
    return pl.pallas_call(
        tile_kernel,
        out_shape=(out(jnp.bfloat16), out(jnp.float32), out(jnp.bfloat16), out(jnp.float32)),
        in_specs=[smem] * 3 + [vmem] * 2 + [any_spec] * len(flat),
        out_specs=(vmem,) * 4,
        scratch_shapes=[
            pltpu.VMEM((64, tile, w), jnp.bfloat16),
            pltpu.VMEM((64, tile, w), jnp.float32),
            pltpu.SemaphoreType.DMA((10,)),
        ],
        compiler_params=pltpu.CompilerParams(vmem_limit_bytes=32 * 1024 * 1024),
        cost_estimate=pl.CostEstimate(
            flops=2 * 2 * slots * tile * tile * w * 4,
            bytes_accessed=64 * tile * w * 8,
            transcendentals=0,
        ),
    )(src, dst, live, c_own, c_other, *flat)


def scatter_sum(send_a, keep_a, send_b, keep_b):
    shape = (2, 8) + send_a.shape[1:]
    dt = send_a.dtype
    sum_a = swap_low(send_a).reshape(shape).astype(jnp.float32) + keep_a.reshape(shape)
    sum_b = swap_far(send_b).reshape(shape).astype(jnp.float32) + keep_b.reshape(shape)
    got_a = swap_far(sum_a[0].astype(dt))
    got_b = swap_low(sum_b[0].astype(dt))
    end_a = sum_a[1] + got_a.astype(jnp.float32)
    end_b = sum_b[1] + got_b.astype(jnp.float32)
    both = jnp.stack([end_a, end_b]).reshape((2, 2, 4) + send_a.shape[1:])
    got = shift(both[:, 0].astype(dt), "x_hi", 1)
    return both[:, 1] + got.astype(jnp.float32)


def local(
    features,
    walk_counts,
    tile_rows,
    tile_cols,
    live_tiles,
    neigh_weight,
    neigh_bias,
    combine_weight,
    combine_bias,
):
    rows_dev, width = features.shape
    tile = walk_counts.shape[3]
    slots = walk_counts.shape[2]
    half = width // 2
    cw = half // CHUNKS
    x_lo, y, z, x_hi, core = (lax.axis_index(a) for a in AXES)

    messages = jax.nn.relu(
        jnp.dot(features, neigh_weight, preferred_element_type=jnp.float32) + neigh_bias
    ).astype(jnp.bfloat16)
    mine = lax.dynamic_slice_in_dim(messages, core * half, half, 1)
    theirs = shift(lax.dynamic_slice_in_dim(messages, (1 - core) * half, half, 1), "core", 1)

    live = live_tiles[0, 0]
    used = jnp.arange(slots, dtype=jnp.int32) < live
    c_own = jnp.where(used[:, None, None], walk_counts[0, 0], 0).astype(jnp.bfloat16)
    meta = jnp.stack(
        [
            jnp.where(used, tile_rows[0, 0], 0),
            jnp.where(used, tile_cols[0, 0], 0),
            jnp.full((slots,), live, jnp.int32),
        ]
    )
    c_other = shift(c_own, "core", 1)
    metas = jnp.stack([meta, shift(meta, "core", 1)])
    k = metas[:, 1]
    src = (
        ((k // 16) ^ x_lo) * 32
        + (((k // 4) % 4 - y) % 4) * 8
        + jnp.arange(2, dtype=jnp.int32)[:, None] * 4
        + k % 4
    ).reshape(-1)

    def place(b):
        dest = b // 16
        theirs_b = ((b // 4) % 2) ^ core
        near = z ^ 1
        far = 3 - z
        slot_a = jnp.where(
            dest == z, 3, jnp.where(dest == far, 2, jnp.where(dest == near, 1, 0))
        )
        slot_b = jnp.where(
            dest == z, 3, jnp.where(dest == near, 2, jnp.where(dest == far, 1, 0))
        )
        slot = jnp.where(theirs_b == 1, slot_b, slot_a)
        x_slot = 1 - (((b // 8) % 2) ^ x_hi)
        return ((theirs_b * 4 + slot) * 2 + x_slot) * 4 + b % 4

    dst = place(metas[:, 0])
    lives = metas[:, 2, 0]

    row_sums = jnp.sum(c_own.astype(jnp.float32), axis=2)
    row_sums = jnp.concatenate([row_sums, shift(row_sums, "core", 1)])
    dst = dst.reshape(-1)
    onehot = (jnp.arange(64, dtype=jnp.int32)[:, None] == dst[None, :]).astype(jnp.float32)
    deg = jnp.dot(onehot, row_sums, precision=lax.Precision.HIGHEST)
    scale = 1.0 / (1.0 + scatter_sum(*jnp.split(deg, 4)))

    hidden = (
        jnp.dot(features, combine_weight[:width], preferred_element_type=jnp.float32)
        + combine_bias
    )
    w_own = lax.dynamic_slice_in_dim(combine_weight, width + core * half, half, 0)
    w_other = lax.dynamic_slice_in_dim(combine_weight, width + (1 - core) * half, half, 0)
    blocks = rows_dev // tile
    for j in range(CHUNKS):
        cols = slice(j * cw, (j + 1) * cw)
        own = jnp.stack(
            [mine[:, cols].reshape(blocks, tile, cw), theirs[:, cols].reshape(blocks, tile, cw)]
        )
        pieces = gather_pieces(own)
        pooled = scatter_sum(*tile_sums(src, dst, lives, c_own, c_other, pieces))
        near = (pooled * scale[..., None]).astype(jnp.bfloat16).reshape(2, rows_dev, cw)
        got = shift(near[1], "core", 1)
        hidden = hidden + jnp.dot(near[0], w_own[cols], preferred_element_type=jnp.float32)
        hidden = hidden + jnp.dot(got, w_other[cols], preferred_element_type=jnp.float32)
    hidden = jax.nn.relu(hidden)
    return hidden / jnp.sqrt(jnp.mean(hidden * hidden, axis=1, keepdims=True) + 1e-06)


def solution(mesh):
    fine = Mesh(mesh.devices.reshape(SIZES), AXES)
    row = AXES[:2]
    col = AXES[2:]
    return jax.shard_map(
        local,
        mesh=fine,
        in_specs=(
            P(AXES, None),
            P(row, col, None, None, None),
            P(row, col, None),
            P(row, col, None),
            P(row, col),
            P(),
            P(),
            P(),
            P(),
        ),
        out_specs=P(AXES, None),
        check_vma=False,
    )
```

time: 598 us -> 223 us (0.37)
  waiting for transfers between devices: 272 us -> 76.6 us
  matrix products: 168 us -> 10.4 us
  starting transfers between devices: 0.04 us -> 91.3 us
  blocking collectives: 63.8 us -> 0 us
  local copies, waits for them, and re-layouts: 66.9 us -> 7.47 us
  Pallas kernels: 0 us -> 24.5 us
  between operations: 14.1 us -> 1.46 us
    reduce_scatter x1 -> x0, waiting for transfers between devices: 178 us -> none  [local(): lax.psum_scatter(sums_band, 'col', scatter_dimension=0, tiled=True)]
    dot_general x11 -> x9, matrix products: 163 us -> 5.21 us  [the longest x4 2.56 us: local(): jnp.dot(got, w_other[cols], preferred_element_type=jnp.float32)]
    all_gather x1 -> x0, waiting for transfers between devices: 93.4 us -> none  [local(): panel_rows = lax.all_gather(messages, 'row', axis=0, tiled=True)]
    ppermute x0 -> x69, starting transfers between devices: none -> 91.3 us  [the longest x49 73.2 us: shift(): return lax.ppermute(x, axis, [(i, (i + step) % n) for i in range(n)])]
    ppermute x0 -> x69, waiting for transfers between devices: none -> 76.6 us  [the longest x49 41.8 us: shift(): return lax.ppermute(x, axis, [(i, (i + step) % n) for i in range(n)])]
    unnamed x1 -> x0, blocking collectives: 63.8 us -> none
    while x7 -> x0, local copies, waits for them, and re-layouts: 54.8 us -> none  [the longest x1 31.7 us: band_terms(): return lax.fori_loop(0, turns, step, start_state)]
    pallas_call x0 -> x4, Pallas kernels: none -> 24.5 us  [tile_sums(): pl.pallas_call(tile_kernel, out_shape=(out(jnp.bfloat16), out(jnp.float32...]
  transfers between devices with their start and end apart: 2 -> 69, of which waited for: 2 -> 26; matrix products, arithmetic and copies ran while one was open for 0% -> 7% of each run, Pallas kernels for 0% -> 11%
where the time goes in v1:
time: 223 us; the launch traced here: 222 us
  starting transfers between devices  91.3 us (41%)
  waiting for transfers between devices  76.6 us (34%)
  Pallas kernels  24.5 us (11%)
  matrix products  10.4 us (5%)
  other arithmetic  10.2 us (5%)
  local copies, waits for them, and re-layouts  7.47 us (3%)
    ppermute x49, starting transfers between devices, shift(): return lax.ppermute(x, axis, [(i, (i + step) % n) for i in range(n)])  73.2 us
    ppermute x49, waiting for transfers between devices, shift(): return lax.ppermute(x, axis, [(i, (i + step) % n) for i in range(n)])  41.8 us
    ppermute x10, waiting for transfers between devices, swap_far(): return lax.ppermute(x, 'z', [(i, 3 - i) for i in range(4)])  28.6 us
    pallas_call x4, Pallas kernels, tile_sums(): pl.pallas_call(tile_kernel, out_shape=(out(jnp.bfloat16), out(jnp.float32...  24.5 us
    ppermute x10, starting transfers between devices, swap_far(): return lax.ppermute(x, 'z', [(i, 3 - i) for i in range(4)])  14.3 us
    ppermute x10, waiting for transfers between devices, swap_low(): return lax.ppermute(x, 'z', [(i, i ^ 1) for i in range(4)])  6.14 us
  transfers between devices with their start and end apart: 69, of which 26 were waited for; matrix products, arithmetic and copies ran while one was open for 7% of the time, Pallas kernels for 11%

profile of v1, /device:TPU:3, one launch (start us, length us, event | category | flops | bytes accessed | tf_op | source)
XLA Modules:
  0.0 222.0 jit_solution(4779733807250477071)
XLA Ops:
  0.0 1.6 copy-done
  1.6 2.6 %maximum_convert_fusion = bf16[512,1024]{1,0:T(8,128)(2,1)S(1)} fusion(bf16[512,1024]{1,0:T(8,128)(2,1)} %param.9, bf16[1024,1024]{1,0:T(8,128)(2,1)S(1)} %copy-done, f32[1024]{0:T(1024)} %param.15), kind=kOutput, calls=%fused_computation.5 | convolution fusion | flops 1075314688 | bytes 4198400 | tf_op jit(solution)/shard_map/dot_general | solution.py:173
  6.6 2.0 convert_reduce_fusion
  10.0 3.1 %collective-permute-done.17 = f32[64,128]{1,0:T(8,128)} collective-permute-done((f32[64,128]{1,0:T(8,128)}, f32[64,128]{1,0:T(8,128)}, u32[]{:S(2)}, u32[]{:S(2)}) %collective-permute-start.17) | collective-permute-done | bytes 32800 | tf_op jit(solution)/shard_map/ppermute | solution.py:16
  14.1 1.7 collective-permute-start.18
  15.8 2.2 %collective-permute-start.20 = (f32[16,128]{1,0:T(8,128)S(1)}, f32[16,128]{1,0:T(8,128)S(1)}, u32[]{:S(2)}, u32[]{:S(2)}) collective-permute-start(f32[16,128]{1,0:T(8,128)S(1)} %get-tuple-element.60), channel_id=1, source_target_pairs={{0,12},{4,8},{8,4},{12,0},{1,13},{5,9},{9,5},{13,1},{2,14},{6,10},... | collective-permute-start | bytes 24584 | tf_op jit(solution)/shard_map/ppermute | solution.py:24
  19.5 2.2 %collective-permute-start.19 = (f32[8,128]{1,0:T(8,128)S(1)}, f32[8,128]{1,0:T(8,128)S(1)}, u32[]{:S(2)}, u32[]{:S(2)}) collective-permute-start(f32[8,128]{1,0:T(8,128)S(1)} %slice.348), channel_id=1, source_target_pairs={{0,12},{4,8},{8,4},{12,0},{1,13},{5,9},{9,5},{13,1},{2,14},{6,10},... | collective-permute-start | bytes 12296 | tf_op jit(solution)/shard_map/ppermute | solution.py:24
  31.0 2.4 %collective-permute-done.55 = bf16[2,4,128,128]{3,2,1,0:T(8,128)(2,1)S(1)} collective-permute-done((bf16[2,4,128,128]{3,2,1,0:T(8,128)(2,1)S(1)}, bf16[2,4,128,128]{3,2,1,0:T(8,128)(2,1)S(1)}, u32[]{:S(2)}, u32[]{:S(2)}) %collective-permute-start.55) | collective-permute-done | bytes 262176 | tf_op jit(solution)/shard_map/ppermute | solution.py:16
  33.7 2.4 %collective-permute-start.39 = (bf16[2,4,128,128]{3,2,1,0:T(8,128)(2,1)S(1)}, bf16[2,4,128,128]{3,2,1,0:T(8,128)(2,1)S(1)}, u32[]{:S(2)}, u32[]{:S(2)}) collective-permute-start(bf16[2,4,128,128]{3,2,1,0:T(8,128)(2,1)S(1)} %pad_maximum_fusion.6), channel_id=1, source_target_pairs={{0,48},{16,0},{32,16},{48,32},{1,49},{17,1},{33,17},{49,33},{2,50}... | collective-permute-start | bytes 786440 | tf_op jit(solution)/shard_map/ppermute | solution.py:16
  36.2 3.7 %collective-permute-done.40 = bf16[2,4,128,128]{3,2,1,0:T(8,128)(2,1)S(1)} collective-permute-done((bf16[2,4,128,128]{3,2,1,0:T(8,128)(2,1)S(1)}, bf16[2,4,128,128]{3,2,1,0:T(8,128)(2,1)S(1)}, u32[]{:S(2)}, u32[]{:S(2)}) %collective-permute-start.40) | collective-permute-done | bytes 262176 | tf_op jit(solution)/shard_map/ppermute | solution.py:16
  40.6 2.3 %collective-permute-start.24 = (bf16[2,4,128,128]{3,2,1,0:T(8,128)(2,1)S(1)}, bf16[2,4,128,128]{3,2,1,0:T(8,128)(2,1)S(1)}, u32[]{:S(2)}, u32[]{:S(2)}) collective-permute-start(bf16[2,4,128,128]{3,2,1,0:T(8,128)(2,1)S(1)} %pad_maximum_fusion.5), channel_id=1, source_target_pairs={{0,48},{16,0},{32,16},{48,32},{1,49},{17,1},{33,17},{49,33},{2,50}... | collective-permute-start | bytes 786440 | tf_op jit(solution)/shard_map/ppermute | solution.py:16
  42.9 4.6 %collective-permute-done.25 = bf16[2,4,128,128]{3,2,1,0:T(8,128)(2,1)S(1)} collective-permute-done((bf16[2,4,128,128]{3,2,1,0:T(8,128)(2,1)S(1)}, bf16[2,4,128,128]{3,2,1,0:T(8,128)(2,1)S(1)}, u32[]{:S(2)}, u32[]{:S(2)}) %collective-permute-start.25) | collective-permute-done | bytes 262176 | tf_op jit(solution)/shard_map/ppermute | solution.py:16
  48.0 2.6 %collective-permute-start.3 = (bf16[2,4,128,128]{3,2,1,0:T(8,128)(2,1)S(1)}, bf16[2,4,128,128]{3,2,1,0:T(8,128)(2,1)S(1)}, u32[]{:S(2)}, u32[]{:S(2)}) collective-permute-start(bf16[2,4,128,128]{3,2,1,0:T(8,128)(2,1)S(1)} %pad_maximum_fusion.4), channel_id=1, source_target_pairs={{0,48},{16,0},{32,16},{48,32},{1,49},{17,1},{33,17},{49,33},{2,50}... | collective-permute-start | bytes 786440 | tf_op jit(solution)/shard_map/ppermute | solution.py:16
  51.9 4.2 %collective-permute-done.4 = bf16[2,4,128,128]{3,2,1,0:T(8,128)(2,1)S(1)} collective-permute-done((bf16[2,4,128,128]{3,2,1,0:T(8,128)(2,1)S(1)}, bf16[2,4,128,128]{3,2,1,0:T(8,128)(2,1)S(1)}, u32[]{:S(2)}, u32[]{:S(2)}) %collective-permute-start.4) | collective-permute-done | bytes 262176 | tf_op jit(solution)/shard_map/ppermute | solution.py:16
  56.4 3.1 %collective-permute-start.59 = (bf16[2,4,128,128]{3,2,1,0:T(8,128)(2,1)S(1)}, bf16[2,4,128,128]{3,2,1,0:T(8,128)(2,1)S(1)}, u32[]{:S(2)}, u32[]{:S(2)}) collective-permute-start(bf16[2,4,128,128]{3,2,1,0:T(8,128)(2,1)S(1)} %collective-permute-done.58), channel_id=1, source_target_pairs={{0,48},{16,0},{32,16},{48,32},{1,49},{17,1},{33,17},{49,33},{2,50}... | collective-permute-start | bytes 786440 | tf_op jit(solution)/shard_map/ppermute | solution.py:16
  60.8 4.3 %collective-permute-done.60 = bf16[2,4,128,128]{3,2,1,0:T(8,128)(2,1)S(1)} collective-permute-done((bf16[2,4,128,128]{3,2,1,0:T(8,128)(2,1)S(1)}, bf16[2,4,128,128]{3,2,1,0:T(8,128)(2,1)S(1)}, u32[]{:S(2)}, u32[]{:S(2)}) %collective-permute-start.60) | collective-permute-done | bytes 262176 | tf_op jit(solution)/shard_map/ppermute | solution.py:16
  65.1 3.1 %collective-permute-start.44 = (bf16[2,4,128,128]{3,2,1,0:T(8,128)(2,1)S(1)}, bf16[2,4,128,128]{3,2,1,0:T(8,128)(2,1)S(1)}, u32[]{:S(2)}, u32[]{:S(2)}) collective-permute-start(bf16[2,4,128,128]{3,2,1,0:T(8,128)(2,1)S(1)} %collective-permute-done.43), channel_id=1, source_target_pairs={{0,48},{16,0},{32,16},{48,32},{1,49},{17,1},{33,17},{49,33},{2,50}... | collective-permute-start | bytes 786440 | tf_op jit(solution)/shard_map/ppermute | solution.py:16
  68.3 4.9 %collective-permute-done.45 = bf16[2,4,128,128]{3,2,1,0:T(8,128)(2,1)S(1)} collective-permute-done((bf16[2,4,128,128]{3,2,1,0:T(8,128)(2,1)S(1)}, bf16[2,4,128,128]{3,2,1,0:T(8,128)(2,1)S(1)}, u32[]{:S(2)}, u32[]{:S(2)}) %collective-permute-start.45) | collective-permute-done | bytes 262176 | tf_op jit(solution)/shard_map/ppermute | solution.py:16
  73.2 2.8 %collective-permute-start.29 = (bf16[2,4,128,128]{3,2,1,0:T(8,128)(2,1)S(1)}, bf16[2,4,128,128]{3,2,1,0:T(8,128)(2,1)S(1)}, u32[]{:S(2)}, u32[]{:S(2)}) collective-permute-start(bf16[2,4,128,128]{3,2,1,0:T(8,128)(2,1)S(1)} %collective-permute-done.28), channel_id=1, source_target_pairs={{0,48},{16,0},{32,16},{48,32},{1,49},{17,1},{33,17},{49,33},{2,50}... | collective-permute-start | bytes 786440 | tf_op jit(solution)/shard_map/ppermute | solution.py:16
  76.1 3.5 %collective-permute-done.30 = bf16[2,4,128,128]{3,2,1,0:T(8,128)(2,1)S(1)} collective-permute-done((bf16[2,4,128,128]{3,2,1,0:T(8,128)(2,1)S(1)}, bf16[2,4,128,128]{3,2,1,0:T(8,128)(2,1)S(1)}, u32[]{:S(2)}, u32[]{:S(2)}) %collective-permute-start.30) | collective-permute-done | bytes 262176 | tf_op jit(solution)/shard_map/ppermute | solution.py:16
  79.6 2.8 %collective-permute-start.8 = (bf16[2,4,128,128]{3,2,1,0:T(8,128)(2,1)S(1)}, bf16[2,4,128,128]{3,2,1,0:T(8,128)(2,1)S(1)}, u32[]{:S(2)}, u32[]{:S(2)}) collective-permute-start(bf16[2,4,128,128]{3,2,1,0:T(8,128)(2,1)S(1)} %collective-permute-done.7), channel_id=1, source_target_pairs={{0,48},{16,0},{32,16},{48,32},{1,49},{17,1},{33,17},{49,33},{2,50}... | collective-permute-start | bytes 786440 | tf_op jit(solution)/shard_map/ppermute | solution.py:16
  82.4 5.1 %collective-permute-done.9 = bf16[2,4,128,128]{3,2,1,0:T(8,128)(2,1)S(1)} collective-permute-done((bf16[2,4,128,128]{3,2,1,0:T(8,128)(2,1)S(1)}, bf16[2,4,128,128]{3,2,1,0:T(8,128)(2,1)S(1)}, u32[]{:S(2)}, u32[]{:S(2)}) %collective-permute-start.9) | collective-permute-done | bytes 262176 | tf_op jit(solution)/shard_map/ppermute | solution.py:16
  87.6 2.7 %collective-permute-start.62 = (bf16[4,128,128]{2,1,0:T(8,128)(2,1)S(1)}, bf16[4,128,128]{2,1,0:T(8,128)(2,1)S(1)}, u32[]{:S(2)}, u32[]{:S(2)}) collective-permute-start(bf16[4,128,128]{2,1,0:T(8,128)(2,1)S(1)} %slice_bitcast_fusion), channel_id=1, source_target_pairs={{0,48},{16,0},{32,16},{48,32},{1,49},{17,1},{33,17},{49,33},{2,50}... | collective-permute-start | bytes 393224 | tf_op jit(solution)/shard_map/ppermute | solution.py:16
  90.4 2.7 %collective-permute-start.42 = (bf16[4,128,128]{2,1,0:T(8,128)(2,1)S(1)}, bf16[4,128,128]{2,1,0:T(8,128)(2,1)S(1)}, u32[]{:S(2)}, u32[]{:S(2)}) collective-permute-start(bf16[4,128,128]{2,1,0:T(8,128)(2,1)S(1)} %slice_bitcast_fusion.6), channel_id=1, source_target_pairs={{0,48},{16,0},{32,16},{48,32},{1,49},{17,1},{33,17},{49,33},{2,50}... | collective-permute-start | bytes 393224 | tf_op jit(solution)/shard_map/ppermute | solution.py:16
  93.7 3.4 %collective-permute-start.47 = (bf16[4,128,128]{2,1,0:T(8,128)(2,1)S(1)}, bf16[4,128,128]{2,1,0:T(8,128)(2,1)S(1)}, u32[]{:S(2)}, u32[]{:S(2)}) collective-permute-start(bf16[4,128,128]{2,1,0:T(8,128)(2,1)S(1)} %slice_bitcast_fusion.4), channel_id=1, source_target_pairs={{0,48},{16,0},{32,16},{48,32},{1,49},{17,1},{33,17},{49,33},{2,50}... | collective-permute-start | bytes 393224 | tf_op jit(solution)/shard_map/ppermute | solution.py:16
  97.1 6.1 %shard_map.94 = (bf16[16,128,128]{2,1,0:T(8,128)(2,1)S(1)}, f32[16,128,128]{2,1,0:T(8,128)S(1)}, bf16[16,128,128]{2,1,0:T(8,128)(2,1)S(1)}, f32[16,128,128]{2,1,0:T(8,128)S(1)}) custom-call(s32[128]{0:T(128)S(1)} %fusion.66.src_ref, s32[128]{0:T(128)S(1)} %fusion.67.dst_ref, s32[2]{0:T(128)S(1)} %fusion.65.live_ref, ...), custom_call_target="tpu_custom_call" | custom-call | flops 2147483648 | bytes 8388608 | tf_op jit(solution)/shard_map/pallas_call | solution.py:121
  105.2 2.2 %collective-permute-start.32 = (bf16[4,128,128]{2,1,0:T(8,128)(2,1)S(1)}, bf16[4,128,128]{2,1,0:T(8,128)(2,1)S(1)}, u32[]{:S(2)}, u32[]{:S(2)}) collective-permute-start(bf16[4,128,128]{2,1,0:T(8,128)(2,1)S(1)} %slice_bitcast_fusion.8), channel_id=1, source_target_pairs={{0,48},{16,0},{32,16},{48,32},{1,49},{17,1},{33,17},{49,33},{2,50}... | collective-permute-start | bytes 393224 | tf_op jit(solution)/shard_map/ppermute | solution.py:16
  108.0 6.1 %shard_map.93 = (bf16[16,128,128]{2,1,0:T(8,128)(2,1)S(1)}, f32[16,128,128]{2,1,0:T(8,128)S(1)}, bf16[16,128,128]{2,1,0:T(8,128)(2,1)S(1)}, f32[16,128,128]{2,1,0:T(8,128)S(1)}) custom-call(s32[128]{0:T(128)S(1)} %fusion.66.src_ref, s32[128]{0:T(128)S(1)} %fusion.67.dst_ref, s32[2]{0:T(128)S(1)} %fusion.65.live_ref, ...), custom_call_target="tpu_custom_call" | custom-call | flops 2147483648 | bytes 8388608 | tf_op jit(solution)/shard_map/pallas_call | solution.py:121
  115.7 1.7 collective-permute-start.11
  117.5 6.1 %shard_map.92 = (bf16[16,128,128]{2,1,0:T(8,128)(2,1)S(1)}, f32[16,128,128]{2,1,0:T(8,128)S(1)}, bf16[16,128,128]{2,1,0:T(8,128)(2,1)S(1)}, f32[16,128,128]{2,1,0:T(8,128)S(1)}) custom-call(s32[128]{0:T(128)S(1)} %fusion.66.src_ref, s32[128]{0:T(128)S(1)} %fusion.67.dst_ref, s32[2]{0:T(128)S(1)} %fusion.65.live_ref, ...), custom_call_target="tpu_custom_call" | custom-call | flops 2147483648 | bytes 8388608 | tf_op jit(solution)/shard_map/pallas_call | solution.py:121
  123.6 3.2 %collective-permute-start.22 = (f32[2,4,128]{2,1,0:T(4,128)S(1)}, f32[2,4,128]{2,1,0:T(4,128)S(1)}, u32[]{:S(2)}, u32[]{:S(2)}) collective-permute-start(f32[2,4,128]{2,1,0:T(4,128)S(1)} %fusion.56), channel_id=1, source_target_pairs={{0,2},{2,0},{1,3},{3,1},{4,6},{6,4},{5,7},{7,5},{8,10},{10,8},{9,1... | collective-permute-start | bytes 12296 | tf_op jit(solution)/shard_map/ppermute | solution.py:16
  128.3 6.1 %shard_map.91 = (bf16[16,128,128]{2,1,0:T(8,128)(2,1)S(1)}, f32[16,128,128]{2,1,0:T(8,128)S(1)}, bf16[16,128,128]{2,1,0:T(8,128)(2,1)S(1)}, f32[16,128,128]{2,1,0:T(8,128)S(1)}) custom-call(s32[128]{0:T(128)S(1)} %fusion.66.src_ref, s32[128]{0:T(128)S(1)} %fusion.67.dst_ref, s32[2]{0:T(128)S(1)} %fusion.65.live_ref, ...), custom_call_target="tpu_custom_call" | custom-call | flops 2147483648 | bytes 8388608 | tf_op jit(solution)/shard_map/pallas_call | solution.py:121
  135.0 1.8 collective-permute-start.35
  139.7 3.9 %collective-permute-done.33 = bf16[16,128,128]{2,1,0:T(8,128)(2,1)S(1)} collective-permute-done((bf16[16,128,128]{2,1,0:T(8,128)(2,1)S(1)}, bf16[16,128,128]{2,1,0:T(8,128)(2,1)S(1)}, u32[]{:S(2)}, u32[]{:S(2)}) %collective-permute-start.33) | collective-permute-done | bytes 524320 | tf_op jit(solution)/shard_map/ppermute | solution.py:20
  144.8 4.6 %collective-permute-done.35 = bf16[16,128,128]{2,1,0:T(8,128)(2,1)S(1)} collective-permute-done((bf16[16,128,128]{2,1,0:T(8,128)(2,1)S(1)}, bf16[16,128,128]{2,1,0:T(8,128)(2,1)S(1)}, u32[]{:S(2)}, u32[]{:S(2)}) %collective-permute-start.35) | collective-permute-done | bytes 524320 | tf_op jit(solution)/shard_map/ppermute | solution.py:24
  149.5 11.1 %collective-permute-done.14 = bf16[16,128,128]{2,1,0:T(8,128)(2,1)S(1)} collective-permute-done((bf16[16,128,128]{2,1,0:T(8,128)(2,1)S(1)}, bf16[16,128,128]{2,1,0:T(8,128)(2,1)S(1)}, u32[]{:S(2)}, u32[]{:S(2)}) %collective-permute-start.14) | collective-permute-done | bytes 524320 | tf_op jit(solution)/shard_map/ppermute | solution.py:24
  162.5 3.7 %collective-permute-done.64 = bf16[8,128,128]{2,1,0:T(8,128)(2,1)S(1)} collective-permute-done((bf16[8,128,128]{2,1,0:T(8,128)(2,1)S(1)}, bf16[8,128,128]{2,1,0:T(8,128)(2,1)S(1)}, u32[]{:S(2)}, u32[]{:S(2)}) %collective-permute-start.64) | collective-permute-done | bytes 262176 | tf_op jit(solution)/shard_map/ppermute | solution.py:24
  167.8 4.0 %collective-permute-done.49 = bf16[8,128,128]{2,1,0:T(8,128)(2,1)S(1)} collective-permute-done((bf16[8,128,128]{2,1,0:T(8,128)(2,1)S(1)}, bf16[8,128,128]{2,1,0:T(8,128)(2,1)S(1)}, u32[]{:S(2)}, u32[]{:S(2)}) %collective-permute-start.49) | collective-permute-done | bytes 262176 | tf_op jit(solution)/shard_map/ppermute | solution.py:24
  171.9 2.0 collective-permute-start.13
  174.8 2.7 %collective-permute-done.34 = bf16[8,128,128]{2,1,0:T(8,128)(2,1)S(1)} collective-permute-done((bf16[8,128,128]{2,1,0:T(8,128)(2,1)S(1)}, bf16[8,128,128]{2,1,0:T(8,128)(2,1)S(1)}, u32[]{:S(2)}, u32[]{:S(2)}) %collective-permute-start.34) | collective-permute-done | bytes 262176 | tf_op jit(solution)/shard_map/ppermute | solution.py:24
  177.5 1.9 collective-permute-start.67
  181.4 1.9 collective-permute-start.37
  186.0 2.6 %fusion.1 = f32[512,1024]{1,0:T(8,128)} fusion(bf16[512,1024]{1,0:T(8,128)(2,1)S(1)} %copy-done.11, bf16[2048,1024]{1,0:T(8,128)(2,1)S(1)} %copy-done.6), kind=kOutput, calls=%fused_computation.6 | convolution fusion | flops 1073741824 | bytes 5242880 | tf_op jit(solution)/shard_map/dot_general | solution.py:224
  188.6 1.7 collective-permute-done.37
  190.3 2.8 %collective-permute-done.16 = bf16[2,4,128,128]{3,2,1,0:T(8,128)(2,1)} collective-permute-done((bf16[2,4,128,128]{3,2,1,0:T(8,128)(2,1)}, bf16[2,4,128,128]{3,2,1,0:T(8,128)(2,1)}, u32[]{:S(2)}, u32[]{:S(2)}) %collective-permute-start.16) | collective-permute-done | bytes 262176 | tf_op jit(solution)/shard_map/ppermute | solution.py:16
  193.2 1.9 fusion.22
  195.1 18.6 %collective-permute-start.53 = (bf16[512,128]{1,0:T(8,128)(2,1)S(1)}, bf16[512,128]{1,0:T(8,128)(2,1)S(1)}, u32[]{:S(2)}, u32[]{:S(2)}) collective-permute-start(bf16[512,128]{1,0:T(8,128)(2,1)S(1)} %bitcast.227), channel_id=1, source_target_pairs={{0,1},{1,0},{2,3},{3,2},{4,5},{5,4},{6,7},{7,6},{8,9},{9,8},{10,11... | collective-permute-start | bytes 393224 | tf_op jit(solution)/shard_map/ppermute | solution.py:16
  219.6 1.6 broadcast_divide_fusion
  (209 shorter events, 45.8 us)
Async XLA Ops:
  5.1 19.4 %collective-permute-start.2 = (bf16[512,512]{1,0:T(8,128)(2,1)}, bf16[512,512]{1,0:T(8,128)(2,1)}, u32[]{:S(2)}, u32[]{:S(2)}) collective-permute-start(bf16[512,512]{1,0:T(8,128)(2,1)} %constant_dynamic-slice_fusion.3), channel_id=1, source_target_pairs={{0,1},{1,0},{2,3},{3,2},{4,5},{5,4},{6,7},{7,6},{8,9},{9,8},{10,11... | collective-permute-start | bytes 1572872 | tf_op jit(solution)/shard_map/ppermute | solution.py:16
  8.6 85.1 %collective-permute-start.1 = (bf16[64,128,128]{2,1,0:T(8,128)(2,1)S(1)}, bf16[64,128,128]{2,1,0:T(8,128)(2,1)}, u32[]{:S(2)}, u32[]{:S(2)}) collective-permute-start(bf16[64,128,128]{2,1,0:T(8,128)(2,1)S(1)} %get-tuple-element.40.c_own), channel_id=1, source_target_pairs={{0,1},{1,0},{2,3},{3,2},{4,5},{5,4},{6,7},{7,6},{8,9},{9,8},{10,11... | collective-permute-start | bytes 6291464 | tf_op jit(solution)/shard_map/ppermute | solution.py:16
  26.6 24.1 %collective-permute-start.58 = (bf16[2,4,128,128]{3,2,1,0:T(8,128)(2,1)S(1)}, bf16[2,4,128,128]{3,2,1,0:T(8,128)(2,1)S(1)}, u32[]{:S(2)}, u32[]{:S(2)}) collective-permute-start(bf16[2,4,128,128]{3,2,1,0:T(8,128)(2,1)S(1)} %pad_maximum_fusion.7), channel_id=1, source_target_pairs={{0,64},{64,0},{1,65},{65,1},{2,66},{66,2},{3,67},{67,3},{4,68},{68... | collective-permute-start | bytes 786440 | tf_op jit(solution)/shard_map/ppermute | solution.py:16
  29.7 29.8 %collective-permute-start.43 = (bf16[2,4,128,128]{3,2,1,0:T(8,128)(2,1)S(1)}, bf16[2,4,128,128]{3,2,1,0:T(8,128)(2,1)S(1)}, u32[]{:S(2)}, u32[]{:S(2)}) collective-permute-start(bf16[2,4,128,128]{3,2,1,0:T(8,128)(2,1)S(1)} %pad_maximum_fusion.6), channel_id=1, source_target_pairs={{0,64},{64,0},{1,65},{65,1},{2,66},{66,2},{3,67},{67,3},{4,68},{68... | collective-permute-start | bytes 786440 | tf_op jit(solution)/shard_map/ppermute | solution.py:16
  47.5 8.7 %collective-permute-start.4 = (bf16[2,4,128,128]{3,2,1,0:T(8,128)(2,1)S(1)}, bf16[2,4,128,128]{3,2,1,0:T(8,128)(2,1)S(1)}, u32[]{:S(2)}, u32[]{:S(2)}) collective-permute-start(bf16[2,4,128,128]{3,2,1,0:T(8,128)(2,1)S(1)} %pad_maximum_fusion.4), channel_id=1, source_target_pairs={{0,16},{16,32},{32,48},{48,0},{1,17},{17,33},{33,49},{49,1},{2,18}... | collective-permute-start | bytes 786440 | tf_op jit(solution)/shard_map/ppermute | solution.py:16
  48.0 8.4 %collective-permute-start.3 = (bf16[2,4,128,128]{3,2,1,0:T(8,128)(2,1)S(1)}, bf16[2,4,128,128]{3,2,1,0:T(8,128)(2,1)S(1)}, u32[]{:S(2)}, u32[]{:S(2)}) collective-permute-start(bf16[2,4,128,128]{3,2,1,0:T(8,128)(2,1)S(1)} %pad_maximum_fusion.4), channel_id=1, source_target_pairs={{0,48},{16,0},{32,16},{48,32},{1,49},{17,1},{33,17},{49,33},{2,50}... | collective-permute-start | bytes 786440 | tf_op jit(solution)/shard_map/ppermute | solution.py:16
  50.6 17.6 %collective-permute-start.28 = (bf16[2,4,128,128]{3,2,1,0:T(8,128)(2,1)S(1)}, bf16[2,4,128,128]{3,2,1,0:T(8,128)(2,1)S(1)}, u32[]{:S(2)}, u32[]{:S(2)}) collective-permute-start(bf16[2,4,128,128]{3,2,1,0:T(8,128)(2,1)S(1)} %pad_maximum_fusion.5), channel_id=1, source_target_pairs={{0,64},{64,0},{1,65},{65,1},{2,66},{66,2},{3,67},{67,3},{4,68},{68... | collective-permute-start | bytes 786440 | tf_op jit(solution)/shard_map/ppermute | solution.py:16
  56.1 9.0 %collective-permute-start.60 = (bf16[2,4,128,128]{3,2,1,0:T(8,128)(2,1)S(1)}, bf16[2,4,128,128]{3,2,1,0:T(8,128)(2,1)S(1)}, u32[]{:S(2)}, u32[]{:S(2)}) collective-permute-start(bf16[2,4,128,128]{3,2,1,0:T(8,128)(2,1)S(1)} %collective-permute-done.58), channel_id=1, source_target_pairs={{0,16},{16,32},{32,48},{48,0},{1,17},{17,33},{33,49},{49,1},{2,18}... | collective-permute-start | bytes 786440 | tf_op jit(solution)/shard_map/ppermute | solution.py:16
  56.4 8.8 %collective-permute-start.59 = (bf16[2,4,128,128]{3,2,1,0:T(8,128)(2,1)S(1)}, bf16[2,4,128,128]{3,2,1,0:T(8,128)(2,1)S(1)}, u32[]{:S(2)}, u32[]{:S(2)}) collective-permute-start(bf16[2,4,128,128]{3,2,1,0:T(8,128)(2,1)S(1)} %collective-permute-done.58), channel_id=1, source_target_pairs={{0,48},{16,0},{32,16},{48,32},{1,49},{17,1},{33,17},{49,33},{2,50}... | collective-permute-start | bytes 786440 | tf_op jit(solution)/shard_map/ppermute | solution.py:16
  59.5 16.5 %collective-permute-start.7 = (bf16[2,4,128,128]{3,2,1,0:T(8,128)(2,1)S(1)}, bf16[2,4,128,128]{3,2,1,0:T(8,128)(2,1)S(1)}, u32[]{:S(2)}, u32[]{:S(2)}) collective-permute-start(bf16[2,4,128,128]{3,2,1,0:T(8,128)(2,1)S(1)} %pad_maximum_fusion.4), channel_id=1, source_target_pairs={{0,64},{64,0},{1,65},{65,1},{2,66},{66,2},{3,67},{67,3},{4,68},{68... | collective-permute-start | bytes 786440 | tf_op jit(solution)/shard_map/ppermute | solution.py:16
  65.1 8.0 %collective-permute-start.45 = (bf16[2,4,128,128]{3,2,1,0:T(8,128)(2,1)S(1)}, bf16[2,4,128,128]{3,2,1,0:T(8,128)(2,1)S(1)}, u32[]{:S(2)}, u32[]{:S(2)}) collective-permute-start(bf16[2,4,128,128]{3,2,1,0:T(8,128)(2,1)S(1)} %collective-permute-done.43), channel_id=1, source_target_pairs={{0,16},{16,32},{32,48},{48,0},{1,17},{17,33},{33,49},{49,1},{2,18}... | collective-permute-start | bytes 786440 | tf_op jit(solution)/shard_map/ppermute | solution.py:16
  65.1 8.0 %collective-permute-start.44 = (bf16[2,4,128,128]{3,2,1,0:T(8,128)(2,1)S(1)}, bf16[2,4,128,128]{3,2,1,0:T(8,128)(2,1)S(1)}, u32[]{:S(2)}, u32[]{:S(2)}) collective-permute-start(bf16[2,4,128,128]{3,2,1,0:T(8,128)(2,1)S(1)} %collective-permute-done.43), channel_id=1, source_target_pairs={{0,48},{16,0},{32,16},{48,32},{1,49},{17,1},{33,17},{49,33},{2,50}... | collective-permute-start | bytes 786440 | tf_op jit(solution)/shard_map/ppermute | solution.py:16
  68.2 22.1 %collective-permute-start.56 = (bf16[4,128,128]{2,1,0:T(8,128)(2,1)S(1)}, bf16[4,128,128]{2,1,0:T(8,128)(2,1)S(1)}, u32[]{:S(2)}, u32[]{:S(2)}) collective-permute-start(bf16[4,128,128]{2,1,0:T(8,128)(2,1)S(1)} %slice_bitcast_fusion.3), channel_id=1, source_target_pairs={{0,16},{16,32},{32,48},{48,0},{1,17},{17,33},{33,49},{49,1},{2,18}... | collective-permute-start | bytes 393224 | tf_op jit(solution)/shard_map/ppermute | solution.py:16
  76.0 14.4 %collective-permute-start.57 = (bf16[4,128,128]{2,1,0:T(8,128)(2,1)S(1)}, bf16[4,128,128]{2,1,0:T(8,128)(2,1)S(1)}, u32[]{:S(2)}, u32[]{:S(2)}) collective-permute-start(bf16[4,128,128]{2,1,0:T(8,128)(2,1)S(1)} %slice_bitcast_fusion.2), channel_id=1, source_target_pairs={{0,48},{16,0},{32,16},{48,32},{1,49},{17,1},{33,17},{49,33},{2,50}... | collective-permute-start | bytes 393224 | tf_op jit(solution)/shard_map/ppermute | solution.py:16
  90.3 12.9 %collective-permute-start.41 = (bf16[4,128,128]{2,1,0:T(8,128)(2,1)S(1)}, bf16[4,128,128]{2,1,0:T(8,128)(2,1)S(1)}, u32[]{:S(2)}, u32[]{:S(2)}) collective-permute-start(bf16[4,128,128]{2,1,0:T(8,128)(2,1)S(1)} %slice_bitcast_fusion.7), channel_id=1, source_target_pairs={{0,16},{16,32},{32,48},{48,0},{1,17},{17,33},{33,49},{49,1},{2,18}... | collective-permute-start | bytes 393224 | tf_op jit(solution)/shard_map/ppermute | solution.py:16
  90.4 13.4 %collective-permute-start.42 = (bf16[4,128,128]{2,1,0:T(8,128)(2,1)S(1)}, bf16[4,128,128]{2,1,0:T(8,128)(2,1)S(1)}, u32[]{:S(2)}, u32[]{:S(2)}) collective-permute-start(bf16[4,128,128]{2,1,0:T(8,128)(2,1)S(1)} %slice_bitcast_fusion.6), channel_id=1, source_target_pairs={{0,48},{16,0},{32,16},{48,32},{1,49},{17,1},{33,17},{49,33},{2,50}... | collective-permute-start | bytes 393224 | tf_op jit(solution)/shard_map/ppermute | solution.py:16
  93.1 11.7 %collective-permute-start.26 = (bf16[4,128,128]{2,1,0:T(8,128)(2,1)S(1)}, bf16[4,128,128]{2,1,0:T(8,128)(2,1)S(1)}, u32[]{:S(2)}, u32[]{:S(2)}) collective-permute-start(bf16[4,128,128]{2,1,0:T(8,128)(2,1)S(1)} %slice_bitcast_fusion.11), channel_id=1, source_target_pairs={{0,16},{16,32},{32,48},{48,0},{1,17},{17,33},{33,49},{49,1},{2,18}... | collective-permute-start | bytes 393224 | tf_op jit(solution)/shard_map/ppermute | solution.py:16
  93.7 11.5 %collective-permute-start.46 = (bf16[4,128,128]{2,1,0:T(8,128)(2,1)S(1)}, bf16[4,128,128]{2,1,0:T(8,128)(2,1)S(1)}, u32[]{:S(2)}, u32[]{:S(2)}) collective-permute-start(bf16[4,128,128]{2,1,0:T(8,128)(2,1)S(1)} %slice_bitcast_fusion.5), channel_id=1, source_target_pairs={{0,16},{16,32},{32,48},{48,0},{1,17},{17,33},{33,49},{49,1},{2,18}... | collective-permute-start | bytes 393224 | tf_op jit(solution)/shard_map/ppermute | solution.py:16
  93.7 13.8 %collective-permute-start.47 = (bf16[4,128,128]{2,1,0:T(8,128)(2,1)S(1)}, bf16[4,128,128]{2,1,0:T(8,128)(2,1)S(1)}, u32[]{:S(2)}, u32[]{:S(2)}) collective-permute-start(bf16[4,128,128]{2,1,0:T(8,128)(2,1)S(1)} %slice_bitcast_fusion.4), channel_id=1, source_target_pairs={{0,48},{16,0},{32,16},{48,32},{1,49},{17,1},{33,17},{49,33},{2,50}... | collective-permute-start | bytes 393224 | tf_op jit(solution)/shard_map/ppermute | solution.py:16
  103.3 10.9 %collective-permute-start.27 = (bf16[4,128,128]{2,1,0:T(8,128)(2,1)S(1)}, bf16[4,128,128]{2,1,0:T(8,128)(2,1)S(1)}, u32[]{:S(2)}, u32[]{:S(2)}) collective-permute-start(bf16[4,128,128]{2,1,0:T(8,128)(2,1)S(1)} %slice_bitcast_fusion.10), channel_id=1, source_target_pairs={{0,48},{16,0},{32,16},{48,32},{1,49},{17,1},{33,17},{49,33},{2,50}... | collective-permute-start | bytes 393224 | tf_op jit(solution)/shard_map/ppermute | solution.py:16
  103.9 10.8 %collective-permute-start.5 = (bf16[4,128,128]{2,1,0:T(8,128)(2,1)S(1)}, bf16[4,128,128]{2,1,0:T(8,128)(2,1)S(1)}, u32[]{:S(2)}, u32[]{:S(2)}) collective-permute-start(bf16[4,128,128]{2,1,0:T(8,128)(2,1)S(1)} %slice_bitcast_fusion.15), channel_id=1, source_target_pairs={{0,16},{16,32},{32,48},{48,0},{1,17},{17,33},{33,49},{49,1},{2,18}... | collective-permute-start | bytes 393224 | tf_op jit(solution)/shard_map/ppermute | solution.py:16
  104.8 10.9 %collective-permute-start.31 = (bf16[4,128,128]{2,1,0:T(8,128)(2,1)S(1)}, bf16[4,128,128]{2,1,0:T(8,128)(2,1)S(1)}, u32[]{:S(2)}, u32[]{:S(2)}) collective-permute-start(bf16[4,128,128]{2,1,0:T(8,128)(2,1)S(1)} %slice_bitcast_fusion.9), channel_id=1, source_target_pairs={{0,16},{16,32},{32,48},{48,0},{1,17},{17,33},{33,49},{49,1},{2,18}... | collective-permute-start | bytes 393224 | tf_op jit(solution)/shard_map/ppermute | solution.py:16
  105.2 12.1 %collective-permute-start.32 = (bf16[4,128,128]{2,1,0:T(8,128)(2,1)S(1)}, bf16[4,128,128]{2,1,0:T(8,128)(2,1)S(1)}, u32[]{:S(2)}, u32[]{:S(2)}) collective-permute-start(bf16[4,128,128]{2,1,0:T(8,128)(2,1)S(1)} %slice_bitcast_fusion.8), channel_id=1, source_target_pairs={{0,48},{16,0},{32,16},{48,32},{1,49},{17,1},{33,17},{49,33},{2,50}... | collective-permute-start | bytes 393224 | tf_op jit(solution)/shard_map/ppermute | solution.py:16
  107.5 26.9 %collective-permute-start.63 = (bf16[16,128,128]{2,1,0:T(8,128)(2,1)S(1)}, bf16[16,128,128]{2,1,0:T(8,128)(2,1)S(1)}, u32[]{:S(2)}, u32[]{:S(2)}) collective-permute-start(bf16[16,128,128]{2,1,0:T(8,128)(2,1)S(1)} %get-tuple-element.33), channel_id=1, source_target_pairs={{0,4},{4,0},{8,12},{12,8},{1,5},{5,1},{9,13},{13,9},{2,6},{6,2},{1... | collective-permute-start | bytes 1572872 | tf_op jit(solution)/shard_map/ppermute | solution.py:20
  114.2 9.4 %collective-permute-start.6 = (bf16[4,128,128]{2,1,0:T(8,128)(2,1)S(1)}, bf16[4,128,128]{2,1,0:T(8,128)(2,1)S(1)}, u32[]{:S(2)}, u32[]{:S(2)}) collective-permute-start(bf16[4,128,128]{2,1,0:T(8,128)(2,1)S(1)} %slice_bitcast_fusion.14), channel_id=1, source_target_pairs={{0,48},{16,0},{32,16},{48,32},{1,49},{17,1},{33,17},{49,33},{2,50}... | collective-permute-start | bytes 393224 | tf_op jit(solution)/shard_map/ppermute | solution.py:16
  114.7 12.1 %collective-permute-start.10 = (bf16[4,128,128]{2,1,0:T(8,128)(2,1)S(1)}, bf16[4,128,128]{2,1,0:T(8,128)(2,1)S(1)}, u32[]{:S(2)}, u32[]{:S(2)}) collective-permute-start(bf16[4,128,128]{2,1,0:T(8,128)(2,1)S(1)} %slice_bitcast_fusion.13), channel_id=1, source_target_pairs={{0,16},{16,32},{32,48},{48,0},{1,17},{17,33},{33,49},{49,1},{2,18}... | collective-permute-start | bytes 393224 | tf_op jit(solution)/shard_map/ppermute | solution.py:16
  115.7 11.3 %collective-permute-start.11 = (bf16[4,128,128]{2,1,0:T(8,128)(2,1)S(1)}, bf16[4,128,128]{2,1,0:T(8,128)(2,1)S(1)}, u32[]{:S(2)}, u32[]{:S(2)}) collective-permute-start(bf16[4,128,128]{2,1,0:T(8,128)(2,1)S(1)} %slice_bitcast_fusion.12), channel_id=1, source_target_pairs={{0,48},{16,0},{32,16},{48,32},{1,49},{17,1},{33,17},{49,33},{2,50}... | collective-permute-start | bytes 393224 | tf_op jit(solution)/shard_map/ppermute | solution.py:16
  117.4 17.6 %collective-permute-start.65 = (bf16[16,128,128]{2,1,0:T(8,128)(2,1)S(1)}, bf16[16,128,128]{2,1,0:T(8,128)(2,1)S(1)}, u32[]{:S(2)}, u32[]{:S(2)}) collective-permute-start(bf16[16,128,128]{2,1,0:T(8,128)(2,1)S(1)} %get-tuple-element.35), channel_id=1, source_target_pairs={{0,12},{4,8},{8,4},{12,0},{1,13},{5,9},{9,5},{13,1},{2,14},{6,10},... | collective-permute-start | bytes 1572872 | tf_op jit(solution)/shard_map/ppermute | solution.py:24
  123.6 65.0 %collective-permute-start.22 = (f32[2,4,128]{2,1,0:T(4,128)S(1)}, f32[2,4,128]{2,1,0:T(4,128)S(1)}, u32[]{:S(2)}, u32[]{:S(2)}) collective-permute-start(f32[2,4,128]{2,1,0:T(4,128)S(1)} %fusion.56), channel_id=1, source_target_pairs={{0,2},{2,0},{1,3},{3,1},{4,6},{6,4},{5,7},{7,5},{8,10},{10,8},{9,1... | collective-permute-start | bytes 12296 | tf_op jit(solution)/shard_map/ppermute | solution.py:16
  126.8 11.2 %collective-permute-start.48 = (bf16[16,128,128]{2,1,0:T(8,128)(2,1)S(1)}, bf16[16,128,128]{2,1,0:T(8,128)(2,1)S(1)}, u32[]{:S(2)}, u32[]{:S(2)}) collective-permute-start(bf16[16,128,128]{2,1,0:T(8,128)(2,1)S(1)} %get-tuple-element.29), channel_id=1, source_target_pairs={{0,4},{4,0},{8,12},{12,8},{1,5},{5,1},{9,13},{13,9},{2,6},{6,2},{1... | collective-permute-start | bytes 1572872 | tf_op jit(solution)/shard_map/ppermute | solution.py:20
  127.0 12.0 %collective-permute-start.50 = (bf16[16,128,128]{2,1,0:T(8,128)(2,1)S(1)}, bf16[16,128,128]{2,1,0:T(8,128)(2,1)S(1)}, u32[]{:S(2)}, u32[]{:S(2)}) collective-permute-start(bf16[16,128,128]{2,1,0:T(8,128)(2,1)S(1)} %get-tuple-element.31), channel_id=1, source_target_pairs={{0,12},{4,8},{8,4},{12,0},{1,13},{5,9},{9,5},{13,1},{2,14},{6,10},... | collective-permute-start | bytes 1572872 | tf_op jit(solution)/shard_map/ppermute | solution.py:24
  134.4 9.1 %collective-permute-start.33 = (bf16[16,128,128]{2,1,0:T(8,128)(2,1)S(1)}, bf16[16,128,128]{2,1,0:T(8,128)(2,1)S(1)}, u32[]{:S(2)}, u32[]{:S(2)}) collective-permute-start(bf16[16,128,128]{2,1,0:T(8,128)(2,1)S(1)} %get-tuple-element.25), channel_id=1, source_target_pairs={{0,4},{4,0},{8,12},{12,8},{1,5},{5,1},{9,13},{13,9},{2,6},{6,2},{1... | collective-permute-start | bytes 1572872 | tf_op jit(solution)/shard_map/ppermute | solution.py:20
  135.0 14.4 %collective-permute-start.35 = (bf16[16,128,128]{2,1,0:T(8,128)(2,1)S(1)}, bf16[16,128,128]{2,1,0:T(8,128)(2,1)S(1)}, u32[]{:S(2)}, u32[]{:S(2)}) collective-permute-start(bf16[16,128,128]{2,1,0:T(8,128)(2,1)S(1)} %get-tuple-element.27), channel_id=1, source_target_pairs={{0,12},{4,8},{8,4},{12,0},{1,13},{5,9},{9,5},{13,1},{2,14},{6,10},... | collective-permute-start | bytes 1572872 | tf_op jit(solution)/shard_map/ppermute | solution.py:24
  138.0 22.7 %collective-permute-start.14 = (bf16[16,128,128]{2,1,0:T(8,128)(2,1)S(1)}, bf16[16,128,128]{2,1,0:T(8,128)(2,1)S(1)}, u32[]{:S(2)}, u32[]{:S(2)}) collective-permute-start(bf16[16,128,128]{2,1,0:T(8,128)(2,1)S(1)} %get-tuple-element.23), channel_id=1, source_target_pairs={{0,12},{4,8},{8,4},{12,0},{1,13},{5,9},{9,5},{13,1},{2,14},{6,10},... | collective-permute-start | bytes 1572872 | tf_op jit(solution)/shard_map/ppermute | solution.py:24
  138.9 23.2 %collective-permute-start.12 = (bf16[16,128,128]{2,1,0:T(8,128)(2,1)S(1)}, bf16[16,128,128]{2,1,0:T(8,128)(2,1)S(1)}, u32[]{:S(2)}, u32[]{:S(2)}) collective-permute-start(bf16[16,128,128]{2,1,0:T(8,128)(2,1)S(1)} %get-tuple-element.21), channel_id=1, source_target_pairs={{0,4},{4,0},{8,12},{12,8},{1,5},{5,1},{9,13},{13,9},{2,6},{6,2},{1... | collective-permute-start | bytes 1572872 | tf_op jit(solution)/shard_map/ppermute | solution.py:20
  143.6 22.7 %collective-permute-start.64 = (bf16[8,128,128]{2,1,0:T(8,128)(2,1)S(1)}, bf16[8,128,128]{2,1,0:T(8,128)(2,1)S(1)}, u32[]{:S(2)}, u32[]{:S(2)}) collective-permute-start(bf16[8,128,128]{2,1,0:T(8,128)(2,1)S(1)} %slice.501), channel_id=1, source_target_pairs={{0,12},{4,8},{8,4},{12,0},{1,13},{5,9},{9,5},{13,1},{2,14},{6,10},... | collective-permute-start | bytes 786440 | tf_op jit(solution)/shard_map/ppermute | solution.py:24
  149.4 18.3 %collective-permute-start.66 = (bf16[8,128,128]{2,1,0:T(8,128)(2,1)S(1)}, bf16[8,128,128]{2,1,0:T(8,128)(2,1)S(1)}, u32[]{:S(2)}, u32[]{:S(2)}) collective-permute-start(bf16[8,128,128]{2,1,0:T(8,128)(2,1)S(1)} %slice.500), channel_id=1, source_target_pairs={{0,4},{4,0},{8,12},{12,8},{1,5},{5,1},{9,13},{13,9},{2,6},{6,2},{1... | collective-permute-start | bytes 786440 | tf_op jit(solution)/shard_map/ppermute | solution.py:20
  160.6 11.2 %collective-permute-start.49 = (bf16[8,128,128]{2,1,0:T(8,128)(2,1)S(1)}, bf16[8,128,128]{2,1,0:T(8,128)(2,1)S(1)}, u32[]{:S(2)}, u32[]{:S(2)}) collective-permute-start(bf16[8,128,128]{2,1,0:T(8,128)(2,1)S(1)} %slice.503), channel_id=1, source_target_pairs={{0,12},{4,8},{8,4},{12,0},{1,13},{5,9},{9,5},{13,1},{2,14},{6,10},... | collective-permute-start | bytes 786440 | tf_op jit(solution)/shard_map/ppermute | solution.py:24
  162.1 9.8 %collective-permute-start.51 = (bf16[8,128,128]{2,1,0:T(8,128)(2,1)S(1)}, bf16[8,128,128]{2,1,0:T(8,128)(2,1)S(1)}, u32[]{:S(2)}, u32[]{:S(2)}) collective-permute-start(bf16[8,128,128]{2,1,0:T(8,128)(2,1)S(1)} %slice.502), channel_id=1, source_target_pairs={{0,4},{4,0},{8,12},{12,8},{1,5},{5,1},{9,13},{13,9},{2,6},{6,2},{1... | collective-permute-start | bytes 786440 | tf_op jit(solution)/shard_map/ppermute | solution.py:20
  166.3 11.2 %collective-permute-start.34 = (bf16[8,128,128]{2,1,0:T(8,128)(2,1)S(1)}, bf16[8,128,128]{2,1,0:T(8,128)(2,1)S(1)}, u32[]{:S(2)}, u32[]{:S(2)}) collective-permute-start(bf16[8,128,128]{2,1,0:T(8,128)(2,1)S(1)} %slice.505), channel_id=1, source_target_pairs={{0,12},{4,8},{8,4},{12,0},{1,13},{5,9},{9,5},{13,1},{2,14},{6,10},... | collective-permute-start | bytes 786440 | tf_op jit(solution)/shard_map/ppermute | solution.py:24
  167.7 11.8 %collective-permute-start.36 = (bf16[8,128,128]{2,1,0:T(8,128)(2,1)S(1)}, bf16[8,128,128]{2,1,0:T(8,128)(2,1)S(1)}, u32[]{:S(2)}, u32[]{:S(2)}) collective-permute-start(bf16[8,128,128]{2,1,0:T(8,128)(2,1)S(1)} %slice.504), channel_id=1, source_target_pairs={{0,4},{4,0},{8,12},{12,8},{1,5},{5,1},{9,13},{13,9},{2,6},{6,2},{1... | collective-permute-start | bytes 786440 | tf_op jit(solution)/shard_map/ppermute | solution.py:20
  171.9 9.5 %collective-permute-start.15 = (bf16[8,128,128]{2,1,0:T(8,128)(2,1)S(1)}, bf16[8,128,128]{2,1,0:T(8,128)(2,1)S(1)}, u32[]{:S(2)}, u32[]{:S(2)}) collective-permute-start(bf16[8,128,128]{2,1,0:T(8,128)(2,1)S(1)} %slice.506), channel_id=1, source_target_pairs={{0,4},{4,0},{8,12},{12,8},{1,5},{5,1},{9,13},{13,9},{2,6},{6,2},{1... | collective-permute-start | bytes 786440 | tf_op jit(solution)/shard_map/ppermute | solution.py:20
  171.9 11.4 %collective-permute-start.13 = (bf16[8,128,128]{2,1,0:T(8,128)(2,1)S(1)}, bf16[8,128,128]{2,1,0:T(8,128)(2,1)S(1)}, u32[]{:S(2)}, u32[]{:S(2)}) collective-permute-start(bf16[8,128,128]{2,1,0:T(8,128)(2,1)S(1)} %slice.507), channel_id=1, source_target_pairs={{0,12},{4,8},{8,4},{12,0},{1,13},{5,9},{9,5},{13,1},{2,14},{6,10},... | collective-permute-start | bytes 786440 | tf_op jit(solution)/shard_map/ppermute | solution.py:24
  177.5 11.1 %collective-permute-start.67 = (bf16[2,4,128,128]{3,2,1,0:T(8,128)(2,1)}, bf16[2,4,128,128]{3,2,1,0:T(8,128)(2,1)}, u32[]{:S(2)}, u32[]{:S(2)}) collective-permute-start(bf16[2,4,128,128]{3,2,1,0:T(8,128)(2,1)} %fusion.30), channel_id=1, source_target_pairs={{0,2},{2,0},{1,3},{3,1},{4,6},{6,4},{5,7},{7,5},{8,10},{10,8},{9,1... | collective-permute-start | bytes 786440 | tf_op jit(solution)/shard_map/ppermute | solution.py:16
  179.5 9.2 %collective-permute-start.52 = (bf16[2,4,128,128]{3,2,1,0:T(8,128)(2,1)S(1)}, bf16[2,4,128,128]{3,2,1,0:T(8,128)(2,1)}, u32[]{:S(2)}, u32[]{:S(2)}) collective-permute-start(bf16[2,4,128,128]{3,2,1,0:T(8,128)(2,1)S(1)} %fusion.29), channel_id=1, source_target_pairs={{0,2},{2,0},{1,3},{3,1},{4,6},{6,4},{5,7},{7,5},{8,10},{10,8},{9,1... | collective-permute-start | bytes 786440 | tf_op jit(solution)/shard_map/ppermute | solution.py:16
  181.4 8.9 %collective-permute-start.37 = (bf16[2,4,128,128]{3,2,1,0:T(8,128)(2,1)}, bf16[2,4,128,128]{3,2,1,0:T(8,128)(2,1)}, u32[]{:S(2)}, u32[]{:S(2)}) collective-permute-start(bf16[2,4,128,128]{3,2,1,0:T(8,128)(2,1)} %fusion.28), channel_id=1, source_target_pairs={{0,2},{2,0},{1,3},{3,1},{4,6},{6,4},{5,7},{7,5},{8,10},{10,8},{9,1... | collective-permute-start | bytes 786440 | tf_op jit(solution)/shard_map/ppermute | solution.py:16
  184.9 8.2 %collective-permute-start.16 = (bf16[2,4,128,128]{3,2,1,0:T(8,128)(2,1)}, bf16[2,4,128,128]{3,2,1,0:T(8,128)(2,1)}, u32[]{:S(2)}, u32[]{:S(2)}) collective-permute-start(bf16[2,4,128,128]{3,2,1,0:T(8,128)(2,1)} %fusion.27), channel_id=1, source_target_pairs={{0,2},{2,0},{1,3},{3,1},{4,6},{6,4},{5,7},{7,5},{8,10},{10,8},{9,1... | collective-permute-start | bytes 786440 | tf_op jit(solution)/shard_map/ppermute | solution.py:16
  195.1 21.6 %collective-permute-start.53 = (bf16[512,128]{1,0:T(8,128)(2,1)S(1)}, bf16[512,128]{1,0:T(8,128)(2,1)S(1)}, u32[]{:S(2)}, u32[]{:S(2)}) collective-permute-start(bf16[512,128]{1,0:T(8,128)(2,1)S(1)} %bitcast.227), channel_id=1, source_target_pairs={{0,1},{1,0},{2,3},{3,2},{4,5},{5,4},{6,7},{7,6},{8,9},{9,8},{10,11... | collective-permute-start | bytes 393224 | tf_op jit(solution)/shard_map/ppermute | solution.py:16
  (33 other events, 166.3 us)

commit v2 on v1

v2 whole, which is shorter than its diff:
```python
import jax
import jax.numpy as jnp
from jax import lax
from jax.experimental import pallas as pl
from jax.experimental.pallas import tpu as pltpu
from jax.sharding import Mesh, PartitionSpec as P

AXES = ("x_lo", "y", "z", "x_hi", "core")
SIZES = (2, 4, 4, 2, 2)
CHUNKS = 4
GROUP = 8


def swap(x, axis):
    return lax.ppermute(x, axis, [(0, 1), (1, 0)])


def step(x, axis, second):
    pairs = []
    for i in range(4):
        for c in range(2):
            to = i ^ 1 if c == second else 3 - i
            pairs.append((i * 2 + c, to * 2 + c))
    return lax.ppermute(x, (axis, "core"), pairs)


def after(x, *earlier):
    return lax.optimization_barrier((x, *earlier))[0]


def ring_slot(place, here, core):
    first = jnp.where(core == 0, here ^ 1, 3 - here)
    second = jnp.where(core == 0, 3 - here, here ^ 1)
    return jnp.where(
        place == here, 0, jnp.where(place == first, 1, jnp.where(place == second, 2, 3))
    )


def tile_kernel(src_ref, dst_ref, live_ref, c_own, c_other, pieces_ref, near, far, *refs):
    send, pass_on, stay, panel, acc, sems = refs[-6:]
    copies = [
        pltpu.make_async_copy(near, panel.at[pl.ds(0, 32)], sems.at[0]),
        pltpu.make_async_copy(far, panel.at[pl.ds(32, 32)], sems.at[1]),
    ]
    for copy in copies:
        copy.start()

    @pl.loop(0, 64)
    def _(i):
        acc[i] = jnp.zeros(acc.shape[1:], jnp.float32)

    for copy in copies:
        copy.wait()

    slots, tile = c_own.shape[:2]
    for q, counts in enumerate((c_own, c_other)):

        def body(g, carry, q=q, counts=counts):
            terms = []
            for i in range(GROUP):
                s = g * GROUP + i
                terms.append(
                    jnp.dot(
                        counts[s],
                        panel[src_ref[q * slots + s]],
                        preferred_element_type=jnp.float32,
                    )
                )
            for i in range(GROUP):
                at = dst_ref[q * slots + g * GROUP + i]
                acc[at] = acc[at] + terms[i]
            return carry

        lax.fori_loop(0, (live_ref[q] + GROUP - 1) // GROUP, body, 0)

    size = stay.shape[0] // 2
    extra = size - 8 * tile
    for part in range(8):
        out = (send, send, send, send, pass_on, pass_on, stay, stay)[part]
        base = (part if part < 4 else part % 2) * size

        @pl.loop(0, 8)
        def _(i, part=part, out=out, base=base):
            at = pl.multiple_of(base + i * tile, 16)
            out[pl.ds(at, tile)] = acc[part * 8 + i].astype(out.dtype)

        if extra:
            out[pl.ds(base + 8 * tile, extra)] = pieces_ref[pl.ds(part * extra, extra)].astype(
                out.dtype
            )


def tile_sums(src, dst, live, c_own, c_other, pieces, with_pieces, near, far, earlier):
    tile, w = near.shape[-2:]
    any_spec = pl.BlockSpec(memory_space=pl.ANY)
    vmem = pl.BlockSpec(memory_space=pltpu.VMEM)
    smem = pl.BlockSpec(memory_space=pltpu.SMEM)
    slots = c_own.shape[0]
    size = 8 * tile + (pieces.shape[0] // 8 if with_pieces else 0)
    return pl.pallas_call(
        tile_kernel,
        out_shape=(
            jax.ShapeDtypeStruct((4 * size, w), jnp.bfloat16),
            jax.ShapeDtypeStruct((2 * size, w), jnp.float32),
            jax.ShapeDtypeStruct((2 * size, w), jnp.float32),
        ),
        in_specs=[smem] * 3 + [vmem] * 3 + [any_spec] * (2 + len(earlier)),
        out_specs=(vmem,) * 3,
        scratch_shapes=[
            pltpu.VMEM((64, tile, w), jnp.bfloat16),
            pltpu.VMEM((64, tile, w), jnp.float32),
            pltpu.SemaphoreType.DMA((2,)),
        ],
        compiler_params=pltpu.CompilerParams(vmem_limit_bytes=32 * 1024 * 1024),
        cost_estimate=pl.CostEstimate(
            flops=2 * 2 * slots * tile * tile * w * 4,
            bytes_accessed=64 * tile * w * 8,
            transcendentals=0,
        ),
    )(src, dst, live, c_own, c_other, pieces, near, far, *earlier)


def local(
    features,
    walk_counts,
    tile_rows,
    tile_cols,
    live_tiles,
    neigh_weight,
    neigh_bias,
    combine_weight,
    combine_bias,
):
    rows_dev, width = features.shape
    tile = walk_counts.shape[3]
    slots = walk_counts.shape[2]
    half = width // 2
    cw = half // CHUNKS
    blocks = rows_dev // tile
    x_lo, y, z, x_hi, core = (lax.axis_index(a) for a in AXES)

    def transform(which):
        weight = lax.dynamic_slice_in_dim(neigh_weight, which * half, half, 1)
        bias = lax.dynamic_slice_in_dim(neigh_bias, which * half, half, 0)
        out = jnp.dot(features, weight, preferred_element_type=jnp.float32) + bias
        return jax.nn.relu(out).astype(jnp.bfloat16)

    theirs = swap(transform(1 - core), "core")
    mine = transform(core)

    def own_chunk(j):
        cols = slice(j * cw, (j + 1) * cw)
        return jnp.concatenate(
            [mine[:, cols].reshape(blocks, tile, cw), theirs[:, cols].reshape(blocks, tile, cw)]
        )

    live = live_tiles[0, 0]
    used = jnp.arange(slots, dtype=jnp.int32) < live
    c_own = jnp.where(used[:, None, None], walk_counts[0, 0], 0).astype(jnp.bfloat16)
    rows_own = jnp.where(used, tile_rows[0, 0], 0)
    meta = jnp.stack(
        [rows_own, jnp.where(used, tile_cols[0, 0], 0), jnp.full((slots,), live, jnp.int32)]
    )
    c_other = swap(after(c_own, theirs), "core")
    metas = jnp.stack([meta, swap(meta, "core")])
    k = metas[:, 1]
    src = (
        (ring_slot((k // 4) % 4, y, core) * 2 + ((k // 16) ^ x_lo)) * 8
        + jnp.arange(2, dtype=jnp.int32)[:, None] * 4
        + k % 4
    ).reshape(-1)
    b = metas[:, 0]
    ring = ring_slot(b // 16, z, core)
    ring = jnp.where(ring == 0, 3, jnp.where(ring == 3, 0, ring))
    dst = (
        ((ring * 2 + 1 - (((b // 8) % 2) ^ x_hi)) * 2)
        + (((b // 4) % 2) ^ core)
    ) * 4 + b % 4
    dst = dst.reshape(-1)
    lives = metas[:, 2, 0]

    row_sums = jnp.concatenate(
        [jnp.sum(c_own.astype(jnp.float32), axis=2), jnp.sum(c_other.astype(jnp.float32), axis=2)]
    )
    onehot = (jnp.arange(64, dtype=jnp.int32)[:, None] == dst[None, :]).astype(jnp.float32)
    deg = jnp.dot(onehot, row_sums, precision=lax.Precision.HIGHEST).astype(jnp.int32)
    parts = (deg[:, None, :] >> (5 * jnp.arange(4, dtype=jnp.int32))[None, :, None]) & 31
    parts = parts.astype(jnp.bfloat16).reshape(256, tile)

    hidden = (
        jnp.dot(features, combine_weight[:width], preferred_element_type=jnp.float32)
        + combine_bias
    )
    w_own = lax.dynamic_slice_in_dim(combine_weight, width + core * half, half, 0)
    w_other = lax.dynamic_slice_in_dim(combine_weight, width + (1 - core) * half, half, 0)

    own = [own_chunk(j) for j in range(CHUNKS)]
    first = swap(own[0], "x_lo")
    rest = swap(jnp.stack(own[1:]), "x_lo")
    partner = [first] + [rest[j] for j in range(CHUNKS - 1)]

    f32, bf16 = jnp.float32, jnp.bfloat16
    near_all, part_all, pass_all, zb_all, swap_all = [], [], [], [], []
    scale = None
    for j in range(CHUNKS):
        pair = jnp.concatenate([own[j], partner[j]])
        if j >= 2:
            pair = after(pair, near_all[j - 1], part_all[j - 2][0])
        elif j == 1:
            pair = after(pair, near_all[0])
        near = jnp.concatenate([pair, step(pair, "y", 0)])
        near_all.append(near)
        far = step(near, "y", 1)
        earlier = ()
        if j >= 2:
            earlier += (pass_all[j - 2],)
        if j >= 3:
            earlier += (zb_all[j - 3],)
        send, pass_on, stay = tile_sums(
            src, dst, lives, c_own, c_other, parts, j == 0, near, far, earlier
        )
        part_all.append((send, pass_on, stay))
        size = stay.shape[0] // 2
        got = step(send, "z", 0)
        passed = (got[: 2 * size].astype(f32) + pass_on).astype(bf16)
        pass_all.append(passed)
        stay = got[2 * size :].astype(f32) + stay
        if j == CHUNKS - 1:
            passed = after(passed, swap_all[j - 2])
        got = step(passed, "z", 1)
        zb_all.append(got)
        passed = (got[:size].astype(f32) + stay[:size]).astype(bf16)
        stay = got[size:].astype(f32) + stay[size:]
        if j == CHUNKS - 1:
            passed = after(passed, swap_all[j - 1])
        pooled = swap(passed, "x_hi").astype(f32) + stay
        if j == 0:
            deg = jnp.sum(
                pooled[8 * tile :].reshape(8, 4, tile)
                * jnp.array([1, 32, 1024, 32768], f32)[None, :, None],
                axis=1,
            )
            scale = 1.0 / (1.0 + deg)
            pooled = pooled[: 8 * tile]
        mean = (pooled.reshape(8, tile, cw) * scale[..., None]).astype(bf16)
        mean = mean.reshape(2, rows_dev, cw)
        got = swap(mean[1], "core")
        swap_all.append(got)
        cols = slice(j * cw, (j + 1) * cw)
        hidden = hidden + jnp.dot(mean[0], w_own[cols], preferred_element_type=f32)
        hidden = hidden + jnp.dot(got, w_other[cols], preferred_element_type=f32)
    hidden = jax.nn.relu(hidden)
    return hidden / jnp.sqrt(jnp.mean(hidden * hidden, axis=1, keepdims=True) + 1e-06)


def solution(mesh):
    fine = Mesh(mesh.devices.reshape(SIZES), AXES)
    row = AXES[:2]
    col = AXES[2:]
    return jax.shard_map(
        local,
        mesh=fine,
        in_specs=(
            P(AXES, None),
            P(row, col, None, None, None),
            P(row, col, None),
            P(row, col, None),
            P(row, col),
            P(),
            P(),
            P(),
            P(),
        ),
        out_specs=P(AXES, None),
        check_vma=False,
    )
```

time: 223 us -> 196 us (0.88)
  starting transfers between devices: 91.3 us -> 48 us
  other arithmetic: 10.2 us -> 21 us
  local copies, waits for them, and re-layouts: 7.47 us -> 13.1 us
    ppermute x69 -> x29, starting transfers between devices: 91.3 us -> 48 us  [the longest x13 26.7 us: swap(): return lax.ppermute(x, axis, [(0, 1), (1, 0)])]
    concatenate x0 -> x6, other arithmetic: none -> 4.06 us  [the longest x4 2.89 us: local(): pair = jnp.concatenate([own[j], partner[j]])]
    reduce_sum x1 -> x3, other arithmetic: 2.01 us -> 5.9 us  [the longest x1 3.61 us: local(): jnp.sum(c_own.astype(jnp.float32), axis=2)]
    add x21 -> x8, other arithmetic: 1.33 us -> 3.92 us  [the longest x4 2.37 us: local(): pooled = swap(passed, 'x_hi').astype(f32) + stay]
    unnamed x24 -> x57, local copies, waits for them, and re-layouts: 3.82 us -> 5.45 us
    dot_general x10 -> x11, matrix products: 7.83 us -> 8.09 us  [the longest x2 3.56 us: transform(): out = jnp.dot(features, weight, preferred_element_type=jnp.float32) + bias]
    ppermute x69 -> x29, waiting for transfers between devices: 76.6 us -> 76.7 us  [the longest x16 46 us: step(): return lax.ppermute(x, (axis, 'core'), pairs)]
  transfers between devices with their start and end apart: 69 -> 29, of which waited for: 26 -> 16; matrix products, arithmetic and copies ran while one was open for 7% -> 17% of each run, Pallas kernels for 11% -> 12%
where the time goes in v2:
time: 196 us; the launch traced here: 195 us
  waiting for transfers between devices  76.7 us (39%)
  starting transfers between devices  48 us (24%)
  Pallas kernels  23.9 us (12%)
  other arithmetic  21 us (11%)
  local copies, waits for them, and re-layouts  13.1 us (7%)
  matrix products  10.7 us (5%)
    ppermute x16, waiting for transfers between devices, step(): return lax.ppermute(x, (axis, 'core'), pairs)  46 us
    ppermute x13, waiting for transfers between devices, swap(): return lax.ppermute(x, axis, [(0, 1), (1, 0)])  30.7 us
    ppermute x13, starting transfers between devices, swap(): return lax.ppermute(x, axis, [(0, 1), (1, 0)])  26.7 us
    pallas_call x4, Pallas kernels, tile_sums(): pl.pallas_call(tile_kernel, out_shape=(jax.ShapeDtypeStruct((4 * size, w)...  23.9 us
    ppermute x16, starting transfers between devices, step(): return lax.ppermute(x, (axis, 'core'), pairs)  21.4 us
    unnamed x57, local copies, waits for them, and re-layouts  5.45 us
  transfers between devices with their start and end apart: 29, of which 16 were waited for; matrix products, arithmetic and copies ran while one was open for 17% of the time, Pallas kernels for 12%

profile of v2, /device:TPU:3, one launch (start us, length us, event | category | flops | bytes accessed | tf_op | source)
XLA Modules:
  0.0 194.8 jit_solution(10308837585198870585)
XLA Ops:
  1.6 2.8 %fusion.8 = bf16[512,512]{0,1:T(8,128)(2,1)} fusion(bf16[512,1024]{1,0:T(8,128)(2,1)} %param.10, bf16[1024,1024]{1,0:T(8,128)(2,1)S(1)} %copy-done, s32[]{:T(128)S(6)} %select_n.205, f32[512]{0:T(512)S(1)} %get-tuple-element.76), kind=kOutput, calls=%fused_computation.15 | convolution fusion | flops 537657344 | bytes 2623492 | tf_op jit(solution)/shard_map/dot_general | solution.py:145
  7.1 3.6 %convert_reduce_fusion.1 = (f32[64,128]{1,0:T(8,128)S(1)}, bf16[64,128,128]{2,1,0:T(8,128)(2,1)S(1)}) fusion(s32[1,1,64,128,128]{4,3,2,1,0:T(8,128)} %param.11, pred[64]{0:T(512)(128)(4,1)S(1)} %iota_compare_fusion.2), kind=kLoop, calls=%fused_computation.3 | loop fusion | flops 4186112 | bytes 6324288 | tf_op jit(solution)/shard_map/reduce_sum | solution.py:183
  10.7 1.1 fusion.66
  13.8 1.4 collective-permute-start.3
  15.2 1.1 collective-permute-start
  16.3 21.7 %collective-permute-done.3 = bf16[8,128,128]{2,1,0:T(8,128)(2,1)S(1)} collective-permute-done((bf16[8,128,128]{2,1,0:T(8,128)(2,1)S(1)}, bf16[8,128,128]{2,1,0:T(8,128)(2,1)S(1)}, u32[]{:S(2)}, u32[]{:S(2)}) %collective-permute-start.3) | collective-permute-done | bytes 262176 | tf_op jit(solution)/shard_map/ppermute | solution.py:15
  38.9 2.7 %collective-permute-start.4 = (bf16[16,128,128]{2,1,0:T(8,128)(2,1)}, bf16[16,128,128]{2,1,0:T(8,128)(2,1)}, u32[]{:S(2)}, u32[]{:S(2)}) collective-permute-start(bf16[16,128,128]{2,1,0:T(8,128)(2,1)} %pad_maximum_fusion.2), channel_id=1, source_target_pairs={{0,16},{1,49},{16,0},{17,33},{32,48},{33,17},{48,32},{49,1},{2,18}... | collective-permute-start | bytes 1572872 | tf_op jit(solution)/shard_map/ppermute | solution.py:24
  42.0 2.0 %slice_bitcast_fusion.2 = (bf16[8,128,128]{2,1,0:T(8,128)(2,1)S(1)}, bf16[8,128,128]{2,1,0:T(8,128)(2,1)}, bf16[8,128,128]{2,1,0:T(8,128)(2,1)}) fusion(bf16[3,8,128,128]{3,2,1,0:T(8,128)(2,1)} %collective-permute-done.10), kind=kLoop, calls=%fused_computation.67 | loop fusion | bytes 1572864 | tf_op jit(solution)/shard_map/squeeze | solution.py:200
  44.9 3.6 %collective-permute-done.4 = bf16[16,128,128]{2,1,0:T(8,128)(2,1)} collective-permute-done((bf16[16,128,128]{2,1,0:T(8,128)(2,1)}, bf16[16,128,128]{2,1,0:T(8,128)(2,1)}, u32[]{:S(2)}, u32[]{:S(2)}) %collective-permute-start.4) | collective-permute-done | bytes 524320 | tf_op jit(solution)/shard_map/ppermute | solution.py:24
  48.5 1.1 pad_maximum_fusion.near
  49.7 2.8 %collective-permute-start.11 = (bf16[16,128,128]{2,1,0:T(8,128)(2,1)}, bf16[16,128,128]{2,1,0:T(8,128)(2,1)}, u32[]{:S(2)}, u32[]{:S(2)}) collective-permute-start(bf16[16,128,128]{2,1,0:T(8,128)(2,1)} %pad_maximum_fusion.3), channel_id=1, source_target_pairs={{0,16},{1,49},{16,0},{17,33},{32,48},{33,17},{48,32},{49,1},{2,18}... | collective-permute-start | bytes 1572872 | tf_op jit(solution)/shard_map/ppermute | solution.py:24
  53.8 1.1 pad_maximum_fusion.4
  54.9 7.1 %collective-permute-done.11 = bf16[16,128,128]{2,1,0:T(8,128)(2,1)} collective-permute-done((bf16[16,128,128]{2,1,0:T(8,128)(2,1)}, bf16[16,128,128]{2,1,0:T(8,128)(2,1)}, u32[]{:S(2)}, u32[]{:S(2)}) %collective-permute-start.11) | collective-permute-done | bytes 524320 | tf_op jit(solution)/shard_map/ppermute | solution.py:24
  62.0 1.1 constant_dynamic-update-slice_fusion.near
  63.2 2.2 %convert_reduce_fusion = f32[64,128]{1,0:T(8,128)S(1)} fusion(bf16[64,128,128]{2,1,0:T(8,128)(2,1)} %collective-permute-done.2.c_other), kind=kLoop, calls=%fused_computation.2 | loop fusion | flops 2088960 | bytes 2129920 | tf_op jit(solution)/shard_map/reduce_sum | solution.py:183
  65.8 5.1 %collective-permute-done.5.far = bf16[32,128,128]{2,1,0:T(8,128)(2,1)S(1)} collective-permute-done((bf16[32,128,128]{2,1,0:T(8,128)(2,1)S(1)}, bf16[32,128,128]{2,1,0:T(8,128)(2,1)S(1)}, u32[]{:S(2)}, u32[]{:S(2)}) %collective-permute-start.5) | collective-permute-done | bytes 1048608 | tf_op jit(solution)/shard_map/ppermute | solution.py:24
  70.9 5.4 %shard_map.100 = (bf16[4224,128]{1,0:T(8,128)(2,1)S(1)}, f32[2112,128]{1,0:T(8,128)S(1)}, f32[2112,128]{1,0:T(8,128)S(1)}) custom-call(s32[128]{0:T(128)S(1)} %fusion.49.src_ref, s32[128]{0:T(128)S(1)} %fusion.50.dst_ref, s32[2]{0:T(128)S(1)} %fusion.48.live_ref, bf16[64,128,128]{2,1,0:T(8,128)(2,1)S(1)} %get-tuple-element.23.c_own, ...), custom_call_target="tpu_custom_call" | custom-call | flops 2147483648 | bytes 8388608 | tf_op jit(solution)/shard_map/pallas_call | solution.py:100
  76.3 1.5 collective-permute-start.17
  77.9 2.7 %collective-permute-start.6 = (bf16[4224,128]{1,0:T(8,128)(2,1)S(1)}, bf16[4224,128]{1,0:T(8,128)(2,1)S(1)}, u32[]{:S(2)}, u32[]{:S(2)}) collective-permute-start(bf16[4224,128]{1,0:T(8,128)(2,1)S(1)} %get-tuple-element.24), channel_id=1, source_target_pairs={{0,4},{1,13},{4,0},{5,9},{8,12},{9,5},{12,8},{13,1},{2,6},{3,15},{... | collective-permute-start | bytes 3244040 | tf_op jit(solution)/shard_map/ppermute | solution.py:24
  80.6 2.6 %collective-permute-done.12.far = bf16[32,128,128]{2,1,0:T(8,128)(2,1)S(1)} collective-permute-done((bf16[32,128,128]{2,1,0:T(8,128)(2,1)S(1)}, bf16[32,128,128]{2,1,0:T(8,128)(2,1)S(1)}, u32[]{:S(2)}, u32[]{:S(2)}) %collective-permute-start.12) | collective-permute-done | bytes 1048608 | tf_op jit(solution)/shard_map/ppermute | solution.py:24
  83.2 5.4 %shard_map.101 = (bf16[4096,128]{1,0:T(8,128)(2,1)S(1)}, f32[2048,128]{1,0:T(8,128)S(1)}, f32[2048,128]{1,0:T(8,128)S(1)}) custom-call(s32[128]{0:T(128)S(1)} %fusion.49.src_ref, s32[128]{0:T(128)S(1)} %fusion.50.dst_ref, s32[2]{0:T(128)S(1)} %fusion.48.live_ref, bf16[64,128,128]{2,1,0:T(8,128)(2,1)S(1)} %get-tuple-element.23.c_own, ...), custom_call_target="tpu_custom_call" | custom-call | flops 2147483648 | bytes 8388608 | tf_op jit(solution)/shard_map/pallas_call | solution.py:100
  88.7 2.6 %collective-permute-start.23 = (bf16[16,128,128]{2,1,0:T(8,128)(2,1)S(1)}, bf16[16,128,128]{2,1,0:T(8,128)(2,1)S(1)}, u32[]{:S(2)}, u32[]{:S(2)}) collective-permute-start(bf16[16,128,128]{2,1,0:T(8,128)(2,1)S(1)} %pad_maximum_fusion.5), channel_id=1, source_target_pairs={{0,16},{1,49},{16,0},{17,33},{32,48},{33,17},{48,32},{49,1},{2,18}... | collective-permute-start | bytes 1572872 | tf_op jit(solution)/shard_map/ppermute | solution.py:24
  91.2 3.8 %collective-permute-start.13 = (bf16[4096,128]{1,0:T(8,128)(2,1)S(1)}, bf16[4096,128]{1,0:T(8,128)(2,1)S(1)}, u32[]{:S(2)}, u32[]{:S(2)}) collective-permute-start(bf16[4096,128]{1,0:T(8,128)(2,1)S(1)} %get-tuple-element.28), channel_id=1, source_target_pairs={{0,4},{1,13},{4,0},{5,9},{8,12},{9,5},{12,8},{13,1},{2,6},{3,15},{... | collective-permute-start | bytes 3145736 | tf_op jit(solution)/shard_map/ppermute | solution.py:24
  95.8 2.1 %collective-permute-done.23 = bf16[16,128,128]{2,1,0:T(8,128)(2,1)S(1)} collective-permute-done((bf16[16,128,128]{2,1,0:T(8,128)(2,1)S(1)}, bf16[16,128,128]{2,1,0:T(8,128)(2,1)S(1)}, u32[]{:S(2)}, u32[]{:S(2)}) %collective-permute-start.23) | collective-permute-done | bytes 524320 | tf_op jit(solution)/shard_map/ppermute | solution.py:24
  99.4 2.7 %collective-permute-start.7 = (bf16[2112,128]{1,0:T(8,128)(2,1)S(1)}, bf16[2112,128]{1,0:T(8,128)(2,1)S(1)}, u32[]{:S(2)}, u32[]{:S(2)}) collective-permute-start(bf16[2112,128]{1,0:T(8,128)(2,1)S(1)} %get-tuple-element.46.refs_0_), channel_id=1, source_target_pairs={{0,12},{1,5},{4,8},{5,1},{8,4},{9,13},{12,0},{13,9},{2,14},{3,7},{... | collective-permute-start | bytes 1622024 | tf_op jit(solution)/shard_map/ppermute | solution.py:24
  102.1 5.4 %collective-permute-done.13 = bf16[4096,128]{1,0:T(8,128)(2,1)S(1)} collective-permute-done((bf16[4096,128]{1,0:T(8,128)(2,1)S(1)}, bf16[4096,128]{1,0:T(8,128)(2,1)S(1)}, u32[]{:S(2)}, u32[]{:S(2)}) %collective-permute-start.13) | collective-permute-done | bytes 1048608 | tf_op jit(solution)/shard_map/ppermute | solution.py:24
  107.5 1.3 convert_add_fusion.3
  108.8 3.1 %collective-permute-done.18.far = bf16[32,128,128]{2,1,0:T(8,128)(2,1)S(1)} collective-permute-done((bf16[32,128,128]{2,1,0:T(8,128)(2,1)S(1)}, bf16[32,128,128]{2,1,0:T(8,128)(2,1)S(1)}, u32[]{:S(2)}, u32[]{:S(2)}) %collective-permute-start.18) | collective-permute-done | bytes 1048608 | tf_op jit(solution)/shard_map/ppermute | solution.py:24
  111.9 6.5 %shard_map.102 = (bf16[4096,128]{1,0:T(8,128)(2,1)}, f32[2048,128]{1,0:T(8,128)S(1)}, f32[2048,128]{1,0:T(8,128)S(1)}) custom-call(s32[128]{0:T(128)S(1)} %fusion.49.src_ref, s32[128]{0:T(128)S(1)} %fusion.50.dst_ref, s32[2]{0:T(128)S(1)} %fusion.48.live_ref, bf16[64,128,128]{2,1,0:T(8,128)(2,1)S(1)} %get-tuple-element.23.c_own, ...), custom_call_target="tpu_custom_call" | custom-call | flops 2147483648 | bytes 8388608 | tf_op jit(solution)/shard_map/pallas_call | solution.py:100
  119.5 1.9 collective-permute-start.19
  123.0 1.3 collective-permute-start.8
  124.4 2.6 %fusion.1 = f32[512,1024]{1,0:T(8,128)} fusion(bf16[512,1024]{1,0:T(8,128)(2,1)S(1)} %copy-done.26, bf16[2048,1024]{1,0:T(8,128)(2,1)S(1)} %copy-done.16), kind=kOutput, calls=%fused_computation.6 | convolution fusion | flops 1073741824 | bytes 5242880 | tf_op jit(solution)/shard_map/dot_general | solution.py:191
  127.0 1.2 fusion.18
  128.2 1.7 collective-permute-start.15
  130.5 1.2 fusion.11
  131.7 6.6 %shard_map.103 = (bf16[4096,128]{1,0:T(8,128)(2,1)S(1)}, f32[2048,128]{1,0:T(8,128)S(1)}, f32[2048,128]{1,0:T(8,128)S(1)}) custom-call(s32[128]{0:T(128)S(1)} %fusion.49.src_ref, s32[128]{0:T(128)S(1)} %fusion.50.dst_ref, s32[2]{0:T(128)S(1)} %fusion.48.live_ref, bf16[64,128,128]{2,1,0:T(8,128)(2,1)S(1)} %get-tuple-element.23.c_own, ...), custom_call_target="tpu_custom_call" | custom-call | flops 2147483648 | bytes 8388608 | tf_op jit(solution)/shard_map/pallas_call | solution.py:100
  138.5 1.3 collective-permute-done.19
  139.8 1.5 add_convert_fusion.2
  142.5 6.9 %collective-permute-done.20 = bf16[2048,128]{1,0:T(8,128)(2,1)S(1)} collective-permute-done((bf16[2048,128]{1,0:T(8,128)(2,1)S(1)}, bf16[2048,128]{1,0:T(8,128)(2,1)S(1)}, u32[]{:S(2)}, u32[]{:S(2)}) %collective-permute-start.20) | collective-permute-done | bytes 524320 | tf_op jit(solution)/shard_map/ppermute | solution.py:24
  149.5 3.2 %collective-permute-start.21 = (bf16[1024,128]{1,0:T(8,128)(2,1)S(1)}, bf16[1024,128]{1,0:T(8,128)(2,1)S(1)}, u32[]{:S(2)}, u32[]{:S(2)}) collective-permute-start(bf16[1024,128]{1,0:T(8,128)(2,1)S(1)} %fusion.16), channel_id=1, source_target_pairs={{0,2},{2,0},{1,3},{3,1},{4,6},{6,4},{5,7},{7,5},{8,10},{10,8},{9,1... | collective-permute-start | bytes 786440 | tf_op jit(solution)/shard_map/ppermute | solution.py:15
  152.6 1.3 collective-permute-done.25
  154.2 2.5 %collective-permute-done.21 = bf16[1024,128]{1,0:T(8,128)(2,1)S(1)} collective-permute-done((bf16[1024,128]{1,0:T(8,128)(2,1)S(1)}, bf16[1024,128]{1,0:T(8,128)(2,1)S(1)}, u32[]{:S(2)}, u32[]{:S(2)}) %collective-permute-start.21) | collective-permute-done | bytes 262176 | tf_op jit(solution)/shard_map/ppermute | solution.py:15
  157.1 11.0 %collective-permute-start.16 = (bf16[512,128]{1,0:T(8,128)(2,1)S(1)}, bf16[512,128]{1,0:T(8,128)(2,1)S(1)}, u32[]{:S(2)}, u32[]{:S(2)}) collective-permute-start(bf16[512,128]{1,0:T(8,128)(2,1)S(1)} %bitcast.95), channel_id=1, source_target_pairs={{0,1},{1,0},{2,3},{3,2},{4,5},{5,4},{6,7},{7,6},{8,9},{9,8},{10,11... | collective-permute-start | bytes 393224 | tf_op jit(solution)/shard_map/ppermute | solution.py:15
  171.1 7.4 %collective-permute-done.26 = bf16[2048,128]{1,0:T(8,128)(2,1)S(1)} collective-permute-done((bf16[2048,128]{1,0:T(8,128)(2,1)S(1)}, bf16[2048,128]{1,0:T(8,128)(2,1)S(1)}, u32[]{:S(2)}, u32[]{:S(2)}) %collective-permute-start.26) | collective-permute-done | bytes 524320 | tf_op jit(solution)/shard_map/ppermute | solution.py:24
  180.0 5.4 %collective-permute-done.27 = bf16[1024,128]{1,0:T(8,128)(2,1)S(1)} collective-permute-done((bf16[1024,128]{1,0:T(8,128)(2,1)S(1)}, bf16[1024,128]{1,0:T(8,128)(2,1)S(1)}, u32[]{:S(2)}, u32[]{:S(2)}) %collective-permute-start.27) | collective-permute-done | bytes 262176 | tf_op jit(solution)/shard_map/ppermute | solution.py:15
  185.7 4.3 %collective-permute-start.28 = (bf16[512,128]{1,0:T(8,128)(2,1)S(1)}, bf16[512,128]{1,0:T(8,128)(2,1)S(1)}, u32[]{:S(2)}, u32[]{:S(2)}) collective-permute-start(bf16[512,128]{1,0:T(8,128)(2,1)S(1)} %bitcast.96), channel_id=1, source_target_pairs={{0,1},{1,0},{2,3},{3,2},{4,5},{5,4},{6,7},{7,6},{8,9},{9,8},{10,11... | collective-permute-start | bytes 393224 | tf_op jit(solution)/shard_map/ppermute | solution.py:15
  191.0 1.4 multiply_reduce_fusion
  192.4 1.6 broadcast_divide_fusion
  (153 shorter events, 23.5 us)
Async XLA Ops:
  0.0 5.1 %copy-start.25 = (bf16[512,1024]{1,0:T(8,128)(2,1)S(1)}, bf16[512,1024]{1,0:T(8,128)(2,1)}, u32[]{:S(2)}) copy-start(bf16[512,1024]{1,0:T(8,128)(2,1)} %param.10) | copy-start | bytes 3145732
  4.4 6.3 %collective-permute-start.1 = (bf16[512,512]{0,1:T(8,128)(2,1)}, bf16[512,512]{0,1:T(8,128)(2,1)}, u32[]{:S(2)}, u32[]{:S(2)}) collective-permute-start(bf16[512,512]{0,1:T(8,128)(2,1)} %fusion.8), channel_id=1, source_target_pairs={{0,1},{1,0},{2,3},{3,2},{4,5},{5,4},{6,7},{7,6},{8,9},{9,8},{10,11... | collective-permute-start | bytes 1572872 | tf_op jit(solution)/shard_map/ppermute | solution.py:15
  7.0 5.6 %copy-start.14 = (bf16[512,128]{1,0:T(8,128)(2,1)}, bf16[512,128]{1,0:T(8,128)(2,1)S(1)}, u32[]{:S(2)}) copy-start(bf16[512,128]{1,0:T(8,128)(2,1)S(1)} %copy.25) | copy-start | bytes 393220
  7.1 5.4 %copy-start.10 = (bf16[512,128]{1,0:T(8,128)(2,1)}, bf16[512,128]{1,0:T(8,128)(2,1)S(1)}, u32[]{:S(2)}) copy-start(bf16[512,128]{1,0:T(8,128)(2,1)S(1)} %copy.27) | copy-start | bytes 393220
  12.0 51.2 %collective-permute-start.2 = (bf16[64,128,128]{2,1,0:T(8,128)(2,1)S(1)}, bf16[64,128,128]{2,1,0:T(8,128)(2,1)}, u32[]{:S(2)}, u32[]{:S(2)}) collective-permute-start(bf16[64,128,128]{2,1,0:T(8,128)(2,1)S(1)} %get-tuple-element.23.c_own), channel_id=1, source_target_pairs={{0,1},{1,0},{2,3},{3,2},{4,5},{5,4},{6,7},{7,6},{8,9},{9,8},{10,11... | collective-permute-start | bytes 6291464 | tf_op jit(solution)/shard_map/ppermute | solution.py:15
  12.4 26.6 %copy-start.15 = (bf16[512,128]{1,0:T(8,128)(2,1)}, bf16[512,128]{1,0:T(8,128)(2,1)S(1)}, u32[]{:S(2)}) copy-start(bf16[512,128]{1,0:T(8,128)(2,1)S(1)} %copy.26) | copy-start | bytes 393220
  12.5 26.4 %copy-start.12 = (bf16[512,128]{1,0:T(8,128)(2,1)}, bf16[512,128]{1,0:T(8,128)(2,1)S(1)}, u32[]{:S(2)}) copy-start(bf16[512,128]{1,0:T(8,128)(2,1)S(1)} %copy.28) | copy-start | bytes 393220
  13.6 28.4 %collective-permute-start.10 = (bf16[3,8,128,128]{3,2,1,0:T(8,128)(2,1)}, bf16[3,8,128,128]{3,2,1,0:T(8,128)(2,1)}, u32[]{:S(2)}, u32[]{:S(2)}) collective-permute-start(bf16[3,8,128,128]{3,2,1,0:T(8,128)(2,1)} %pad_maximum_fusion.1), channel_id=1, source_target_pairs={{0,64},{64,0},{1,65},{65,1},{2,66},{66,2},{3,67},{67,3},{4,68},{68... | collective-permute-start | bytes 2359304 | tf_op jit(solution)/shard_map/ppermute | solution.py:15
  13.8 24.2 %collective-permute-start.3 = (bf16[8,128,128]{2,1,0:T(8,128)(2,1)S(1)}, bf16[8,128,128]{2,1,0:T(8,128)(2,1)S(1)}, u32[]{:S(2)}, u32[]{:S(2)}) collective-permute-start(bf16[8,128,128]{2,1,0:T(8,128)(2,1)S(1)} %pad_maximum_fusion.6), channel_id=1, source_target_pairs={{0,64},{64,0},{1,65},{65,1},{2,66},{66,2},{3,67},{67,3},{4,68},{68... | collective-permute-start | bytes 786440 | tf_op jit(solution)/shard_map/ppermute | solution.py:15
  15.2 26.7 %collective-permute-start = (s32[3,64]{1,0:T(4,128)S(1)}, s32[3,64]{1,0:T(4,128)S(1)}, u32[]{:S(2)}, u32[]{:S(2)}) collective-permute-start(s32[3,64]{1,0:T(4,128)S(1)} %get-tuple-element.78), channel_id=1, source_target_pairs={{0,1},{1,0},{2,3},{3,2},{4,5},{5,4},{6,7},{7,6},{8,9},{9,8},{10,11... | collective-permute-start | bytes 2312 | tf_op jit(solution)/shard_map/ppermute | solution.py:15
  38.0 4.0 %copy-start.19 = (bf16[8,128,128]{2,1,0:T(8,128)(2,1)}, bf16[8,128,128]{2,1,0:T(8,128)(2,1)S(1)}, u32[]{:S(2)}) copy-start(bf16[8,128,128]{2,1,0:T(8,128)(2,1)S(1)} %collective-permute-done.3) | copy-start | bytes 786436
  38.9 9.6 %collective-permute-start.4 = (bf16[16,128,128]{2,1,0:T(8,128)(2,1)}, bf16[16,128,128]{2,1,0:T(8,128)(2,1)}, u32[]{:S(2)}, u32[]{:S(2)}) collective-permute-start(bf16[16,128,128]{2,1,0:T(8,128)(2,1)} %pad_maximum_fusion.2), channel_id=1, source_target_pairs={{0,16},{1,49},{16,0},{17,33},{32,48},{33,17},{48,32},{49,1},{2,18}... | collective-permute-start | bytes 1572872 | tf_op jit(solution)/shard_map/ppermute | solution.py:24
  42.0 6.5 %copy-start.20 = (bf16[8,128,128]{2,1,0:T(8,128)(2,1)S(1)}, bf16[8,128,128]{2,1,0:T(8,128)(2,1)}, u32[]{:S(2)}) copy-start(bf16[8,128,128]{2,1,0:T(8,128)(2,1)} %copy-done.19) | copy-start | bytes 786436
  49.7 12.3 %collective-permute-start.11 = (bf16[16,128,128]{2,1,0:T(8,128)(2,1)}, bf16[16,128,128]{2,1,0:T(8,128)(2,1)}, u32[]{:S(2)}, u32[]{:S(2)}) collective-permute-start(bf16[16,128,128]{2,1,0:T(8,128)(2,1)} %pad_maximum_fusion.3), channel_id=1, source_target_pairs={{0,16},{1,49},{16,0},{17,33},{32,48},{33,17},{48,32},{49,1},{2,18}... | collective-permute-start | bytes 1572872 | tf_op jit(solution)/shard_map/ppermute | solution.py:24
  52.5 18.4 %collective-permute-start.5 = (bf16[32,128,128]{2,1,0:T(8,128)(2,1)S(1)}, bf16[32,128,128]{2,1,0:T(8,128)(2,1)S(1)}, u32[]{:S(2)}, u32[]{:S(2)}) collective-permute-start(bf16[32,128,128]{2,1,0:T(8,128)(2,1)S(1)} %pad_maximum_fusion.near), channel_id=1, source_target_pairs={{0,48},{1,17},{16,32},{17,1},{32,16},{33,49},{48,0},{49,33},{2,50}... | collective-permute-start | bytes 3145736 | tf_op jit(solution)/shard_map/ppermute | solution.py:24
  63.1 20.1 %collective-permute-start.12 = (bf16[32,128,128]{2,1,0:T(8,128)(2,1)S(1)}, bf16[32,128,128]{2,1,0:T(8,128)(2,1)S(1)}, u32[]{:S(2)}, u32[]{:S(2)}) collective-permute-start(bf16[32,128,128]{2,1,0:T(8,128)(2,1)S(1)} %constant_dynamic-update-slice_fusion.near), channel_id=1, source_target_pairs={{0,48},{1,17},{16,32},{17,1},{32,16},{33,49},{48,0},{49,33},{2,50}... | collective-permute-start | bytes 3145736 | tf_op jit(solution)/shard_map/ppermute | solution.py:24
  65.8 12.0 %copy-start.11 = (bf16[512,128]{1,0:T(8,128)(2,1)S(1)}, bf16[512,128]{1,0:T(8,128)(2,1)}, u32[]{:S(2)}) copy-start(bf16[512,128]{1,0:T(8,128)(2,1)} %copy-done.10) | copy-start | bytes 393220
  65.8 12.0 %copy-start.13 = (bf16[512,128]{1,0:T(8,128)(2,1)S(1)}, bf16[512,128]{1,0:T(8,128)(2,1)}, u32[]{:S(2)}) copy-start(bf16[512,128]{1,0:T(8,128)(2,1)} %copy-done.12) | copy-start | bytes 393220
  65.8 12.0 %copy-start.18 = (bf16[8,128,128]{2,1,0:T(8,128)(2,1)S(1)}, bf16[8,128,128]{2,1,0:T(8,128)(2,1)}, u32[]{:S(2)}) copy-start(bf16[8,128,128]{2,1,0:T(8,128)(2,1)} %get-tuple-element.54) | copy-start | bytes 786436
  76.3 12.3 %collective-permute-start.17 = (bf16[16,128,128]{2,1,0:T(8,128)(2,1)S(1)}, bf16[16,128,128]{2,1,0:T(8,128)(2,1)S(1)}, u32[]{:S(2)}, u32[]{:S(2)}) collective-permute-start(bf16[16,128,128]{2,1,0:T(8,128)(2,1)S(1)} %pad_maximum_fusion.4), channel_id=1, source_target_pairs={{0,16},{1,49},{16,0},{17,33},{32,48},{33,17},{48,32},{49,1},{2,18}... | collective-permute-start | bytes 1572872 | tf_op jit(solution)/shard_map/ppermute | solution.py:24
  77.9 21.4 %collective-permute-start.6 = (bf16[4224,128]{1,0:T(8,128)(2,1)S(1)}, bf16[4224,128]{1,0:T(8,128)(2,1)S(1)}, u32[]{:S(2)}, u32[]{:S(2)}) collective-permute-start(bf16[4224,128]{1,0:T(8,128)(2,1)S(1)} %get-tuple-element.24), channel_id=1, source_target_pairs={{0,4},{1,13},{4,0},{5,9},{8,12},{9,5},{12,8},{13,1},{2,6},{3,15},{... | collective-permute-start | bytes 3244040 | tf_op jit(solution)/shard_map/ppermute | solution.py:24
  88.7 9.3 %collective-permute-start.23 = (bf16[16,128,128]{2,1,0:T(8,128)(2,1)S(1)}, bf16[16,128,128]{2,1,0:T(8,128)(2,1)S(1)}, u32[]{:S(2)}, u32[]{:S(2)}) collective-permute-start(bf16[16,128,128]{2,1,0:T(8,128)(2,1)S(1)} %pad_maximum_fusion.5), channel_id=1, source_target_pairs={{0,16},{1,49},{16,0},{17,33},{32,48},{33,17},{48,32},{49,1},{2,18}... | collective-permute-start | bytes 1572872 | tf_op jit(solution)/shard_map/ppermute | solution.py:24
  91.2 16.2 %collective-permute-start.13 = (bf16[4096,128]{1,0:T(8,128)(2,1)S(1)}, bf16[4096,128]{1,0:T(8,128)(2,1)S(1)}, u32[]{:S(2)}, u32[]{:S(2)}) collective-permute-start(bf16[4096,128]{1,0:T(8,128)(2,1)S(1)} %get-tuple-element.28), channel_id=1, source_target_pairs={{0,4},{1,13},{4,0},{5,9},{8,12},{9,5},{12,8},{13,1},{2,6},{3,15},{... | collective-permute-start | bytes 3145736 | tf_op jit(solution)/shard_map/ppermute | solution.py:24
  95.0 16.9 %collective-permute-start.18 = (bf16[32,128,128]{2,1,0:T(8,128)(2,1)S(1)}, bf16[32,128,128]{2,1,0:T(8,128)(2,1)S(1)}, u32[]{:S(2)}, u32[]{:S(2)}) collective-permute-start(bf16[32,128,128]{2,1,0:T(8,128)(2,1)S(1)} %constant_dynamic-update-slice_fusion.2.near), channel_id=1, source_target_pairs={{0,48},{1,17},{16,32},{17,1},{32,16},{33,49},{48,0},{49,33},{2,50}... | collective-permute-start | bytes 3145736 | tf_op jit(solution)/shard_map/ppermute | solution.py:24
  98.8 32.9 %collective-permute-start.24 = (bf16[32,128,128]{2,1,0:T(8,128)(2,1)}, bf16[32,128,128]{2,1,0:T(8,128)(2,1)}, u32[]{:S(2)}, u32[]{:S(2)}) collective-permute-start(bf16[32,128,128]{2,1,0:T(8,128)(2,1)} %constant_dynamic-update-slice_fusion.4.near), channel_id=1, source_target_pairs={{0,48},{1,17},{16,32},{17,1},{32,16},{33,49},{48,0},{49,33},{2,50}... | collective-permute-start | bytes 3145736 | tf_op jit(solution)/shard_map/ppermute | solution.py:24
  99.4 22.0 %copy-start.6 = (f32[2112,128]{1,0:T(8,128)}, f32[2112,128]{1,0:T(8,128)S(1)}, u32[]{:S(2)}) copy-start(f32[2112,128]{1,0:T(8,128)S(1)} %get-tuple-element.45) | copy-start | bytes 3244036
  99.4 22.0 %collective-permute-start.7 = (bf16[2112,128]{1,0:T(8,128)(2,1)S(1)}, bf16[2112,128]{1,0:T(8,128)(2,1)S(1)}, u32[]{:S(2)}, u32[]{:S(2)}) collective-permute-start(bf16[2112,128]{1,0:T(8,128)(2,1)S(1)} %get-tuple-element.46.refs_0_), channel_id=1, source_target_pairs={{0,12},{1,5},{4,8},{5,1},{8,4},{9,13},{12,0},{13,9},{2,14},{3,7},{... | collective-permute-start | bytes 1622024 | tf_op jit(solution)/shard_map/ppermute | solution.py:24
  108.8 15.6 %copy-start.16 = (bf16[2048,1024]{1,0:T(8,128)(2,1)S(1)}, bf16[2048,1024]{1,0:T(8,128)(2,1)}, u32[]{:S(2)}) copy-start(bf16[2048,1024]{1,0:T(8,128)(2,1)} %param.17) | copy-start | bytes 12582916
  108.8 15.6 %copy-start.26 = (bf16[512,1024]{1,0:T(8,128)(2,1)S(1)}, bf16[512,1024]{1,0:T(8,128)(2,1)}, u32[]{:S(2)}) copy-start(bf16[512,1024]{1,0:T(8,128)(2,1)} %param.10) | copy-start | bytes 3145732
  108.8 18.2 %collective-permute-start.14 = (bf16[2048,128]{1,0:T(8,128)(2,1)}, bf16[2048,128]{1,0:T(8,128)(2,1)}, u32[]{:S(2)}, u32[]{:S(2)}) collective-permute-start(bf16[2048,128]{1,0:T(8,128)(2,1)} %get-tuple-element.50.refs_0_), channel_id=1, source_target_pairs={{0,12},{1,5},{4,8},{5,1},{8,4},{9,13},{12,0},{13,9},{2,14},{3,7},{... | collective-permute-start | bytes 1572872 | tf_op jit(solution)/shard_map/ppermute | solution.py:24
  119.5 20.2 %collective-permute-start.19 = (bf16[4096,128]{1,0:T(8,128)(2,1)}, bf16[4096,128]{1,0:T(8,128)(2,1)}, u32[]{:S(2)}, u32[]{:S(2)}) collective-permute-start(bf16[4096,128]{1,0:T(8,128)(2,1)} %get-tuple-element.32), channel_id=1, source_target_pairs={{0,4},{1,13},{4,0},{5,9},{8,12},{9,5},{12,8},{13,1},{2,6},{3,15},{... | collective-permute-start | bytes 3145736 | tf_op jit(solution)/shard_map/ppermute | solution.py:24
  123.0 7.4 %collective-permute-start.8 = (bf16[1056,128]{1,0:T(8,128)(2,1)}, bf16[1056,128]{1,0:T(8,128)(2,1)S(1)}, u32[]{:S(2)}, u32[]{:S(2)}) collective-permute-start(bf16[1056,128]{1,0:T(8,128)(2,1)} %fusion.12), channel_id=1, source_target_pairs={{0,2},{2,0},{1,3},{3,1},{4,6},{6,4},{5,7},{7,5},{8,10},{10,8},{9,1... | collective-permute-start | bytes 811016 | tf_op jit(solution)/shard_map/ppermute | solution.py:15
  126.9 4.8 %copy-start.5 = (bf16[2112,128]{1,0:T(8,128)(2,1)S(1)}, bf16[2112,128]{1,0:T(8,128)(2,1)}, u32[]{:S(2)}) copy-start(bf16[2112,128]{1,0:T(8,128)(2,1)} %copy-done.4) | copy-start | bytes 1622020
  128.2 13.3 %collective-permute-start.15 = (bf16[1024,128]{1,0:T(8,128)(2,1)S(1)}, bf16[1024,128]{1,0:T(8,128)(2,1)S(1)}, u32[]{:S(2)}, u32[]{:S(2)}) collective-permute-start(bf16[1024,128]{1,0:T(8,128)(2,1)S(1)} %fusion.18), channel_id=1, source_target_pairs={{0,2},{2,0},{1,3},{3,1},{4,6},{6,4},{5,7},{7,5},{8,10},{10,8},{9,1... | collective-permute-start | bytes 786440 | tf_op jit(solution)/shard_map/ppermute | solution.py:15
  131.7 6.7 %copy-start.8 = (f32[1056,128]{1,0:T(8,128)}, f32[1056,128]{1,0:T(8,128)S(1)}, u32[]{:S(2)}) copy-start(f32[1056,128]{1,0:T(8,128)S(1)} %fusion.11) | copy-start | bytes 1622020
  131.7 8.1 %copy-start.3 = (f32[2048,128]{1,0:T(8,128)S(1)}, f32[2048,128]{1,0:T(8,128)}, u32[]{:S(2)}) copy-start(f32[2048,128]{1,0:T(8,128)} %copy-done.2) | copy-start | bytes 3145732
  138.4 15.6 %collective-permute-start.25 = (bf16[4096,128]{1,0:T(8,128)(2,1)S(1)}, bf16[4096,128]{1,0:T(8,128)(2,1)S(1)}, u32[]{:S(2)}, u32[]{:S(2)}) collective-permute-start(bf16[4096,128]{1,0:T(8,128)(2,1)S(1)} %get-tuple-element.36), channel_id=1, source_target_pairs={{0,4},{1,13},{4,0},{5,9},{8,12},{9,5},{12,8},{13,1},{2,6},{3,15},{... | collective-permute-start | bytes 3145736 | tf_op jit(solution)/shard_map/ppermute | solution.py:24
  141.3 8.1 %collective-permute-start.20 = (bf16[2048,128]{1,0:T(8,128)(2,1)S(1)}, bf16[2048,128]{1,0:T(8,128)(2,1)S(1)}, u32[]{:S(2)}, u32[]{:S(2)}) collective-permute-start(bf16[2048,128]{1,0:T(8,128)(2,1)S(1)} %get-tuple-element.47), channel_id=1, source_target_pairs={{0,12},{1,5},{4,8},{5,1},{8,4},{9,13},{12,0},{13,9},{2,14},{3,7},{... | collective-permute-start | bytes 1572872 | tf_op jit(solution)/shard_map/ppermute | solution.py:24
  149.5 7.2 %collective-permute-start.21 = (bf16[1024,128]{1,0:T(8,128)(2,1)S(1)}, bf16[1024,128]{1,0:T(8,128)(2,1)S(1)}, u32[]{:S(2)}, u32[]{:S(2)}) collective-permute-start(bf16[1024,128]{1,0:T(8,128)(2,1)S(1)} %fusion.16), channel_id=1, source_target_pairs={{0,2},{2,0},{1,3},{3,1},{4,6},{6,4},{5,7},{7,5},{8,10},{10,8},{9,1... | collective-permute-start | bytes 786440 | tf_op jit(solution)/shard_map/ppermute | solution.py:15
  156.7 12.1 %copy-start.17 = (bf16[2048,1024]{1,0:T(8,128)(2,1)S(1)}, bf16[2048,1024]{1,0:T(8,128)(2,1)}, u32[]{:S(2)}) copy-start(bf16[2048,1024]{1,0:T(8,128)(2,1)} %param.17) | copy-start | bytes 12582916
  157.1 13.0 %collective-permute-start.16 = (bf16[512,128]{1,0:T(8,128)(2,1)S(1)}, bf16[512,128]{1,0:T(8,128)(2,1)S(1)}, u32[]{:S(2)}, u32[]{:S(2)}) collective-permute-start(bf16[512,128]{1,0:T(8,128)(2,1)S(1)} %bitcast.95), channel_id=1, source_target_pairs={{0,1},{1,0},{2,3},{3,2},{4,5},{5,4},{6,7},{7,6},{8,9},{9,8},{10,11... | collective-permute-start | bytes 393224 | tf_op jit(solution)/shard_map/ppermute | solution.py:15
  168.1 2.5 %collective-permute-start.22 = (bf16[512,128]{1,0:T(8,128)(2,1)S(1)}, bf16[512,128]{1,0:T(8,128)(2,1)S(1)}, u32[]{:S(2)}, u32[]{:S(2)}) collective-permute-start(bf16[512,128]{1,0:T(8,128)(2,1)S(1)} %bitcast.94), channel_id=1, source_target_pairs={{0,1},{1,0},{2,3},{3,2},{4,5},{5,4},{6,7},{7,6},{8,9},{9,8},{10,11... | collective-permute-start | bytes 393224 | tf_op jit(solution)/shard_map/ppermute | solution.py:15
  168.2 11.4 %collective-permute-start.9 = (bf16[512,128]{1,0:T(8,128)(2,1)S(1)}, bf16[512,128]{1,0:T(8,128)(2,1)S(1)}, u32[]{:S(2)}, u32[]{:S(2)}) collective-permute-start(bf16[512,128]{1,0:T(8,128)(2,1)S(1)} %bitcast.93), channel_id=1, source_target_pairs={{0,1},{1,0},{2,3},{3,2},{4,5},{5,4},{6,7},{7,6},{8,9},{9,8},{10,11... | collective-permute-start | bytes 393224 | tf_op jit(solution)/shard_map/ppermute | solution.py:15
  170.1 8.4 %collective-permute-start.26 = (bf16[2048,128]{1,0:T(8,128)(2,1)S(1)}, bf16[2048,128]{1,0:T(8,128)(2,1)S(1)}, u32[]{:S(2)}, u32[]{:S(2)}) collective-permute-start(bf16[2048,128]{1,0:T(8,128)(2,1)S(1)} %get-tuple-element.38), channel_id=1, source_target_pairs={{0,12},{1,5},{4,8},{5,1},{8,4},{9,13},{12,0},{13,9},{2,14},{3,7},{... | collective-permute-start | bytes 1572872 | tf_op jit(solution)/shard_map/ppermute | solution.py:24
  178.6 6.8 %collective-permute-start.27 = (bf16[1024,128]{1,0:T(8,128)(2,1)S(1)}, bf16[1024,128]{1,0:T(8,128)(2,1)S(1)}, u32[]{:S(2)}, u32[]{:S(2)}) collective-permute-start(bf16[1024,128]{1,0:T(8,128)(2,1)S(1)} %fusion.14), channel_id=1, source_target_pairs={{0,2},{2,0},{1,3},{3,1},{4,6},{6,4},{5,7},{7,5},{8,10},{10,8},{9,1... | collective-permute-start | bytes 786440 | tf_op jit(solution)/shard_map/ppermute | solution.py:15
  185.4 5.5 %copy-start.9 = (f32[512,1024]{1,0:T(8,128)S(1)}, f32[512,1024]{1,0:T(8,128)}, u32[]{:S(2)}) copy-start(f32[512,1024]{1,0:T(8,128)} %fusion.1) | copy-start | bytes 6291460
  185.5 5.5 %copy-start.21 = (f32[1024]{0:T(1024)S(1)}, f32[1024]{0:T(1024)}, u32[]{:S(2)}) copy-start(f32[1024]{0:T(1024)} %param.18) | copy-start | bytes 12292
  185.7 5.3 %collective-permute-start.28 = (bf16[512,128]{1,0:T(8,128)(2,1)S(1)}, bf16[512,128]{1,0:T(8,128)(2,1)S(1)}, u32[]{:S(2)}, u32[]{:S(2)}) collective-permute-start(bf16[512,128]{1,0:T(8,128)(2,1)S(1)} %bitcast.96), channel_id=1, source_target_pairs={{0,1},{1,0},{2,3},{3,2},{4,5},{5,4},{6,7},{7,6},{8,9},{9,8},{10,11... | collective-permute-start | bytes 393224 | tf_op jit(solution)/shard_map/ppermute | solution.py:15
  (10 other events, 19.6 us)

commit v3 on v2

--- a/solution.py
+++ b/solution.py
@@ -139,20 +139,30 @@
     blocks = rows_dev // tile
     x_lo, y, z, x_hi, core = (lax.axis_index(a) for a in AXES)
 
-    def transform(which):
-        weight = lax.dynamic_slice_in_dim(neigh_weight, which * half, half, 1)
-        bias = lax.dynamic_slice_in_dim(neigh_bias, which * half, half, 0)
+    def transform(features, which, first, size):
+        weight = lax.dynamic_slice_in_dim(neigh_weight, which * half + first, size, 1)
+        bias = jnp.where(
+            which == 0,
+            neigh_bias[first : first + size],
+            neigh_bias[half + first : half + first + size],
+        )
         out = jnp.dot(features, weight, preferred_element_type=jnp.float32) + bias
         return jax.nn.relu(out).astype(jnp.bfloat16)
 
-    theirs = swap(transform(1 - core), "core")
-    mine = transform(core)
-
-    def own_chunk(j):
+    def as_blocks(a, b):
+        return jnp.concatenate([a.reshape(blocks, tile, cw), b.reshape(blocks, tile, cw)])
+
+    theirs0 = transform(features, 1 - core, 0, cw)
+    later = after(features, theirs0)
+    mine0 = transform(later, core, 0, cw)
+    own = [as_blocks(mine0, swap(theirs0, "core"))]
+    later = after(later, mine0)
+    theirs = swap(transform(later, 1 - core, cw, half - cw), "core")
+    mine = transform(later, core, cw, half - cw)
+    for j in range(CHUNKS - 1):
         cols = slice(j * cw, (j + 1) * cw)
-        return jnp.concatenate(
-            [mine[:, cols].reshape(blocks, tile, cw), theirs[:, cols].reshape(blocks, tile, cw)]
-        )
+        own.append(as_blocks(mine[:, cols], theirs[:, cols]))
+    first = swap(own[0], "x_lo")
 
     live = live_tiles[0, 0]
     used = jnp.arange(slots, dtype=jnp.int32) < live
@@ -161,7 +171,7 @@
     meta = jnp.stack(
         [rows_own, jnp.where(used, tile_cols[0, 0], 0), jnp.full((slots,), live, jnp.int32)]
     )
-    c_other = swap(after(c_own, theirs), "core")
+    c_other = swap(after(c_own, theirs, own[0]), "core")
     metas = jnp.stack([meta, swap(meta, "core")])
     k = metas[:, 1]
     src = (
@@ -194,13 +204,12 @@
     w_own = lax.dynamic_slice_in_dim(combine_weight, width + core * half, half, 0)
     w_other = lax.dynamic_slice_in_dim(combine_weight, width + (1 - core) * half, half, 0)
 
-    own = [own_chunk(j) for j in range(CHUNKS)]
-    first = swap(own[0], "x_lo")
-    rest = swap(jnp.stack(own[1:]), "x_lo")
-    partner = [first] + [rest[j] for j in range(CHUNKS - 1)]
+    second = swap(after(own[1], first), "x_lo")
+    rest = swap(after(jnp.stack(own[2:]), second), "x_lo")
+    partner = [first, second] + [rest[j] for j in range(CHUNKS - 2)]
 
     f32, bf16 = jnp.float32, jnp.bfloat16
-    near_all, part_all, pass_all, zb_all, swap_all = [], [], [], [], []
+    near_all, part_all, pass_all, zb_all, hidden_all = [], [], [], [], []
     scale = None
     for j in range(CHUNKS):
         pair = jnp.concatenate([own[j], partner[j]])
@@ -213,26 +222,24 @@
         far = step(near, "y", 1)
         earlier = ()
         if j >= 2:
-            earlier += (pass_all[j - 2],)
-        if j >= 3:
-            earlier += (zb_all[j - 3],)
+            earlier += (pass_all[j - 2], zb_all[j - 2])
         send, pass_on, stay = tile_sums(
             src, dst, lives, c_own, c_other, parts, j == 0, near, far, earlier
         )
         part_all.append((send, pass_on, stay))
+        if j >= 1:
+            send = after(send, pass_all[j - 1])
         size = stay.shape[0] // 2
         got = step(send, "z", 0)
         passed = (got[: 2 * size].astype(f32) + pass_on).astype(bf16)
         pass_all.append(passed)
         stay = got[2 * size :].astype(f32) + stay
-        if j == CHUNKS - 1:
-            passed = after(passed, swap_all[j - 2])
         got = step(passed, "z", 1)
         zb_all.append(got)
         passed = (got[:size].astype(f32) + stay[:size]).astype(bf16)
         stay = got[size:].astype(f32) + stay[size:]
         if j == CHUNKS - 1:
-            passed = after(passed, swap_all[j - 1])
+            passed = after(passed, hidden_all[j - 2])
         pooled = swap(passed, "x_hi").astype(f32) + stay
         if j == 0:
             deg = jnp.sum(
@@ -242,13 +249,14 @@
             )
             scale = 1.0 / (1.0 + deg)
             pooled = pooled[: 8 * tile]
-        mean = (pooled.reshape(8, tile, cw) * scale[..., None]).astype(bf16)
+        factor = after(scale, passed)[..., None]
+        mean = (pooled.reshape(8, tile, cw) * factor).astype(bf16)
         mean = mean.reshape(2, rows_dev, cw)
         got = swap(mean[1], "core")
-        swap_all.append(got)
         cols = slice(j * cw, (j + 1) * cw)
         hidden = hidden + jnp.dot(mean[0], w_own[cols], preferred_element_type=f32)
         hidden = hidden + jnp.dot(got, w_other[cols], preferred_element_type=f32)
+        hidden_all.append(hidden)
     hidden = jax.nn.relu(hidden)
     return hidden / jnp.sqrt(jnp.mean(hidden * hidden, axis=1, keepdims=True) + 1e-06)
 

time: 196 us -> 199 us (1.015)
  waiting for transfers between devices: 76.7 us -> 85.4 us
  other arithmetic: 21 us -> 16.8 us
  local copies, waits for them, and re-layouts: 13.1 us -> 9.69 us
  matrix products: 10.7 us -> 13.1 us
    ppermute x16, waiting for transfers between devices: 46 us -> 66.8 us  [step(): return lax.ppermute(x, (axis, 'core'), pairs)]
    ppermute x13 -> x15, waiting for transfers between devices: 30.7 us -> 18.6 us  [swap(): return lax.ppermute(x, axis, [(0, 1), (1, 0)])]
    ppermute x13 -> x15, starting transfers between devices: 26.7 us -> 20.7 us  [swap(): return lax.ppermute(x, axis, [(0, 1), (1, 0)])]
    ppermute x16, starting transfers between devices: 21.4 us -> 27.2 us  [step(): return lax.ppermute(x, (axis, 'core'), pairs)]
    dot_general x2 -> x4, matrix products: 3.56 us -> 6.34 us  [transform(): out = jnp.dot(features, weight, preferred_element_type=jnp.float32) + bias]
    add x4, other arithmetic: 2.37 us -> 0.31 us  [local(): pooled = swap(passed, 'x_hi').astype(f32) + stay]
    unnamed x57 -> x37, local copies, waits for them, and re-layouts: 5.45 us -> 3.56 us
  transfers between devices with their start and end apart: 29 -> 31, of which waited for: 16 -> 17; matrix products, arithmetic and copies ran while one was open for 17% -> 17% of each run, Pallas kernels for 12% -> 12%
where the time goes in v3:
time: 199 us; the launch traced here: 198 us
  waiting for transfers between devices  85.4 us (43%)
  starting transfers between devices  47.9 us (24%)
  Pallas kernels  23.6 us (12%)
  other arithmetic  16.8 us (8%)
  matrix products  13.1 us (7%)
  local copies, waits for them, and re-layouts  9.69 us (5%)
    ppermute x16, waiting for transfers between devices, step(): return lax.ppermute(x, (axis, 'core'), pairs)  66.8 us
    ppermute x16, starting transfers between devices, step(): return lax.ppermute(x, (axis, 'core'), pairs)  27.2 us
    pallas_call x4, Pallas kernels, tile_sums(): pl.pallas_call(tile_kernel, out_shape=(jax.ShapeDtypeStruct((4 * size, w)...  23.6 us
    ppermute x15, starting transfers between devices, swap(): return lax.ppermute(x, axis, [(0, 1), (1, 0)])  20.7 us
    ppermute x15, waiting for transfers between devices, swap(): return lax.ppermute(x, axis, [(0, 1), (1, 0)])  18.6 us
    dot_general x4, matrix products, transform(): out = jnp.dot(features, weight, preferred_element_type=jnp.float32) + bias  6.34 us
    reduce_sum x1, other arithmetic, local(): jnp.sum(c_own.astype(jnp.float32), axis=2)  4.15 us
  transfers between devices with their start and end apart: 31, of which 17 were waited for; matrix products, arithmetic and copies ran while one was open for 17% of the time, Pallas kernels for 12%

profile of v3, /device:TPU:3, one launch (start us, length us, event | category | flops | bytes accessed | tf_op | source)
XLA Modules:
  0.0 197.9 jit_solution(11210197925856118313)
XLA Ops:
  3.2 1.7 fusion.11
  5.8 1.7 fusion.10
  7.5 1.5 fusion.6
  9.4 4.2 %convert_reduce_fusion.1 = (f32[64,128]{1,0:T(8,128)S(1)}, bf16[64,128,128]{2,1,0:T(8,128)(2,1)}) fusion(s32[1,1,64,128,128]{4,3,2,1,0:T(8,128)} %param.11, pred[64]{0:T(512)(128)(4,1)S(1)} %iota_compare_fusion.2), kind=kLoop, calls=%fused_computation.3 | loop fusion | flops 4186112 | bytes 6324288 | tf_op jit(solution)/shard_map/reduce_sum | solution.py:193
  13.6 1.0 copy.12
  15.4 1.5 fusion.5
  17.0 1.1 fusion.71
  18.6 5.9 %collective-permute-done.4 = bf16[8,128,128]{2,1,0:T(8,128)(2,1)S(1)} collective-permute-done((bf16[8,128,128]{2,1,0:T(8,128)(2,1)}, bf16[8,128,128]{2,1,0:T(8,128)(2,1)S(1)}, u32[]{:S(2)}, u32[]{:S(2)}) %collective-permute-start.4) | collective-permute-done | bytes 262176 | tf_op jit(solution)/shard_map/ppermute | solution.py:15
  24.5 2.8 %collective-permute-start.5 = (bf16[16,128,128]{2,1,0:T(8,128)(2,1)S(1)}, bf16[16,128,128]{2,1,0:T(8,128)(2,1)S(1)}, u32[]{:S(2)}, u32[]{:S(2)}) collective-permute-start(bf16[16,128,128]{2,1,0:T(8,128)(2,1)S(1)} %pad_maximum_fusion.1), channel_id=1, source_target_pairs={{0,16},{1,49},{16,0},{17,33},{32,48},{33,17},{48,32},{49,1},{2,18}... | collective-permute-start | bytes 1572872 | tf_op jit(solution)/shard_map/ppermute | solution.py:24
  27.4 1.1 fusion.72
  28.8 5.1 %collective-permute-done.5 = bf16[16,128,128]{2,1,0:T(8,128)(2,1)S(1)} collective-permute-done((bf16[16,128,128]{2,1,0:T(8,128)(2,1)S(1)}, bf16[16,128,128]{2,1,0:T(8,128)(2,1)S(1)}, u32[]{:S(2)}, u32[]{:S(2)}) %collective-permute-start.5) | collective-permute-done | bytes 524320 | tf_op jit(solution)/shard_map/ppermute | solution.py:24
  37.4 1.6 collective-permute-start.12
  39.1 2.2 %convert_reduce_fusion = f32[64,128]{1,0:T(8,128)S(1)} fusion(bf16[64,128,128]{2,1,0:T(8,128)(2,1)} %collective-permute-done.3.c_other), kind=kLoop, calls=%fused_computation.2 | loop fusion | flops 2088960 | bytes 2129920 | tf_op jit(solution)/shard_map/reduce_sum | solution.py:193
  41.6 10.2 %collective-permute-done.6.far = bf16[32,128,128]{2,1,0:T(8,128)(2,1)S(1)} collective-permute-done((bf16[32,128,128]{2,1,0:T(8,128)(2,1)S(1)}, bf16[32,128,128]{2,1,0:T(8,128)(2,1)S(1)}, u32[]{:S(2)}, u32[]{:S(2)}) %collective-permute-start.6) | collective-permute-done | bytes 1048608 | tf_op jit(solution)/shard_map/ppermute | solution.py:24
  51.9 6.6 %shard_map.100 = (bf16[4224,128]{1,0:T(8,128)(2,1)}, f32[2112,128]{1,0:T(8,128)S(1)}, f32[2112,128]{1,0:T(8,128)S(1)}) custom-call(s32[128]{0:T(128)S(1)} %fusion.55.src_ref, s32[128]{0:T(128)S(1)} %fusion.56.dst_ref, s32[2]{0:T(128)S(1)} %fusion.54.live_ref, bf16[64,128,128]{2,1,0:T(8,128)(2,1)S(1)} %copy-done.2, ...), custom_call_target="tpu_custom_call" | custom-call | flops 2147483648 | bytes 8388608 | tf_op jit(solution)/shard_map/pallas_call | solution.py:100
  58.5 1.0 copy-done.4
  59.5 2.1 %collective-permute-start.7 = (bf16[4224,128]{1,0:T(8,128)(2,1)}, bf16[4224,128]{1,0:T(8,128)(2,1)}, u32[]{:S(2)}, u32[]{:S(2)}) collective-permute-start(bf16[4224,128]{1,0:T(8,128)(2,1)} %get-tuple-element.36), channel_id=1, source_target_pairs={{0,4},{1,13},{4,0},{5,9},{8,12},{9,5},{12,8},{13,1},{2,6},{3,15},{... | collective-permute-start | bytes 3244040 | tf_op jit(solution)/shard_map/ppermute | solution.py:24
  61.6 2.6 %fusion.1 = f32[512,1024]{1,0:T(8,128)} fusion(bf16[512,1024]{1,0:T(8,128)(2,1)S(1)} %copy-done.12, bf16[2048,1024]{1,0:T(8,128)(2,1)S(1)} %copy-done.13), kind=kOutput, calls=%fused_computation.7 | convolution fusion | flops 1073741824 | bytes 5242880 | tf_op jit(solution)/shard_map/dot_general | solution.py:201
  64.2 1.1 constant_dynamic-update-slice_fusion.1
  65.4 1.2 slice_bitcast_fusion.1
  66.6 1.1 constant_dynamic-update-slice_fusion.near
  67.7 2.5 %collective-permute-start.13 = (bf16[32,128,128]{2,1,0:T(8,128)(2,1)S(1)}, bf16[32,128,128]{2,1,0:T(8,128)(2,1)S(1)}, u32[]{:S(2)}, u32[]{:S(2)}) collective-permute-start(bf16[32,128,128]{2,1,0:T(8,128)(2,1)S(1)} %constant_dynamic-update-slice_fusion.near), channel_id=1, source_target_pairs={{0,48},{1,17},{16,32},{17,1},{32,16},{33,49},{48,0},{49,33},{2,50}... | collective-permute-start | bytes 3145736 | tf_op jit(solution)/shard_map/ppermute | solution.py:24
  70.2 4.0 %collective-permute-start.19 = (bf16[16,128,128]{2,1,0:T(8,128)(2,1)S(1)}, bf16[16,128,128]{2,1,0:T(8,128)(2,1)S(1)}, u32[]{:S(2)}, u32[]{:S(2)}) collective-permute-start(bf16[16,128,128]{2,1,0:T(8,128)(2,1)S(1)} %pad_maximum_fusion.4), channel_id=1, source_target_pairs={{0,16},{1,49},{16,0},{17,33},{32,48},{33,17},{48,32},{49,1},{2,18}... | collective-permute-start | bytes 1572872 | tf_op jit(solution)/shard_map/ppermute | solution.py:24
  75.0 1.4 convert_add_fusion
  76.8 9.7 %collective-permute-done.19 = bf16[16,128,128]{2,1,0:T(8,128)(2,1)S(1)} collective-permute-done((bf16[16,128,128]{2,1,0:T(8,128)(2,1)S(1)}, bf16[16,128,128]{2,1,0:T(8,128)(2,1)S(1)}, u32[]{:S(2)}, u32[]{:S(2)}) %collective-permute-start.19) | collective-permute-done | bytes 524320 | tf_op jit(solution)/shard_map/ppermute | solution.py:24
  86.6 1.2 collective-permute-start.20
  87.9 5.8 %shard_map.101 = (bf16[4096,128]{1,0:T(8,128)(2,1)S(1)}, f32[2048,128]{1,0:T(8,128)S(1)}, f32[2048,128]{1,0:T(8,128)S(1)}) custom-call(s32[128]{0:T(128)S(1)} %fusion.55.src_ref, s32[128]{0:T(128)S(1)} %fusion.56.dst_ref, s32[2]{0:T(128)S(1)} %fusion.54.live_ref, bf16[64,128,128]{2,1,0:T(8,128)(2,1)S(1)} %copy-done.3, ...), custom_call_target="tpu_custom_call" | custom-call | flops 2147483648 | bytes 8388608 | tf_op jit(solution)/shard_map/pallas_call | solution.py:100
  93.7 5.4 %collective-permute-start.25 = (bf16[16,128,128]{2,1,0:T(8,128)(2,1)S(1)}, bf16[16,128,128]{2,1,0:T(8,128)(2,1)S(1)}, u32[]{:S(2)}, u32[]{:S(2)}) collective-permute-start(bf16[16,128,128]{2,1,0:T(8,128)(2,1)S(1)} %pad_maximum_fusion.5), channel_id=1, source_target_pairs={{0,16},{1,49},{16,0},{17,33},{32,48},{33,17},{48,32},{49,1},{2,18}... | collective-permute-start | bytes 1572872 | tf_op jit(solution)/shard_map/ppermute | solution.py:24
  99.3 10.5 %collective-permute-done.25 = bf16[16,128,128]{2,1,0:T(8,128)(2,1)S(1)} collective-permute-done((bf16[16,128,128]{2,1,0:T(8,128)(2,1)S(1)}, bf16[16,128,128]{2,1,0:T(8,128)(2,1)S(1)}, u32[]{:S(2)}, u32[]{:S(2)}) %collective-permute-start.25) | collective-permute-done | bytes 524320 | tf_op jit(solution)/shard_map/ppermute | solution.py:24
  110.9 5.6 %shard_map.102 = (bf16[4096,128]{1,0:T(8,128)(2,1)S(1)}, f32[2048,128]{1,0:T(8,128)S(1)}, f32[2048,128]{1,0:T(8,128)S(1)}) custom-call(s32[128]{0:T(128)S(1)} %fusion.55.src_ref, s32[128]{0:T(128)S(1)} %fusion.56.dst_ref, s32[2]{0:T(128)S(1)} %fusion.54.live_ref, bf16[64,128,128]{2,1,0:T(8,128)(2,1)S(1)} %copy-done.3, ...), custom_call_target="tpu_custom_call" | custom-call | flops 2147483648 | bytes 8388608 | tf_op jit(solution)/shard_map/pallas_call | solution.py:100
  117.3 7.7 %collective-permute-done.14 = bf16[4096,128]{1,0:T(8,128)(2,1)S(1)} collective-permute-done((bf16[4096,128]{1,0:T(8,128)(2,1)S(1)}, bf16[4096,128]{1,0:T(8,128)(2,1)S(1)}, u32[]{:S(2)}, u32[]{:S(2)}) %collective-permute-start.14) | collective-permute-done | bytes 1048608 | tf_op jit(solution)/shard_map/ppermute | solution.py:24
  125.5 1.6 collective-permute-start.10
  127.1 2.7 %collective-permute-start.21 = (bf16[4096,128]{1,0:T(8,128)(2,1)S(1)}, bf16[4096,128]{1,0:T(8,128)(2,1)S(1)}, u32[]{:S(2)}, u32[]{:S(2)}) collective-permute-start(bf16[4096,128]{1,0:T(8,128)(2,1)S(1)} %get-tuple-element.50), channel_id=1, source_target_pairs={{0,4},{1,13},{4,0},{5,9},{8,12},{9,5},{12,8},{13,1},{2,6},{3,15},{... | collective-permute-start | bytes 3145736 | tf_op jit(solution)/shard_map/ppermute | solution.py:24
  130.2 6.5 %collective-permute-done.15.refs_1_ = bf16[2048,128]{1,0:T(8,128)(2,1)S(1)} collective-permute-done((bf16[2048,128]{1,0:T(8,128)(2,1)S(1)}, bf16[2048,128]{1,0:T(8,128)(2,1)S(1)}, u32[]{:S(2)}, u32[]{:S(2)}) %collective-permute-start.15) | collective-permute-done | bytes 524320 | tf_op jit(solution)/shard_map/ppermute | solution.py:24
  136.7 3.3 %collective-permute-start.16 = (bf16[1024,128]{1,0:T(8,128)(2,1)S(1)}, bf16[1024,128]{1,0:T(8,128)(2,1)S(1)}, u32[]{:S(2)}, u32[]{:S(2)}) collective-permute-start(bf16[1024,128]{1,0:T(8,128)(2,1)S(1)} %fusion.21), channel_id=1, source_target_pairs={{0,2},{2,0},{1,3},{3,1},{4,6},{6,4},{5,7},{7,5},{8,10},{10,8},{9,1... | collective-permute-start | bytes 786440 | tf_op jit(solution)/shard_map/ppermute | solution.py:15
  140.4 5.6 %shard_map.103 = (bf16[4096,128]{1,0:T(8,128)(2,1)S(1)}, f32[2048,128]{1,0:T(8,128)S(1)}, f32[2048,128]{1,0:T(8,128)S(1)}) custom-call(s32[128]{0:T(128)S(1)} %fusion.55.src_ref, s32[128]{0:T(128)S(1)} %fusion.56.dst_ref, s32[2]{0:T(128)S(1)} %fusion.54.live_ref, bf16[64,128,128]{2,1,0:T(8,128)(2,1)S(1)} %copy-done.3, ...), custom_call_target="tpu_custom_call" | custom-call | flops 2147483648 | bytes 8388608 | tf_op jit(solution)/shard_map/pallas_call | solution.py:100
  146.1 1.4 collective-permute-done.21
  148.1 3.0 %collective-permute-start.17 = (bf16[512,128]{1,0:T(8,128)(2,1)S(1)}, bf16[512,128]{1,0:T(8,128)(2,1)S(1)}, u32[]{:S(2)}, u32[]{:S(2)}) collective-permute-start(bf16[512,128]{1,0:T(8,128)(2,1)S(1)} %bitcast.88), channel_id=1, source_target_pairs={{0,1},{1,0},{2,3},{3,2},{4,5},{5,4},{6,7},{7,6},{8,9},{9,8},{10,11... | collective-permute-start | bytes 393224 | tf_op jit(solution)/shard_map/ppermute | solution.py:15
  151.1 2.9 %collective-permute-start.27 = (bf16[4096,128]{1,0:T(8,128)(2,1)S(1)}, bf16[4096,128]{1,0:T(8,128)(2,1)S(1)}, u32[]{:S(2)}, u32[]{:S(2)}) collective-permute-start(bf16[4096,128]{1,0:T(8,128)(2,1)S(1)} %get-tuple-element.56), channel_id=1, source_target_pairs={{0,4},{1,13},{4,0},{5,9},{8,12},{9,5},{12,8},{13,1},{2,6},{3,15},{... | collective-permute-start | bytes 3145736 | tf_op jit(solution)/shard_map/ppermute | solution.py:24
  154.5 3.4 %collective-permute-done.22 = bf16[2048,128]{1,0:T(8,128)(2,1)S(1)} collective-permute-done((bf16[2048,128]{1,0:T(8,128)(2,1)S(1)}, bf16[2048,128]{1,0:T(8,128)(2,1)S(1)}, u32[]{:S(2)}, u32[]{:S(2)}) %collective-permute-start.22) | collective-permute-done | bytes 524320 | tf_op jit(solution)/shard_map/ppermute | solution.py:24
  157.9 0.9 collective-permute-start.23
  159.6 5.5 %collective-permute-done.23 = bf16[1024,128]{1,0:T(8,128)(2,1)S(1)} collective-permute-done((bf16[1024,128]{1,0:T(8,128)(2,1)S(1)}, bf16[1024,128]{1,0:T(8,128)(2,1)S(1)}, u32[]{:S(2)}, u32[]{:S(2)}) %collective-permute-start.23) | collective-permute-done | bytes 262176 | tf_op jit(solution)/shard_map/ppermute | solution.py:15
  165.1 6.7 %collective-permute-done.27 = bf16[4096,128]{1,0:T(8,128)(2,1)S(1)} collective-permute-done((bf16[4096,128]{1,0:T(8,128)(2,1)S(1)}, bf16[4096,128]{1,0:T(8,128)(2,1)S(1)}, u32[]{:S(2)}, u32[]{:S(2)}) %collective-permute-start.27) | collective-permute-done | bytes 1048608 | tf_op jit(solution)/shard_map/ppermute | solution.py:24
  172.3 3.0 %collective-permute-start.24 = (bf16[512,128]{1,0:T(8,128)(2,1)S(1)}, bf16[512,128]{1,0:T(8,128)(2,1)S(1)}, u32[]{:S(2)}, u32[]{:S(2)}) collective-permute-start(bf16[512,128]{1,0:T(8,128)(2,1)S(1)} %bitcast.90), channel_id=1, source_target_pairs={{0,1},{1,0},{2,3},{3,2},{4,5},{5,4},{6,7},{7,6},{8,9},{9,8},{10,11... | collective-permute-start | bytes 393224 | tf_op jit(solution)/shard_map/ppermute | solution.py:15
  175.7 4.7 %collective-permute-done.28 = bf16[2048,128]{1,0:T(8,128)(2,1)S(1)} collective-permute-done((bf16[2048,128]{1,0:T(8,128)(2,1)S(1)}, bf16[2048,128]{1,0:T(8,128)(2,1)S(1)}, u32[]{:S(2)}, u32[]{:S(2)}) %collective-permute-start.28) | collective-permute-done | bytes 524320 | tf_op jit(solution)/shard_map/ppermute | solution.py:24
  181.4 5.8 %collective-permute-done.29 = bf16[1024,128]{1,0:T(8,128)(2,1)S(1)} collective-permute-done((bf16[1024,128]{1,0:T(8,128)(2,1)S(1)}, bf16[1024,128]{1,0:T(8,128)(2,1)S(1)}, u32[]{:S(2)}, u32[]{:S(2)}) %collective-permute-start.29) | collective-permute-done | bytes 262176 | tf_op jit(solution)/shard_map/ppermute | solution.py:15
  187.6 6.2 %collective-permute-start.30 = (bf16[512,128]{1,0:T(8,128)(2,1)S(1)}, bf16[512,128]{1,0:T(8,128)(2,1)S(1)}, u32[]{:S(2)}, u32[]{:S(2)}) collective-permute-start(bf16[512,128]{1,0:T(8,128)(2,1)S(1)} %bitcast.91), channel_id=1, source_target_pairs={{0,1},{1,0},{2,3},{3,2},{4,5},{5,4},{6,7},{7,6},{8,9},{9,8},{10,11... | collective-permute-start | bytes 393224 | tf_op jit(solution)/shard_map/ppermute | solution.py:15
  195.6 1.6 broadcast_divide_fusion
  (133 shorter events, 20.7 us)
Async XLA Ops:
  0.0 3.2 %copy-start = (bf16[1024,1024]{1,0:T(8,128)(2,1)S(1)}, bf16[1024,1024]{1,0:T(8,128)(2,1)}, u32[]{:S(2)}) copy-start(bf16[1024,1024]{1,0:T(8,128)(2,1)} %param.15) | copy-start | bytes 6291460
  0.0 7.5 %copy-start.11 = (bf16[512,1024]{1,0:T(8,128)(2,1)S(1)}, bf16[512,1024]{1,0:T(8,128)(2,1)}, u32[]{:S(2)}) copy-start(bf16[512,1024]{1,0:T(8,128)(2,1)} %param.10) | copy-start | bytes 3145732
  1.7 16.7 %collective-permute-start = (s32[3,64]{1,0:T(4,128)S(1)}, s32[3,64]{1,0:T(4,128)S(1)}, u32[]{:S(2)}, u32[]{:S(2)}) collective-permute-start(s32[3,64]{1,0:T(4,128)S(1)} %get-tuple-element.94), channel_id=1, source_target_pairs={{0,1},{1,0},{2,3},{3,2},{4,5},{5,4},{6,7},{7,6},{8,9},{9,8},{10,11... | collective-permute-start | bytes 2312 | tf_op jit(solution)/shard_map/ppermute | solution.py:15
  4.9 8.7 %collective-permute-start.2 = (bf16[512,128]{0,1:T(8,128)(2,1)S(1)}, bf16[512,128]{0,1:T(8,128)(2,1)}, u32[]{:S(2)}, u32[]{:S(2)}) collective-permute-start(bf16[512,128]{0,1:T(8,128)(2,1)S(1)} %fusion.11), channel_id=1, source_target_pairs={{0,1},{1,0},{2,3},{3,2},{4,5},{5,4},{6,7},{7,6},{8,9},{9,8},{10,11... | collective-permute-start | bytes 393224 | tf_op jit(solution)/shard_map/ppermute | solution.py:15
  8.9 6.4 %collective-permute-start.1 = (bf16[512,384]{1,0:T(8,128)(2,1)}, bf16[512,384]{1,0:T(8,128)(2,1)}, u32[]{:S(2)}, u32[]{:S(2)}) collective-permute-start(bf16[512,384]{1,0:T(8,128)(2,1)} %fusion.6), channel_id=1, source_target_pairs={{0,1},{1,0},{2,3},{3,2},{4,5},{5,4},{6,7},{7,6},{8,9},{9,8},{10,11... | collective-permute-start | bytes 1179656 | tf_op jit(solution)/shard_map/ppermute | solution.py:15
  15.3 23.8 %collective-permute-start.3 = (bf16[64,128,128]{2,1,0:T(8,128)(2,1)}, bf16[64,128,128]{2,1,0:T(8,128)(2,1)}, u32[]{:S(2)}, u32[]{:S(2)}) collective-permute-start(bf16[64,128,128]{2,1,0:T(8,128)(2,1)} %get-tuple-element.35.c_own), channel_id=1, source_target_pairs={{0,1},{1,0},{2,3},{3,2},{4,5},{5,4},{6,7},{7,6},{8,9},{9,8},{10,11... | collective-permute-start | bytes 6291464 | tf_op jit(solution)/shard_map/ppermute | solution.py:15
  16.9 7.6 %collective-permute-start.4 = (bf16[8,128,128]{2,1,0:T(8,128)(2,1)}, bf16[8,128,128]{2,1,0:T(8,128)(2,1)S(1)}, u32[]{:S(2)}, u32[]{:S(2)}) collective-permute-start(bf16[8,128,128]{2,1,0:T(8,128)(2,1)} %pad_maximum_fusion.6), channel_id=1, source_target_pairs={{0,64},{64,0},{1,65},{65,1},{2,66},{66,2},{3,67},{67,3},{4,68},{68... | collective-permute-start | bytes 786440 | tf_op jit(solution)/shard_map/ppermute | solution.py:15
  24.5 9.4 %collective-permute-start.5 = (bf16[16,128,128]{2,1,0:T(8,128)(2,1)S(1)}, bf16[16,128,128]{2,1,0:T(8,128)(2,1)S(1)}, u32[]{:S(2)}, u32[]{:S(2)}) collective-permute-start(bf16[16,128,128]{2,1,0:T(8,128)(2,1)S(1)} %pad_maximum_fusion.1), channel_id=1, source_target_pairs={{0,16},{1,49},{16,0},{17,33},{32,48},{33,17},{48,32},{49,1},{2,18}... | collective-permute-start | bytes 1572872 | tf_op jit(solution)/shard_map/ppermute | solution.py:24
  28.4 7.1 %copy-start.7 = (bf16[512,128]{1,0:T(8,128)(2,1)}, bf16[512,128]{1,0:T(8,128)(2,1)S(1)}, u32[]{:S(2)}) copy-start(bf16[512,128]{1,0:T(8,128)(2,1)S(1)} %get-tuple-element.79) | copy-start | bytes 393220
  28.4 7.1 %copy-start.9 = (bf16[512,128]{1,0:T(8,128)(2,1)}, bf16[512,128]{1,0:T(8,128)(2,1)S(1)}, u32[]{:S(2)}) copy-start(bf16[512,128]{1,0:T(8,128)(2,1)S(1)} %get-tuple-element.80) | copy-start | bytes 393220
  28.5 7.8 %collective-permute-start.11 = (bf16[8,128,128]{2,1,0:T(8,128)(2,1)S(1)}, bf16[8,128,128]{2,1,0:T(8,128)(2,1)S(1)}, u32[]{:S(2)}, u32[]{:S(2)}) collective-permute-start(bf16[8,128,128]{2,1,0:T(8,128)(2,1)S(1)} %pad_maximum_fusion.7), channel_id=1, source_target_pairs={{0,64},{64,0},{1,65},{65,1},{2,66},{66,2},{3,67},{67,3},{4,68},{68... | collective-permute-start | bytes 786440 | tf_op jit(solution)/shard_map/ppermute | solution.py:15
  34.0 17.8 %collective-permute-start.6 = (bf16[32,128,128]{2,1,0:T(8,128)(2,1)S(1)}, bf16[32,128,128]{2,1,0:T(8,128)(2,1)S(1)}, u32[]{:S(2)}, u32[]{:S(2)}) collective-permute-start(bf16[32,128,128]{2,1,0:T(8,128)(2,1)S(1)} %pad_maximum_fusion.near), channel_id=1, source_target_pairs={{0,48},{1,17},{16,32},{17,1},{32,16},{33,49},{48,0},{49,33},{2,50}... | collective-permute-start | bytes 3145736 | tf_op jit(solution)/shard_map/ppermute | solution.py:24
  34.6 17.2 %copy-start.2 = (bf16[64,128,128]{2,1,0:T(8,128)(2,1)S(1)}, bf16[64,128,128]{2,1,0:T(8,128)(2,1)}, u32[]{:S(2)}) copy-start(bf16[64,128,128]{2,1,0:T(8,128)(2,1)} %get-tuple-element.35.c_own) | copy-start | bytes 6291460
  36.3 29.0 %collective-permute-start.18 = (bf16[2,8,128,128]{3,2,1,0:T(8,128)(2,1)}, bf16[2,8,128,128]{3,2,1,0:T(8,128)(2,1)}, u32[]{:S(2)}, u32[]{:S(2)}) collective-permute-start(bf16[2,8,128,128]{3,2,1,0:T(8,128)(2,1)} %pad_maximum_fusion.3), channel_id=1, source_target_pairs={{0,64},{64,0},{1,65},{65,1},{2,66},{66,2},{3,67},{67,3},{4,68},{68... | collective-permute-start | bytes 1572872 | tf_op jit(solution)/shard_map/ppermute | solution.py:15
  37.4 29.1 %collective-permute-start.12 = (bf16[16,128,128]{2,1,0:T(8,128)(2,1)}, bf16[16,128,128]{2,1,0:T(8,128)(2,1)}, u32[]{:S(2)}, u32[]{:S(2)}) collective-permute-start(bf16[16,128,128]{2,1,0:T(8,128)(2,1)} %pad_maximum_fusion.2), channel_id=1, source_target_pairs={{0,16},{1,49},{16,0},{17,33},{32,48},{33,17},{48,32},{49,1},{2,18}... | collective-permute-start | bytes 1572872 | tf_op jit(solution)/shard_map/ppermute | solution.py:24
  41.6 20.0 %copy-start.12 = (bf16[512,1024]{1,0:T(8,128)(2,1)S(1)}, bf16[512,1024]{1,0:T(8,128)(2,1)}, u32[]{:S(2)}) copy-start(bf16[512,1024]{1,0:T(8,128)(2,1)} %param.10) | copy-start | bytes 3145732
  41.6 20.0 %copy-start.13 = (bf16[2048,1024]{1,0:T(8,128)(2,1)S(1)}, bf16[2048,1024]{1,0:T(8,128)(2,1)}, u32[]{:S(2)}) copy-start(bf16[2048,1024]{1,0:T(8,128)(2,1)} %param.17) | copy-start | bytes 12582916
  58.5 1.0 copy-start.4
  59.5 15.5 %collective-permute-start.7 = (bf16[4224,128]{1,0:T(8,128)(2,1)}, bf16[4224,128]{1,0:T(8,128)(2,1)}, u32[]{:S(2)}, u32[]{:S(2)}) collective-permute-start(bf16[4224,128]{1,0:T(8,128)(2,1)} %get-tuple-element.36), channel_id=1, source_target_pairs={{0,4},{1,13},{4,0},{5,9},{8,12},{9,5},{12,8},{13,1},{2,6},{3,15},{... | collective-permute-start | bytes 3244040 | tf_op jit(solution)/shard_map/ppermute | solution.py:24
  64.2 2.3 %copy-start.10 = (bf16[512,128]{1,0:T(8,128)(2,1)S(1)}, bf16[512,128]{1,0:T(8,128)(2,1)}, u32[]{:S(2)}) copy-start(bf16[512,128]{1,0:T(8,128)(2,1)} %copy-done.9) | copy-start | bytes 393220
  65.3 9.7 %copy-start.5 = (f32[2112,128]{1,0:T(8,128)S(1)}, f32[2112,128]{1,0:T(8,128)}, u32[]{:S(2)}) copy-start(f32[2112,128]{1,0:T(8,128)} %copy-done.4) | copy-start | bytes 3244036
  67.7 20.2 %collective-permute-start.13 = (bf16[32,128,128]{2,1,0:T(8,128)(2,1)S(1)}, bf16[32,128,128]{2,1,0:T(8,128)(2,1)S(1)}, u32[]{:S(2)}, u32[]{:S(2)}) collective-permute-start(bf16[32,128,128]{2,1,0:T(8,128)(2,1)S(1)} %constant_dynamic-update-slice_fusion.near), channel_id=1, source_target_pairs={{0,48},{1,17},{16,32},{17,1},{32,16},{33,49},{48,0},{49,33},{2,50}... | collective-permute-start | bytes 3145736 | tf_op jit(solution)/shard_map/ppermute | solution.py:24
  70.2 16.2 %collective-permute-start.19 = (bf16[16,128,128]{2,1,0:T(8,128)(2,1)S(1)}, bf16[16,128,128]{2,1,0:T(8,128)(2,1)S(1)}, u32[]{:S(2)}, u32[]{:S(2)}) collective-permute-start(bf16[16,128,128]{2,1,0:T(8,128)(2,1)S(1)} %pad_maximum_fusion.4), channel_id=1, source_target_pairs={{0,16},{1,49},{16,0},{17,33},{32,48},{33,17},{48,32},{49,1},{2,18}... | collective-permute-start | bytes 1572872 | tf_op jit(solution)/shard_map/ppermute | solution.py:24
  75.0 12.7 %copy-start.8 = (bf16[512,128]{1,0:T(8,128)(2,1)S(1)}, bf16[512,128]{1,0:T(8,128)(2,1)}, u32[]{:S(2)}) copy-start(bf16[512,128]{1,0:T(8,128)(2,1)} %copy-done.7) | copy-start | bytes 393220
  76.5 11.4 %copy-start.3 = (bf16[64,128,128]{2,1,0:T(8,128)(2,1)S(1)}, bf16[64,128,128]{2,1,0:T(8,128)(2,1)}, u32[]{:S(2)}) copy-start(bf16[64,128,128]{2,1,0:T(8,128)(2,1)} %get-tuple-element.35.c_own) | copy-start | bytes 6291460
  76.5 22.7 %collective-permute-start.8 = (bf16[2112,128]{1,0:T(8,128)(2,1)S(1)}, bf16[2112,128]{1,0:T(8,128)(2,1)S(1)}, u32[]{:S(2)}, u32[]{:S(2)}) collective-permute-start(bf16[2112,128]{1,0:T(8,128)(2,1)S(1)} %get-tuple-element.66.refs_0_), channel_id=1, source_target_pairs={{0,12},{1,5},{4,8},{5,1},{8,4},{9,13},{12,0},{13,9},{2,14},{3,7},{... | collective-permute-start | bytes 1622024 | tf_op jit(solution)/shard_map/ppermute | solution.py:24
  86.6 24.4 %collective-permute-start.20 = (bf16[32,128,128]{2,1,0:T(8,128)(2,1)S(1)}, bf16[32,128,128]{2,1,0:T(8,128)(2,1)S(1)}, u32[]{:S(2)}, u32[]{:S(2)}) collective-permute-start(bf16[32,128,128]{2,1,0:T(8,128)(2,1)S(1)} %constant_dynamic-update-slice_fusion.2.near), channel_id=1, source_target_pairs={{0,48},{1,17},{16,32},{17,1},{32,16},{33,49},{48,0},{49,33},{2,50}... | collective-permute-start | bytes 3145736 | tf_op jit(solution)/shard_map/ppermute | solution.py:24
  93.7 16.1 %collective-permute-start.25 = (bf16[16,128,128]{2,1,0:T(8,128)(2,1)S(1)}, bf16[16,128,128]{2,1,0:T(8,128)(2,1)S(1)}, u32[]{:S(2)}, u32[]{:S(2)}) collective-permute-start(bf16[16,128,128]{2,1,0:T(8,128)(2,1)S(1)} %pad_maximum_fusion.5), channel_id=1, source_target_pairs={{0,16},{1,49},{16,0},{17,33},{32,48},{33,17},{48,32},{49,1},{2,18}... | collective-permute-start | bytes 1572872 | tf_op jit(solution)/shard_map/ppermute | solution.py:24
  99.2 17.3 %collective-permute-start.9 = (bf16[1056,128]{1,0:T(8,128)(2,1)S(1)}, bf16[1056,128]{1,0:T(8,128)(2,1)S(1)}, u32[]{:S(2)}, u32[]{:S(2)}) collective-permute-start(bf16[1056,128]{1,0:T(8,128)(2,1)S(1)} %fusion.15), channel_id=1, source_target_pairs={{0,2},{2,0},{1,3},{3,1},{4,6},{6,4},{5,7},{7,5},{8,10},{10,8},{9,1... | collective-permute-start | bytes 811016 | tf_op jit(solution)/shard_map/ppermute | solution.py:15
  109.9 30.5 %collective-permute-start.26 = (bf16[32,128,128]{2,1,0:T(8,128)(2,1)S(1)}, bf16[32,128,128]{2,1,0:T(8,128)(2,1)S(1)}, u32[]{:S(2)}, u32[]{:S(2)}) collective-permute-start(bf16[32,128,128]{2,1,0:T(8,128)(2,1)S(1)} %constant_dynamic-update-slice_fusion.4.near), channel_id=1, source_target_pairs={{0,48},{1,17},{16,32},{17,1},{32,16},{33,49},{48,0},{49,33},{2,50}... | collective-permute-start | bytes 3145736 | tf_op jit(solution)/shard_map/ppermute | solution.py:24
  110.0 14.9 %collective-permute-start.14 = (bf16[4096,128]{1,0:T(8,128)(2,1)S(1)}, bf16[4096,128]{1,0:T(8,128)(2,1)S(1)}, u32[]{:S(2)}, u32[]{:S(2)}) collective-permute-start(bf16[4096,128]{1,0:T(8,128)(2,1)S(1)} %get-tuple-element.43), channel_id=1, source_target_pairs={{0,4},{1,13},{4,0},{5,9},{8,12},{9,5},{12,8},{13,1},{2,6},{3,15},{... | collective-permute-start | bytes 3145736 | tf_op jit(solution)/shard_map/ppermute | solution.py:24
  116.5 0.7 copy-start.16
  124.9 4.8 %copy-start.14 = (bf16[2048,1024]{1,0:T(8,128)(2,1)S(1)}, bf16[2048,1024]{1,0:T(8,128)(2,1)}, u32[]{:S(2)}) copy-start(bf16[2048,1024]{1,0:T(8,128)(2,1)} %param.17) | copy-start | bytes 12582916
  125.1 11.5 %collective-permute-start.15 = (bf16[2048,128]{1,0:T(8,128)(2,1)S(1)}, bf16[2048,128]{1,0:T(8,128)(2,1)S(1)}, u32[]{:S(2)}, u32[]{:S(2)}) collective-permute-start(bf16[2048,128]{1,0:T(8,128)(2,1)S(1)} %get-tuple-element.70.refs_0_), channel_id=1, source_target_pairs={{0,12},{1,5},{4,8},{5,1},{8,4},{9,13},{12,0},{13,9},{2,14},{3,7},{... | collective-permute-start | bytes 1572872 | tf_op jit(solution)/shard_map/ppermute | solution.py:24
  125.5 14.5 %collective-permute-start.10 = (bf16[512,128]{1,0:T(8,128)(2,1)S(1)}, bf16[512,128]{1,0:T(8,128)(2,1)S(1)}, u32[]{:S(2)}, u32[]{:S(2)}) collective-permute-start(bf16[512,128]{1,0:T(8,128)(2,1)S(1)} %bitcast.89), channel_id=1, source_target_pairs={{0,1},{1,0},{2,3},{3,2},{4,5},{5,4},{6,7},{7,6},{8,9},{9,8},{10,11... | collective-permute-start | bytes 393224 | tf_op jit(solution)/shard_map/ppermute | solution.py:15
  127.1 20.5 %collective-permute-start.21 = (bf16[4096,128]{1,0:T(8,128)(2,1)S(1)}, bf16[4096,128]{1,0:T(8,128)(2,1)S(1)}, u32[]{:S(2)}, u32[]{:S(2)}) collective-permute-start(bf16[4096,128]{1,0:T(8,128)(2,1)S(1)} %get-tuple-element.50), channel_id=1, source_target_pairs={{0,4},{1,13},{4,0},{5,9},{8,12},{9,5},{12,8},{13,1},{2,6},{3,15},{... | collective-permute-start | bytes 3145736 | tf_op jit(solution)/shard_map/ppermute | solution.py:24
  136.7 9.3 %collective-permute-start.16 = (bf16[1024,128]{1,0:T(8,128)(2,1)S(1)}, bf16[1024,128]{1,0:T(8,128)(2,1)S(1)}, u32[]{:S(2)}, u32[]{:S(2)}) collective-permute-start(bf16[1024,128]{1,0:T(8,128)(2,1)S(1)} %fusion.21), channel_id=1, source_target_pairs={{0,2},{2,0},{1,3},{3,1},{4,6},{6,4},{5,7},{7,5},{8,10},{10,8},{9,1... | collective-permute-start | bytes 786440 | tf_op jit(solution)/shard_map/ppermute | solution.py:15
  147.7 10.1 %collective-permute-start.22 = (bf16[2048,128]{1,0:T(8,128)(2,1)S(1)}, bf16[2048,128]{1,0:T(8,128)(2,1)S(1)}, u32[]{:S(2)}, u32[]{:S(2)}) collective-permute-start(bf16[2048,128]{1,0:T(8,128)(2,1)S(1)} %get-tuple-element.68), channel_id=1, source_target_pairs={{0,12},{1,5},{4,8},{5,1},{8,4},{9,13},{12,0},{13,9},{2,14},{3,7},{... | collective-permute-start | bytes 1572872 | tf_op jit(solution)/shard_map/ppermute | solution.py:24
  148.0 10.9 %copy-start.6 = (f32[512,1024]{1,0:T(8,128)S(1)}, f32[512,1024]{1,0:T(8,128)}, u32[]{:S(2)}) copy-start(f32[512,1024]{1,0:T(8,128)} %fusion.1) | copy-start | bytes 6291460
  148.1 10.8 %copy-start.15 = (f32[1024]{0:T(1024)S(1)}, f32[1024]{0:T(1024)}, u32[]{:S(2)}) copy-start(f32[1024]{0:T(1024)} %param.18) | copy-start | bytes 12292
  148.1 10.8 %collective-permute-start.17 = (bf16[512,128]{1,0:T(8,128)(2,1)S(1)}, bf16[512,128]{1,0:T(8,128)(2,1)S(1)}, u32[]{:S(2)}, u32[]{:S(2)}) collective-permute-start(bf16[512,128]{1,0:T(8,128)(2,1)S(1)} %bitcast.88), channel_id=1, source_target_pairs={{0,1},{1,0},{2,3},{3,2},{4,5},{5,4},{6,7},{7,6},{8,9},{9,8},{10,11... | collective-permute-start | bytes 393224 | tf_op jit(solution)/shard_map/ppermute | solution.py:15
  151.1 20.7 %collective-permute-start.27 = (bf16[4096,128]{1,0:T(8,128)(2,1)S(1)}, bf16[4096,128]{1,0:T(8,128)(2,1)S(1)}, u32[]{:S(2)}, u32[]{:S(2)}) collective-permute-start(bf16[4096,128]{1,0:T(8,128)(2,1)S(1)} %get-tuple-element.56), channel_id=1, source_target_pairs={{0,4},{1,13},{4,0},{5,9},{8,12},{9,5},{12,8},{13,1},{2,6},{3,15},{... | collective-permute-start | bytes 3145736 | tf_op jit(solution)/shard_map/ppermute | solution.py:24
  157.9 7.1 %collective-permute-start.23 = (bf16[1024,128]{1,0:T(8,128)(2,1)S(1)}, bf16[1024,128]{1,0:T(8,128)(2,1)S(1)}, u32[]{:S(2)}, u32[]{:S(2)}) collective-permute-start(bf16[1024,128]{1,0:T(8,128)(2,1)S(1)} %fusion.19), channel_id=1, source_target_pairs={{0,2},{2,0},{1,3},{3,1},{4,6},{6,4},{5,7},{7,5},{8,10},{10,8},{9,1... | collective-permute-start | bytes 786440 | tf_op jit(solution)/shard_map/ppermute | solution.py:15
  172.0 8.4 %collective-permute-start.28 = (bf16[2048,128]{1,0:T(8,128)(2,1)S(1)}, bf16[2048,128]{1,0:T(8,128)(2,1)S(1)}, u32[]{:S(2)}, u32[]{:S(2)}) collective-permute-start(bf16[2048,128]{1,0:T(8,128)(2,1)S(1)} %get-tuple-element.71), channel_id=1, source_target_pairs={{0,12},{1,5},{4,8},{5,1},{8,4},{9,13},{12,0},{13,9},{2,14},{3,7},{... | collective-permute-start | bytes 1572872 | tf_op jit(solution)/shard_map/ppermute | solution.py:24
  172.3 8.7 %collective-permute-start.24 = (bf16[512,128]{1,0:T(8,128)(2,1)S(1)}, bf16[512,128]{1,0:T(8,128)(2,1)S(1)}, u32[]{:S(2)}, u32[]{:S(2)}) collective-permute-start(bf16[512,128]{1,0:T(8,128)(2,1)S(1)} %bitcast.90), channel_id=1, source_target_pairs={{0,1},{1,0},{2,3},{3,2},{4,5},{5,4},{6,7},{7,6},{8,9},{9,8},{10,11... | collective-permute-start | bytes 393224 | tf_op jit(solution)/shard_map/ppermute | solution.py:15
  180.5 6.8 %collective-permute-start.29 = (bf16[1024,128]{1,0:T(8,128)(2,1)S(1)}, bf16[1024,128]{1,0:T(8,128)(2,1)S(1)}, u32[]{:S(2)}, u32[]{:S(2)}) collective-permute-start(bf16[1024,128]{1,0:T(8,128)(2,1)S(1)} %fusion.17), channel_id=1, source_target_pairs={{0,2},{2,0},{1,3},{3,1},{4,6},{6,4},{5,7},{7,5},{8,10},{10,8},{9,1... | collective-permute-start | bytes 786440 | tf_op jit(solution)/shard_map/ppermute | solution.py:15
  187.6 7.2 %collective-permute-start.30 = (bf16[512,128]{1,0:T(8,128)(2,1)S(1)}, bf16[512,128]{1,0:T(8,128)(2,1)S(1)}, u32[]{:S(2)}, u32[]{:S(2)}) collective-permute-start(bf16[512,128]{1,0:T(8,128)(2,1)S(1)} %bitcast.91), channel_id=1, source_target_pairs={{0,1},{1,0},{2,3},{3,2},{4,5},{5,4},{6,7},{7,6},{8,9},{9,8},{10,11... | collective-permute-start | bytes 393224 | tf_op jit(solution)/shard_map/ppermute | solution.py:15
  195.6 2.4 %copy-start.1 = (bf16[1024,1024]{1,0:T(8,128)(2,1)S(1)}, bf16[1024,1024]{1,0:T(8,128)(2,1)}, u32[]{:S(2)}) copy-start(bf16[1024,1024]{1,0:T(8,128)(2,1)} %param.15) | copy-start | bytes 6291460

commit v4 on v2

--- a/solution.py
+++ b/solution.py
@@ -1,3 +1,5 @@
+import functools
+
 import jax
 import jax.numpy as jnp
 from jax import lax
@@ -11,17 +13,19 @@
 GROUP = 8
 
 
-def swap(x, axis):
-    return lax.ppermute(x, axis, [(0, 1), (1, 0)])
-
-
-def step(x, axis, second):
+def swap(x, axis, name):
+    with jax.named_scope(name):
+        return lax.ppermute(x, axis, [(0, 1), (1, 0)])
+
+
+def step(x, axis, second, name):
     pairs = []
     for i in range(4):
         for c in range(2):
             to = i ^ 1 if c == second else 3 - i
             pairs.append((i * 2 + c, to * 2 + c))
-    return lax.ppermute(x, (axis, "core"), pairs)
+    with jax.named_scope(name):
+        return lax.ppermute(x, (axis, "core"), pairs)
 
 
 def after(x, *earlier):
@@ -120,6 +124,57 @@
     )(src, dst, live, c_own, c_other, pieces, near, far, *earlier)
 
 
+def message_kernel(first, core_ref, x, weight, bias, theirs, mine, held, sems):
+    core = core_ref[0]
+    chunks, blocks, tile, w = mine.shape
+    half = weight.shape[1] // 2
+    size = chunks * w
+    starts = [
+        pl.multiple_of((1 - core) * half + first, 128),
+        pl.multiple_of(core * half + first, 128),
+    ]
+    copies = [
+        pltpu.make_async_copy(weight.at[:, pl.ds(starts[i], size)], held.at[i], sems.at[i])
+        for i in range(2)
+    ]
+    for copy in copies:
+        copy.start()
+    for i, out in enumerate((theirs, mine)):
+        copies[i].wait()
+        row = bias[:, pl.ds(starts[i], size)]
+        for j in range(chunks):
+            cols = slice(j * w, (j + 1) * w)
+            total = jnp.dot(x[...], held[i, :, cols], preferred_element_type=jnp.float32)
+            total = jnp.maximum(total + row[:, cols], 0.0)
+            out[j] = total.astype(out.dtype).reshape(blocks, tile, w)
+
+
+def transform(core, features, weight, bias, first, chunks, tile, w):
+    vmem = pl.BlockSpec(memory_space=pltpu.VMEM)
+    out = jax.ShapeDtypeStruct((chunks, features.shape[0] // tile, tile, w), jnp.bfloat16)
+    return pl.pallas_call(
+        functools.partial(message_kernel, first),
+        out_shape=(out, out),
+        in_specs=[
+            pl.BlockSpec(memory_space=pltpu.SMEM),
+            vmem,
+            pl.BlockSpec(memory_space=pl.ANY),
+            vmem,
+        ],
+        out_specs=(vmem, vmem),
+        scratch_shapes=[
+            pltpu.VMEM((2, features.shape[1], chunks * w), jnp.bfloat16),
+            pltpu.SemaphoreType.DMA((2,)),
+        ],
+        compiler_params=pltpu.CompilerParams(vmem_limit_bytes=32 * 1024 * 1024),
+        cost_estimate=pl.CostEstimate(
+            flops=4 * features.size * chunks * w,
+            bytes_accessed=2 * features.size + 4 * features.shape[1] * chunks * w,
+            transcendentals=0,
+        ),
+    )(core.astype(jnp.int32).reshape(1), features, weight, bias.reshape(1, -1))
+
+
 def local(
     features,
     walk_counts,
@@ -139,30 +194,27 @@
     blocks = rows_dev // tile
     x_lo, y, z, x_hi, core = (lax.axis_index(a) for a in AXES)
 
-    def transform(which):
-        weight = lax.dynamic_slice_in_dim(neigh_weight, which * half, half, 1)
-        bias = lax.dynamic_slice_in_dim(neigh_bias, which * half, half, 0)
-        out = jnp.dot(features, weight, preferred_element_type=jnp.float32) + bias
-        return jax.nn.relu(out).astype(jnp.bfloat16)
-
-    theirs = swap(transform(1 - core), "core")
-    mine = transform(core)
-
-    def own_chunk(j):
-        cols = slice(j * cw, (j + 1) * cw)
-        return jnp.concatenate(
-            [mine[:, cols].reshape(blocks, tile, cw), theirs[:, cols].reshape(blocks, tile, cw)]
-        )
+    make = functools.partial(transform, core)
+    theirs, mine = make(features, neigh_weight, neigh_bias, 0, 1, tile, cw)
+    own = [jnp.concatenate([mine[0], swap(theirs[0], "core", "other_core_0")])]
+    first = swap(own[0], "x_lo", "gather_x_0")
+    theirs, mine = make(
+        after(features, theirs), neigh_weight, neigh_bias, cw, CHUNKS - 1, tile, cw
+    )
+    theirs = swap(after(theirs, own[0]), "core", "other_core_rest")
+    own += [jnp.concatenate([mine[j], theirs[j]]) for j in range(CHUNKS - 1)]
 
     live = live_tiles[0, 0]
     used = jnp.arange(slots, dtype=jnp.int32) < live
-    c_own = jnp.where(used[:, None, None], walk_counts[0, 0], 0).astype(jnp.bfloat16)
+    counts = after(walk_counts, own[0])[0, 0]
+    c_own = jnp.where(used[:, None, None], counts, 0).astype(jnp.bfloat16)
+    pair0 = jnp.concatenate([own[0], after(first, c_own)])
     rows_own = jnp.where(used, tile_rows[0, 0], 0)
     meta = jnp.stack(
         [rows_own, jnp.where(used, tile_cols[0, 0], 0), jnp.full((slots,), live, jnp.int32)]
     )
-    c_other = swap(after(c_own, theirs), "core")
-    metas = jnp.stack([meta, swap(meta, "core")])
+    c_other = swap(after(c_own, theirs), "core", "other_tiles")
+    metas = jnp.stack([meta, swap(after(meta, own[0]), "core", "other_meta")])
     k = metas[:, 1]
     src = (
         (ring_slot((k // 4) % 4, y, core) * 2 + ((k // 16) ^ x_lo)) * 8
@@ -194,46 +246,62 @@
     w_own = lax.dynamic_slice_in_dim(combine_weight, width + core * half, half, 0)
     w_other = lax.dynamic_slice_in_dim(combine_weight, width + (1 - core) * half, half, 0)
 
-    own = [own_chunk(j) for j in range(CHUNKS)]
-    first = swap(own[0], "x_lo")
-    rest = swap(jnp.stack(own[1:]), "x_lo")
-    partner = [first] + [rest[j] for j in range(CHUNKS - 1)]
+    second = swap(after(own[1], first), "x_lo", "gather_x_1")
+    rest = swap(after(jnp.stack(own[2:]), second), "x_lo", "gather_x_rest")
+    partner = [first, second] + [rest[j] for j in range(CHUNKS - 2)]
 
     f32, bf16 = jnp.float32, jnp.bfloat16
-    near_all, part_all, pass_all, zb_all, swap_all = [], [], [], [], []
+    near_all, far_all, part_all, pass_all, zb_all, hidden_all = [], [], [], [], [], []
     scale = None
-    for j in range(CHUNKS):
-        pair = jnp.concatenate([own[j], partner[j]])
+
+    def gather(j):
+        pair = jnp.concatenate([own[j], partner[j]]) if j else pair0
         if j >= 2:
             pair = after(pair, near_all[j - 1], part_all[j - 2][0])
         elif j == 1:
             pair = after(pair, near_all[0])
-        near = jnp.concatenate([pair, step(pair, "y", 0)])
-        near_all.append(near)
-        far = step(near, "y", 1)
-        earlier = ()
+        near_all.append(jnp.concatenate([pair, step(pair, "y", 0, f"gather_near_{j}")]))
+        far_all.append(step(near_all[j], "y", 1, f"gather_far_{j}"))
+
+    def tiles(j):
+        earlier = (rest,) if j == 0 else ()
+        if j + 1 < CHUNKS:
+            earlier += (near_all[j + 1],)
         if j >= 2:
             earlier += (pass_all[j - 2],)
         if j >= 3:
             earlier += (zb_all[j - 3],)
-        send, pass_on, stay = tile_sums(
-            src, dst, lives, c_own, c_other, parts, j == 0, near, far, earlier
-        )
-        part_all.append((send, pass_on, stay))
+        with jax.named_scope(f"tiles_{j}"):
+            part_all.append(
+                tile_sums(
+                    src, dst, lives, c_own, c_other, parts, j == 0, near_all[j], far_all[j], earlier
+                )
+            )
+        if j + 2 < CHUNKS:
+            gather(j + 2)
+
+    gather(0)
+    gather(1)
+    tiles(0)
+    for j in range(CHUNKS):
+        send, pass_on, stay = part_all[j]
         size = stay.shape[0] // 2
-        got = step(send, "z", 0)
+        if j >= 1:
+            send = after(send, pass_all[j - 1])
+        got = step(send, "z", 0, f"sum_near_{j}")
+        if j + 1 < CHUNKS:
+            tiles(j + 1)
+            got = after(got, part_all[j + 1][0])
         passed = (got[: 2 * size].astype(f32) + pass_on).astype(bf16)
         pass_all.append(passed)
         stay = got[2 * size :].astype(f32) + stay
-        if j == CHUNKS - 1:
-            passed = after(passed, swap_all[j - 2])
-        got = step(passed, "z", 1)
+        got = step(passed, "z", 1, f"sum_far_{j}")
         zb_all.append(got)
         passed = (got[:size].astype(f32) + stay[:size]).astype(bf16)
         stay = got[size:].astype(f32) + stay[size:]
         if j == CHUNKS - 1:
-            passed = after(passed, swap_all[j - 1])
-        pooled = swap(passed, "x_hi").astype(f32) + stay
+            passed = after(passed, hidden_all[j - 2])
+        pooled = swap(passed, "x_hi", f"sum_x_{j}").astype(f32) + stay
         if j == 0:
             deg = jnp.sum(
                 pooled[8 * tile :].reshape(8, 4, tile)
@@ -242,13 +310,14 @@
             )
             scale = 1.0 / (1.0 + deg)
             pooled = pooled[: 8 * tile]
-        mean = (pooled.reshape(8, tile, cw) * scale[..., None]).astype(bf16)
+        factor = after(scale, passed)[..., None]
+        mean = (pooled.reshape(8, tile, cw) * factor).astype(bf16)
         mean = mean.reshape(2, rows_dev, cw)
-        got = swap(mean[1], "core")
-        swap_all.append(got)
+        got = swap(mean[1], "core", f"mean_core_{j}")
         cols = slice(j * cw, (j + 1) * cw)
         hidden = hidden + jnp.dot(mean[0], w_own[cols], preferred_element_type=f32)
         hidden = hidden + jnp.dot(got, w_other[cols], preferred_element_type=f32)
+        hidden_all.append(hidden)
     hidden = jax.nn.relu(hidden)
     return hidden / jnp.sqrt(jnp.mean(hidden * hidden, axis=1, keepdims=True) + 1e-06)
 

time: 196 us -> 187 us (0.954); the launches traced: 195 us -> 183 us
  local copies, waits for them, and re-layouts: 13.1 us -> 6.04 us
  other arithmetic: 21 us -> 15.9 us
  matrix products: 10.7 us -> 6.8 us
  waiting for transfers between devices: 76.7 us -> 79.9 us
  starting transfers between devices: 48 us -> 50.5 us
    ppermute x16, waiting for transfers between devices: 46 us -> 59.6 us  [step(): return lax.ppermute(x, (axis, 'core'), pairs)]
    ppermute x13 -> x15, waiting for transfers between devices: 30.7 us -> 20.4 us  [swap(): return lax.ppermute(x, axis, [(0, 1), (1, 0)])]
    pallas_call x4, Pallas kernels: 23.9 us -> 18.6 us  [tile_sums(): pl.pallas_call(tile_kernel, out_shape=(jax.ShapeDtypeStruct((4 * size, w)...]
    ppermute x13 -> x15, starting transfers between devices: 26.7 us -> 31.6 us  [swap(): return lax.ppermute(x, axis, [(0, 1), (1, 0)])]
    pallas_call x0 -> x2, Pallas kernels: none -> 4.26 us  [transform(): pl.pallas_call(functools.partial(message_kernel, first), out_shape=(out,...]
    dot_general x2 -> x0, matrix products: 3.56 us -> none  [transform(): out = jnp.dot(features, weight, preferred_element_type=jnp.float32) + bias]
    ppermute x16, starting transfers between devices: 21.4 us -> 18.9 us  [step(): return lax.ppermute(x, (axis, 'core'), pairs)]
    reduce_sum x1, other arithmetic: 3.61 us -> 1.37 us  [local(): jnp.sum(c_own.astype(jnp.float32), axis=2)]
  transfers between devices with their start and end apart: 29 -> 31, of which waited for: 16 -> 19; matrix products, arithmetic and copies ran while one was open for 17% -> 12% of each run, Pallas kernels for 12% -> 12%
where the time goes in v4:
time: 187 us; the launch traced here: 183 us
  waiting for transfers between devices  79.9 us (43%)
  starting transfers between devices  50.5 us (27%)
  Pallas kernels  22.9 us (12%)
  other arithmetic  15.9 us (9%)
  matrix products  6.8 us (4%)
  local copies, waits for them, and re-layouts  6.04 us (3%)
    ppermute x16, waiting for transfers between devices, step(): return lax.ppermute(x, (axis, 'core'), pairs)  59.6 us
    ppermute x15, starting transfers between devices, swap(): return lax.ppermute(x, axis, [(0, 1), (1, 0)])  31.6 us
    ppermute x15, waiting for transfers between devices, swap(): return lax.ppermute(x, axis, [(0, 1), (1, 0)])  20.4 us
    ppermute x16, starting transfers between devices, step(): return lax.ppermute(x, (axis, 'core'), pairs)  18.9 us
    pallas_call x4, Pallas kernels, tile_sums(): pl.pallas_call(tile_kernel, out_shape=(jax.ShapeDtypeStruct((4 * size, w)...  18.6 us
    unnamed x41, local copies, waits for them, and re-layouts  4.43 us
    pallas_call x2, Pallas kernels, transform(): pl.pallas_call(functools.partial(message_kernel, first), out_shape=(out,...  4.26 us
  transfers between devices with their start and end apart: 31, of which 19 were waited for; matrix products, arithmetic and copies ran while one was open for 12% of the time, Pallas kernels for 12%

profile of v4, /device:TPU:3, one launch (start us, length us, event | category | flops | bytes accessed | tf_op | source)
XLA Modules:
  0.0 183.3 jit_solution(18429877861466866787)
XLA Ops:
  0.0 1.6 copy-done
  1.6 1.2 copy-done.1
  3.5 1.5 shard_map.100
  6.5 2.7 %shard_map.101 = (bf16[3,4,128,128]{3,2,1,0:T(8,128)(2,1)S(1)}, bf16[3,4,128,128]{3,2,1,0:T(8,128)(2,1)S(1)}) custom-call(s32[1]{0:T(128)} %bitcast.4.core_ref, bf16[512,1024]{1,0:T(8,128)(2,1)S(1)} %copy-done.1, bf16[1024,1024]{1,0:T(8,128)(2,1)S(1)} %copy-done, f32[1,1024]{1,0:T(1,128)S(1)} %bitcast.67), custom_call_target="tpu_custom_call" | custom-call | flops 805306368 | bytes 2621440 | tf_op jit(solution)/shard_map/pallas_call | solution.py:155
  9.7 1.4 convert_reduce_fusion.1
  11.9 5.1 %collective-permute-done.4 = bf16[8,128,128]{2,1,0:T(8,128)(2,1)S(1)} collective-permute-done((bf16[8,128,128]{2,1,0:T(8,128)(2,1)S(1)}, bf16[8,128,128]{2,1,0:T(8,128)(2,1)S(1)}, u32[]{:S(2)}, u32[]{:S(2)}) %collective-permute-start.4) | collective-permute-done | bytes 262176 | tf_op jit(solution)/shard_map/gather_x_0/ppermute | solution.py:18
  17.8 2.7 %collective-permute-start.5 = (bf16[16,128,128]{2,1,0:T(8,128)(2,1)}, bf16[16,128,128]{2,1,0:T(8,128)(2,1)}, u32[]{:S(2)}, u32[]{:S(2)}) collective-permute-start(bf16[16,128,128]{2,1,0:T(8,128)(2,1)} %pad_maximum_fusion.1), channel_id=1, source_target_pairs={{0,16},{1,49},{16,0},{17,33},{32,48},{33,17},{48,32},{49,1},{2,18}... | collective-permute-start | bytes 1572872 | tf_op jit(solution)/shard_map/gather_near_0/ppermute | solution.py:28
  23.1 6.4 %collective-permute-done.7 = bf16[8,128,128]{2,1,0:T(8,128)(2,1)} collective-permute-done((bf16[8,128,128]{2,1,0:T(8,128)(2,1)}, bf16[8,128,128]{2,1,0:T(8,128)(2,1)}, u32[]{:S(2)}, u32[]{:S(2)}) %collective-permute-start.7) | collective-permute-done | bytes 262176 | tf_op jit(solution)/shard_map/gather_x_1/ppermute | solution.py:18
  29.5 1.0 pad_maximum_fusion.3
  30.5 1.1 pad_maximum_fusion.near
  32.4 12.9 %collective-permute-done.9 = bf16[16,128,128]{2,1,0:T(8,128)(2,1)S(1)} collective-permute-done((bf16[16,128,128]{2,1,0:T(8,128)(2,1)S(1)}, bf16[16,128,128]{2,1,0:T(8,128)(2,1)S(1)}, u32[]{:S(2)}, u32[]{:S(2)}) %collective-permute-start.9) | collective-permute-done | bytes 524320 | tf_op jit(solution)/shard_map/gather_near_1/ppermute | solution.py:28
  45.5 2.2 %convert_reduce_fusion = f32[64,128]{1,0:T(8,128)S(1)} fusion(bf16[64,128,128]{2,1,0:T(8,128)(2,1)} %collective-permute-done.3.c_other), kind=kLoop, calls=%fused_computation.2 | loop fusion | flops 2088960 | bytes 2129920 | tf_op jit(solution)/shard_map/reduce_sum | solution.py:235
  48.0 3.4 %collective-permute-done.6.far = bf16[32,128,128]{2,1,0:T(8,128)(2,1)S(1)} collective-permute-done((bf16[32,128,128]{2,1,0:T(8,128)(2,1)S(1)}, bf16[32,128,128]{2,1,0:T(8,128)(2,1)S(1)}, u32[]{:S(2)}, u32[]{:S(2)}) %collective-permute-start.6) | collective-permute-done | bytes 1048608 | tf_op jit(solution)/shard_map/gather_far_0/ppermute | solution.py:28
  51.5 4.4 %tiles_0.1 = (bf16[4224,128]{1,0:T(8,128)(2,1)S(1)}, f32[2112,128]{1,0:T(8,128)S(1)}, f32[2112,128]{1,0:T(8,128)S(1)}) custom-call(s32[128]{0:T(128)S(1)} %fusion.38.src_ref, s32[128]{0:T(128)S(1)} %fusion.39.dst_ref, s32[2]{0:T(128)S(1)} %fusion.37.live_ref, bf16[64,128,128]{2,1,0:T(8,128)(2,1)S(1)} %get-tuple-element.50.c_own, ...), custom_call_target="tpu_custom_call" | custom-call | flops 2147483648 | bytes 8388608 | tf_op jit(solution)/shard_map/tiles_0/pallas_call | solution.py:104
  55.9 5.7 %collective-permute-start.10 = (bf16[4224,128]{1,0:T(8,128)(2,1)S(1)}, bf16[4224,128]{1,0:T(8,128)(2,1)S(1)}, u32[]{:S(2)}, u32[]{:S(2)}) collective-permute-start(bf16[4224,128]{1,0:T(8,128)(2,1)S(1)} %get-tuple-element.56), channel_id=1, source_target_pairs={{0,4},{1,13},{4,0},{5,9},{8,12},{9,5},{12,8},{13,1},{2,6},{3,15},{... | collective-permute-start | bytes 3244040 | tf_op jit(solution)/shard_map/sum_near_0/ppermute | solution.py:28
  62.5 9.2 %collective-permute-done.12 = bf16[16,128,128]{2,1,0:T(8,128)(2,1)S(1)} collective-permute-done((bf16[16,128,128]{2,1,0:T(8,128)(2,1)S(1)}, bf16[16,128,128]{2,1,0:T(8,128)(2,1)S(1)}, u32[]{:S(2)}, u32[]{:S(2)}) %collective-permute-start.12) | collective-permute-done | bytes 524320 | tf_op jit(solution)/shard_map/gather_near_2/ppermute | solution.py:28
  71.9 4.6 %tiles_1.1 = (bf16[4096,128]{1,0:T(8,128)(2,1)S(1)}, f32[2048,128]{1,0:T(8,128)S(1)}, f32[2048,128]{1,0:T(8,128)S(1)}) custom-call(s32[128]{0:T(128)S(1)} %fusion.38.src_ref, s32[128]{0:T(128)S(1)} %fusion.39.dst_ref, s32[2]{0:T(128)S(1)} %fusion.37.live_ref, bf16[64,128,128]{2,1,0:T(8,128)(2,1)S(1)} %get-tuple-element.50.c_own, ...), custom_call_target="tpu_custom_call" | custom-call | flops 2147483648 | bytes 8388608 | tf_op jit(solution)/shard_map/tiles_1/pallas_call | solution.py:104
  76.6 1.4 convert_add_fusion
  78.7 2.6 %fusion.1 = f32[512,1024]{1,0:T(8,128)} fusion(bf16[512,1024]{1,0:T(8,128)(2,1)S(1)} %copy-done.2, bf16[2048,1024]{1,0:T(8,128)(2,1)S(1)} %copy-done.13), kind=kOutput, calls=%fused_computation.7 | convolution fusion | flops 1073741824 | bytes 5242880 | tf_op jit(solution)/shard_map/dot_general | solution.py:243
  81.3 1.2 pad_maximum_fusion.5
  82.4 1.8 %collective-permute-start.18 = (bf16[16,128,128]{2,1,0:T(8,128)(2,1)S(1)}, bf16[16,128,128]{2,1,0:T(8,128)(2,1)S(1)}, u32[]{:S(2)}, u32[]{:S(2)}) collective-permute-start(bf16[16,128,128]{2,1,0:T(8,128)(2,1)S(1)} %pad_maximum_fusion.5), channel_id=1, source_target_pairs={{0,16},{1,49},{16,0},{17,33},{32,48},{33,17},{48,32},{49,1},{2,18}... | collective-permute-start | bytes 1572872 | tf_op jit(solution)/shard_map/gather_near_3/ppermute | solution.py:28
  84.3 3.2 %collective-permute-done.13.refs_1_ = bf16[2112,128]{1,0:T(8,128)(2,1)} collective-permute-done((bf16[2112,128]{1,0:T(8,128)(2,1)}, bf16[2112,128]{1,0:T(8,128)(2,1)}, u32[]{:S(2)}, u32[]{:S(2)}) %collective-permute-start.13) | collective-permute-done | bytes 540704 | tf_op jit(solution)/shard_map/sum_far_0/ppermute | solution.py:28
  87.5 1.0 fusion.4
  88.5 1.2 collective-permute-start.14
  89.7 2.0 %collective-permute-done.18 = bf16[16,128,128]{2,1,0:T(8,128)(2,1)S(1)} collective-permute-done((bf16[16,128,128]{2,1,0:T(8,128)(2,1)S(1)}, bf16[16,128,128]{2,1,0:T(8,128)(2,1)S(1)}, u32[]{:S(2)}, u32[]{:S(2)}) %collective-permute-start.18) | collective-permute-done | bytes 524320 | tf_op jit(solution)/shard_map/gather_near_3/ppermute | solution.py:28
  91.8 1.5 collective-permute-start.23
  93.4 1.6 collective-permute-start.16
  95.0 5.2 %tiles_2.1 = (bf16[4096,128]{1,0:T(8,128)(2,1)S(1)}, f32[2048,128]{1,0:T(8,128)S(1)}, f32[2048,128]{1,0:T(8,128)S(1)}) custom-call(s32[128]{0:T(128)S(1)} %fusion.38.src_ref, s32[128]{0:T(128)S(1)} %fusion.39.dst_ref, s32[2]{0:T(128)S(1)} %fusion.37.live_ref, bf16[64,128,128]{2,1,0:T(8,128)(2,1)S(1)} %get-tuple-element.50.c_own, ...), custom_call_target="tpu_custom_call" | custom-call | flops 2147483648 | bytes 8388608 | tf_op jit(solution)/shard_map/tiles_2/pallas_call | solution.py:104
  100.3 1.2 fusion.3
  101.6 6.9 %collective-permute-done.16 = bf16[4096,128]{1,0:T(8,128)(2,1)S(1)} collective-permute-done((bf16[4096,128]{1,0:T(8,128)(2,1)S(1)}, bf16[4096,128]{1,0:T(8,128)(2,1)S(1)}, u32[]{:S(2)}, u32[]{:S(2)}) %collective-permute-start.16) | collective-permute-done | bytes 1048608 | tf_op jit(solution)/shard_map/sum_near_1/ppermute | solution.py:28
  109.3 3.3 %collective-permute-start.15 = (bf16[512,128]{1,0:T(8,128)(2,1)S(1)}, bf16[512,128]{1,0:T(8,128)(2,1)S(1)}, u32[]{:S(2)}, u32[]{:S(2)}) collective-permute-start(bf16[512,128]{1,0:T(8,128)(2,1)S(1)} %bitcast.79), channel_id=1, source_target_pairs={{0,1},{1,0},{2,3},{3,2},{4,5},{5,4},{6,7},{7,6},{8,9},{9,8},{10,11... | collective-permute-start | bytes 393224 | tf_op jit(solution)/shard_map/mean_core_0/ppermute | solution.py:18
  112.6 2.9 %collective-permute-start.22 = (bf16[4096,128]{1,0:T(8,128)(2,1)S(1)}, bf16[4096,128]{1,0:T(8,128)(2,1)S(1)}, u32[]{:S(2)}, u32[]{:S(2)}) collective-permute-start(bf16[4096,128]{1,0:T(8,128)(2,1)S(1)} %get-tuple-element.70), channel_id=1, source_target_pairs={{0,4},{1,13},{4,0},{5,9},{8,12},{9,5},{12,8},{13,1},{2,6},{3,15},{... | collective-permute-start | bytes 3145736 | tf_op jit(solution)/shard_map/sum_near_2/ppermute | solution.py:28
  116.0 2.5 %collective-permute-done.19 = bf16[2048,128]{1,0:T(8,128)(2,1)S(1)} collective-permute-done((bf16[2048,128]{1,0:T(8,128)(2,1)S(1)}, bf16[2048,128]{1,0:T(8,128)(2,1)S(1)}, u32[]{:S(2)}, u32[]{:S(2)}) %collective-permute-start.19) | collective-permute-done | bytes 524320 | tf_op jit(solution)/shard_map/sum_far_1/ppermute | solution.py:28
  118.5 1.2 collective-permute-start.20
  120.2 4.4 %tiles_3.1 = (bf16[4096,128]{1,0:T(8,128)(2,1)S(1)}, f32[2048,128]{1,0:T(8,128)S(1)}, f32[2048,128]{1,0:T(8,128)S(1)}) custom-call(s32[128]{0:T(128)S(1)} %fusion.38.src_ref, s32[128]{0:T(128)S(1)} %fusion.39.dst_ref, s32[2]{0:T(128)S(1)} %fusion.37.live_ref, bf16[64,128,128]{2,1,0:T(8,128)(2,1)S(1)} %get-tuple-element.50.c_own, ...), custom_call_target="tpu_custom_call" | custom-call | flops 2147483648 | bytes 8388608 | tf_op jit(solution)/shard_map/tiles_3/pallas_call | solution.py:104
  124.6 1.0 collective-permute-done.20
  125.7 7.5 %collective-permute-done.22 = bf16[4096,128]{1,0:T(8,128)(2,1)S(1)} collective-permute-done((bf16[4096,128]{1,0:T(8,128)(2,1)S(1)}, bf16[4096,128]{1,0:T(8,128)(2,1)S(1)}, u32[]{:S(2)}, u32[]{:S(2)}) %collective-permute-start.22) | collective-permute-done | bytes 1048608 | tf_op jit(solution)/shard_map/sum_near_2/ppermute | solution.py:28
  133.7 5.5 %collective-permute-start.21 = (bf16[512,128]{1,0:T(8,128)(2,1)S(1)}, bf16[512,128]{1,0:T(8,128)(2,1)S(1)}, u32[]{:S(2)}, u32[]{:S(2)}) collective-permute-start(bf16[512,128]{1,0:T(8,128)(2,1)S(1)} %bitcast.78), channel_id=1, source_target_pairs={{0,1},{1,0},{2,3},{3,2},{4,5},{5,4},{6,7},{7,6},{8,9},{9,8},{10,11... | collective-permute-start | bytes 393224 | tf_op jit(solution)/shard_map/mean_core_1/ppermute | solution.py:18
  139.2 1.5 collective-permute-start.27
  141.6 6.2 %collective-permute-start.25 = (bf16[1024,128]{1,0:T(8,128)(2,1)S(1)}, bf16[1024,128]{1,0:T(8,128)(2,1)S(1)}, u32[]{:S(2)}, u32[]{:S(2)}) collective-permute-start(bf16[1024,128]{1,0:T(8,128)(2,1)S(1)} %fusion.8), channel_id=1, source_target_pairs={{0,2},{2,0},{1,3},{3,1},{4,6},{6,4},{5,7},{7,5},{8,10},{10,8},{9,1... | collective-permute-start | bytes 786440 | tf_op jit(solution)/shard_map/sum_x_2/ppermute | solution.py:18
  148.5 3.2 %collective-permute-done.25 = bf16[1024,128]{1,0:T(8,128)(2,1)S(1)} collective-permute-done((bf16[1024,128]{1,0:T(8,128)(2,1)S(1)}, bf16[1024,128]{1,0:T(8,128)(2,1)S(1)}, u32[]{:S(2)}, u32[]{:S(2)}) %collective-permute-start.25) | collective-permute-done | bytes 262176 | tf_op jit(solution)/shard_map/sum_x_2/ppermute | solution.py:18
  151.8 6.7 %collective-permute-done.27 = bf16[4096,128]{1,0:T(8,128)(2,1)S(1)} collective-permute-done((bf16[4096,128]{1,0:T(8,128)(2,1)S(1)}, bf16[4096,128]{1,0:T(8,128)(2,1)S(1)}, u32[]{:S(2)}, u32[]{:S(2)}) %collective-permute-start.27) | collective-permute-done | bytes 1048608 | tf_op jit(solution)/shard_map/sum_near_3/ppermute | solution.py:28
  159.0 2.8 %collective-permute-start.26 = (bf16[512,128]{1,0:T(8,128)(2,1)S(1)}, bf16[512,128]{1,0:T(8,128)(2,1)S(1)}, u32[]{:S(2)}, u32[]{:S(2)}) collective-permute-start(bf16[512,128]{1,0:T(8,128)(2,1)S(1)} %bitcast.80), channel_id=1, source_target_pairs={{0,1},{1,0},{2,3},{3,2},{4,5},{5,4},{6,7},{7,6},{8,9},{9,8},{10,11... | collective-permute-start | bytes 393224 | tf_op jit(solution)/shard_map/mean_core_2/ppermute | solution.py:18
  162.2 4.9 %collective-permute-done.28 = bf16[2048,128]{1,0:T(8,128)(2,1)S(1)} collective-permute-done((bf16[2048,128]{1,0:T(8,128)(2,1)S(1)}, bf16[2048,128]{1,0:T(8,128)(2,1)S(1)}, u32[]{:S(2)}, u32[]{:S(2)}) %collective-permute-start.28) | collective-permute-done | bytes 524320 | tf_op jit(solution)/shard_map/sum_far_3/ppermute | solution.py:28
  167.2 3.0 %collective-permute-start.29 = (bf16[1024,128]{1,0:T(8,128)(2,1)S(1)}, bf16[1024,128]{1,0:T(8,128)(2,1)S(1)}, u32[]{:S(2)}, u32[]{:S(2)}) collective-permute-start(bf16[1024,128]{1,0:T(8,128)(2,1)S(1)} %fusion.6), channel_id=1, source_target_pairs={{0,2},{2,0},{1,3},{3,1},{4,6},{6,4},{5,7},{7,5},{8,10},{10,8},{9,1... | collective-permute-start | bytes 786440 | tf_op jit(solution)/shard_map/sum_x_3/ppermute | solution.py:18
  170.5 3.4 %collective-permute-done.29 = bf16[1024,128]{1,0:T(8,128)(2,1)S(1)} collective-permute-done((bf16[1024,128]{1,0:T(8,128)(2,1)S(1)}, bf16[1024,128]{1,0:T(8,128)(2,1)S(1)}, u32[]{:S(2)}, u32[]{:S(2)}) %collective-permute-start.29) | collective-permute-done | bytes 262176 | tf_op jit(solution)/shard_map/sum_x_3/ppermute | solution.py:18
  174.3 5.6 %collective-permute-start.30 = (bf16[512,128]{1,0:T(8,128)(2,1)S(1)}, bf16[512,128]{1,0:T(8,128)(2,1)S(1)}, u32[]{:S(2)}, u32[]{:S(2)}) collective-permute-start(bf16[512,128]{1,0:T(8,128)(2,1)S(1)} %bitcast.81), channel_id=1, source_target_pairs={{0,1},{1,0},{2,3},{3,2},{4,5},{5,4},{6,7},{7,6},{8,9},{9,8},{10,11... | collective-permute-start | bytes 393224 | tf_op jit(solution)/shard_map/mean_core_3/ppermute | solution.py:18
  181.8 1.6 broadcast_divide_fusion
  (132 shorter events, 16.6 us)
Async XLA Ops:
  0.0 6.5 %copy-start.16 = (s32[1,1,64]{2,1,0:T(1,128)S(1)}, s32[1,1,64]{2,1,0:T(1,128)}, u32[]{:S(2)}) copy-start(s32[1,1,64]{2,1,0:T(1,128)} %param.13) | copy-start | bytes 772
  0.0 6.5 %copy-start.17 = (s32[1,1,64]{2,1,0:T(1,128)S(1)}, s32[1,1,64]{2,1,0:T(1,128)}, u32[]{:S(2)}) copy-start(s32[1,1,64]{2,1,0:T(1,128)} %param.12) | copy-start | bytes 772
  0.0 1.6 copy-start
  3.5 6.2 %copy-start.11 = (s32[1,1,64,128,128]{4,3,2,1,0:T(8,128)S(1)}, s32[1,1,64,128,128]{4,3,2,1,0:T(8,128)}, u32[]{:S(2)}) copy-start(s32[1,1,64,128,128]{4,3,2,1,0:T(8,128)} %param.11) | copy-start | bytes 12582916
  5.1 4.2 %collective-permute-start = (bf16[4,128,128]{2,1,0:T(8,128)(2,1)S(1)}, bf16[4,128,128]{2,1,0:T(8,128)(2,1)S(1)}, u32[]{:S(2)}, u32[]{:S(2)}) collective-permute-start(bf16[4,128,128]{2,1,0:T(8,128)(2,1)S(1)} %bitcast.68), channel_id=1, source_target_pairs={{0,1},{1,0},{2,3},{3,2},{4,5},{5,4},{6,7},{7,6},{8,9},{9,8},{10,11... | collective-permute-start | bytes 393224 | tf_op jit(solution)/shard_map/other_core_0/ppermute | solution.py:18
  9.3 1.8 collective-permute-start.2
  9.4 7.6 %collective-permute-start.4 = (bf16[8,128,128]{2,1,0:T(8,128)(2,1)S(1)}, bf16[8,128,128]{2,1,0:T(8,128)(2,1)S(1)}, u32[]{:S(2)}, u32[]{:S(2)}) collective-permute-start(bf16[8,128,128]{2,1,0:T(8,128)(2,1)S(1)} %pad_maximum_fusion.6), channel_id=1, source_target_pairs={{0,64},{64,0},{1,65},{65,1},{2,66},{66,2},{3,67},{67,3},{4,68},{68... | collective-permute-start | bytes 786440 | tf_op jit(solution)/shard_map/gather_x_0/ppermute | solution.py:18
  11.1 34.4 %collective-permute-start.3 = (bf16[64,128,128]{2,1,0:T(8,128)(2,1)S(1)}, bf16[64,128,128]{2,1,0:T(8,128)(2,1)}, u32[]{:S(2)}, u32[]{:S(2)}) collective-permute-start(bf16[64,128,128]{2,1,0:T(8,128)(2,1)S(1)} %get-tuple-element.50.c_own), channel_id=1, source_target_pairs={{0,1},{1,0},{2,3},{3,2},{4,5},{5,4},{6,7},{7,6},{8,9},{9,8},{10,11... | collective-permute-start | bytes 6291464 | tf_op jit(solution)/shard_map/other_tiles/ppermute | solution.py:18
  17.8 12.7 %collective-permute-start.5 = (bf16[16,128,128]{2,1,0:T(8,128)(2,1)}, bf16[16,128,128]{2,1,0:T(8,128)(2,1)}, u32[]{:S(2)}, u32[]{:S(2)}) collective-permute-start(bf16[16,128,128]{2,1,0:T(8,128)(2,1)} %pad_maximum_fusion.1), channel_id=1, source_target_pairs={{0,16},{1,49},{16,0},{17,33},{32,48},{33,17},{48,32},{49,1},{2,18}... | collective-permute-start | bytes 1572872 | tf_op jit(solution)/shard_map/gather_near_0/ppermute | solution.py:28
  21.3 8.2 %collective-permute-start.7 = (bf16[8,128,128]{2,1,0:T(8,128)(2,1)}, bf16[8,128,128]{2,1,0:T(8,128)(2,1)}, u32[]{:S(2)}, u32[]{:S(2)}) collective-permute-start(bf16[8,128,128]{2,1,0:T(8,128)(2,1)} %pad_maximum_fusion.7), channel_id=1, source_target_pairs={{0,64},{64,0},{1,65},{65,1},{2,66},{66,2},{3,67},{67,3},{4,68},{68... | collective-permute-start | bytes 786440 | tf_op jit(solution)/shard_map/gather_x_1/ppermute | solution.py:18
  21.6 1.2 collective-permute-start.1
  31.7 13.6 %collective-permute-start.9 = (bf16[16,128,128]{2,1,0:T(8,128)(2,1)S(1)}, bf16[16,128,128]{2,1,0:T(8,128)(2,1)S(1)}, u32[]{:S(2)}, u32[]{:S(2)}) collective-permute-start(bf16[16,128,128]{2,1,0:T(8,128)(2,1)S(1)} %pad_maximum_fusion.3), channel_id=1, source_target_pairs={{0,16},{1,49},{16,0},{17,33},{32,48},{33,17},{48,32},{49,1},{2,18}... | collective-permute-start | bytes 1572872 | tf_op jit(solution)/shard_map/gather_near_1/ppermute | solution.py:28
  31.8 19.6 %collective-permute-start.6 = (bf16[32,128,128]{2,1,0:T(8,128)(2,1)S(1)}, bf16[32,128,128]{2,1,0:T(8,128)(2,1)S(1)}, u32[]{:S(2)}, u32[]{:S(2)}) collective-permute-start(bf16[32,128,128]{2,1,0:T(8,128)(2,1)S(1)} %pad_maximum_fusion.near), channel_id=1, source_target_pairs={{0,48},{1,17},{16,32},{17,1},{32,16},{33,49},{48,0},{49,33},{2,50}... | collective-permute-start | bytes 3145736 | tf_op jit(solution)/shard_map/gather_far_0/ppermute | solution.py:28
  32.0 16.0 %collective-permute-start.8 = (bf16[2,8,128,128]{3,2,1,0:T(8,128)(2,1)S(1)}, bf16[2,8,128,128]{3,2,1,0:T(8,128)(2,1)S(1)}, u32[]{:S(2)}, u32[]{:S(2)}) collective-permute-start(bf16[2,8,128,128]{3,2,1,0:T(8,128)(2,1)S(1)} %pad_maximum_fusion.2), channel_id=1, source_target_pairs={{0,64},{64,0},{1,65},{65,1},{2,66},{66,2},{3,67},{67,3},{4,68},{68... | collective-permute-start | bytes 1572872 | tf_op jit(solution)/shard_map/gather_x_rest/ppermute | solution.py:18
  45.4 26.5 %collective-permute-start.11 = (bf16[32,128,128]{2,1,0:T(8,128)(2,1)S(1)}, bf16[32,128,128]{2,1,0:T(8,128)(2,1)S(1)}, u32[]{:S(2)}, u32[]{:S(2)}) collective-permute-start(bf16[32,128,128]{2,1,0:T(8,128)(2,1)S(1)} %constant_dynamic-update-slice_fusion.refs_1_.near), channel_id=1, source_target_pairs={{0,48},{1,17},{16,32},{17,1},{32,16},{33,49},{48,0},{49,33},{2,50}... | collective-permute-start | bytes 3145736 | tf_op jit(solution)/shard_map/gather_far_1/ppermute | solution.py:28
  55.9 20.7 %collective-permute-start.10 = (bf16[4224,128]{1,0:T(8,128)(2,1)S(1)}, bf16[4224,128]{1,0:T(8,128)(2,1)S(1)}, u32[]{:S(2)}, u32[]{:S(2)}) collective-permute-start(bf16[4224,128]{1,0:T(8,128)(2,1)S(1)} %get-tuple-element.56), channel_id=1, source_target_pairs={{0,4},{1,13},{4,0},{5,9},{8,12},{9,5},{12,8},{13,1},{2,6},{3,15},{... | collective-permute-start | bytes 3244040 | tf_op jit(solution)/shard_map/sum_near_0/ppermute | solution.py:28
  62.4 9.3 %collective-permute-start.12 = (bf16[16,128,128]{2,1,0:T(8,128)(2,1)S(1)}, bf16[16,128,128]{2,1,0:T(8,128)(2,1)S(1)}, u32[]{:S(2)}, u32[]{:S(2)}) collective-permute-start(bf16[16,128,128]{2,1,0:T(8,128)(2,1)S(1)} %pad_maximum_fusion.4), channel_id=1, source_target_pairs={{0,16},{1,49},{16,0},{17,33},{32,48},{33,17},{48,32},{49,1},{2,18}... | collective-permute-start | bytes 1572872 | tf_op jit(solution)/shard_map/gather_near_2/ppermute | solution.py:28
  71.8 23.2 %collective-permute-start.17 = (bf16[32,128,128]{2,1,0:T(8,128)(2,1)S(1)}, bf16[32,128,128]{2,1,0:T(8,128)(2,1)}, u32[]{:S(2)}, u32[]{:S(2)}) collective-permute-start(bf16[32,128,128]{2,1,0:T(8,128)(2,1)S(1)} %constant_dynamic-update-slice_fusion.2.refs_0_.near), channel_id=1, source_target_pairs={{0,48},{1,17},{16,32},{17,1},{32,16},{33,49},{48,0},{49,33},{2,50}... | collective-permute-start | bytes 3145736 | tf_op jit(solution)/shard_map/gather_far_2/ppermute | solution.py:28
  71.9 6.8 %copy-start.13 = (bf16[2048,1024]{1,0:T(8,128)(2,1)S(1)}, bf16[2048,1024]{1,0:T(8,128)(2,1)}, u32[]{:S(2)}) copy-start(bf16[2048,1024]{1,0:T(8,128)(2,1)} %param.17) | copy-start | bytes 12582916
  76.5 1.5 copy-start.3
  76.5 1.8 copy-start.5
  76.5 2.2 %copy-start.8 = (bf16[4096,128]{1,0:T(8,128)(2,1)}, bf16[4096,128]{1,0:T(8,128)(2,1)S(1)}, u32[]{:S(2)}) copy-start(bf16[4096,128]{1,0:T(8,128)(2,1)S(1)} %get-tuple-element.63) | copy-start | bytes 3145732
  76.5 2.1 %copy-start.2 = (bf16[512,1024]{1,0:T(8,128)(2,1)S(1)}, bf16[512,1024]{1,0:T(8,128)(2,1)}, u32[]{:S(2)}) copy-start(bf16[512,1024]{1,0:T(8,128)(2,1)} %x.2) | copy-start | bytes 3145732
  78.7 8.8 %collective-permute-start.13 = (bf16[2112,128]{1,0:T(8,128)(2,1)}, bf16[2112,128]{1,0:T(8,128)(2,1)}, u32[]{:S(2)}, u32[]{:S(2)}) collective-permute-start(bf16[2112,128]{1,0:T(8,128)(2,1)} %get-tuple-element.86.refs_1_), channel_id=1, source_target_pairs={{0,12},{1,5},{4,8},{5,1},{8,4},{9,13},{12,0},{13,9},{2,14},{3,7},{... | collective-permute-start | bytes 1622024 | tf_op jit(solution)/shard_map/sum_far_0/ppermute | solution.py:28
  81.3 6.2 %copy-start.10 = (f32[2112,128]{1,0:T(8,128)S(1)}, f32[2112,128]{1,0:T(8,128)}, u32[]{:S(2)}) copy-start(f32[2112,128]{1,0:T(8,128)} %get-tuple-element.85) | copy-start | bytes 3244036
  81.3 12.1 %copy-start.9 = (bf16[4096,128]{1,0:T(8,128)(2,1)S(1)}, bf16[4096,128]{1,0:T(8,128)(2,1)}, u32[]{:S(2)}) copy-start(bf16[4096,128]{1,0:T(8,128)(2,1)} %copy-done.8) | copy-start | bytes 3145732
  82.4 9.3 %collective-permute-start.18 = (bf16[16,128,128]{2,1,0:T(8,128)(2,1)S(1)}, bf16[16,128,128]{2,1,0:T(8,128)(2,1)S(1)}, u32[]{:S(2)}, u32[]{:S(2)}) collective-permute-start(bf16[16,128,128]{2,1,0:T(8,128)(2,1)S(1)} %pad_maximum_fusion.5), channel_id=1, source_target_pairs={{0,16},{1,49},{16,0},{17,33},{32,48},{33,17},{48,32},{49,1},{2,18}... | collective-permute-start | bytes 1572872 | tf_op jit(solution)/shard_map/gather_near_3/ppermute | solution.py:28
  88.5 11.8 %collective-permute-start.14 = (bf16[1056,128]{1,0:T(8,128)(2,1)S(1)}, bf16[1056,128]{1,0:T(8,128)(2,1)S(1)}, u32[]{:S(2)}, u32[]{:S(2)}) collective-permute-start(bf16[1056,128]{1,0:T(8,128)(2,1)S(1)} %fusion.4), channel_id=1, source_target_pairs={{0,2},{2,0},{1,3},{3,1},{4,6},{6,4},{5,7},{7,5},{8,10},{10,8},{9,1... | collective-permute-start | bytes 811016 | tf_op jit(solution)/shard_map/sum_x_0/ppermute | solution.py:18
  91.8 28.4 %collective-permute-start.23 = (bf16[32,128,128]{2,1,0:T(8,128)(2,1)S(1)}, bf16[32,128,128]{2,1,0:T(8,128)(2,1)S(1)}, u32[]{:S(2)}, u32[]{:S(2)}) collective-permute-start(bf16[32,128,128]{2,1,0:T(8,128)(2,1)S(1)} %constant_dynamic-update-slice_fusion.4.refs_0_.near), channel_id=1, source_target_pairs={{0,48},{1,17},{16,32},{17,1},{32,16},{33,49},{48,0},{49,33},{2,50}... | collective-permute-start | bytes 3145736 | tf_op jit(solution)/shard_map/gather_far_3/ppermute | solution.py:28
  93.4 15.2 %collective-permute-start.16 = (bf16[4096,128]{1,0:T(8,128)(2,1)S(1)}, bf16[4096,128]{1,0:T(8,128)(2,1)S(1)}, u32[]{:S(2)}, u32[]{:S(2)}) collective-permute-start(bf16[4096,128]{1,0:T(8,128)(2,1)S(1)} %copy-done.9), channel_id=1, source_target_pairs={{0,4},{1,13},{4,0},{5,9},{8,12},{9,5},{12,8},{13,1},{2,6},{3,15},{... | collective-permute-start | bytes 3145736 | tf_op jit(solution)/shard_map/sum_near_1/ppermute | solution.py:28
  100.2 1.3 copy-start.18
  100.3 8.3 %copy-start.4 = (f32[2048,128]{1,0:T(8,128)S(1)}, f32[2048,128]{1,0:T(8,128)}, u32[]{:S(2)}) copy-start(f32[2048,128]{1,0:T(8,128)} %copy-done.3) | copy-start | bytes 3145732
  100.3 8.3 %copy-start.6 = (f32[2048,128]{1,0:T(8,128)S(1)}, f32[2048,128]{1,0:T(8,128)}, u32[]{:S(2)}) copy-start(f32[2048,128]{1,0:T(8,128)} %copy-done.5) | copy-start | bytes 3145732
  108.5 7.0 %copy-start.14 = (bf16[2048,1024]{1,0:T(8,128)(2,1)S(1)}, bf16[2048,1024]{1,0:T(8,128)(2,1)}, u32[]{:S(2)}) copy-start(bf16[2048,1024]{1,0:T(8,128)(2,1)} %param.17) | copy-start | bytes 12582916
  108.7 9.8 %collective-permute-start.19 = (bf16[2048,128]{1,0:T(8,128)(2,1)S(1)}, bf16[2048,128]{1,0:T(8,128)(2,1)S(1)}, u32[]{:S(2)}, u32[]{:S(2)}) collective-permute-start(bf16[2048,128]{1,0:T(8,128)(2,1)S(1)} %get-tuple-element.90.refs_0_), channel_id=1, source_target_pairs={{0,12},{1,5},{4,8},{5,1},{8,4},{9,13},{12,0},{13,9},{2,14},{3,7},{... | collective-permute-start | bytes 1572872 | tf_op jit(solution)/shard_map/sum_far_1/ppermute | solution.py:28
  109.3 10.5 %collective-permute-start.15 = (bf16[512,128]{1,0:T(8,128)(2,1)S(1)}, bf16[512,128]{1,0:T(8,128)(2,1)S(1)}, u32[]{:S(2)}, u32[]{:S(2)}) collective-permute-start(bf16[512,128]{1,0:T(8,128)(2,1)S(1)} %bitcast.79), channel_id=1, source_target_pairs={{0,1},{1,0},{2,3},{3,2},{4,5},{5,4},{6,7},{7,6},{8,9},{9,8},{10,11... | collective-permute-start | bytes 393224 | tf_op jit(solution)/shard_map/mean_core_0/ppermute | solution.py:18
  112.6 20.6 %collective-permute-start.22 = (bf16[4096,128]{1,0:T(8,128)(2,1)S(1)}, bf16[4096,128]{1,0:T(8,128)(2,1)S(1)}, u32[]{:S(2)}, u32[]{:S(2)}) collective-permute-start(bf16[4096,128]{1,0:T(8,128)(2,1)S(1)} %get-tuple-element.70), channel_id=1, source_target_pairs={{0,4},{1,13},{4,0},{5,9},{8,12},{9,5},{12,8},{13,1},{2,6},{3,15},{... | collective-permute-start | bytes 3145736 | tf_op jit(solution)/shard_map/sum_near_2/ppermute | solution.py:28
  118.5 7.1 %collective-permute-start.20 = (bf16[1024,128]{1,0:T(8,128)(2,1)S(1)}, bf16[1024,128]{1,0:T(8,128)(2,1)S(1)}, u32[]{:S(2)}, u32[]{:S(2)}) collective-permute-start(bf16[1024,128]{1,0:T(8,128)(2,1)S(1)} %fusion.10), channel_id=1, source_target_pairs={{0,2},{2,0},{1,3},{3,1},{4,6},{6,4},{5,7},{7,5},{8,10},{10,8},{9,1... | collective-permute-start | bytes 786440 | tf_op jit(solution)/shard_map/sum_x_1/ppermute | solution.py:18
  133.4 8.1 %collective-permute-start.24 = (bf16[2048,128]{1,0:T(8,128)(2,1)S(1)}, bf16[2048,128]{1,0:T(8,128)(2,1)S(1)}, u32[]{:S(2)}, u32[]{:S(2)}) collective-permute-start(bf16[2048,128]{1,0:T(8,128)(2,1)S(1)} %get-tuple-element.88), channel_id=1, source_target_pairs={{0,12},{1,5},{4,8},{5,1},{8,4},{9,13},{12,0},{13,9},{2,14},{3,7},{... | collective-permute-start | bytes 1572872 | tf_op jit(solution)/shard_map/sum_far_2/ppermute | solution.py:28
  133.7 14.1 %copy-start.12 = (f32[512,1024]{1,0:T(8,128)S(1)}, f32[512,1024]{1,0:T(8,128)}, u32[]{:S(2)}) copy-start(f32[512,1024]{1,0:T(8,128)} %fusion.1) | copy-start | bytes 6291460
  133.7 14.1 %copy-start.15 = (f32[1024]{0:T(1024)S(1)}, f32[1024]{0:T(1024)}, u32[]{:S(2)}) copy-start(f32[1024]{0:T(1024)} %param.18) | copy-start | bytes 12292
  133.7 14.0 %collective-permute-start.21 = (bf16[512,128]{1,0:T(8,128)(2,1)S(1)}, bf16[512,128]{1,0:T(8,128)(2,1)S(1)}, u32[]{:S(2)}, u32[]{:S(2)}) collective-permute-start(bf16[512,128]{1,0:T(8,128)(2,1)S(1)} %bitcast.78), channel_id=1, source_target_pairs={{0,1},{1,0},{2,3},{3,2},{4,5},{5,4},{6,7},{7,6},{8,9},{9,8},{10,11... | collective-permute-start | bytes 393224 | tf_op jit(solution)/shard_map/mean_core_1/ppermute | solution.py:18
  139.2 19.3 %collective-permute-start.27 = (bf16[4096,128]{1,0:T(8,128)(2,1)S(1)}, bf16[4096,128]{1,0:T(8,128)(2,1)S(1)}, u32[]{:S(2)}, u32[]{:S(2)}) collective-permute-start(bf16[4096,128]{1,0:T(8,128)(2,1)S(1)} %get-tuple-element.76), channel_id=1, source_target_pairs={{0,4},{1,13},{4,0},{5,9},{8,12},{9,5},{12,8},{13,1},{2,6},{3,15},{... | collective-permute-start | bytes 3145736 | tf_op jit(solution)/shard_map/sum_near_3/ppermute | solution.py:28
  141.6 10.1 %collective-permute-start.25 = (bf16[1024,128]{1,0:T(8,128)(2,1)S(1)}, bf16[1024,128]{1,0:T(8,128)(2,1)S(1)}, u32[]{:S(2)}, u32[]{:S(2)}) collective-permute-start(bf16[1024,128]{1,0:T(8,128)(2,1)S(1)} %fusion.8), channel_id=1, source_target_pairs={{0,2},{2,0},{1,3},{3,1},{4,6},{6,4},{5,7},{7,5},{8,10},{10,8},{9,1... | collective-permute-start | bytes 786440 | tf_op jit(solution)/shard_map/sum_x_2/ppermute | solution.py:18
  158.7 8.4 %collective-permute-start.28 = (bf16[2048,128]{1,0:T(8,128)(2,1)S(1)}, bf16[2048,128]{1,0:T(8,128)(2,1)S(1)}, u32[]{:S(2)}, u32[]{:S(2)}) collective-permute-start(bf16[2048,128]{1,0:T(8,128)(2,1)S(1)} %get-tuple-element.91), channel_id=1, source_target_pairs={{0,12},{1,5},{4,8},{5,1},{8,4},{9,13},{12,0},{13,9},{2,14},{3,7},{... | collective-permute-start | bytes 1572872 | tf_op jit(solution)/shard_map/sum_far_3/ppermute | solution.py:28
  159.0 11.1 %collective-permute-start.26 = (bf16[512,128]{1,0:T(8,128)(2,1)S(1)}, bf16[512,128]{1,0:T(8,128)(2,1)S(1)}, u32[]{:S(2)}, u32[]{:S(2)}) collective-permute-start(bf16[512,128]{1,0:T(8,128)(2,1)S(1)} %bitcast.80), channel_id=1, source_target_pairs={{0,1},{1,0},{2,3},{3,2},{4,5},{5,4},{6,7},{7,6},{8,9},{9,8},{10,11... | collective-permute-start | bytes 393224 | tf_op jit(solution)/shard_map/mean_core_2/ppermute | solution.py:18
  167.2 6.8 %collective-permute-start.29 = (bf16[1024,128]{1,0:T(8,128)(2,1)S(1)}, bf16[1024,128]{1,0:T(8,128)(2,1)S(1)}, u32[]{:S(2)}, u32[]{:S(2)}) collective-permute-start(bf16[1024,128]{1,0:T(8,128)(2,1)S(1)} %fusion.6), channel_id=1, source_target_pairs={{0,2},{2,0},{1,3},{3,1},{4,6},{6,4},{5,7},{7,5},{8,10},{10,8},{9,1... | collective-permute-start | bytes 786440 | tf_op jit(solution)/shard_map/sum_x_3/ppermute | solution.py:18
  174.3 6.6 %collective-permute-start.30 = (bf16[512,128]{1,0:T(8,128)(2,1)S(1)}, bf16[512,128]{1,0:T(8,128)(2,1)S(1)}, u32[]{:S(2)}, u32[]{:S(2)}) collective-permute-start(bf16[512,128]{1,0:T(8,128)(2,1)S(1)} %bitcast.81), channel_id=1, source_target_pairs={{0,1},{1,0},{2,3},{3,2},{4,5},{5,4},{6,7},{7,6},{8,9},{9,8},{10,11... | collective-permute-start | bytes 393224 | tf_op jit(solution)/shard_map/mean_core_3/ppermute | solution.py:18
  (2 other events, 1.9 us)

commit v5 on v4

--- a/solution.py
+++ b/solution.py
@@ -94,7 +94,7 @@
             )
 
 
-def tile_sums(src, dst, live, c_own, c_other, pieces, with_pieces, near, far, earlier):
+def tile_sums(src, dst, live, c_own, c_other, pieces, with_pieces, near, far, earlier, cost):
     tile, w = near.shape[-2:]
     any_spec = pl.BlockSpec(memory_space=pl.ANY)
     vmem = pl.BlockSpec(memory_space=pltpu.VMEM)
@@ -117,14 +117,12 @@
         ],
         compiler_params=pltpu.CompilerParams(vmem_limit_bytes=32 * 1024 * 1024),
         cost_estimate=pl.CostEstimate(
-            flops=2 * 2 * slots * tile * tile * w * 4,
-            bytes_accessed=64 * tile * w * 8,
-            transcendentals=0,
+            flops=cost, bytes_accessed=64 * tile * w, transcendentals=0
         ),
     )(src, dst, live, c_own, c_other, pieces, near, far, *earlier)
 
 
-def message_kernel(first, core_ref, x, weight, bias, theirs, mine, held, sems):
+def message_kernel(first, core_ref, x_hbm, weight, bias, theirs, mine, x, held, row, sems):
     core = core_ref[0]
     chunks, blocks, tile, w = mine.shape
     half = weight.shape[1] // 2
@@ -137,36 +135,42 @@
         pltpu.make_async_copy(weight.at[:, pl.ds(starts[i], size)], held.at[i], sems.at[i])
         for i in range(2)
     ]
-    for copy in copies:
-        copy.start()
+    whole = [
+        pltpu.make_async_copy(x_hbm, x, sems.at[2]),
+        pltpu.make_async_copy(bias, row, sems.at[3]),
+    ]
+    copies[0].start()
+    whole[0].start()
+    whole[1].start()
+    copies[1].start()
+    whole[0].wait()
+    whole[1].wait()
     for i, out in enumerate((theirs, mine)):
         copies[i].wait()
-        row = bias[:, pl.ds(starts[i], size)]
         for j in range(chunks):
-            cols = slice(j * w, (j + 1) * w)
-            total = jnp.dot(x[...], held[i, :, cols], preferred_element_type=jnp.float32)
-            total = jnp.maximum(total + row[:, cols], 0.0)
+            total = jnp.dot(
+                x[...], held[i, :, j * w : (j + 1) * w], preferred_element_type=jnp.float32
+            )
+            total = jnp.maximum(total + row[:, pl.ds(starts[i] + j * w, w)], 0.0)
             out[j] = total.astype(out.dtype).reshape(blocks, tile, w)
 
 
 def transform(core, features, weight, bias, first, chunks, tile, w):
     vmem = pl.BlockSpec(memory_space=pltpu.VMEM)
+    any_spec = pl.BlockSpec(memory_space=pl.ANY)
     out = jax.ShapeDtypeStruct((chunks, features.shape[0] // tile, tile, w), jnp.bfloat16)
     return pl.pallas_call(
         functools.partial(message_kernel, first),
         out_shape=(out, out),
-        in_specs=[
-            pl.BlockSpec(memory_space=pltpu.SMEM),
-            vmem,
-            pl.BlockSpec(memory_space=pl.ANY),
-            vmem,
-        ],
+        in_specs=[pl.BlockSpec(memory_space=pltpu.SMEM), any_spec, any_spec, any_spec],
         out_specs=(vmem, vmem),
         scratch_shapes=[
+            pltpu.VMEM(features.shape, jnp.bfloat16),
             pltpu.VMEM((2, features.shape[1], chunks * w), jnp.bfloat16),
-            pltpu.SemaphoreType.DMA((2,)),
+            pltpu.VMEM((1, bias.shape[0]), jnp.float32),
+            pltpu.SemaphoreType.DMA((4,)),
         ],
-        compiler_params=pltpu.CompilerParams(vmem_limit_bytes=32 * 1024 * 1024),
+        compiler_params=pltpu.CompilerParams(vmem_limit_bytes=60 * 1024 * 1024),
         cost_estimate=pl.CostEstimate(
             flops=4 * features.size * chunks * w,
             bytes_accessed=2 * features.size + 4 * features.shape[1] * chunks * w,
@@ -248,40 +252,37 @@
 
     second = swap(after(own[1], first), "x_lo", "gather_x_1")
     rest = swap(after(jnp.stack(own[2:]), second), "x_lo", "gather_x_rest")
-    partner = [first, second] + [rest[j] for j in range(CHUNKS - 2)]
-
     f32, bf16 = jnp.float32, jnp.bfloat16
     near_all, far_all, part_all, pass_all, zb_all, hidden_all = [], [], [], [], [], []
     scale = None
 
-    def gather(j):
-        pair = jnp.concatenate([own[j], partner[j]]) if j else pair0
-        if j >= 2:
-            pair = after(pair, near_all[j - 1], part_all[j - 2][0])
-        elif j == 1:
-            pair = after(pair, near_all[0])
-        near_all.append(jnp.concatenate([pair, step(pair, "y", 0, f"gather_near_{j}")]))
+    def far(pair, got, j):
+        near_all.append(jnp.concatenate([pair, got]))
         far_all.append(step(near_all[j], "y", 1, f"gather_far_{j}"))
 
+    far(pair0, step(pair0, "y", 0, "gather_near_0"), 0)
+    pair = after(jnp.concatenate([own[1], second]), near_all[0])
+    far(pair, step(pair, "y", 0, "gather_near_1"), 1)
+    pairs = jnp.stack([jnp.concatenate([own[j], rest[j - 2]]) for j in range(2, CHUNKS)])
+    pairs = after(pairs, near_all[1])
+    got = step(pairs, "y", 0, "gather_near_rest")
+    for j in range(2, CHUNKS):
+        far(pairs[j - 2], got[j - 2], j)
+
     def tiles(j):
-        earlier = (rest,) if j == 0 else ()
-        if j + 1 < CHUNKS:
-            earlier += (near_all[j + 1],)
+        earlier = (rest, near_all[1]) if j == 0 else ()
+        if j == 1:
+            earlier += tuple(near_all[2:])
         if j >= 2:
             earlier += (pass_all[j - 2],)
-        if j >= 3:
-            earlier += (zb_all[j - 3],)
         with jax.named_scope(f"tiles_{j}"):
             part_all.append(
                 tile_sums(
-                    src, dst, lives, c_own, c_other, parts, j == 0, near_all[j], far_all[j], earlier
+                    src, dst, lives, c_own, c_other, parts, j == 0, near_all[j], far_all[j], earlier,
+                    2**31 if j < 2 else 2**20,
                 )
             )
-        if j + 2 < CHUNKS:
-            gather(j + 2)
-
-    gather(0)
-    gather(1)
+
     tiles(0)
     for j in range(CHUNKS):
         send, pass_on, stay = part_all[j]
@@ -289,13 +290,17 @@
         if j >= 1:
             send = after(send, pass_all[j - 1])
         got = step(send, "z", 0, f"sum_near_{j}")
+        if j == 0:
+            tiles(1)
         if j + 1 < CHUNKS:
-            tiles(j + 1)
             got = after(got, part_all[j + 1][0])
         passed = (got[: 2 * size].astype(f32) + pass_on).astype(bf16)
         pass_all.append(passed)
         stay = got[2 * size :].astype(f32) + stay
         got = step(passed, "z", 1, f"sum_far_{j}")
+        if j + 2 < CHUNKS:
+            tiles(j + 2)
+            got = after(got, part_all[j + 2][0])
         zb_all.append(got)
         passed = (got[:size].astype(f32) + stay[:size]).astype(bf16)
         stay = got[size:].astype(f32) + stay[size:]

time: 187 us -> 185 us (0.989)
  other arithmetic: 15.9 us -> 13.1 us
  Pallas kernels: 22.9 us -> 25.6 us
  waiting for transfers between devices: 79.9 us -> 77.5 us
  starting transfers between devices: 50.5 us -> 52.5 us
    ppermute x16 -> x15, waiting for transfers between devices: 59.6 us -> 37.8 us  [step(): return lax.ppermute(x, (axis, 'core'), pairs)]
    ppermute x15, waiting for transfers between devices: 20.4 us -> 39.7 us  [swap(): return lax.ppermute(x, axis, [(0, 1), (1, 0)])]
    ppermute x15, starting transfers between devices: 31.6 us -> 36.7 us  [swap(): return lax.ppermute(x, axis, [(0, 1), (1, 0)])]
    pallas_call x2, Pallas kernels: 4.26 us -> 8.16 us  [transform(): pl.pallas_call(functools.partial(message_kernel, first), out_shape=(out,...]
    ppermute x16 -> x15, starting transfers between devices: 18.9 us -> 15.8 us  [step(): return lax.ppermute(x, (axis, 'core'), pairs)]
    concatenate x4, other arithmetic: 3.36 us -> 0.35 us  [the longest x3 0.29 us: far(): near_all.append(jnp.concatenate([pair, got]))]
    reduce_sum x1, other arithmetic: 1.37 us -> 3.56 us  [local(): jnp.sum(c_own.astype(jnp.float32), axis=2)]
    unnamed x41 -> x47, local copies, waits for them, and re-layouts: 4.43 us -> 4.29 us
  transfers between devices with their start and end apart: 31 -> 30, of which waited for: 19 -> 18; matrix products, arithmetic and copies ran while one was open for 12% -> 10% of each run, Pallas kernels for 12% -> 12%
where the time goes in v5:
time: 185 us; the launch traced here: 183 us
  waiting for transfers between devices  77.5 us (42%)
  starting transfers between devices  52.5 us (28%)
  Pallas kernels  25.6 us (14%)
  other arithmetic  13.1 us (7%)
  matrix products  6.74 us (4%)
  local copies, waits for them, and re-layouts  6.25 us (3%)
    ppermute x15, waiting for transfers between devices, swap(): return lax.ppermute(x, axis, [(0, 1), (1, 0)])  39.7 us
    ppermute x15, waiting for transfers between devices, step(): return lax.ppermute(x, (axis, 'core'), pairs)  37.8 us
    ppermute x15, starting transfers between devices, swap(): return lax.ppermute(x, axis, [(0, 1), (1, 0)])  36.7 us
    pallas_call x4, Pallas kernels, tile_sums(): pl.pallas_call(tile_kernel, out_shape=(jax.ShapeDtypeStruct((4 * size, w)...  17.4 us
    ppermute x15, starting transfers between devices, step(): return lax.ppermute(x, (axis, 'core'), pairs)  15.8 us
    pallas_call x2, Pallas kernels, transform(): pl.pallas_call(functools.partial(message_kernel, first), out_shape=(out,...  8.16 us
    unnamed x47, local copies, waits for them, and re-layouts  4.29 us
  transfers between devices with their start and end apart: 30, of which 18 were waited for; matrix products, arithmetic and copies ran while one was open for 10% of the time, Pallas kernels for 12%

profile of v5, /device:TPU:3, one launch (start us, length us, event | category | flops | bytes accessed | tf_op | source)
XLA Modules:
  0.0 182.9 jit_solution(7150941653354401783)
XLA Ops:
  0.0 3.4 %shard_map.100 = (bf16[1,4,128,128]{3,2,1,0:T(8,128)(2,1)}, bf16[1,4,128,128]{3,2,1,0:T(8,128)(2,1)}) custom-call(s32[1]{0:T(128)} %bitcast.4.core_ref, bf16[512,1024]{1,0:T(8,128)(2,1)} %x_hbm.2, bf16[1024,1024]{1,0:T(8,128)(2,1)} %weight.3, f32[1,1024]{1,0:T(1,128)} %bitcast.92), custom_call_target="tpu_custom_call" | custom-call | flops 268435456 | bytes 1572864 | tf_op jit(solution)/shard_map/pallas_call | solution.py:162
  4.2 4.8 %shard_map.101 = (bf16[3,4,128,128]{3,2,1,0:T(8,128)(2,1)}, bf16[3,4,128,128]{3,2,1,0:T(8,128)(2,1)}) custom-call(s32[1]{0:T(128)} %bitcast.4.core_ref, bf16[512,1024]{1,0:T(8,128)(2,1)} %x_hbm.2, bf16[1024,1024]{1,0:T(8,128)(2,1)} %weight.3, f32[1,1024]{1,0:T(1,128)} %bitcast.93), custom_call_target="tpu_custom_call" | custom-call | flops 805306368 | bytes 2621440 | tf_op jit(solution)/shard_map/pallas_call | solution.py:162
  9.0 1.1 slice_bitcast_fusion.9
  12.5 3.6 %convert_reduce_fusion.1 = (f32[64,128]{1,0:T(8,128)S(1)}, bf16[64,128,128]{2,1,0:T(8,128)(2,1)S(1)}) fusion(s32[1,1,64,128,128]{4,3,2,1,0:T(8,128)} %param.11, pred[64]{0:T(512)(128)(4,1)S(1)} %iota_compare_fusion.2), kind=kLoop, calls=%fused_computation.3 | loop fusion | flops 4186112 | bytes 6324288 | tf_op jit(solution)/shard_map/reduce_sum | solution.py:239
  16.4 3.5 %collective-permute-done.4 = bf16[8,128,128]{2,1,0:T(8,128)(2,1)S(1)} collective-permute-done((bf16[8,128,128]{2,1,0:T(8,128)(2,1)}, bf16[8,128,128]{2,1,0:T(8,128)(2,1)S(1)}, u32[]{:S(2)}, u32[]{:S(2)}) %collective-permute-start.4) | collective-permute-done | bytes 262176 | tf_op jit(solution)/shard_map/gather_x_0/ppermute | solution.py:18
  19.9 0.8 collective-permute-start.3
  20.8 2.8 %collective-permute-start.5 = (bf16[16,128,128]{2,1,0:T(8,128)(2,1)S(1)}, bf16[16,128,128]{2,1,0:T(8,128)(2,1)S(1)}, u32[]{:S(2)}, u32[]{:S(2)}) collective-permute-start(bf16[16,128,128]{2,1,0:T(8,128)(2,1)S(1)} %pad_maximum_fusion.4), channel_id=1, source_target_pairs={{0,16},{1,49},{16,0},{17,33},{32,48},{33,17},{48,32},{49,1},{2,18}... | collective-permute-start | bytes 1572872 | tf_op jit(solution)/shard_map/gather_near_0/ppermute | solution.py:28
  24.1 7.0 %collective-permute-done.7 = bf16[8,128,128]{2,1,0:T(8,128)(2,1)S(1)} collective-permute-done((bf16[8,128,128]{2,1,0:T(8,128)(2,1)S(1)}, bf16[8,128,128]{2,1,0:T(8,128)(2,1)S(1)}, u32[]{:S(2)}, u32[]{:S(2)}) %collective-permute-start.7) | collective-permute-done | bytes 262176 | tf_op jit(solution)/shard_map/gather_x_1/ppermute | solution.py:18
  31.5 1.5 collective-permute-start.9
  33.2 11.4 %collective-permute-done.8.refs_0_ = bf16[2,8,128,128]{3,2,1,0:T(8,128)(2,1)S(1)} collective-permute-done((bf16[2,8,128,128]{3,2,1,0:T(8,128)(2,1)S(1)}, bf16[2,8,128,128]{3,2,1,0:T(8,128)(2,1)S(1)}, u32[]{:S(2)}, u32[]{:S(2)}) %collective-permute-start.8) | collective-permute-done | bytes 524320 | tf_op jit(solution)/shard_map/gather_x_rest/ppermute | solution.py:18
  45.3 1.3 collective-permute-start.12
  47.5 5.2 %collective-permute-done.6.far = bf16[32,128,128]{2,1,0:T(8,128)(2,1)S(1)} collective-permute-done((bf16[32,128,128]{2,1,0:T(8,128)(2,1)S(1)}, bf16[32,128,128]{2,1,0:T(8,128)(2,1)S(1)}, u32[]{:S(2)}, u32[]{:S(2)}) %collective-permute-start.6) | collective-permute-done | bytes 1048608 | tf_op jit(solution)/shard_map/gather_far_0/ppermute | solution.py:28
  52.7 4.1 %tiles_0.1 = (bf16[4224,128]{1,0:T(8,128)(2,1)S(1)}, f32[2112,128]{1,0:T(8,128)S(1)}, f32[2112,128]{1,0:T(8,128)S(1)}) custom-call(s32[128]{0:T(128)S(1)} %fusion.38.src_ref, s32[128]{0:T(128)S(1)} %fusion.39.dst_ref, s32[2]{0:T(128)S(1)} %fusion.37.live_ref, bf16[64,128,128]{2,1,0:T(8,128)(2,1)S(1)} %get-tuple-element.51.c_own, ...), custom_call_target="tpu_custom_call" | custom-call | flops 2147483648 | bytes 1048576 | tf_op jit(solution)/shard_map/tiles_0/pallas_call | solution.py:104
  56.8 4.3 %collective-permute-start.10 = (bf16[4224,128]{1,0:T(8,128)(2,1)S(1)}, bf16[4224,128]{1,0:T(8,128)(2,1)S(1)}, u32[]{:S(2)}, u32[]{:S(2)}) collective-permute-start(bf16[4224,128]{1,0:T(8,128)(2,1)S(1)} %get-tuple-element.57), channel_id=1, source_target_pairs={{0,4},{1,13},{4,0},{5,9},{8,12},{9,5},{12,8},{13,1},{2,6},{3,15},{... | collective-permute-start | bytes 3244040 | tf_op jit(solution)/shard_map/sum_near_0/ppermute | solution.py:28
  61.2 10.6 %collective-permute-done.12 = bf16[2,16,128,128]{3,2,1,0:T(8,128)(2,1)S(1)} collective-permute-done((bf16[2,16,128,128]{3,2,1,0:T(8,128)(2,1)S(1)}, bf16[2,16,128,128]{3,2,1,0:T(8,128)(2,1)S(1)}, u32[]{:S(2)}, u32[]{:S(2)}) %collective-permute-start.12) | collective-permute-done | bytes 1048608 | tf_op jit(solution)/shard_map/gather_near_rest/ppermute | solution.py:28
  72.4 2.0 %collective-permute-done.11.far = bf16[32,128,128]{2,1,0:T(8,128)(2,1)S(1)} collective-permute-done((bf16[32,128,128]{2,1,0:T(8,128)(2,1)S(1)}, bf16[32,128,128]{2,1,0:T(8,128)(2,1)S(1)}, u32[]{:S(2)}, u32[]{:S(2)}) %collective-permute-start.11) | collective-permute-done | bytes 1048608 | tf_op jit(solution)/shard_map/gather_far_1/ppermute | solution.py:28
  74.4 5.0 %tiles_1.1 = (bf16[4096,128]{1,0:T(8,128)(2,1)}, f32[2048,128]{1,0:T(8,128)S(1)}, f32[2048,128]{1,0:T(8,128)S(1)}) custom-call(s32[128]{0:T(128)S(1)} %fusion.38.src_ref, s32[128]{0:T(128)S(1)} %fusion.39.dst_ref, s32[2]{0:T(128)S(1)} %fusion.37.live_ref, bf16[64,128,128]{2,1,0:T(8,128)(2,1)S(1)} %get-tuple-element.51.c_own, ...), custom_call_target="tpu_custom_call" | custom-call | flops 2147483648 | bytes 1048576 | tf_op jit(solution)/shard_map/tiles_1/pallas_call | solution.py:104
  80.8 2.1 %collective-permute-start.13 = (bf16[2112,128]{1,0:T(8,128)(2,1)S(1)}, bf16[2112,128]{1,0:T(8,128)(2,1)S(1)}, u32[]{:S(2)}, u32[]{:S(2)}) collective-permute-start(bf16[2112,128]{1,0:T(8,128)(2,1)S(1)} %get-tuple-element.88.refs_0_), channel_id=1, source_target_pairs={{0,12},{1,5},{4,8},{5,1},{8,4},{9,13},{12,0},{13,9},{2,14},{3,7},{... | collective-permute-start | bytes 1622024 | tf_op jit(solution)/shard_map/sum_far_0/ppermute | solution.py:28
  82.9 2.2 %collective-permute-start.17 = (bf16[4096,128]{1,0:T(8,128)(2,1)}, bf16[4096,128]{1,0:T(8,128)(2,1)}, u32[]{:S(2)}, u32[]{:S(2)}) collective-permute-start(bf16[4096,128]{1,0:T(8,128)(2,1)} %get-tuple-element.66), channel_id=1, source_target_pairs={{0,4},{1,13},{4,0},{5,9},{8,12},{9,5},{12,8},{13,1},{2,6},{3,15},{... | collective-permute-start | bytes 3145736 | tf_op jit(solution)/shard_map/sum_near_1/ppermute | solution.py:28
  85.1 1.0 collective-permute-done.14.far
  86.1 4.3 %tiles_2.1 = (bf16[4096,128]{1,0:T(8,128)(2,1)S(1)}, f32[2048,128]{1,0:T(8,128)S(1)}, f32[2048,128]{1,0:T(8,128)S(1)}) custom-call(s32[128]{0:T(128)S(1)} %fusion.38.src_ref, s32[128]{0:T(128)S(1)} %fusion.39.dst_ref, s32[2]{0:T(128)S(1)} %fusion.37.live_ref, bf16[64,128,128]{2,1,0:T(8,128)(2,1)S(1)} %get-tuple-element.51.c_own, ...), custom_call_target="tpu_custom_call" | custom-call | flops 1048576 | bytes 1048576 | tf_op jit(solution)/shard_map/tiles_2/pallas_call | solution.py:104
  90.4 1.0 copy-done.2
  91.4 1.0 copy-done.4
  92.4 1.0 copy-done.10
  93.4 0.8 fusion.4
  94.3 1.5 collective-permute-start.15
  95.8 2.6 %fusion.1 = f32[512,1024]{1,0:T(8,128)} fusion(bf16[512,1024]{1,0:T(8,128)(2,1)S(1)} %copy-done.13, bf16[2048,1024]{1,0:T(8,128)(2,1)S(1)} %copy-done.16), kind=kOutput, calls=%fused_computation.7 | convolution fusion | flops 1073741824 | bytes 5242880 | tf_op jit(solution)/shard_map/dot_general | solution.py:247
  98.6 2.7 %collective-permute-done.15 = bf16[1056,128]{1,0:T(8,128)(2,1)S(1)} collective-permute-done((bf16[1056,128]{1,0:T(8,128)(2,1)}, bf16[1056,128]{1,0:T(8,128)(2,1)S(1)}, u32[]{:S(2)}, u32[]{:S(2)}) %collective-permute-start.15) | collective-permute-done | bytes 270368 | tf_op jit(solution)/shard_map/sum_x_0/ppermute | solution.py:18
  101.3 1.2 fusion.3
  102.7 1.2 collective-permute-done.17
  103.9 1.5 convert_add_fusion.3
  105.4 0.9 collective-permute-start.18
  106.5 9.1 %collective-permute-start.16 = (bf16[512,128]{1,0:T(8,128)(2,1)S(1)}, bf16[512,128]{1,0:T(8,128)(2,1)S(1)}, u32[]{:S(2)}, u32[]{:S(2)}) collective-permute-start(bf16[512,128]{1,0:T(8,128)(2,1)S(1)} %bitcast.87), channel_id=1, source_target_pairs={{0,1},{1,0},{2,3},{3,2},{4,5},{5,4},{6,7},{7,6},{8,9},{9,8},{10,11... | collective-permute-start | bytes 393224 | tf_op jit(solution)/shard_map/mean_core_0/ppermute | solution.py:18
  116.1 4.1 %tiles_3.1 = (bf16[4096,128]{1,0:T(8,128)(2,1)S(1)}, f32[2048,128]{1,0:T(8,128)S(1)}, f32[2048,128]{1,0:T(8,128)S(1)}) custom-call(s32[128]{0:T(128)S(1)} %fusion.38.src_ref, s32[128]{0:T(128)S(1)} %fusion.39.dst_ref, s32[2]{0:T(128)S(1)} %fusion.37.live_ref, bf16[64,128,128]{2,1,0:T(8,128)(2,1)S(1)} %get-tuple-element.51.c_own, ...), custom_call_target="tpu_custom_call" | custom-call | flops 1048576 | bytes 1048576 | tf_op jit(solution)/shard_map/tiles_3/pallas_call | solution.py:104
  120.3 1.1 collective-permute-start.20
  121.8 5.3 %collective-permute-done.20 = bf16[1024,128]{1,0:T(8,128)(2,1)S(1)} collective-permute-done((bf16[1024,128]{1,0:T(8,128)(2,1)S(1)}, bf16[1024,128]{1,0:T(8,128)(2,1)S(1)}, u32[]{:S(2)}, u32[]{:S(2)}) %collective-permute-start.20) | collective-permute-done | bytes 262176 | tf_op jit(solution)/shard_map/sum_x_1/ppermute | solution.py:18
  127.2 6.0 %collective-permute-done.22 = bf16[4096,128]{1,0:T(8,128)(2,1)S(1)} collective-permute-done((bf16[4096,128]{1,0:T(8,128)(2,1)S(1)}, bf16[4096,128]{1,0:T(8,128)(2,1)S(1)}, u32[]{:S(2)}, u32[]{:S(2)}) %collective-permute-start.22) | collective-permute-done | bytes 1048608 | tf_op jit(solution)/shard_map/sum_near_2/ppermute | solution.py:28
  133.8 6.2 %collective-permute-start.21 = (bf16[512,128]{1,0:T(8,128)(2,1)S(1)}, bf16[512,128]{1,0:T(8,128)(2,1)S(1)}, u32[]{:S(2)}, u32[]{:S(2)}) collective-permute-start(bf16[512,128]{1,0:T(8,128)(2,1)S(1)} %bitcast.88), channel_id=1, source_target_pairs={{0,1},{1,0},{2,3},{3,2},{4,5},{5,4},{6,7},{7,6},{8,9},{9,8},{10,11... | collective-permute-start | bytes 393224 | tf_op jit(solution)/shard_map/mean_core_1/ppermute | solution.py:18
  140.4 1.4 collective-permute-done.23
  141.9 1.7 collective-permute-start.24
  144.3 4.6 %collective-permute-done.24 = bf16[1024,128]{1,0:T(8,128)(2,1)S(1)} collective-permute-done((bf16[1024,128]{1,0:T(8,128)(2,1)S(1)}, bf16[1024,128]{1,0:T(8,128)(2,1)S(1)}, u32[]{:S(2)}, u32[]{:S(2)}) %collective-permute-start.24) | collective-permute-done | bytes 262176 | tf_op jit(solution)/shard_map/sum_x_2/ppermute | solution.py:18
  149.0 8.5 %collective-permute-done.26 = bf16[4096,128]{1,0:T(8,128)(2,1)S(1)} collective-permute-done((bf16[4096,128]{1,0:T(8,128)(2,1)S(1)}, bf16[4096,128]{1,0:T(8,128)(2,1)S(1)}, u32[]{:S(2)}, u32[]{:S(2)}) %collective-permute-start.26) | collective-permute-done | bytes 1048608 | tf_op jit(solution)/shard_map/sum_near_3/ppermute | solution.py:28
  158.1 6.2 %collective-permute-start.25 = (bf16[512,128]{1,0:T(8,128)(2,1)S(1)}, bf16[512,128]{1,0:T(8,128)(2,1)S(1)}, u32[]{:S(2)}, u32[]{:S(2)}) collective-permute-start(bf16[512,128]{1,0:T(8,128)(2,1)S(1)} %bitcast.89), channel_id=1, source_target_pairs={{0,1},{1,0},{2,3},{3,2},{4,5},{5,4},{6,7},{7,6},{8,9},{9,8},{10,11... | collective-permute-start | bytes 393224 | tf_op jit(solution)/shard_map/mean_core_2/ppermute | solution.py:18
  164.7 1.5 collective-permute-done.27
  166.3 1.7 collective-permute-start.28
  168.4 4.6 %collective-permute-done.28 = bf16[1024,128]{1,0:T(8,128)(2,1)S(1)} collective-permute-done((bf16[1024,128]{1,0:T(8,128)(2,1)S(1)}, bf16[1024,128]{1,0:T(8,128)(2,1)S(1)}, u32[]{:S(2)}, u32[]{:S(2)}) %collective-permute-start.28) | collective-permute-done | bytes 262176 | tf_op jit(solution)/shard_map/sum_x_3/ppermute | solution.py:18
  173.4 6.2 %collective-permute-start.29 = (bf16[512,128]{1,0:T(8,128)(2,1)S(1)}, bf16[512,128]{1,0:T(8,128)(2,1)S(1)}, u32[]{:S(2)}, u32[]{:S(2)}) collective-permute-start(bf16[512,128]{1,0:T(8,128)(2,1)S(1)} %bitcast.90), channel_id=1, source_target_pairs={{0,1},{1,0},{2,3},{3,2},{4,5},{5,4},{6,7},{7,6},{8,9},{9,8},{10,11... | collective-permute-start | bytes 393224 | tf_op jit(solution)/shard_map/mean_core_3/ppermute | solution.py:18
  181.3 1.6 broadcast_divide_fusion
  (139 shorter events, 14.4 us)
Async XLA Ops:
  3.4 7.3 %copy-start.20 = (s32[1,1,64]{2,1,0:T(1,128)S(1)}, s32[1,1,64]{2,1,0:T(1,128)}, u32[]{:S(2)}) copy-start(s32[1,1,64]{2,1,0:T(1,128)} %param.13) | copy-start | bytes 772
  3.4 7.3 %copy-start.21 = (s32[1,1,64]{2,1,0:T(1,128)S(1)}, s32[1,1,64]{2,1,0:T(1,128)}, u32[]{:S(2)}) copy-start(s32[1,1,64]{2,1,0:T(1,128)} %param.12) | copy-start | bytes 772
  3.4 7.6 %copy-start.15 = (bf16[1,4,128,128]{3,2,1,0:T(8,128)(2,1)S(1)}, bf16[1,4,128,128]{3,2,1,0:T(8,128)(2,1)}, u32[]{:S(2)}) copy-start(bf16[1,4,128,128]{3,2,1,0:T(8,128)(2,1)} %get-tuple-element.44) | copy-start | bytes 393220
  3.4 7.6 %collective-permute-start = (bf16[4,128,128]{2,1,0:T(8,128)(2,1)}, bf16[4,128,128]{2,1,0:T(8,128)(2,1)S(1)}, u32[]{:S(2)}, u32[]{:S(2)}) collective-permute-start(bf16[4,128,128]{2,1,0:T(8,128)(2,1)} %bitcast.96), channel_id=1, source_target_pairs={{0,1},{1,0},{2,3},{3,2},{4,5},{5,4},{6,7},{7,6},{8,9},{9,8},{10,11... | collective-permute-start | bytes 393224 | tf_op jit(solution)/shard_map/other_core_0/ppermute | solution.py:18
  11.8 8.1 %collective-permute-start.4 = (bf16[8,128,128]{2,1,0:T(8,128)(2,1)}, bf16[8,128,128]{2,1,0:T(8,128)(2,1)S(1)}, u32[]{:S(2)}, u32[]{:S(2)}) collective-permute-start(bf16[8,128,128]{2,1,0:T(8,128)(2,1)} %pad_maximum_fusion.7), channel_id=1, source_target_pairs={{0,64},{64,0},{1,65},{65,1},{2,66},{66,2},{3,67},{67,3},{4,68},{68... | collective-permute-start | bytes 786440 | tf_op jit(solution)/shard_map/gather_x_0/ppermute | solution.py:18
  12.0 7.9 %collective-permute-start.2 = (bf16[3,4,128,128]{3,2,1,0:T(8,128)(2,1)}, bf16[3,4,128,128]{3,2,1,0:T(8,128)(2,1)S(1)}, u32[]{:S(2)}, u32[]{:S(2)}) collective-permute-start(bf16[3,4,128,128]{3,2,1,0:T(8,128)(2,1)} %get-tuple-element.50), channel_id=1, source_target_pairs={{0,1},{1,0},{2,3},{3,2},{4,5},{5,4},{6,7},{7,6},{8,9},{9,8},{10,11... | collective-permute-start | bytes 1179656 | tf_op jit(solution)/shard_map/other_core_rest/ppermute | solution.py:18
  12.3 3.8 %collective-permute-start.1 = (s32[3,64]{1,0:T(4,128)S(1)}, s32[3,64]{1,0:T(4,128)S(1)}, u32[]{:S(2)}, u32[]{:S(2)}) collective-permute-start(s32[3,64]{1,0:T(4,128)S(1)} %get-tuple-element.46), channel_id=1, source_target_pairs={{0,1},{1,0},{2,3},{3,2},{4,5},{5,4},{6,7},{7,6},{8,9},{9,8},{10,11... | collective-permute-start | bytes 2312 | tf_op jit(solution)/shard_map/other_meta/ppermute | solution.py:18
  19.9 26.7 %collective-permute-start.3 = (bf16[64,128,128]{2,1,0:T(8,128)(2,1)S(1)}, bf16[64,128,128]{2,1,0:T(8,128)(2,1)S(1)}, u32[]{:S(2)}, u32[]{:S(2)}) collective-permute-start(bf16[64,128,128]{2,1,0:T(8,128)(2,1)S(1)} %get-tuple-element.51.c_own), channel_id=1, source_target_pairs={{0,1},{1,0},{2,3},{3,2},{4,5},{5,4},{6,7},{7,6},{8,9},{9,8},{10,11... | collective-permute-start | bytes 6291464 | tf_op jit(solution)/shard_map/other_tiles/ppermute | solution.py:18
  20.8 10.6 %collective-permute-start.5 = (bf16[16,128,128]{2,1,0:T(8,128)(2,1)S(1)}, bf16[16,128,128]{2,1,0:T(8,128)(2,1)S(1)}, u32[]{:S(2)}, u32[]{:S(2)}) collective-permute-start(bf16[16,128,128]{2,1,0:T(8,128)(2,1)S(1)} %pad_maximum_fusion.4), channel_id=1, source_target_pairs={{0,16},{1,49},{16,0},{17,33},{32,48},{33,17},{48,32},{49,1},{2,18}... | collective-permute-start | bytes 1572872 | tf_op jit(solution)/shard_map/gather_near_0/ppermute | solution.py:28
  23.7 7.4 %collective-permute-start.7 = (bf16[8,128,128]{2,1,0:T(8,128)(2,1)S(1)}, bf16[8,128,128]{2,1,0:T(8,128)(2,1)S(1)}, u32[]{:S(2)}, u32[]{:S(2)}) collective-permute-start(bf16[8,128,128]{2,1,0:T(8,128)(2,1)S(1)} %pad_maximum_fusion.8), channel_id=1, source_target_pairs={{0,64},{64,0},{1,65},{65,1},{2,66},{66,2},{3,67},{67,3},{4,68},{68... | collective-permute-start | bytes 786440 | tf_op jit(solution)/shard_map/gather_x_1/ppermute | solution.py:18
  31.1 13.5 %collective-permute-start.8 = (bf16[2,8,128,128]{3,2,1,0:T(8,128)(2,1)S(1)}, bf16[2,8,128,128]{3,2,1,0:T(8,128)(2,1)S(1)}, u32[]{:S(2)}, u32[]{:S(2)}) collective-permute-start(bf16[2,8,128,128]{3,2,1,0:T(8,128)(2,1)S(1)} %pad_maximum_fusion.5), channel_id=1, source_target_pairs={{0,64},{64,0},{1,65},{65,1},{2,66},{66,2},{3,67},{67,3},{4,68},{68... | collective-permute-start | bytes 1572872 | tf_op jit(solution)/shard_map/gather_x_rest/ppermute | solution.py:18
  31.5 13.6 %collective-permute-start.9 = (bf16[16,128,128]{2,1,0:T(8,128)(2,1)S(1)}, bf16[16,128,128]{2,1,0:T(8,128)(2,1)S(1)}, u32[]{:S(2)}, u32[]{:S(2)}) collective-permute-start(bf16[16,128,128]{2,1,0:T(8,128)(2,1)S(1)} %pad_maximum_fusion.6), channel_id=1, source_target_pairs={{0,16},{1,49},{16,0},{17,33},{32,48},{33,17},{48,32},{49,1},{2,18}... | collective-permute-start | bytes 1572872 | tf_op jit(solution)/shard_map/gather_near_1/ppermute | solution.py:28
  33.1 19.7 %collective-permute-start.6 = (bf16[32,128,128]{2,1,0:T(8,128)(2,1)S(1)}, bf16[32,128,128]{2,1,0:T(8,128)(2,1)S(1)}, u32[]{:S(2)}, u32[]{:S(2)}) collective-permute-start(bf16[32,128,128]{2,1,0:T(8,128)(2,1)S(1)} %pad_maximum_fusion.near), channel_id=1, source_target_pairs={{0,48},{1,17},{16,32},{17,1},{32,16},{33,49},{48,0},{49,33},{2,50}... | collective-permute-start | bytes 3145736 | tf_op jit(solution)/shard_map/gather_far_0/ppermute | solution.py:28
  45.2 29.2 %collective-permute-start.11 = (bf16[32,128,128]{2,1,0:T(8,128)(2,1)S(1)}, bf16[32,128,128]{2,1,0:T(8,128)(2,1)S(1)}, u32[]{:S(2)}, u32[]{:S(2)}) collective-permute-start(bf16[32,128,128]{2,1,0:T(8,128)(2,1)S(1)} %constant_dynamic-update-slice_fusion.refs_1_.near), channel_id=1, source_target_pairs={{0,48},{1,17},{16,32},{17,1},{32,16},{33,49},{48,0},{49,33},{2,50}... | collective-permute-start | bytes 3145736 | tf_op jit(solution)/shard_map/gather_far_1/ppermute | solution.py:28
  45.3 26.5 %collective-permute-start.12 = (bf16[2,16,128,128]{3,2,1,0:T(8,128)(2,1)S(1)}, bf16[2,16,128,128]{3,2,1,0:T(8,128)(2,1)S(1)}, u32[]{:S(2)}, u32[]{:S(2)}) collective-permute-start(bf16[2,16,128,128]{3,2,1,0:T(8,128)(2,1)S(1)} %pad_maximum_fusion.1), channel_id=1, source_target_pairs={{0,16},{1,49},{16,0},{17,33},{32,48},{33,17},{48,32},{49,1},{2,18}... | collective-permute-start | bytes 3145736 | tf_op jit(solution)/shard_map/gather_near_rest/ppermute | solution.py:28
  46.6 39.5 %copy-start = (bf16[64,128,128]{2,1,0:T(8,128)(2,1)}, bf16[64,128,128]{2,1,0:T(8,128)(2,1)S(1)}, u32[]{:S(2)}) copy-start(bf16[64,128,128]{2,1,0:T(8,128)(2,1)S(1)} %collective-permute-done.3.c_other) | copy-start | bytes 6291460
  56.8 22.7 %collective-permute-start.10 = (bf16[4224,128]{1,0:T(8,128)(2,1)S(1)}, bf16[4224,128]{1,0:T(8,128)(2,1)S(1)}, u32[]{:S(2)}, u32[]{:S(2)}) collective-permute-start(bf16[4224,128]{1,0:T(8,128)(2,1)S(1)} %get-tuple-element.57), channel_id=1, source_target_pairs={{0,4},{1,13},{4,0},{5,9},{8,12},{9,5},{12,8},{13,1},{2,6},{3,15},{... | collective-permute-start | bytes 3244040 | tf_op jit(solution)/shard_map/sum_near_0/ppermute | solution.py:28
  72.1 14.0 %collective-permute-start.14 = (bf16[32,128,128]{2,1,0:T(8,128)(2,1)S(1)}, bf16[32,128,128]{2,1,0:T(8,128)(2,1)S(1)}, u32[]{:S(2)}, u32[]{:S(2)}) collective-permute-start(bf16[32,128,128]{2,1,0:T(8,128)(2,1)S(1)} %pad_maximum_fusion.2.refs_0_.near), channel_id=1, source_target_pairs={{0,48},{1,17},{16,32},{17,1},{32,16},{33,49},{48,0},{49,33},{2,50}... | collective-permute-start | bytes 3145736 | tf_op jit(solution)/shard_map/gather_far_2/ppermute | solution.py:28
  79.5 1.3 copy-start.8
  80.8 12.6 %copy-start.12 = (f32[2112,128]{1,0:T(8,128)}, f32[2112,128]{1,0:T(8,128)S(1)}, u32[]{:S(2)}) copy-start(f32[2112,128]{1,0:T(8,128)S(1)} %get-tuple-element.87) | copy-start | bytes 3244036
  80.8 15.0 %copy-start.13 = (bf16[512,1024]{1,0:T(8,128)(2,1)S(1)}, bf16[512,1024]{1,0:T(8,128)(2,1)}, u32[]{:S(2)}) copy-start(bf16[512,1024]{1,0:T(8,128)(2,1)} %x_hbm.2) | copy-start | bytes 3145732
  80.8 15.0 %copy-start.16 = (bf16[2048,1024]{1,0:T(8,128)(2,1)S(1)}, bf16[2048,1024]{1,0:T(8,128)(2,1)}, u32[]{:S(2)}) copy-start(bf16[2048,1024]{1,0:T(8,128)(2,1)} %param.17) | copy-start | bytes 12582916
  80.8 12.6 %collective-permute-start.13 = (bf16[2112,128]{1,0:T(8,128)(2,1)S(1)}, bf16[2112,128]{1,0:T(8,128)(2,1)S(1)}, u32[]{:S(2)}, u32[]{:S(2)}) collective-permute-start(bf16[2112,128]{1,0:T(8,128)(2,1)S(1)} %get-tuple-element.88.refs_0_), channel_id=1, source_target_pairs={{0,12},{1,5},{4,8},{5,1},{8,4},{9,13},{12,0},{13,9},{2,14},{3,7},{... | collective-permute-start | bytes 1622024 | tf_op jit(solution)/shard_map/sum_far_0/ppermute | solution.py:28
  82.9 21.0 %collective-permute-start.17 = (bf16[4096,128]{1,0:T(8,128)(2,1)}, bf16[4096,128]{1,0:T(8,128)(2,1)}, u32[]{:S(2)}, u32[]{:S(2)}) collective-permute-start(bf16[4096,128]{1,0:T(8,128)(2,1)} %get-tuple-element.66), channel_id=1, source_target_pairs={{0,4},{1,13},{4,0},{5,9},{8,12},{9,5},{12,8},{13,1},{2,6},{3,15},{... | collective-permute-start | bytes 3145736 | tf_op jit(solution)/shard_map/sum_near_1/ppermute | solution.py:28
  94.3 7.0 %collective-permute-start.15 = (bf16[1056,128]{1,0:T(8,128)(2,1)}, bf16[1056,128]{1,0:T(8,128)(2,1)S(1)}, u32[]{:S(2)}, u32[]{:S(2)}) collective-permute-start(bf16[1056,128]{1,0:T(8,128)(2,1)} %fusion.4), channel_id=1, source_target_pairs={{0,2},{2,0},{1,3},{3,1},{4,6},{6,4},{5,7},{7,5},{8,10},{10,8},{9,1... | collective-permute-start | bytes 811016 | tf_op jit(solution)/shard_map/sum_x_0/ppermute | solution.py:18
  98.4 4.2 %copy-start.22 = (f32[4]{0:T(128)S(1)}, f32[4]{0:T(128)}, u32[]{:S(2)}) copy-start(f32[4]{0:T(128)} %constant.147.clone) | copy-start | bytes 52
  98.4 5.5 %copy-start.7 = (f32[2048,128]{1,0:T(8,128)S(1)}, f32[2048,128]{1,0:T(8,128)}, u32[]{:S(2)}) copy-start(f32[2048,128]{1,0:T(8,128)} %copy-done.6) | copy-start | bytes 3145732
  98.4 5.5 %copy-start.9 = (f32[2048,128]{1,0:T(8,128)S(1)}, f32[2048,128]{1,0:T(8,128)}, u32[]{:S(2)}) copy-start(f32[2048,128]{1,0:T(8,128)} %copy-done.8) | copy-start | bytes 3145732
  98.4 17.7 %collective-permute-start.19 = (bf16[32,128,128]{2,1,0:T(8,128)(2,1)S(1)}, bf16[32,128,128]{2,1,0:T(8,128)(2,1)S(1)}, u32[]{:S(2)}, u32[]{:S(2)}) collective-permute-start(bf16[32,128,128]{2,1,0:T(8,128)(2,1)S(1)} %pad_maximum_fusion.3.refs_1_.near), channel_id=1, source_target_pairs={{0,48},{1,17},{16,32},{17,1},{32,16},{33,49},{48,0},{49,33},{2,50}... | collective-permute-start | bytes 3145736 | tf_op jit(solution)/shard_map/gather_far_3/ppermute | solution.py:28
  103.9 11.8 %copy-start.11 = (bf16[4096,128]{1,0:T(8,128)(2,1)S(1)}, bf16[4096,128]{1,0:T(8,128)(2,1)}, u32[]{:S(2)}) copy-start(bf16[4096,128]{1,0:T(8,128)(2,1)} %copy-done.10) | copy-start | bytes 3145732
  103.9 11.8 %copy-start.17 = (bf16[2048,1024]{1,0:T(8,128)(2,1)S(1)}, bf16[2048,1024]{1,0:T(8,128)(2,1)}, u32[]{:S(2)}) copy-start(bf16[2048,1024]{1,0:T(8,128)(2,1)} %param.17) | copy-start | bytes 12582916
  105.4 10.7 %copy-start.1 = (bf16[64,128,128]{2,1,0:T(8,128)(2,1)S(1)}, bf16[64,128,128]{2,1,0:T(8,128)(2,1)}, u32[]{:S(2)}) copy-start(bf16[64,128,128]{2,1,0:T(8,128)(2,1)} %copy-done) | copy-start | bytes 6291460
  105.4 14.8 %collective-permute-start.18 = (bf16[2048,128]{1,0:T(8,128)(2,1)S(1)}, bf16[2048,128]{1,0:T(8,128)(2,1)S(1)}, u32[]{:S(2)}, u32[]{:S(2)}) collective-permute-start(bf16[2048,128]{1,0:T(8,128)(2,1)S(1)} %get-tuple-element.92.refs_0_), channel_id=1, source_target_pairs={{0,12},{1,5},{4,8},{5,1},{8,4},{9,13},{12,0},{13,9},{2,14},{3,7},{... | collective-permute-start | bytes 1572872 | tf_op jit(solution)/shard_map/sum_far_1/ppermute | solution.py:28
  106.5 14.9 %collective-permute-start.16 = (bf16[512,128]{1,0:T(8,128)(2,1)S(1)}, bf16[512,128]{1,0:T(8,128)(2,1)S(1)}, u32[]{:S(2)}, u32[]{:S(2)}) collective-permute-start(bf16[512,128]{1,0:T(8,128)(2,1)S(1)} %bitcast.87), channel_id=1, source_target_pairs={{0,1},{1,0},{2,3},{3,2},{4,5},{5,4},{6,7},{7,6},{8,9},{9,8},{10,11... | collective-permute-start | bytes 393224 | tf_op jit(solution)/shard_map/mean_core_0/ppermute | solution.py:18
  115.7 17.5 %collective-permute-start.22 = (bf16[4096,128]{1,0:T(8,128)(2,1)S(1)}, bf16[4096,128]{1,0:T(8,128)(2,1)S(1)}, u32[]{:S(2)}, u32[]{:S(2)}) collective-permute-start(bf16[4096,128]{1,0:T(8,128)(2,1)S(1)} %copy-done.11), channel_id=1, source_target_pairs={{0,4},{1,13},{4,0},{5,9},{8,12},{9,5},{12,8},{13,1},{2,6},{3,15},{... | collective-permute-start | bytes 3145736 | tf_op jit(solution)/shard_map/sum_near_2/ppermute | solution.py:28
  120.3 12.9 %copy-start.3 = (f32[2048,128]{1,0:T(8,128)S(1)}, f32[2048,128]{1,0:T(8,128)}, u32[]{:S(2)}) copy-start(f32[2048,128]{1,0:T(8,128)} %copy-done.2) | copy-start | bytes 3145732
  120.3 12.9 %copy-start.5 = (f32[2048,128]{1,0:T(8,128)S(1)}, f32[2048,128]{1,0:T(8,128)}, u32[]{:S(2)}) copy-start(f32[2048,128]{1,0:T(8,128)} %copy-done.4) | copy-start | bytes 3145732
  120.3 6.8 %collective-permute-start.20 = (bf16[1024,128]{1,0:T(8,128)(2,1)S(1)}, bf16[1024,128]{1,0:T(8,128)(2,1)S(1)}, u32[]{:S(2)}, u32[]{:S(2)}) collective-permute-start(bf16[1024,128]{1,0:T(8,128)(2,1)S(1)} %fusion.10), channel_id=1, source_target_pairs={{0,2},{2,0},{1,3},{3,1},{4,6},{6,4},{5,7},{7,5},{8,10},{10,8},{9,1... | collective-permute-start | bytes 786440 | tf_op jit(solution)/shard_map/sum_x_1/ppermute | solution.py:18
  133.4 8.4 %collective-permute-start.23 = (bf16[2048,128]{1,0:T(8,128)(2,1)S(1)}, bf16[2048,128]{1,0:T(8,128)(2,1)S(1)}, u32[]{:S(2)}, u32[]{:S(2)}) collective-permute-start(bf16[2048,128]{1,0:T(8,128)(2,1)S(1)} %get-tuple-element.90), channel_id=1, source_target_pairs={{0,12},{1,5},{4,8},{5,1},{8,4},{9,13},{12,0},{13,9},{2,14},{3,7},{... | collective-permute-start | bytes 1572872 | tf_op jit(solution)/shard_map/sum_far_2/ppermute | solution.py:28
  133.7 9.9 %copy-start.14 = (f32[512,1024]{1,0:T(8,128)S(1)}, f32[512,1024]{1,0:T(8,128)}, u32[]{:S(2)}) copy-start(f32[512,1024]{1,0:T(8,128)} %fusion.1) | copy-start | bytes 6291460
  133.8 9.9 %copy-start.19 = (f32[1024]{0:T(1024)S(1)}, f32[1024]{0:T(1024)}, u32[]{:S(2)}) copy-start(f32[1024]{0:T(1024)} %param.18) | copy-start | bytes 12292
  133.8 9.9 %collective-permute-start.21 = (bf16[512,128]{1,0:T(8,128)(2,1)S(1)}, bf16[512,128]{1,0:T(8,128)(2,1)S(1)}, u32[]{:S(2)}, u32[]{:S(2)}) collective-permute-start(bf16[512,128]{1,0:T(8,128)(2,1)S(1)} %bitcast.88), channel_id=1, source_target_pairs={{0,1},{1,0},{2,3},{3,2},{4,5},{5,4},{6,7},{7,6},{8,9},{9,8},{10,11... | collective-permute-start | bytes 393224 | tf_op jit(solution)/shard_map/mean_core_1/ppermute | solution.py:18
  140.0 17.5 %collective-permute-start.26 = (bf16[4096,128]{1,0:T(8,128)(2,1)S(1)}, bf16[4096,128]{1,0:T(8,128)(2,1)S(1)}, u32[]{:S(2)}, u32[]{:S(2)}) collective-permute-start(bf16[4096,128]{1,0:T(8,128)(2,1)S(1)} %get-tuple-element.78), channel_id=1, source_target_pairs={{0,4},{1,13},{4,0},{5,9},{8,12},{9,5},{12,8},{13,1},{2,6},{3,15},{... | collective-permute-start | bytes 3145736 | tf_op jit(solution)/shard_map/sum_near_3/ppermute | solution.py:28
  141.9 7.0 %collective-permute-start.24 = (bf16[1024,128]{1,0:T(8,128)(2,1)S(1)}, bf16[1024,128]{1,0:T(8,128)(2,1)S(1)}, u32[]{:S(2)}, u32[]{:S(2)}) collective-permute-start(bf16[1024,128]{1,0:T(8,128)(2,1)S(1)} %fusion.8), channel_id=1, source_target_pairs={{0,2},{2,0},{1,3},{3,1},{4,6},{6,4},{5,7},{7,5},{8,10},{10,8},{9,1... | collective-permute-start | bytes 786440 | tf_op jit(solution)/shard_map/sum_x_2/ppermute | solution.py:18
  157.8 8.4 %collective-permute-start.27 = (bf16[2048,128]{1,0:T(8,128)(2,1)S(1)}, bf16[2048,128]{1,0:T(8,128)(2,1)S(1)}, u32[]{:S(2)}, u32[]{:S(2)}) collective-permute-start(bf16[2048,128]{1,0:T(8,128)(2,1)S(1)} %get-tuple-element.93), channel_id=1, source_target_pairs={{0,12},{1,5},{4,8},{5,1},{8,4},{9,13},{12,0},{13,9},{2,14},{3,7},{... | collective-permute-start | bytes 1572872 | tf_op jit(solution)/shard_map/sum_far_3/ppermute | solution.py:28
  158.1 9.9 %collective-permute-start.25 = (bf16[512,128]{1,0:T(8,128)(2,1)S(1)}, bf16[512,128]{1,0:T(8,128)(2,1)S(1)}, u32[]{:S(2)}, u32[]{:S(2)}) collective-permute-start(bf16[512,128]{1,0:T(8,128)(2,1)S(1)} %bitcast.89), channel_id=1, source_target_pairs={{0,1},{1,0},{2,3},{3,2},{4,5},{5,4},{6,7},{7,6},{8,9},{9,8},{10,11... | collective-permute-start | bytes 393224 | tf_op jit(solution)/shard_map/mean_core_2/ppermute | solution.py:18
  166.3 6.8 %collective-permute-start.28 = (bf16[1024,128]{1,0:T(8,128)(2,1)S(1)}, bf16[1024,128]{1,0:T(8,128)(2,1)S(1)}, u32[]{:S(2)}, u32[]{:S(2)}) collective-permute-start(bf16[1024,128]{1,0:T(8,128)(2,1)S(1)} %fusion.6), channel_id=1, source_target_pairs={{0,2},{2,0},{1,3},{3,1},{4,6},{6,4},{5,7},{7,5},{8,10},{10,8},{9,1... | collective-permute-start | bytes 786440 | tf_op jit(solution)/shard_map/sum_x_3/ppermute | solution.py:18
  173.4 7.2 %collective-permute-start.29 = (bf16[512,128]{1,0:T(8,128)(2,1)S(1)}, bf16[512,128]{1,0:T(8,128)(2,1)S(1)}, u32[]{:S(2)}, u32[]{:S(2)}) collective-permute-start(bf16[512,128]{1,0:T(8,128)(2,1)S(1)} %bitcast.90), channel_id=1, source_target_pairs={{0,1},{1,0},{2,3},{3,2},{4,5},{5,4},{6,7},{7,6},{8,9},{9,8},{10,11... | collective-permute-start | bytes 393224 | tf_op jit(solution)/shard_map/mean_core_3/ppermute | solution.py:18
  (5 other events, 4.9 us)

commit v6 on v5

--- a/solution.py
+++ b/solution.py
@@ -124,7 +124,9 @@
 
 def message_kernel(first, core_ref, x_hbm, weight, bias, theirs, mine, x, held, row, sems):
     core = core_ref[0]
-    chunks, blocks, tile, w = mine.shape
+    tile, w = mine.shape[1:]
+    blocks = x.shape[0] // tile
+    chunks = mine.shape[0] // blocks
     half = weight.shape[1] // 2
     size = chunks * w
     starts = [
@@ -152,13 +154,13 @@
                 x[...], held[i, :, j * w : (j + 1) * w], preferred_element_type=jnp.float32
             )
             total = jnp.maximum(total + row[:, pl.ds(starts[i] + j * w, w)], 0.0)
-            out[j] = total.astype(out.dtype).reshape(blocks, tile, w)
+            out[j * blocks : (j + 1) * blocks] = total.astype(out.dtype).reshape(blocks, tile, w)
 
 
 def transform(core, features, weight, bias, first, chunks, tile, w):
     vmem = pl.BlockSpec(memory_space=pltpu.VMEM)
     any_spec = pl.BlockSpec(memory_space=pl.ANY)
-    out = jax.ShapeDtypeStruct((chunks, features.shape[0] // tile, tile, w), jnp.bfloat16)
+    out = jax.ShapeDtypeStruct((chunks * features.shape[0] // tile, tile, w), jnp.bfloat16)
     return pl.pallas_call(
         functools.partial(message_kernel, first),
         out_shape=(out, out),
@@ -172,7 +174,7 @@
         ],
         compiler_params=pltpu.CompilerParams(vmem_limit_bytes=60 * 1024 * 1024),
         cost_estimate=pl.CostEstimate(
-            flops=4 * features.size * chunks * w,
+            flops=32 * features.size * chunks * w,
             bytes_accessed=2 * features.size + 4 * features.shape[1] * chunks * w,
             transcendentals=0,
         ),
@@ -200,19 +202,22 @@
 
     make = functools.partial(transform, core)
     theirs, mine = make(features, neigh_weight, neigh_bias, 0, 1, tile, cw)
-    own = [jnp.concatenate([mine[0], swap(theirs[0], "core", "other_core_0")])]
+    mine0 = mine
+    own = [jnp.concatenate([mine, swap(theirs, "core", "other_core_0")])]
     first = swap(own[0], "x_lo", "gather_x_0")
     theirs, mine = make(
-        after(features, theirs), neigh_weight, neigh_bias, cw, CHUNKS - 1, tile, cw
-    )
-    theirs = swap(after(theirs, own[0]), "core", "other_core_rest")
-    own += [jnp.concatenate([mine[j], theirs[j]]) for j in range(CHUNKS - 1)]
+        after(features, own[0]), neigh_weight, neigh_bias, cw, CHUNKS - 1, tile, cw
+    )
+    theirs = swap(theirs, "core", "other_core_rest")
+    for j in range(CHUNKS - 1):
+        part = slice(j * blocks, (j + 1) * blocks)
+        own.append(jnp.concatenate([mine[part], theirs[part]]))
 
     live = live_tiles[0, 0]
     used = jnp.arange(slots, dtype=jnp.int32) < live
-    counts = after(walk_counts, own[0])[0, 0]
+    counts = after(walk_counts, mine0)[0, 0]
     c_own = jnp.where(used[:, None, None], counts, 0).astype(jnp.bfloat16)
-    pair0 = jnp.concatenate([own[0], after(first, c_own)])
+    pair0 = jnp.concatenate([own[0], first])
     rows_own = jnp.where(used, tile_rows[0, 0], 0)
     meta = jnp.stack(
         [rows_own, jnp.where(used, tile_cols[0, 0], 0), jnp.full((slots,), live, jnp.int32)]
@@ -253,7 +258,7 @@
     second = swap(after(own[1], first), "x_lo", "gather_x_1")
     rest = swap(after(jnp.stack(own[2:]), second), "x_lo", "gather_x_rest")
     f32, bf16 = jnp.float32, jnp.bfloat16
-    near_all, far_all, part_all, pass_all, zb_all, hidden_all = [], [], [], [], [], []
+    near_all, far_all, part_all, pass_all, hidden_all = [], [], [], [], []
     scale = None
 
     def far(pair, got, j):
@@ -264,7 +269,7 @@
     pair = after(jnp.concatenate([own[1], second]), near_all[0])
     far(pair, step(pair, "y", 0, "gather_near_1"), 1)
     pairs = jnp.stack([jnp.concatenate([own[j], rest[j - 2]]) for j in range(2, CHUNKS)])
-    pairs = after(pairs, near_all[1])
+    pairs = after(pairs, near_all[1], far_all[0])
     got = step(pairs, "y", 0, "gather_near_rest")
     for j in range(2, CHUNKS):
         far(pairs[j - 2], got[j - 2], j)
@@ -274,7 +279,7 @@
         if j == 1:
             earlier += tuple(near_all[2:])
         if j >= 2:
-            earlier += (pass_all[j - 2],)
+            earlier += (pass_all[0],)
         with jax.named_scope(f"tiles_{j}"):
             part_all.append(
                 tile_sums(
@@ -287,21 +292,20 @@
     for j in range(CHUNKS):
         send, pass_on, stay = part_all[j]
         size = stay.shape[0] // 2
-        if j >= 1:
-            send = after(send, pass_all[j - 1])
         got = step(send, "z", 0, f"sum_near_{j}")
         if j == 0:
             tiles(1)
-        if j + 1 < CHUNKS:
-            got = after(got, part_all[j + 1][0])
+            got = after(got, part_all[1][0])
+        else:
+            got = after(got, part_all[-1][0])
         passed = (got[: 2 * size].astype(f32) + pass_on).astype(bf16)
         pass_all.append(passed)
         stay = got[2 * size :].astype(f32) + stay
         got = step(passed, "z", 1, f"sum_far_{j}")
-        if j + 2 < CHUNKS:
-            tiles(j + 2)
-            got = after(got, part_all[j + 2][0])
-        zb_all.append(got)
+        if j == 0:
+            for i in range(2, CHUNKS):
+                tiles(i)
+            got = after(got, part_all[-1][0])
         passed = (got[:size].astype(f32) + stay[:size]).astype(bf16)
         stay = got[size:].astype(f32) + stay[size:]
         if j == CHUNKS - 1:

time: 185 us -> 172 us (0.930)
  waiting for transfers between devices: 77.5 us -> 57.5 us
  matrix products: 6.74 us -> 15.2 us
  other arithmetic: 13.1 us -> 20 us
  Pallas kernels: 25.6 us -> 19.9 us
  starting transfers between devices: 52.5 us -> 49.7 us
    ppermute x15, waiting for transfers between devices: 39.7 us -> 22.6 us  [swap(): return lax.ppermute(x, axis, [(0, 1), (1, 0)])]
    ppermute x15, starting transfers between devices: 36.7 us -> 25.2 us  [swap(): return lax.ppermute(x, axis, [(0, 1), (1, 0)])]
    ppermute x15, starting transfers between devices: 15.8 us -> 24.5 us  [step(): return lax.ppermute(x, (axis, 'core'), pairs)]
    pallas_call x4, Pallas kernels: 17.4 us -> 11.7 us  [tile_sums(): pl.pallas_call(tile_kernel, out_shape=(jax.ShapeDtypeStruct((4 * size, w)...]
    dot_general x4, matrix products: 2.29 us -> 6.23 us  [local(): hidden = hidden + jnp.dot(got, w_other[cols], preferred_element_type=f32)]
    dot_general x4, matrix products: 1.69 us -> 5.49 us  [local(): hidden = hidden + jnp.dot(mean[0], w_own[cols], preferred_element_type=f32)]
    ppermute x15, waiting for transfers between devices: 37.8 us -> 34.9 us  [step(): return lax.ppermute(x, (axis, 'core'), pairs)]
    slice x0 -> x2, local copies, waits for them, and re-layouts: none -> 2.76 us  [local(): own.append(jnp.concatenate([mine[part], theirs[part]]))]
  transfers between devices with their start and end apart: 30 -> 30, of which waited for: 18 -> 11; matrix products, arithmetic and copies ran while one was open for 10% -> 22% of each run, Pallas kernels for 12% -> 10%
where the time goes in v6:
time: 172 us; the launch traced here: 170 us
  waiting for transfers between devices  57.5 us (33%)
  starting transfers between devices  49.7 us (29%)
  other arithmetic  20 us (12%)
  Pallas kernels  19.9 us (12%)
  matrix products  15.2 us (9%)
  local copies, waits for them, and re-layouts  6.26 us (4%)
    ppermute x15, waiting for transfers between devices, step(): return lax.ppermute(x, (axis, 'core'), pairs)  34.9 us
    ppermute x15, starting transfers between devices, swap(): return lax.ppermute(x, axis, [(0, 1), (1, 0)])  25.2 us
    ppermute x15, starting transfers between devices, step(): return lax.ppermute(x, (axis, 'core'), pairs)  24.5 us
    ppermute x15, waiting for transfers between devices, swap(): return lax.ppermute(x, axis, [(0, 1), (1, 0)])  22.6 us
    pallas_call x4, Pallas kernels, tile_sums(): pl.pallas_call(tile_kernel, out_shape=(jax.ShapeDtypeStruct((4 * size, w)...  11.7 us
    pallas_call x2, Pallas kernels, transform(): pl.pallas_call(functools.partial(message_kernel, first), out_shape=(out,...  8.15 us
    dot_general x4, matrix products, local(): hidden = hidden + jnp.dot(got, w_other[cols], preferred_element_type=f32)  6.23 us
    dot_general x4, matrix products, local(): hidden = hidden + jnp.dot(mean[0], w_own[cols], preferred_element_type=f32)  5.49 us
  transfers between devices with their start and end apart: 30, of which 11 were waited for; matrix products, arithmetic and copies ran while one was open for 22% of the time, Pallas kernels for 10%

profile of v6, /device:TPU:3, one launch (start us, length us, event | category | flops | bytes accessed | tf_op | source)
XLA Modules:
  0.0 169.8 jit_solution(16695186110321093918)
XLA Ops:
  0.0 3.4 %shard_map.100 = (bf16[4,128,128]{2,1,0:T(8,128)(2,1)}, bf16[4,128,128]{2,1,0:T(8,128)(2,1)}) custom-call(s32[1]{0:T(128)} %bitcast.4.core_ref, bf16[512,1024]{1,0:T(8,128)(2,1)} %x_hbm.2, bf16[1024,1024]{1,0:T(8,128)(2,1)} %weight.3, f32[1,1024]{1,0:T(1,128)} %bitcast.77), custom_call_target="tpu_custom_call" | custom-call | flops 2147483648 | bytes 1572864 | tf_op jit(solution)/shard_map/pallas_call | solution.py:164
  4.9 3.6 %convert_reduce_fusion.1 = (f32[64,128]{1,0:T(8,128)S(1)}, bf16[64,128,128]{2,1,0:T(8,128)(2,1)S(1)}) fusion(s32[1,1,64,128,128]{4,3,2,1,0:T(8,128)} %param.11, pred[64]{0:T(512)(128)(4,1)S(1)} %iota_compare_fusion.2), kind=kLoop, calls=%fused_computation.3 | loop fusion | flops 4186112 | bytes 6324288 | tf_op jit(solution)/shard_map/reduce_sum | solution.py:244
  10.7 4.8 %shard_map.101 = (bf16[12,128,128]{2,1,0:T(8,128)(2,1)}, bf16[12,128,128]{2,1,0:T(8,128)(2,1)}) custom-call(s32[1]{0:T(128)} %bitcast.4.core_ref, bf16[512,1024]{1,0:T(8,128)(2,1)} %x_hbm.2, bf16[1024,1024]{1,0:T(8,128)(2,1)} %weight.3, f32[1,1024]{1,0:T(1,128)} %bitcast.78), custom_call_target="tpu_custom_call" | custom-call | flops 6442450944 | bytes 2621440 | tf_op jit(solution)/shard_map/pallas_call | solution.py:164
  15.8 1.7 %fusion.54 = (bf16[4,128,128]{2,1,0:T(8,128)(2,1)}, bf16[4,128,128]{2,1,0:T(8,128)(2,1)S(1)}, bf16[4,128,128]{2,1,0:T(8,128)(2,1)S(1)}) fusion(bf16[12,128,128]{2,1,0:T(8,128)(2,1)} %get-tuple-element.46), kind=kLoop, calls=%fused_computation.157 | loop fusion | bytes 786432 | tf_op jit(solution)/shard_map/slice | solution.py:214
  18.5 1.1 pad_maximum_fusion.3
  19.6 2.8 %collective-permute-start.5 = (bf16[16,128,128]{2,1,0:T(8,128)(2,1)S(1)}, bf16[16,128,128]{2,1,0:T(8,128)(2,1)S(1)}, u32[]{:S(2)}, u32[]{:S(2)}) collective-permute-start(bf16[16,128,128]{2,1,0:T(8,128)(2,1)S(1)} %pad_maximum_fusion.3), channel_id=1, source_target_pairs={{0,16},{1,49},{16,0},{17,33},{32,48},{33,17},{48,32},{49,1},{2,18}... | collective-permute-start | bytes 1572872 | tf_op jit(solution)/shard_map/gather_near_0/ppermute | solution.py:28
  23.4 1.1 fusion.55
  24.5 1.1 collective-permute-start.7
  25.7 7.1 %collective-permute-done.7 = bf16[8,128,128]{2,1,0:T(8,128)(2,1)S(1)} collective-permute-done((bf16[8,128,128]{2,1,0:T(8,128)(2,1)S(1)}, bf16[8,128,128]{2,1,0:T(8,128)(2,1)S(1)}, u32[]{:S(2)}, u32[]{:S(2)}) %collective-permute-start.7) | collective-permute-done | bytes 262176 | tf_op jit(solution)/shard_map/gather_x_1/ppermute | solution.py:18
  33.8 12.0 %collective-permute-done.8.refs_0_ = bf16[2,8,128,128]{3,2,1,0:T(8,128)(2,1)S(1)} collective-permute-done((bf16[2,8,128,128]{3,2,1,0:T(8,128)(2,1)S(1)}, bf16[2,8,128,128]{3,2,1,0:T(8,128)(2,1)S(1)}, u32[]{:S(2)}, u32[]{:S(2)}) %collective-permute-start.8) | collective-permute-done | bytes 524320 | tf_op jit(solution)/shard_map/gather_x_rest/ppermute | solution.py:18
  46.1 2.3 %collective-permute-done.9 = bf16[16,128,128]{2,1,0:T(8,128)(2,1)S(1)} collective-permute-done((bf16[16,128,128]{2,1,0:T(8,128)(2,1)S(1)}, bf16[16,128,128]{2,1,0:T(8,128)(2,1)S(1)}, u32[]{:S(2)}, u32[]{:S(2)}) %collective-permute-start.9) | collective-permute-done | bytes 524320 | tf_op jit(solution)/shard_map/gather_near_1/ppermute | solution.py:28
  49.1 3.8 %collective-permute-done.6.far = bf16[32,128,128]{2,1,0:T(8,128)(2,1)S(1)} collective-permute-done((bf16[32,128,128]{2,1,0:T(8,128)(2,1)S(1)}, bf16[32,128,128]{2,1,0:T(8,128)(2,1)S(1)}, u32[]{:S(2)}, u32[]{:S(2)}) %collective-permute-start.6) | collective-permute-done | bytes 1048608 | tf_op jit(solution)/shard_map/gather_far_0/ppermute | solution.py:28
  53.8 2.4 %tiles_0.1 = (bf16[4224,128]{1,0:T(8,128)(2,1)S(1)}, f32[2112,128]{1,0:T(8,128)S(1)}, f32[2112,128]{1,0:T(8,128)S(1)}) custom-call(s32[128]{0:T(128)S(1)} %fusion.38.src_ref, s32[128]{0:T(128)S(1)} %fusion.39.dst_ref, s32[2]{0:T(128)S(1)} %fusion.37.live_ref, bf16[64,128,128]{2,1,0:T(8,128)(2,1)S(1)} %get-tuple-element.45.c_own, ...), custom_call_target="tpu_custom_call" | custom-call | flops 2147483648 | bytes 1048576 | tf_op jit(solution)/shard_map/tiles_0/pallas_call | solution.py:104
  56.3 4.8 %collective-permute-start.10 = (bf16[4224,128]{1,0:T(8,128)(2,1)S(1)}, bf16[4224,128]{1,0:T(8,128)(2,1)S(1)}, u32[]{:S(2)}, u32[]{:S(2)}) collective-permute-start(bf16[4224,128]{1,0:T(8,128)(2,1)S(1)} %get-tuple-element.50), channel_id=1, source_target_pairs={{0,4},{1,13},{4,0},{5,9},{8,12},{9,5},{12,8},{13,1},{2,6},{3,15},{... | collective-permute-start | bytes 3244040 | tf_op jit(solution)/shard_map/sum_near_0/ppermute | solution.py:28
  61.2 15.7 %collective-permute-done.12 = bf16[2,16,128,128]{3,2,1,0:T(8,128)(2,1)S(1)} collective-permute-done((bf16[2,16,128,128]{3,2,1,0:T(8,128)(2,1)S(1)}, bf16[2,16,128,128]{3,2,1,0:T(8,128)(2,1)S(1)}, u32[]{:S(2)}, u32[]{:S(2)}) %collective-permute-start.12) | collective-permute-done | bytes 1048608 | tf_op jit(solution)/shard_map/gather_near_rest/ppermute | solution.py:28
  76.9 1.1 pad_maximum_fusion.2.refs_1_.near
  78.1 3.4 %tiles_1.1 = (bf16[4096,128]{1,0:T(8,128)(2,1)}, f32[2048,128]{1,0:T(8,128)S(1)}, f32[2048,128]{1,0:T(8,128)S(1)}) custom-call(s32[128]{0:T(128)S(1)} %fusion.38.src_ref, s32[128]{0:T(128)S(1)} %fusion.39.dst_ref, s32[2]{0:T(128)S(1)} %fusion.37.live_ref, bf16[64,128,128]{2,1,0:T(8,128)(2,1)S(1)} %get-tuple-element.45.c_own, ...), custom_call_target="tpu_custom_call" | custom-call | flops 2147483648 | bytes 1048576 | tf_op jit(solution)/shard_map/tiles_1/pallas_call | solution.py:104
  81.6 4.8 %collective-permute-start.17 = (bf16[4096,128]{1,0:T(8,128)(2,1)}, bf16[4096,128]{1,0:T(8,128)(2,1)}, u32[]{:S(2)}, u32[]{:S(2)}) collective-permute-start(bf16[4096,128]{1,0:T(8,128)(2,1)} %get-tuple-element.52), channel_id=1, source_target_pairs={{0,4},{1,13},{4,0},{5,9},{8,12},{9,5},{12,8},{13,1},{2,6},{3,15},{... | collective-permute-start | bytes 3145736 | tf_op jit(solution)/shard_map/sum_near_1/ppermute | solution.py:28
  86.3 1.4 convert_add_fusion
  87.8 3.3 %fusion.1 = f32[512,1024]{1,0:T(8,128)S(1)} fusion(bf16[512,1024]{1,0:T(8,128)(2,1)} %x_hbm.2, bf16[2048,1024]{1,0:T(8,128)(2,1)} %param.17), kind=kOutput, calls=%fused_computation.7 | convolution fusion | flops 1073741824 | bytes 5242880 | tf_op jit(solution)/shard_map/dot_general | solution.py:252
  91.1 1.3 collective-permute-start.21
  92.4 3.5 %tiles_3.1 = (bf16[4096,128]{1,0:T(8,128)(2,1)S(1)}, f32[2048,128]{1,0:T(8,128)S(1)}, f32[2048,128]{1,0:T(8,128)S(1)}) custom-call(s32[128]{0:T(128)S(1)} %fusion.38.src_ref, s32[128]{0:T(128)S(1)} %fusion.39.dst_ref, s32[2]{0:T(128)S(1)} %fusion.37.live_ref, bf16[64,128,128]{2,1,0:T(8,128)(2,1)S(1)} %get-tuple-element.45.c_own, ...), custom_call_target="tpu_custom_call" | custom-call | flops 1048576 | bytes 1048576 | tf_op jit(solution)/shard_map/tiles_3/pallas_call | solution.py:104
  95.9 4.7 %collective-permute-start.26 = (bf16[4096,128]{1,0:T(8,128)(2,1)S(1)}, bf16[4096,128]{1,0:T(8,128)(2,1)S(1)}, u32[]{:S(2)}, u32[]{:S(2)}) collective-permute-start(bf16[4096,128]{1,0:T(8,128)(2,1)S(1)} %get-tuple-element.55), channel_id=1, source_target_pairs={{0,4},{1,13},{4,0},{5,9},{8,12},{9,5},{12,8},{13,1},{2,6},{3,15},{... | collective-permute-start | bytes 3145736 | tf_op jit(solution)/shard_map/sum_near_3/ppermute | solution.py:28
  100.5 4.3 %collective-permute-done.17 = bf16[4096,128]{1,0:T(8,128)(2,1)} collective-permute-done((bf16[4096,128]{1,0:T(8,128)(2,1)}, bf16[4096,128]{1,0:T(8,128)(2,1)}, u32[]{:S(2)}, u32[]{:S(2)}) %collective-permute-start.17) | collective-permute-done | bytes 1048608 | tf_op jit(solution)/shard_map/sum_near_1/ppermute | solution.py:28
  105.9 2.5 %collective-permute-start.15 = (bf16[1056,128]{1,0:T(8,128)(2,1)S(1)}, bf16[1056,128]{1,0:T(8,128)(2,1)S(1)}, u32[]{:S(2)}, u32[]{:S(2)}) collective-permute-start(bf16[1056,128]{1,0:T(8,128)(2,1)S(1)} %fusion.4), channel_id=1, source_target_pairs={{0,2},{2,0},{1,3},{3,1},{4,6},{6,4},{5,7},{7,5},{8,10},{10,8},{9,1... | collective-permute-start | bytes 811016 | tf_op jit(solution)/shard_map/sum_x_0/ppermute | solution.py:18
  108.4 1.4 add_convert_fusion.3
  109.9 2.4 %tiles_2.1 = (bf16[4096,128]{1,0:T(8,128)(2,1)S(1)}, f32[2048,128]{1,0:T(8,128)S(1)}, f32[2048,128]{1,0:T(8,128)S(1)}) custom-call(s32[128]{0:T(128)S(1)} %fusion.38.src_ref, s32[128]{0:T(128)S(1)} %fusion.39.dst_ref, s32[2]{0:T(128)S(1)} %fusion.37.live_ref, bf16[64,128,128]{2,1,0:T(8,128)(2,1)S(1)} %get-tuple-element.45.c_own, ...), custom_call_target="tpu_custom_call" | custom-call | flops 1048576 | bytes 1048576 | tf_op jit(solution)/shard_map/tiles_2/pallas_call | solution.py:104
  112.4 3.5 %collective-permute-start.22 = (bf16[4096,128]{1,0:T(8,128)(2,1)S(1)}, bf16[4096,128]{1,0:T(8,128)(2,1)S(1)}, u32[]{:S(2)}, u32[]{:S(2)}) collective-permute-start(bf16[4096,128]{1,0:T(8,128)(2,1)S(1)} %get-tuple-element.63), channel_id=1, source_target_pairs={{0,4},{1,13},{4,0},{5,9},{8,12},{9,5},{12,8},{13,1},{2,6},{3,15},{... | collective-permute-start | bytes 3145736 | tf_op jit(solution)/shard_map/sum_near_2/ppermute | solution.py:28
  117.4 1.4 fusion.23
  118.8 1.8 %collective-permute-done.18 = bf16[2048,128]{1,0:T(8,128)(2,1)S(1)} collective-permute-done((bf16[2048,128]{1,0:T(8,128)(2,1)S(1)}, bf16[2048,128]{1,0:T(8,128)(2,1)S(1)}, u32[]{:S(2)}, u32[]{:S(2)}) %collective-permute-start.18) | collective-permute-done | bytes 524320 | tf_op jit(solution)/shard_map/sum_far_1/ppermute | solution.py:28
  120.7 3.7 %collective-permute-start.19 = (bf16[1024,128]{1,0:T(8,128)(2,1)S(1)}, bf16[1024,128]{1,0:T(8,128)(2,1)S(1)}, u32[]{:S(2)}, u32[]{:S(2)}) collective-permute-start(bf16[1024,128]{1,0:T(8,128)(2,1)S(1)} %fusion.10), channel_id=1, source_target_pairs={{0,2},{2,0},{1,3},{3,1},{4,6},{6,4},{5,7},{7,5},{8,10},{10,8},{9,1... | collective-permute-start | bytes 786440 | tf_op jit(solution)/shard_map/sum_x_1/ppermute | solution.py:18
  124.4 1.4 fusion.21
  125.8 3.3 %collective-permute-done.19 = bf16[1024,128]{1,0:T(8,128)(2,1)S(1)} collective-permute-done((bf16[1024,128]{1,0:T(8,128)(2,1)S(1)}, bf16[1024,128]{1,0:T(8,128)(2,1)S(1)}, u32[]{:S(2)}, u32[]{:S(2)}) %collective-permute-start.19) | collective-permute-done | bytes 262176 | tf_op jit(solution)/shard_map/sum_x_1/ppermute | solution.py:18
  129.3 3.7 %collective-permute-start.20 = (bf16[512,128]{1,0:T(8,128)(2,1)S(1)}, bf16[512,128]{1,0:T(8,128)(2,1)S(1)}, u32[]{:S(2)}, u32[]{:S(2)}) collective-permute-start(bf16[512,128]{1,0:T(8,128)(2,1)S(1)} %bitcast.70), channel_id=1, source_target_pairs={{0,1},{1,0},{2,3},{3,2},{4,5},{5,4},{6,7},{7,6},{8,9},{9,8},{10,11... | collective-permute-start | bytes 393224 | tf_op jit(solution)/shard_map/mean_core_1/ppermute | solution.py:18
  133.0 1.4 fusion.19
  137.2 1.7 add_add_fusion
  138.8 4.2 %collective-permute-done.27 = bf16[2048,128]{1,0:T(8,128)(2,1)S(1)} collective-permute-done((bf16[2048,128]{1,0:T(8,128)(2,1)S(1)}, bf16[2048,128]{1,0:T(8,128)(2,1)S(1)}, u32[]{:S(2)}, u32[]{:S(2)}) %collective-permute-start.27) | collective-permute-done | bytes 524320 | tf_op jit(solution)/shard_map/sum_far_3/ppermute | solution.py:28
  143.9 2.0 %collective-permute-start.28 = (bf16[1024,128]{1,0:T(8,128)(2,1)}, bf16[1024,128]{1,0:T(8,128)(2,1)S(1)}, u32[]{:S(2)}, u32[]{:S(2)}) collective-permute-start(bf16[1024,128]{1,0:T(8,128)(2,1)} %fusion.6), channel_id=1, source_target_pairs={{0,2},{2,0},{1,3},{3,1},{4,6},{6,4},{5,7},{7,5},{8,10},{10,8},{9,1... | collective-permute-start | bytes 786440 | tf_op jit(solution)/shard_map/sum_x_3/ppermute | solution.py:18
  145.9 2.9 %collective-permute-done.23 = bf16[2048,128]{1,0:T(8,128)(2,1)} collective-permute-done((bf16[2048,128]{1,0:T(8,128)(2,1)}, bf16[2048,128]{1,0:T(8,128)(2,1)}, u32[]{:S(2)}, u32[]{:S(2)}) %collective-permute-start.23) | collective-permute-done | bytes 524320 | tf_op jit(solution)/shard_map/sum_far_2/ppermute | solution.py:28
  149.7 2.1 %collective-permute-start.24 = (bf16[1024,128]{1,0:T(8,128)(2,1)S(1)}, bf16[1024,128]{1,0:T(8,128)(2,1)S(1)}, u32[]{:S(2)}, u32[]{:S(2)}) collective-permute-start(bf16[1024,128]{1,0:T(8,128)(2,1)S(1)} %fusion.8), channel_id=1, source_target_pairs={{0,2},{2,0},{1,3},{3,1},{4,6},{6,4},{5,7},{7,5},{8,10},{10,8},{9,1... | collective-permute-start | bytes 786440 | tf_op jit(solution)/shard_map/sum_x_2/ppermute | solution.py:18
  151.8 1.2 fusion.5
  153.2 4.2 %collective-permute-start.29 = (bf16[512,128]{1,0:T(8,128)(2,1)S(1)}, bf16[512,128]{1,0:T(8,128)(2,1)S(1)}, u32[]{:S(2)}, u32[]{:S(2)}) collective-permute-start(bf16[512,128]{1,0:T(8,128)(2,1)S(1)} %bitcast.71), channel_id=1, source_target_pairs={{0,1},{1,0},{2,3},{3,2},{4,5},{5,4},{6,7},{7,6},{8,9},{9,8},{10,11... | collective-permute-start | bytes 393224 | tf_op jit(solution)/shard_map/mean_core_3/ppermute | solution.py:18
  158.7 3.6 %collective-permute-start.25 = (bf16[512,128]{1,0:T(8,128)(2,1)S(1)}, bf16[512,128]{1,0:T(8,128)(2,1)S(1)}, u32[]{:S(2)}, u32[]{:S(2)}) collective-permute-start(bf16[512,128]{1,0:T(8,128)(2,1)S(1)} %bitcast.73), channel_id=1, source_target_pairs={{0,1},{1,0},{2,3},{3,2},{4,5},{5,4},{6,7},{7,6},{8,9},{9,8},{10,11... | collective-permute-start | bytes 393224 | tf_op jit(solution)/shard_map/mean_core_2/ppermute | solution.py:18
  162.3 1.4 fusion.12
  163.7 1.4 fusion.16
  165.0 1.4 fusion.14
  166.4 1.8 %multiply_reduce_fusion = (f32[512]{0:T(512)S(1)}, f32[512,1024]{1,0:T(8,128)S(1)}) fusion(bf16[512,128]{1,0:T(8,128)(2,1)S(1)} %collective-permute-done.29, bf16[2048,1024]{1,0:T(8,128)(2,1)} %param.17, s32[]{:T(128)S(6)} %add.292, f32[512,1024]{1,0:T(8,128)S(1)} %fusion.12, f32[512,1024]{1,0:T(8,128)S(1)} %fusion.14, f32[512,1024]{1,0:T(8,128)S(1)} %add_add_fusion, ...), kind=kOutput, calls=%fused_computation.4 | convolution fusion | flops 137887232 | bytes 10881028 | tf_op jit(solution)/shard_map/dot_general | solution.py:328
  168.2 1.6 broadcast_divide_fusion
  (127 shorter events, 17.6 us)
Async XLA Ops:
  3.4 6.1 %collective-permute-start = (bf16[4,128,128]{2,1,0:T(8,128)(2,1)}, bf16[4,128,128]{2,1,0:T(8,128)(2,1)S(1)}, u32[]{:S(2)}, u32[]{:S(2)}) collective-permute-start(bf16[4,128,128]{2,1,0:T(8,128)(2,1)} %get-tuple-element.40), channel_id=1, source_target_pairs={{0,1},{1,0},{2,3},{3,2},{4,5},{5,4},{6,7},{7,6},{8,9},{9,8},{10,11... | collective-permute-start | bytes 393224 | tf_op jit(solution)/shard_map/other_core_0/ppermute | solution.py:18
  4.8 3.6 %copy-start.13 = (s32[1,1,64]{2,1,0:T(1,128)S(1)}, s32[1,1,64]{2,1,0:T(1,128)}, u32[]{:S(2)}) copy-start(s32[1,1,64]{2,1,0:T(1,128)} %param.13) | copy-start | bytes 772
  4.8 3.6 %copy-start.14 = (s32[1,1,64]{2,1,0:T(1,128)S(1)}, s32[1,1,64]{2,1,0:T(1,128)}, u32[]{:S(2)}) copy-start(s32[1,1,64]{2,1,0:T(1,128)} %param.12) | copy-start | bytes 772
  4.9 4.0 %copy-start.10 = (bf16[4,128,128]{2,1,0:T(8,128)(2,1)S(1)}, bf16[4,128,128]{2,1,0:T(8,128)(2,1)}, u32[]{:S(2)}) copy-start(bf16[4,128,128]{2,1,0:T(8,128)(2,1)} %get-tuple-element.39) | copy-start | bytes 393220
  9.5 5.9 %copy-start.11 = (bf16[4,128,128]{2,1,0:T(8,128)(2,1)}, bf16[4,128,128]{2,1,0:T(8,128)(2,1)S(1)}, u32[]{:S(2)}) copy-start(bf16[4,128,128]{2,1,0:T(8,128)(2,1)S(1)} %collective-permute-done) | copy-start | bytes 393220
  10.2 8.2 %collective-permute-start.4 = (bf16[8,128,128]{2,1,0:T(8,128)(2,1)}, bf16[8,128,128]{2,1,0:T(8,128)(2,1)}, u32[]{:S(2)}, u32[]{:S(2)}) collective-permute-start(bf16[8,128,128]{2,1,0:T(8,128)(2,1)} %get-tuple-element.106), channel_id=1, source_target_pairs={{0,64},{64,0},{1,65},{65,1},{2,66},{66,2},{3,67},{67,3},{4,68},{68... | collective-permute-start | bytes 786440 | tf_op jit(solution)/shard_map/gather_x_0/ppermute | solution.py:18
  10.4 7.1 %collective-permute-start.1 = (s32[3,64]{1,0:T(4,128)S(1)}, s32[3,64]{1,0:T(4,128)S(1)}, u32[]{:S(2)}, u32[]{:S(2)}) collective-permute-start(s32[3,64]{1,0:T(4,128)S(1)} %get-tuple-element.41), channel_id=1, source_target_pairs={{0,1},{1,0},{2,3},{3,2},{4,5},{5,4},{6,7},{7,6},{8,9},{9,8},{10,11... | collective-permute-start | bytes 2312 | tf_op jit(solution)/shard_map/other_meta/ppermute | solution.py:18
  15.5 2.4 %collective-permute-start.2 = (bf16[12,128,128]{2,1,0:T(8,128)(2,1)}, bf16[12,128,128]{2,1,0:T(8,128)(2,1)}, u32[]{:S(2)}, u32[]{:S(2)}) collective-permute-start(bf16[12,128,128]{2,1,0:T(8,128)(2,1)} %get-tuple-element.44), channel_id=1, source_target_pairs={{0,1},{1,0},{2,3},{3,2},{4,5},{5,4},{6,7},{7,6},{8,9},{9,8},{10,11... | collective-permute-start | bytes 1179656 | tf_op jit(solution)/shard_map/other_core_rest/ppermute | solution.py:18
  17.7 6.8 %copy-start.8 = (bf16[4,128,128]{2,1,0:T(8,128)(2,1)S(1)}, bf16[4,128,128]{2,1,0:T(8,128)(2,1)}, u32[]{:S(2)}) copy-start(bf16[4,128,128]{2,1,0:T(8,128)(2,1)} %get-tuple-element.91) | copy-start | bytes 393220
  17.9 35.0 %collective-permute-start.3 = (bf16[64,128,128]{2,1,0:T(8,128)(2,1)S(1)}, bf16[64,128,128]{2,1,0:T(8,128)(2,1)S(1)}, u32[]{:S(2)}, u32[]{:S(2)}) collective-permute-start(bf16[64,128,128]{2,1,0:T(8,128)(2,1)S(1)} %get-tuple-element.45.c_own), channel_id=1, source_target_pairs={{0,1},{1,0},{2,3},{3,2},{4,5},{5,4},{6,7},{7,6},{8,9},{9,8},{10,11... | collective-permute-start | bytes 6291464 | tf_op jit(solution)/shard_map/other_tiles/ppermute | solution.py:18
  19.6 13.6 %collective-permute-start.5 = (bf16[16,128,128]{2,1,0:T(8,128)(2,1)S(1)}, bf16[16,128,128]{2,1,0:T(8,128)(2,1)S(1)}, u32[]{:S(2)}, u32[]{:S(2)}) collective-permute-start(bf16[16,128,128]{2,1,0:T(8,128)(2,1)S(1)} %pad_maximum_fusion.3), channel_id=1, source_target_pairs={{0,16},{1,49},{16,0},{17,33},{32,48},{33,17},{48,32},{49,1},{2,18}... | collective-permute-start | bytes 1572872 | tf_op jit(solution)/shard_map/gather_near_0/ppermute | solution.py:28
  24.5 8.3 %collective-permute-start.7 = (bf16[8,128,128]{2,1,0:T(8,128)(2,1)S(1)}, bf16[8,128,128]{2,1,0:T(8,128)(2,1)S(1)}, u32[]{:S(2)}, u32[]{:S(2)}) collective-permute-start(bf16[8,128,128]{2,1,0:T(8,128)(2,1)S(1)} %pad_maximum_fusion.6), channel_id=1, source_target_pairs={{0,64},{64,0},{1,65},{65,1},{2,66},{66,2},{3,67},{67,3},{4,68},{68... | collective-permute-start | bytes 786440 | tf_op jit(solution)/shard_map/gather_x_1/ppermute | solution.py:18
  32.8 13.0 %collective-permute-start.8 = (bf16[2,8,128,128]{3,2,1,0:T(8,128)(2,1)S(1)}, bf16[2,8,128,128]{3,2,1,0:T(8,128)(2,1)S(1)}, u32[]{:S(2)}, u32[]{:S(2)}) collective-permute-start(bf16[2,8,128,128]{3,2,1,0:T(8,128)(2,1)S(1)} %pad_maximum_fusion.4), channel_id=1, source_target_pairs={{0,64},{64,0},{1,65},{65,1},{2,66},{66,2},{3,67},{67,3},{4,68},{68... | collective-permute-start | bytes 1572872 | tf_op jit(solution)/shard_map/gather_x_rest/ppermute | solution.py:18
  33.3 19.6 %collective-permute-start.6 = (bf16[32,128,128]{2,1,0:T(8,128)(2,1)S(1)}, bf16[32,128,128]{2,1,0:T(8,128)(2,1)S(1)}, u32[]{:S(2)}, u32[]{:S(2)}) collective-permute-start(bf16[32,128,128]{2,1,0:T(8,128)(2,1)S(1)} %constant_dynamic-update-slice_fusion.2.near), channel_id=1, source_target_pairs={{0,48},{1,17},{16,32},{17,1},{32,16},{33,49},{48,0},{49,33},{2,50}... | collective-permute-start | bytes 3145736 | tf_op jit(solution)/shard_map/gather_far_0/ppermute | solution.py:28
  33.7 14.7 %collective-permute-start.9 = (bf16[16,128,128]{2,1,0:T(8,128)(2,1)S(1)}, bf16[16,128,128]{2,1,0:T(8,128)(2,1)S(1)}, u32[]{:S(2)}, u32[]{:S(2)}) collective-permute-start(bf16[16,128,128]{2,1,0:T(8,128)(2,1)S(1)} %pad_maximum_fusion.5), channel_id=1, source_target_pairs={{0,16},{1,49},{16,0},{17,33},{32,48},{33,17},{48,32},{49,1},{2,18}... | collective-permute-start | bytes 1572872 | tf_op jit(solution)/shard_map/gather_near_1/ppermute | solution.py:28
  48.5 29.7 %collective-permute-start.11 = (bf16[32,128,128]{2,1,0:T(8,128)(2,1)S(1)}, bf16[32,128,128]{2,1,0:T(8,128)(2,1)S(1)}, u32[]{:S(2)}, u32[]{:S(2)}) collective-permute-start(bf16[32,128,128]{2,1,0:T(8,128)(2,1)S(1)} %constant_dynamic-update-slice_fusion.6.refs_1_.near), channel_id=1, source_target_pairs={{0,48},{1,17},{16,32},{17,1},{32,16},{33,49},{48,0},{49,33},{2,50}... | collective-permute-start | bytes 3145736 | tf_op jit(solution)/shard_map/gather_far_1/ppermute | solution.py:28
  52.9 23.9 %collective-permute-start.12 = (bf16[2,16,128,128]{3,2,1,0:T(8,128)(2,1)S(1)}, bf16[2,16,128,128]{3,2,1,0:T(8,128)(2,1)S(1)}, u32[]{:S(2)}, u32[]{:S(2)}) collective-permute-start(bf16[2,16,128,128]{3,2,1,0:T(8,128)(2,1)S(1)} %pad_maximum_fusion), channel_id=1, source_target_pairs={{0,16},{1,49},{16,0},{17,33},{32,48},{33,17},{48,32},{49,1},{2,18}... | collective-permute-start | bytes 3145736 | tf_op jit(solution)/shard_map/gather_near_rest/ppermute | solution.py:28
  52.9 25.2 %copy-start = (bf16[64,128,128]{2,1,0:T(8,128)(2,1)}, bf16[64,128,128]{2,1,0:T(8,128)(2,1)S(1)}, u32[]{:S(2)}) copy-start(bf16[64,128,128]{2,1,0:T(8,128)(2,1)S(1)} %collective-permute-done.3.c_other) | copy-start | bytes 6291460
  56.3 30.1 %collective-permute-start.10 = (bf16[4224,128]{1,0:T(8,128)(2,1)S(1)}, bf16[4224,128]{1,0:T(8,128)(2,1)S(1)}, u32[]{:S(2)}, u32[]{:S(2)}) collective-permute-start(bf16[4224,128]{1,0:T(8,128)(2,1)S(1)} %get-tuple-element.50), channel_id=1, source_target_pairs={{0,4},{1,13},{4,0},{5,9},{8,12},{9,5},{12,8},{13,1},{2,6},{3,15},{... | collective-permute-start | bytes 3244040 | tf_op jit(solution)/shard_map/sum_near_0/ppermute | solution.py:28
  78.0 14.4 %collective-permute-start.14 = (bf16[32,128,128]{2,1,0:T(8,128)(2,1)}, bf16[32,128,128]{2,1,0:T(8,128)(2,1)}, u32[]{:S(2)}, u32[]{:S(2)}) collective-permute-start(bf16[32,128,128]{2,1,0:T(8,128)(2,1)} %pad_maximum_fusion.2.refs_1_.near), channel_id=1, source_target_pairs={{0,48},{1,17},{16,32},{17,1},{32,16},{33,49},{48,0},{49,33},{2,50}... | collective-permute-start | bytes 3145736 | tf_op jit(solution)/shard_map/gather_far_3/ppermute | solution.py:28
  81.5 6.2 %copy-start.2 = (f32[2048,128]{1,0:T(8,128)}, f32[2048,128]{1,0:T(8,128)S(1)}, u32[]{:S(2)}) copy-start(f32[2048,128]{1,0:T(8,128)S(1)} %get-tuple-element.60) | copy-start | bytes 3145732
  81.5 6.2 %copy-start.4 = (f32[2048,128]{1,0:T(8,128)}, f32[2048,128]{1,0:T(8,128)S(1)}, u32[]{:S(2)}) copy-start(f32[2048,128]{1,0:T(8,128)S(1)} %get-tuple-element.61) | copy-start | bytes 3145732
  81.6 23.3 %collective-permute-start.17 = (bf16[4096,128]{1,0:T(8,128)(2,1)}, bf16[4096,128]{1,0:T(8,128)(2,1)}, u32[]{:S(2)}, u32[]{:S(2)}) collective-permute-start(bf16[4096,128]{1,0:T(8,128)(2,1)} %get-tuple-element.52), channel_id=1, source_target_pairs={{0,4},{1,13},{4,0},{5,9},{8,12},{9,5},{12,8},{13,1},{2,6},{3,15},{... | collective-permute-start | bytes 3145736 | tf_op jit(solution)/shard_map/sum_near_1/ppermute | solution.py:28
  87.7 17.1 %collective-permute-start.13 = (bf16[2112,128]{1,0:T(8,128)(2,1)}, bf16[2112,128]{1,0:T(8,128)(2,1)}, u32[]{:S(2)}, u32[]{:S(2)}) collective-permute-start(bf16[2112,128]{1,0:T(8,128)(2,1)} %get-tuple-element.78.refs_0_), channel_id=1, source_target_pairs={{0,12},{1,5},{4,8},{5,1},{8,4},{9,13},{12,0},{13,9},{2,14},{3,7},{... | collective-permute-start | bytes 1622024 | tf_op jit(solution)/shard_map/sum_far_0/ppermute | solution.py:28
  87.8 4.6 %copy-start.1 = (bf16[64,128,128]{2,1,0:T(8,128)(2,1)S(1)}, bf16[64,128,128]{2,1,0:T(8,128)(2,1)}, u32[]{:S(2)}) copy-start(bf16[64,128,128]{2,1,0:T(8,128)(2,1)} %copy-done) | copy-start | bytes 6291460
  91.1 13.7 %copy-start.6 = (f32[2112,128]{1,0:T(8,128)S(1)}, f32[2112,128]{1,0:T(8,128)}, u32[]{:S(2)}) copy-start(f32[2112,128]{1,0:T(8,128)} %get-tuple-element.77) | copy-start | bytes 3244036
  91.1 17.3 %copy-start.3 = (f32[2048,128]{1,0:T(8,128)S(1)}, f32[2048,128]{1,0:T(8,128)}, u32[]{:S(2)}) copy-start(f32[2048,128]{1,0:T(8,128)} %copy-done.2) | copy-start | bytes 3145732
  91.1 17.3 %copy-start.5 = (f32[2048,128]{1,0:T(8,128)S(1)}, f32[2048,128]{1,0:T(8,128)}, u32[]{:S(2)}) copy-start(f32[2048,128]{1,0:T(8,128)} %copy-done.4) | copy-start | bytes 3145732
  91.1 18.8 %collective-permute-start.21 = (bf16[32,128,128]{2,1,0:T(8,128)(2,1)S(1)}, bf16[32,128,128]{2,1,0:T(8,128)(2,1)S(1)}, u32[]{:S(2)}, u32[]{:S(2)}) collective-permute-start(bf16[32,128,128]{2,1,0:T(8,128)(2,1)S(1)} %pad_maximum_fusion.1.refs_0_.near), channel_id=1, source_target_pairs={{0,48},{1,17},{16,32},{17,1},{32,16},{33,49},{48,0},{49,33},{2,50}... | collective-permute-start | bytes 3145736 | tf_op jit(solution)/shard_map/gather_far_2/ppermute | solution.py:28
  95.9 38.5 %collective-permute-start.26 = (bf16[4096,128]{1,0:T(8,128)(2,1)S(1)}, bf16[4096,128]{1,0:T(8,128)(2,1)S(1)}, u32[]{:S(2)}, u32[]{:S(2)}) collective-permute-start(bf16[4096,128]{1,0:T(8,128)(2,1)S(1)} %get-tuple-element.55), channel_id=1, source_target_pairs={{0,4},{1,13},{4,0},{5,9},{8,12},{9,5},{12,8},{13,1},{2,6},{3,15},{... | collective-permute-start | bytes 3145736 | tf_op jit(solution)/shard_map/sum_near_3/ppermute | solution.py:28
  105.9 10.0 %collective-permute-start.15 = (bf16[1056,128]{1,0:T(8,128)(2,1)S(1)}, bf16[1056,128]{1,0:T(8,128)(2,1)S(1)}, u32[]{:S(2)}, u32[]{:S(2)}) collective-permute-start(bf16[1056,128]{1,0:T(8,128)(2,1)S(1)} %fusion.4), channel_id=1, source_target_pairs={{0,2},{2,0},{1,3},{3,1},{4,6},{6,4},{5,7},{7,5},{8,10},{10,8},{9,1... | collective-permute-start | bytes 811016 | tf_op jit(solution)/shard_map/sum_x_0/ppermute | solution.py:18
  109.8 10.8 %collective-permute-start.18 = (bf16[2048,128]{1,0:T(8,128)(2,1)S(1)}, bf16[2048,128]{1,0:T(8,128)(2,1)S(1)}, u32[]{:S(2)}, u32[]{:S(2)}) collective-permute-start(bf16[2048,128]{1,0:T(8,128)(2,1)S(1)} %get-tuple-element.81), channel_id=1, source_target_pairs={{0,12},{1,5},{4,8},{5,1},{8,4},{9,13},{12,0},{13,9},{2,14},{3,7},{... | collective-permute-start | bytes 1572872 | tf_op jit(solution)/shard_map/sum_far_1/ppermute | solution.py:28
  112.3 4.6 %copy-start.15 = (f32[4]{0:T(128)S(1)}, f32[4]{0:T(128)}, u32[]{:S(2)}) copy-start(f32[4]{0:T(128)} %constant.147.clone) | copy-start | bytes 52
  112.4 22.9 %collective-permute-start.22 = (bf16[4096,128]{1,0:T(8,128)(2,1)S(1)}, bf16[4096,128]{1,0:T(8,128)(2,1)S(1)}, u32[]{:S(2)}, u32[]{:S(2)}) collective-permute-start(bf16[4096,128]{1,0:T(8,128)(2,1)S(1)} %get-tuple-element.63), channel_id=1, source_target_pairs={{0,4},{1,13},{4,0},{5,9},{8,12},{9,5},{12,8},{13,1},{2,6},{3,15},{... | collective-permute-start | bytes 3145736 | tf_op jit(solution)/shard_map/sum_near_2/ppermute | solution.py:28
  117.3 7.1 %collective-permute-start.16 = (bf16[512,128]{1,0:T(8,128)(2,1)S(1)}, bf16[512,128]{1,0:T(8,128)(2,1)S(1)}, u32[]{:S(2)}, u32[]{:S(2)}) collective-permute-start(bf16[512,128]{1,0:T(8,128)(2,1)S(1)} %bitcast.72), channel_id=1, source_target_pairs={{0,1},{1,0},{2,3},{3,2},{4,5},{5,4},{6,7},{7,6},{8,9},{9,8},{10,11... | collective-permute-start | bytes 393224 | tf_op jit(solution)/shard_map/mean_core_0/ppermute | solution.py:18
  120.7 8.4 %collective-permute-start.19 = (bf16[1024,128]{1,0:T(8,128)(2,1)S(1)}, bf16[1024,128]{1,0:T(8,128)(2,1)S(1)}, u32[]{:S(2)}, u32[]{:S(2)}) collective-permute-start(bf16[1024,128]{1,0:T(8,128)(2,1)S(1)} %fusion.10), channel_id=1, source_target_pairs={{0,2},{2,0},{1,3},{3,1},{4,6},{6,4},{5,7},{7,5},{8,10},{10,8},{9,1... | collective-permute-start | bytes 786440 | tf_op jit(solution)/shard_map/sum_x_1/ppermute | solution.py:18
  129.3 7.8 %collective-permute-start.20 = (bf16[512,128]{1,0:T(8,128)(2,1)S(1)}, bf16[512,128]{1,0:T(8,128)(2,1)S(1)}, u32[]{:S(2)}, u32[]{:S(2)}) collective-permute-start(bf16[512,128]{1,0:T(8,128)(2,1)S(1)} %bitcast.70), channel_id=1, source_target_pairs={{0,1},{1,0},{2,3},{3,2},{4,5},{5,4},{6,7},{7,6},{8,9},{9,8},{10,11... | collective-permute-start | bytes 393224 | tf_op jit(solution)/shard_map/mean_core_1/ppermute | solution.py:18
  134.6 8.4 %copy-start.7 = (f32[2048,128]{1,0:T(8,128)}, f32[2048,128]{1,0:T(8,128)S(1)}, u32[]{:S(2)}) copy-start(f32[2048,128]{1,0:T(8,128)S(1)} %get-tuple-element.84) | copy-start | bytes 3145732
  134.6 8.4 %collective-permute-start.27 = (bf16[2048,128]{1,0:T(8,128)(2,1)S(1)}, bf16[2048,128]{1,0:T(8,128)(2,1)S(1)}, u32[]{:S(2)}, u32[]{:S(2)}) collective-permute-start(bf16[2048,128]{1,0:T(8,128)(2,1)S(1)} %get-tuple-element.83), channel_id=1, source_target_pairs={{0,12},{1,5},{4,8},{5,1},{8,4},{9,13},{12,0},{13,9},{2,14},{3,7},{... | collective-permute-start | bytes 1572872 | tf_op jit(solution)/shard_map/sum_far_3/ppermute | solution.py:28
  135.2 1.9 %copy-start.12 = (f32[1024]{0:T(1024)S(1)}, f32[1024]{0:T(1024)}, u32[]{:S(2)}) copy-start(f32[1024]{0:T(1024)} %param.18) | copy-start | bytes 12292
  136.2 12.5 %collective-permute-start.23 = (bf16[2048,128]{1,0:T(8,128)(2,1)}, bf16[2048,128]{1,0:T(8,128)(2,1)}, u32[]{:S(2)}, u32[]{:S(2)}) collective-permute-start(bf16[2048,128]{1,0:T(8,128)(2,1)} %get-tuple-element.79), channel_id=1, source_target_pairs={{0,12},{1,5},{4,8},{5,1},{8,4},{9,13},{12,0},{13,9},{2,14},{3,7},{... | collective-permute-start | bytes 1572872 | tf_op jit(solution)/shard_map/sum_far_2/ppermute | solution.py:28
  143.0 0.9 copy-start.9
  143.9 7.9 %collective-permute-start.28 = (bf16[1024,128]{1,0:T(8,128)(2,1)}, bf16[1024,128]{1,0:T(8,128)(2,1)S(1)}, u32[]{:S(2)}, u32[]{:S(2)}) collective-permute-start(bf16[1024,128]{1,0:T(8,128)(2,1)} %fusion.6), channel_id=1, source_target_pairs={{0,2},{2,0},{1,3},{3,1},{4,6},{6,4},{5,7},{7,5},{8,10},{10,8},{9,1... | collective-permute-start | bytes 786440 | tf_op jit(solution)/shard_map/sum_x_3/ppermute | solution.py:18
  149.7 7.7 %collective-permute-start.24 = (bf16[1024,128]{1,0:T(8,128)(2,1)S(1)}, bf16[1024,128]{1,0:T(8,128)(2,1)S(1)}, u32[]{:S(2)}, u32[]{:S(2)}) collective-permute-start(bf16[1024,128]{1,0:T(8,128)(2,1)S(1)} %fusion.8), channel_id=1, source_target_pairs={{0,2},{2,0},{1,3},{3,1},{4,6},{6,4},{5,7},{7,5},{8,10},{10,8},{9,1... | collective-permute-start | bytes 786440 | tf_op jit(solution)/shard_map/sum_x_2/ppermute | solution.py:18
  153.2 13.2 %collective-permute-start.29 = (bf16[512,128]{1,0:T(8,128)(2,1)S(1)}, bf16[512,128]{1,0:T(8,128)(2,1)S(1)}, u32[]{:S(2)}, u32[]{:S(2)}) collective-permute-start(bf16[512,128]{1,0:T(8,128)(2,1)S(1)} %bitcast.71), channel_id=1, source_target_pairs={{0,1},{1,0},{2,3},{3,2},{4,5},{5,4},{6,7},{7,6},{8,9},{9,8},{10,11... | collective-permute-start | bytes 393224 | tf_op jit(solution)/shard_map/mean_core_3/ppermute | solution.py:18
  158.7 6.3 %collective-permute-start.25 = (bf16[512,128]{1,0:T(8,128)(2,1)S(1)}, bf16[512,128]{1,0:T(8,128)(2,1)S(1)}, u32[]{:S(2)}, u32[]{:S(2)}) collective-permute-start(bf16[512,128]{1,0:T(8,128)(2,1)S(1)} %bitcast.73), channel_id=1, source_target_pairs={{0,1},{1,0},{2,3},{3,2},{4,5},{5,4},{6,7},{7,6},{8,9},{9,8},{10,11... | collective-permute-start | bytes 393224 | tf_op jit(solution)/shard_map/mean_core_2/ppermute | solution.py:18

commit v7 on v6

--- a/solution.py
+++ b/solution.py
@@ -181,6 +181,35 @@
     )(core.astype(jnp.int32).reshape(1), features, weight, bias.reshape(1, -1))
 
 
+def finish_kernel(hidden, near, got, weight, out):
+    total = hidden[...]
+    w = near.shape[1]
+    total += jnp.dot(near[...], weight[:w], preferred_element_type=jnp.float32)
+    total += jnp.dot(got[...], weight[w:], preferred_element_type=jnp.float32)
+    total = jnp.maximum(total, 0.0)
+    mean = jnp.mean(total * total, axis=1, keepdims=True)
+    out[...] = total / jnp.sqrt(mean + 1e-06)
+
+
+def finish(hidden, near, got, weight):
+    rows, width = hidden.shape
+    block = 128
+    by_row = lambda w: pl.BlockSpec((block, w), lambda i: (i, 0))
+    return pl.pallas_call(
+        finish_kernel,
+        grid=(rows // block,),
+        out_shape=jax.ShapeDtypeStruct(hidden.shape, jnp.float32),
+        in_specs=[
+            by_row(width),
+            by_row(near.shape[1]),
+            by_row(near.shape[1]),
+            pl.BlockSpec(weight.shape, lambda i: (0, 0)),
+        ],
+        out_specs=by_row(width),
+        compiler_params=pltpu.CompilerParams(vmem_limit_bytes=32 * 1024 * 1024),
+    )(hidden, near, got, weight)
+
+
 def local(
     features,
     walk_counts,
@@ -202,11 +231,10 @@
 
     make = functools.partial(transform, core)
     theirs, mine = make(features, neigh_weight, neigh_bias, 0, 1, tile, cw)
-    mine0 = mine
     own = [jnp.concatenate([mine, swap(theirs, "core", "other_core_0")])]
     first = swap(own[0], "x_lo", "gather_x_0")
     theirs, mine = make(
-        after(features, own[0]), neigh_weight, neigh_bias, cw, CHUNKS - 1, tile, cw
+        after(features, theirs), neigh_weight, neigh_bias, cw, CHUNKS - 1, tile, cw
     )
     theirs = swap(theirs, "core", "other_core_rest")
     for j in range(CHUNKS - 1):
@@ -215,9 +243,9 @@
 
     live = live_tiles[0, 0]
     used = jnp.arange(slots, dtype=jnp.int32) < live
-    counts = after(walk_counts, mine0)[0, 0]
+    counts = after(walk_counts, own[0])[0, 0]
     c_own = jnp.where(used[:, None, None], counts, 0).astype(jnp.bfloat16)
-    pair0 = jnp.concatenate([own[0], first])
+    pair0 = jnp.concatenate([own[0], after(first, c_own)])
     rows_own = jnp.where(used, tile_rows[0, 0], 0)
     meta = jnp.stack(
         [rows_own, jnp.where(used, tile_cols[0, 0], 0), jnp.full((slots,), live, jnp.int32)]
@@ -256,7 +284,6 @@
     w_other = lax.dynamic_slice_in_dim(combine_weight, width + (1 - core) * half, half, 0)
 
     second = swap(after(own[1], first), "x_lo", "gather_x_1")
-    rest = swap(after(jnp.stack(own[2:]), second), "x_lo", "gather_x_rest")
     f32, bf16 = jnp.float32, jnp.bfloat16
     near_all, far_all, part_all, pass_all, hidden_all = [], [], [], [], []
     scale = None
@@ -266,18 +293,18 @@
         far_all.append(step(near_all[j], "y", 1, f"gather_far_{j}"))
 
     far(pair0, step(pair0, "y", 0, "gather_near_0"), 0)
-    pair = after(jnp.concatenate([own[1], second]), near_all[0])
-    far(pair, step(pair, "y", 0, "gather_near_1"), 1)
-    pairs = jnp.stack([jnp.concatenate([own[j], rest[j - 2]]) for j in range(2, CHUNKS)])
-    pairs = after(pairs, near_all[1], far_all[0])
-    got = step(pairs, "y", 0, "gather_near_rest")
-    for j in range(2, CHUNKS):
-        far(pairs[j - 2], got[j - 2], j)
+    second = after(second, near_all[0])
+    rest = swap(after(jnp.stack(own[2:]), second), "x_lo", "gather_x_rest")
+    partner = [first, second] + [rest[j] for j in range(CHUNKS - 2)]
+    for j in range(1, CHUNKS):
+        pair = jnp.concatenate([own[j], partner[j]])
+        pair = after(pair, near_all[j - 1], *far_all[: j - 1])
+        far(pair, step(pair, "y", 0, f"gather_near_{j}"), j)
 
     def tiles(j):
         earlier = (rest, near_all[1]) if j == 0 else ()
-        if j == 1:
-            earlier += tuple(near_all[2:])
+        if 0 < j < CHUNKS - 1:
+            earlier += (near_all[j + 1],)
         if j >= 2:
             earlier += (pass_all[0],)
         with jax.named_scope(f"tiles_{j}"):
@@ -324,11 +351,12 @@
         mean = mean.reshape(2, rows_dev, cw)
         got = swap(mean[1], "core", f"mean_core_{j}")
         cols = slice(j * cw, (j + 1) * cw)
+        if j == CHUNKS - 1:
+            weight = jnp.concatenate([w_own[cols], w_other[cols]])
+            return finish(hidden, mean[0], got, weight)
         hidden = hidden + jnp.dot(mean[0], w_own[cols], preferred_element_type=f32)
         hidden = hidden + jnp.dot(got, w_other[cols], preferred_element_type=f32)
         hidden_all.append(hidden)
-    hidden = jax.nn.relu(hidden)
-    return hidden / jnp.sqrt(jnp.mean(hidden * hidden, axis=1, keepdims=True) + 1e-06)
 
 
 def solution(mesh):

time: 172 us -> 177 us (1.029)
  waiting for transfers between devices: 57.5 us -> 42.7 us
  Pallas kernels: 19.9 us -> 32.7 us
  local copies, waits for them, and re-layouts: 6.26 us -> 17.1 us
  matrix products: 15.2 us -> 11.9 us
  other arithmetic: 20 us -> 18.1 us
    pallas_call x4, Pallas kernels: 11.7 us -> 21.7 us  [tile_sums(): pl.pallas_call(tile_kernel, out_shape=(jax.ShapeDtypeStruct((4 * size, w)...]
    ppermute x15 -> x16, waiting for transfers between devices: 34.9 us -> 25.2 us  [step(): return lax.ppermute(x, (axis, 'core'), pairs)]
    unnamed x36 -> x54, local copies, waits for them, and re-layouts: 2.54 us -> 8.48 us
    ppermute x15, waiting for transfers between devices: 22.6 us -> 17.5 us  [swap(): return lax.ppermute(x, axis, [(0, 1), (1, 0)])]
    concatenate x2 -> x4, local copies, waits for them, and re-layouts: 0.15 us -> 3.97 us  [far(): near_all.append(jnp.concatenate([pair, got]))]
    ppermute x15, starting transfers between devices: 25.2 us -> 29 us  [swap(): return lax.ppermute(x, axis, [(0, 1), (1, 0)])]
    ppermute x15 -> x16, starting transfers between devices: 24.5 us -> 21.5 us  [step(): return lax.ppermute(x, (axis, 'core'), pairs)]
    pallas_call x0 -> x1, Pallas kernels: none -> 2.83 us  [finish(): pl.pallas_call(finish_kernel, grid=(rows // block,), out_shape=jax.ShapeD...]
  transfers between devices with their start and end apart: 30 -> 31, of which waited for: 11 -> 13; matrix products, arithmetic and copies ran while one was open for 22% -> 25% of each run, Pallas kernels for 10% -> 15%
where the time goes in v7:
time: 177 us; the launch traced here: 174 us
  starting transfers between devices  50.4 us (28%)
  waiting for transfers between devices  42.7 us (24%)
  Pallas kernels  32.7 us (18%)
  other arithmetic  18.1 us (10%)
  local copies, waits for them, and re-layouts  17.1 us (10%)
  matrix products  11.9 us (7%)
    ppermute x15, starting transfers between devices, swap(): return lax.ppermute(x, axis, [(0, 1), (1, 0)])  29 us
    ppermute x16, waiting for transfers between devices, step(): return lax.ppermute(x, (axis, 'core'), pairs)  25.2 us
    pallas_call x4, Pallas kernels, tile_sums(): pl.pallas_call(tile_kernel, out_shape=(jax.ShapeDtypeStruct((4 * size, w)...  21.7 us
    ppermute x16, starting transfers between devices, step(): return lax.ppermute(x, (axis, 'core'), pairs)  21.5 us
    ppermute x15, waiting for transfers between devices, swap(): return lax.ppermute(x, axis, [(0, 1), (1, 0)])  17.5 us
    unnamed x54, local copies, waits for them, and re-layouts  8.48 us
    pallas_call x2, Pallas kernels, transform(): pl.pallas_call(functools.partial(message_kernel, first), out_shape=(out,...  8.14 us
    dot_general x3, matrix products, local(): hidden = hidden + jnp.dot(got, w_other[cols], preferred_element_type=f32)  4.5 us
  transfers between devices with their start and end apart: 31, of which 13 were waited for; matrix products, arithmetic and copies ran while one was open for 25% of the time, Pallas kernels for 15%

profile of v7, /device:TPU:3, one launch (start us, length us, event | category | flops | bytes accessed | tf_op | source)
XLA Modules:
  0.0 174.3 jit_solution(8277977875100599697)
XLA Ops:
  0.0 3.4 %shard_map.100 = (bf16[4,128,128]{2,1,0:T(8,128)(2,1)}, bf16[4,128,128]{2,1,0:T(8,128)(2,1)}) custom-call(s32[1]{0:T(128)} %bitcast.4.core_ref, bf16[512,1024]{1,0:T(8,128)(2,1)} %x_hbm.2, bf16[1024,1024]{1,0:T(8,128)(2,1)} %weight.3, f32[1,1024]{1,0:T(1,128)} %bitcast.63), custom_call_target="tpu_custom_call" | custom-call | flops 2147483648 | bytes 1572864 | tf_op jit(solution)/shard_map/pallas_call | solution.py:164
  4.2 4.7 %shard_map.101 = (bf16[12,128,128]{2,1,0:T(8,128)(2,1)}, bf16[12,128,128]{2,1,0:T(8,128)(2,1)}) custom-call(s32[1]{0:T(128)} %bitcast.4.core_ref, bf16[512,1024]{1,0:T(8,128)(2,1)} %x_hbm.2, bf16[1024,1024]{1,0:T(8,128)(2,1)} %weight.3, f32[1,1024]{1,0:T(1,128)} %bitcast.64), custom_call_target="tpu_custom_call" | custom-call | flops 6442450944 | bytes 2621440 | tf_op jit(solution)/shard_map/pallas_call | solution.py:164
  14.1 4.2 %convert_reduce_fusion.1 = (f32[64,128]{1,0:T(8,128)}, bf16[64,128,128]{2,1,0:T(8,128)(2,1)S(1)}) fusion(s32[1,1,64,128,128]{4,3,2,1,0:T(8,128)} %param.11, pred[64]{0:T(512)(128)(4,1)S(1)} %iota_compare_fusion.2), kind=kLoop, calls=%fused_computation.3 | loop fusion | flops 4186112 | bytes 6324288 | tf_op jit(solution)/shard_map/reduce_sum | solution.py:272
  19.0 1.8 %collective-permute-done.4 = bf16[8,128,128]{2,1,0:T(8,128)(2,1)S(1)} collective-permute-done((bf16[8,128,128]{2,1,0:T(8,128)(2,1)}, bf16[8,128,128]{2,1,0:T(8,128)(2,1)S(1)}, u32[]{:S(2)}, u32[]{:S(2)}) %collective-permute-start.4) | collective-permute-done | bytes 262176 | tf_op jit(solution)/shard_map/gather_x_0/ppermute | solution.py:18
  20.8 1.3 collective-permute-start.3
  22.2 2.8 %collective-permute-start.5 = (bf16[16,128,128]{2,1,0:T(8,128)(2,1)S(1)}, bf16[16,128,128]{2,1,0:T(8,128)(2,1)S(1)}, u32[]{:S(2)}, u32[]{:S(2)}) collective-permute-start(bf16[16,128,128]{2,1,0:T(8,128)(2,1)S(1)} %pad_maximum_fusion), channel_id=1, source_target_pairs={{0,16},{1,49},{16,0},{17,33},{32,48},{33,17},{48,32},{49,1},{2,18}... | collective-permute-start | bytes 1572872 | tf_op jit(solution)/shard_map/gather_near_0/ppermute | solution.py:28
  27.1 4.5 %collective-permute-done.5 = bf16[16,128,128]{2,1,0:T(8,128)(2,1)S(1)} collective-permute-done((bf16[16,128,128]{2,1,0:T(8,128)(2,1)S(1)}, bf16[16,128,128]{2,1,0:T(8,128)(2,1)S(1)}, u32[]{:S(2)}, u32[]{:S(2)}) %collective-permute-start.5) | collective-permute-done | bytes 524320 | tf_op jit(solution)/shard_map/gather_near_0/ppermute | solution.py:28
  33.6 2.1 %collective-permute-start.9 = (bf16[16,128,128]{2,1,0:T(8,128)(2,1)S(1)}, bf16[16,128,128]{2,1,0:T(8,128)(2,1)}, u32[]{:S(2)}, u32[]{:S(2)}) collective-permute-start(bf16[16,128,128]{2,1,0:T(8,128)(2,1)S(1)} %pad_maximum_fusion.2), channel_id=1, source_target_pairs={{0,16},{1,49},{16,0},{17,33},{32,48},{33,17},{48,32},{49,1},{2,18}... | collective-permute-start | bytes 1572872 | tf_op jit(solution)/shard_map/gather_near_1/ppermute | solution.py:28
  36.6 12.2 %collective-permute-done.9 = bf16[16,128,128]{2,1,0:T(8,128)(2,1)} collective-permute-done((bf16[16,128,128]{2,1,0:T(8,128)(2,1)S(1)}, bf16[16,128,128]{2,1,0:T(8,128)(2,1)}, u32[]{:S(2)}, u32[]{:S(2)}) %collective-permute-start.9) | collective-permute-done | bytes 524320 | tf_op jit(solution)/shard_map/gather_near_1/ppermute | solution.py:28
  48.8 1.1 constant_dynamic-update-slice_fusion.6.refs_1_.near
  50.4 2.0 %collective-permute-done.6.far = bf16[32,128,128]{2,1,0:T(8,128)(2,1)} collective-permute-done((bf16[32,128,128]{2,1,0:T(8,128)(2,1)}, bf16[32,128,128]{2,1,0:T(8,128)(2,1)}, u32[]{:S(2)}, u32[]{:S(2)}) %collective-permute-start.6) | collective-permute-done | bytes 1048608 | tf_op jit(solution)/shard_map/gather_far_0/ppermute | solution.py:28
  52.3 2.7 %collective-permute-start.12 = (bf16[16,128,128]{2,1,0:T(8,128)(2,1)S(1)}, bf16[16,128,128]{2,1,0:T(8,128)(2,1)S(1)}, u32[]{:S(2)}, u32[]{:S(2)}) collective-permute-start(bf16[16,128,128]{2,1,0:T(8,128)(2,1)S(1)} %pad_maximum_fusion.3), channel_id=1, source_target_pairs={{0,16},{1,49},{16,0},{17,33},{32,48},{33,17},{48,32},{49,1},{2,18}... | collective-permute-start | bytes 1572872 | tf_op jit(solution)/shard_map/gather_near_2/ppermute | solution.py:28
  55.0 2.2 %convert_reduce_fusion = f32[64,128]{1,0:T(8,128)S(1)} fusion(bf16[64,128,128]{2,1,0:T(8,128)(2,1)} %collective-permute-done.3.c_other), kind=kLoop, calls=%fused_computation.2 | loop fusion | flops 2088960 | bytes 2129920 | tf_op jit(solution)/shard_map/reduce_sum | solution.py:272
  57.6 6.3 %tiles_0.1 = (bf16[4224,128]{1,0:T(8,128)(2,1)}, f32[2112,128]{1,0:T(8,128)S(1)}, f32[2112,128]{1,0:T(8,128)S(1)}) custom-call(s32[128]{0:T(128)S(1)} %fusion.32.src_ref, s32[128]{0:T(128)S(1)} %fusion.33.dst_ref, s32[2]{0:T(128)S(1)} %fusion.31.live_ref, bf16[64,128,128]{2,1,0:T(8,128)(2,1)S(1)} %get-tuple-element.48.c_own, ...), custom_call_target="tpu_custom_call" | custom-call | flops 2147483648 | bytes 1048576 | tf_op jit(solution)/shard_map/tiles_0/pallas_call | solution.py:104
  65.8 4.2 %collective-permute-start.10 = (bf16[4224,128]{1,0:T(8,128)(2,1)}, bf16[4224,128]{1,0:T(8,128)(2,1)}, u32[]{:S(2)}, u32[]{:S(2)}) collective-permute-start(bf16[4224,128]{1,0:T(8,128)(2,1)} %get-tuple-element.55), channel_id=1, source_target_pairs={{0,4},{1,13},{4,0},{5,9},{8,12},{9,5},{12,8},{13,1},{2,6},{3,15},{... | collective-permute-start | bytes 3244040 | tf_op jit(solution)/shard_map/sum_near_0/ppermute | solution.py:28
  73.6 1.2 copy-done.11
  74.9 5.2 %tiles_1.1 = (bf16[4096,128]{1,0:T(8,128)(2,1)}, f32[2048,128]{1,0:T(8,128)S(1)}, f32[2048,128]{1,0:T(8,128)S(1)}) custom-call(s32[128]{0:T(128)S(1)} %fusion.32.src_ref, s32[128]{0:T(128)S(1)} %fusion.33.dst_ref, s32[2]{0:T(128)S(1)} %fusion.31.live_ref, bf16[64,128,128]{2,1,0:T(8,128)(2,1)S(1)} %get-tuple-element.48.c_own, ...), custom_call_target="tpu_custom_call" | custom-call | flops 2147483648 | bytes 1048576 | tf_op jit(solution)/shard_map/tiles_1/pallas_call | solution.py:104
  80.1 3.5 %collective-permute-start.18 = (bf16[4096,128]{1,0:T(8,128)(2,1)}, bf16[4096,128]{1,0:T(8,128)(2,1)}, u32[]{:S(2)}, u32[]{:S(2)}) collective-permute-start(bf16[4096,128]{1,0:T(8,128)(2,1)} %get-tuple-element.57), channel_id=1, source_target_pairs={{0,4},{1,13},{4,0},{5,9},{8,12},{9,5},{12,8},{13,1},{2,6},{3,15},{... | collective-permute-start | bytes 3145736 | tf_op jit(solution)/shard_map/sum_near_1/ppermute | solution.py:28
  84.7 3.0 %collective-permute-done.14 = bf16[16,128,128]{2,1,0:T(8,128)(2,1)} collective-permute-done((bf16[16,128,128]{2,1,0:T(8,128)(2,1)}, bf16[16,128,128]{2,1,0:T(8,128)(2,1)}, u32[]{:S(2)}, u32[]{:S(2)}) %collective-permute-start.14) | collective-permute-done | bytes 524320 | tf_op jit(solution)/shard_map/gather_near_3/ppermute | solution.py:28
  87.7 1.1 constant_dynamic-update-slice_fusion.10.near.refs_0_
  89.2 2.6 %convert_add_fusion = (f32[2112,128]{1,0:T(8,128)}, bf16[2112,128]{1,0:T(8,128)(2,1)}) fusion(f32[2112,128]{1,0:T(8,128)S(1)} %copy-done.3, bf16[4224,128]{1,0:T(8,128)(2,1)} %collective-permute-done.10, f32[2112,128]{1,0:T(8,128)S(1)} %copy-done.1), kind=kLoop, calls=%fused_computation.9 | loop fusion | flops 1351680 | bytes 4866048 | tf_op jit(solution)/shard_map/add | solution.py:330
  91.8 1.8 %constant_dynamic-slice_fusion.1 = (bf16[128,1024]{1,0:T(8,128)(2,1)S(1)}, bf16[128,1024]{1,0:T(8,128)(2,1)}) fusion(bf16[2048,1024]{1,0:T(8,128)(2,1)} %param.17, s32[]{:T(128)S(6)} %add.270, s32[]{:T(128)S(6)} %add.271), kind=kLoop, calls=%fused_computation.93 | loop fusion | bytes 1048584 | tf_op jit(solution)/shard_map/slice | solution.py:355
  94.5 3.2 %fusion.1 = f32[512,1024]{1,0:T(8,128)S(1)} fusion(bf16[512,1024]{1,0:T(8,128)(2,1)} %x_hbm.2, bf16[2048,1024]{1,0:T(8,128)(2,1)} %param.17), kind=kOutput, calls=%fused_computation.6 | convolution fusion | flops 1073741824 | bytes 5242880 | tf_op jit(solution)/shard_map/dot_general | solution.py:280
  97.7 5.2 %tiles_2.1 = (bf16[4096,128]{1,0:T(8,128)(2,1)S(1)}, f32[2048,128]{1,0:T(8,128)S(1)}, f32[2048,128]{1,0:T(8,128)S(1)}) custom-call(s32[128]{0:T(128)S(1)} %fusion.32.src_ref, s32[128]{0:T(128)S(1)} %fusion.33.dst_ref, s32[2]{0:T(128)S(1)} %fusion.31.live_ref, bf16[64,128,128]{2,1,0:T(8,128)(2,1)S(1)} %get-tuple-element.48.c_own, ...), custom_call_target="tpu_custom_call" | custom-call | flops 1048576 | bytes 1048576 | tf_op jit(solution)/shard_map/tiles_2/pallas_call | solution.py:104
  103.2 1.5 collective-permute-done.15.far
  104.7 5.0 %tiles_3.1 = (bf16[4096,128]{1,0:T(8,128)(2,1)S(1)}, f32[2048,128]{1,0:T(8,128)S(1)}, f32[2048,128]{1,0:T(8,128)S(1)}) custom-call(s32[128]{0:T(128)S(1)} %fusion.32.src_ref, s32[128]{0:T(128)S(1)} %fusion.33.dst_ref, s32[2]{0:T(128)S(1)} %fusion.31.live_ref, bf16[64,128,128]{2,1,0:T(8,128)(2,1)S(1)} %get-tuple-element.48.c_own, ...), custom_call_target="tpu_custom_call" | custom-call | flops 1048576 | bytes 1048576 | tf_op jit(solution)/shard_map/tiles_3/pallas_call | solution.py:104
  109.7 3.5 %collective-permute-start.27 = (bf16[4096,128]{1,0:T(8,128)(2,1)S(1)}, bf16[4096,128]{1,0:T(8,128)(2,1)S(1)}, u32[]{:S(2)}, u32[]{:S(2)}) collective-permute-start(bf16[4096,128]{1,0:T(8,128)(2,1)S(1)} %get-tuple-element.61), channel_id=1, source_target_pairs={{0,4},{1,13},{4,0},{5,9},{8,12},{9,5},{12,8},{13,1},{2,6},{3,15},{... | collective-permute-start | bytes 3145736 | tf_op jit(solution)/shard_map/sum_near_3/ppermute | solution.py:28
  114.3 2.0 %collective-permute-start.16 = (bf16[1056,128]{1,0:T(8,128)(2,1)S(1)}, bf16[1056,128]{1,0:T(8,128)(2,1)S(1)}, u32[]{:S(2)}, u32[]{:S(2)}) collective-permute-start(bf16[1056,128]{1,0:T(8,128)(2,1)S(1)} %fusion.4), channel_id=1, source_target_pairs={{0,2},{2,0},{1,3},{3,1},{4,6},{6,4},{5,7},{7,5},{8,10},{10,8},{9,1... | collective-permute-start | bytes 811016 | tf_op jit(solution)/shard_map/sum_x_0/ppermute | solution.py:18
  116.3 1.4 add_convert_fusion.3
  117.9 3.3 %collective-permute-done.16 = bf16[1056,128]{1,0:T(8,128)(2,1)S(1)} collective-permute-done((bf16[1056,128]{1,0:T(8,128)(2,1)S(1)}, bf16[1056,128]{1,0:T(8,128)(2,1)S(1)}, u32[]{:S(2)}, u32[]{:S(2)}) %collective-permute-start.16) | collective-permute-done | bytes 270368 | tf_op jit(solution)/shard_map/sum_x_0/ppermute | solution.py:18
  122.6 5.4 %collective-permute-start.17 = (bf16[512,128]{1,0:T(8,128)(2,1)S(1)}, bf16[512,128]{1,0:T(8,128)(2,1)S(1)}, u32[]{:S(2)}, u32[]{:S(2)}) collective-permute-start(bf16[512,128]{1,0:T(8,128)(2,1)S(1)} %bitcast.58), channel_id=1, source_target_pairs={{0,1},{1,0},{2,3},{3,2},{4,5},{5,4},{6,7},{7,6},{8,9},{9,8},{10,11... | collective-permute-start | bytes 393224 | tf_op jit(solution)/shard_map/mean_core_0/ppermute | solution.py:18
  128.0 1.4 fusion.19
  129.4 1.4 fusion.17
  131.9 1.9 %collective-permute-start.20 = (bf16[1024,128]{1,0:T(8,128)(2,1)S(1)}, bf16[1024,128]{1,0:T(8,128)(2,1)S(1)}, u32[]{:S(2)}, u32[]{:S(2)}) collective-permute-start(bf16[1024,128]{1,0:T(8,128)(2,1)S(1)} %fusion.10), channel_id=1, source_target_pairs={{0,2},{2,0},{1,3},{3,1},{4,6},{6,4},{5,7},{7,5},{8,10},{10,8},{9,1... | collective-permute-start | bytes 786440 | tf_op jit(solution)/shard_map/sum_x_1/ppermute | solution.py:18
  134.0 1.4 collective-permute-start.24
  135.4 3.3 %collective-permute-done.20 = bf16[1024,128]{1,0:T(8,128)(2,1)S(1)} collective-permute-done((bf16[1024,128]{1,0:T(8,128)(2,1)S(1)}, bf16[1024,128]{1,0:T(8,128)(2,1)S(1)}, u32[]{:S(2)}, u32[]{:S(2)}) %collective-permute-start.20) | collective-permute-done | bytes 262176 | tf_op jit(solution)/shard_map/sum_x_1/ppermute | solution.py:18
  139.1 4.8 %collective-permute-start.21 = (bf16[512,128]{1,0:T(8,128)(2,1)S(1)}, bf16[512,128]{1,0:T(8,128)(2,1)S(1)}, u32[]{:S(2)}, u32[]{:S(2)}) collective-permute-start(bf16[512,128]{1,0:T(8,128)(2,1)S(1)} %bitcast.59), channel_id=1, source_target_pairs={{0,1},{1,0},{2,3},{3,2},{4,5},{5,4},{6,7},{7,6},{8,9},{9,8},{10,11... | collective-permute-start | bytes 393224 | tf_op jit(solution)/shard_map/mean_core_1/ppermute | solution.py:18
  143.9 1.4 fusion.15
  145.3 1.7 add_add_fusion.1
  147.1 3.3 %collective-permute-start.25 = (bf16[1024,128]{1,0:T(8,128)(2,1)S(1)}, bf16[1024,128]{1,0:T(8,128)(2,1)S(1)}, u32[]{:S(2)}, u32[]{:S(2)}) collective-permute-start(bf16[1024,128]{1,0:T(8,128)(2,1)S(1)} %fusion.8), channel_id=1, source_target_pairs={{0,2},{2,0},{1,3},{3,1},{4,6},{6,4},{5,7},{7,5},{8,10},{10,8},{9,1... | collective-permute-start | bytes 786440 | tf_op jit(solution)/shard_map/sum_x_2/ppermute | solution.py:18
  150.7 5.2 %collective-permute-done.25 = bf16[1024,128]{1,0:T(8,128)(2,1)S(1)} collective-permute-done((bf16[1024,128]{1,0:T(8,128)(2,1)S(1)}, bf16[1024,128]{1,0:T(8,128)(2,1)S(1)}, u32[]{:S(2)}, u32[]{:S(2)}) %collective-permute-start.25) | collective-permute-done | bytes 262176 | tf_op jit(solution)/shard_map/sum_x_2/ppermute | solution.py:18
  156.2 2.0 %collective-permute-start.26 = (bf16[512,128]{1,0:T(8,128)(2,1)S(1)}, bf16[512,128]{1,0:T(8,128)(2,1)S(1)}, u32[]{:S(2)}, u32[]{:S(2)}) collective-permute-start(bf16[512,128]{1,0:T(8,128)(2,1)S(1)} %bitcast.56), channel_id=1, source_target_pairs={{0,1},{1,0},{2,3},{3,2},{4,5},{5,4},{6,7},{7,6},{8,9},{9,8},{10,11... | collective-permute-start | bytes 393224 | tf_op jit(solution)/shard_map/mean_core_2/ppermute | solution.py:18
  159.1 2.1 %collective-permute-start.29 = (bf16[1024,128]{1,0:T(8,128)(2,1)S(1)}, bf16[1024,128]{1,0:T(8,128)(2,1)S(1)}, u32[]{:S(2)}, u32[]{:S(2)}) collective-permute-start(bf16[1024,128]{1,0:T(8,128)(2,1)S(1)} %fusion.6), channel_id=1, source_target_pairs={{0,2},{2,0},{1,3},{3,1},{4,6},{6,4},{5,7},{7,5},{8,10},{10,8},{9,1... | collective-permute-start | bytes 786440 | tf_op jit(solution)/shard_map/sum_x_3/ppermute | solution.py:18
  161.2 1.4 fusion.12
  162.6 3.4 %collective-permute-done.29 = bf16[1024,128]{1,0:T(8,128)(2,1)S(1)} collective-permute-done((bf16[1024,128]{1,0:T(8,128)(2,1)S(1)}, bf16[1024,128]{1,0:T(8,128)(2,1)S(1)}, u32[]{:S(2)}, u32[]{:S(2)}) %collective-permute-start.29) | collective-permute-done | bytes 262176 | tf_op jit(solution)/shard_map/sum_x_3/ppermute | solution.py:18
  166.2 3.8 %collective-permute-start.30 = (bf16[512,128]{1,0:T(8,128)(2,1)S(1)}, bf16[512,128]{1,0:T(8,128)(2,1)S(1)}, u32[]{:S(2)}, u32[]{:S(2)}) collective-permute-start(bf16[512,128]{1,0:T(8,128)(2,1)S(1)} %bitcast.57), channel_id=1, source_target_pairs={{0,1},{1,0},{2,3},{3,2},{4,5},{5,4},{6,7},{7,6},{8,9},{9,8},{10,11... | collective-permute-start | bytes 393224 | tf_op jit(solution)/shard_map/mean_core_3/ppermute | solution.py:18
  170.0 1.4 add_add_fusion.hidden
  171.4 2.8 %shard_map.102 = f32[512,1024]{1,0:T(8,128)} custom-call(f32[512,1024]{1,0:T(8,128)S(1)} %add_add_fusion.hidden, bf16[512,128]{1,0:T(8,128)(2,1)S(1)} %bitcast.47, bf16[512,128]{1,0:T(8,128)(2,1)S(1)} %collective-permute-done.30.got, bf16[256,1024]{1,0:T(8,128)(2,1)S(1)} %pad_maximum_fusion.5.weight), custom_call_target="tpu_custom_call" | custom-call | tf_op jit(solution)/shard_map/pallas_call | solution.py:198
  (143 shorter events, 25.7 us)
Async XLA Ops:
  3.4 7.4 %copy-start.20 = (s32[1,1,64]{2,1,0:T(1,128)S(1)}, s32[1,1,64]{2,1,0:T(1,128)}, u32[]{:S(2)}) copy-start(s32[1,1,64]{2,1,0:T(1,128)} %param.13) | copy-start | bytes 772
  3.4 7.4 %copy-start.21 = (s32[1,1,64]{2,1,0:T(1,128)S(1)}, s32[1,1,64]{2,1,0:T(1,128)}, u32[]{:S(2)}) copy-start(s32[1,1,64]{2,1,0:T(1,128)} %param.12) | copy-start | bytes 772
  3.4 8.3 %copy-start.17 = (bf16[4,128,128]{2,1,0:T(8,128)(2,1)S(1)}, bf16[4,128,128]{2,1,0:T(8,128)(2,1)}, u32[]{:S(2)}) copy-start(bf16[4,128,128]{2,1,0:T(8,128)(2,1)} %get-tuple-element.42) | copy-start | bytes 393220
  3.4 9.0 %collective-permute-start = (bf16[4,128,128]{2,1,0:T(8,128)(2,1)}, bf16[4,128,128]{2,1,0:T(8,128)(2,1)S(1)}, u32[]{:S(2)}, u32[]{:S(2)}) collective-permute-start(bf16[4,128,128]{2,1,0:T(8,128)(2,1)} %get-tuple-element.43), channel_id=1, source_target_pairs={{0,1},{1,0},{2,3},{3,2},{4,5},{5,4},{6,7},{7,6},{8,9},{9,8},{10,11... | collective-permute-start | bytes 393224 | tf_op jit(solution)/shard_map/other_core_0/ppermute | solution.py:18
  8.9 11.9 %collective-permute-start.2 = (bf16[12,128,128]{2,1,0:T(8,128)(2,1)}, bf16[12,128,128]{2,1,0:T(8,128)(2,1)S(1)}, u32[]{:S(2)}, u32[]{:S(2)}) collective-permute-start(bf16[12,128,128]{2,1,0:T(8,128)(2,1)} %get-tuple-element.47), channel_id=1, source_target_pairs={{0,1},{1,0},{2,3},{3,2},{4,5},{5,4},{6,7},{7,6},{8,9},{9,8},{10,11... | collective-permute-start | bytes 1179656 | tf_op jit(solution)/shard_map/other_core_rest/ppermute | solution.py:18
  13.2 7.6 %collective-permute-start.4 = (bf16[8,128,128]{2,1,0:T(8,128)(2,1)}, bf16[8,128,128]{2,1,0:T(8,128)(2,1)S(1)}, u32[]{:S(2)}, u32[]{:S(2)}) collective-permute-start(bf16[8,128,128]{2,1,0:T(8,128)(2,1)} %get-tuple-element.110), channel_id=1, source_target_pairs={{0,64},{64,0},{1,65},{65,1},{2,66},{66,2},{3,67},{67,3},{4,68},{68... | collective-permute-start | bytes 786440 | tf_op jit(solution)/shard_map/gather_x_0/ppermute | solution.py:18
  13.4 4.9 %collective-permute-start.1 = (s32[3,64]{1,0:T(4,128)S(1)}, s32[3,64]{1,0:T(4,128)S(1)}, u32[]{:S(2)}, u32[]{:S(2)}) collective-permute-start(s32[3,64]{1,0:T(4,128)S(1)} %get-tuple-element.44), channel_id=1, source_target_pairs={{0,1},{1,0},{2,3},{3,2},{4,5},{5,4},{6,7},{7,6},{8,9},{9,8},{10,11... | collective-permute-start | bytes 2312 | tf_op jit(solution)/shard_map/other_meta/ppermute | solution.py:18
  20.8 34.2 %collective-permute-start.3 = (bf16[64,128,128]{2,1,0:T(8,128)(2,1)S(1)}, bf16[64,128,128]{2,1,0:T(8,128)(2,1)}, u32[]{:S(2)}, u32[]{:S(2)}) collective-permute-start(bf16[64,128,128]{2,1,0:T(8,128)(2,1)S(1)} %get-tuple-element.48.c_own), channel_id=1, source_target_pairs={{0,1},{1,0},{2,3},{3,2},{4,5},{5,4},{6,7},{7,6},{8,9},{9,8},{10,11... | collective-permute-start | bytes 6291464 | tf_op jit(solution)/shard_map/other_tiles/ppermute | solution.py:18
  22.2 9.4 %collective-permute-start.5 = (bf16[16,128,128]{2,1,0:T(8,128)(2,1)S(1)}, bf16[16,128,128]{2,1,0:T(8,128)(2,1)S(1)}, u32[]{:S(2)}, u32[]{:S(2)}) collective-permute-start(bf16[16,128,128]{2,1,0:T(8,128)(2,1)S(1)} %pad_maximum_fusion), channel_id=1, source_target_pairs={{0,16},{1,49},{16,0},{17,33},{32,48},{33,17},{48,32},{49,1},{2,18}... | collective-permute-start | bytes 1572872 | tf_op jit(solution)/shard_map/gather_near_0/ppermute | solution.py:28
  25.8 7.0 %copy-start.13 = (bf16[4,128,128]{2,1,0:T(8,128)(2,1)}, bf16[4,128,128]{2,1,0:T(8,128)(2,1)S(1)}, u32[]{:S(2)}) copy-start(bf16[4,128,128]{2,1,0:T(8,128)(2,1)S(1)} %get-tuple-element.100) | copy-start | bytes 393220
  25.8 7.4 %collective-permute-start.7 = (bf16[8,128,128]{2,1,0:T(8,128)(2,1)S(1)}, bf16[8,128,128]{2,1,0:T(8,128)(2,1)S(1)}, u32[]{:S(2)}, u32[]{:S(2)}) collective-permute-start(bf16[8,128,128]{2,1,0:T(8,128)(2,1)S(1)} %pad_maximum_fusion.6), channel_id=1, source_target_pairs={{0,64},{64,0},{1,65},{65,1},{2,66},{66,2},{3,67},{67,3},{4,68},{68... | collective-permute-start | bytes 786440 | tf_op jit(solution)/shard_map/gather_x_1/ppermute | solution.py:18
  26.2 9.4 %copy-start.22 = (s32[128]{0:T(128)S(1)}, s32[128]{0:T(128)}, u32[]{:S(2)}) copy-start(s32[128]{0:T(128)} %squeeze.55) | copy-start | bytes 1540
  32.5 19.9 %collective-permute-start.6 = (bf16[32,128,128]{2,1,0:T(8,128)(2,1)}, bf16[32,128,128]{2,1,0:T(8,128)(2,1)}, u32[]{:S(2)}, u32[]{:S(2)}) collective-permute-start(bf16[32,128,128]{2,1,0:T(8,128)(2,1)} %constant_dynamic-update-slice_fusion.2.near), channel_id=1, source_target_pairs={{0,48},{1,17},{16,32},{17,1},{32,16},{33,49},{48,0},{49,33},{2,50}... | collective-permute-start | bytes 3145736 | tf_op jit(solution)/shard_map/gather_far_0/ppermute | solution.py:28
  33.2 17.0 %collective-permute-start.8 = (bf16[2,8,128,128]{3,2,1,0:T(8,128)(2,1)}, bf16[2,8,128,128]{3,2,1,0:T(8,128)(2,1)S(1)}, u32[]{:S(2)}, u32[]{:S(2)}) collective-permute-start(bf16[2,8,128,128]{3,2,1,0:T(8,128)(2,1)} %pad_maximum_fusion.1), channel_id=1, source_target_pairs={{0,64},{64,0},{1,65},{65,1},{2,66},{66,2},{3,67},{67,3},{4,68},{68... | collective-permute-start | bytes 1572872 | tf_op jit(solution)/shard_map/gather_x_rest/ppermute | solution.py:18
  33.6 15.3 %collective-permute-start.9 = (bf16[16,128,128]{2,1,0:T(8,128)(2,1)S(1)}, bf16[16,128,128]{2,1,0:T(8,128)(2,1)}, u32[]{:S(2)}, u32[]{:S(2)}) collective-permute-start(bf16[16,128,128]{2,1,0:T(8,128)(2,1)S(1)} %pad_maximum_fusion.2), channel_id=1, source_target_pairs={{0,16},{1,49},{16,0},{17,33},{32,48},{33,17},{48,32},{49,1},{2,18}... | collective-permute-start | bytes 1572872 | tf_op jit(solution)/shard_map/gather_near_1/ppermute | solution.py:28
  35.7 14.6 %copy-start.16 = (bf16[4,128,128]{2,1,0:T(8,128)(2,1)S(1)}, bf16[4,128,128]{2,1,0:T(8,128)(2,1)}, u32[]{:S(2)}) copy-start(bf16[4,128,128]{2,1,0:T(8,128)(2,1)} %copy-done.15) | copy-start | bytes 393220
  50.0 7.6 %copy-start.8 = (bf16[32,128,128]{2,1,0:T(8,128)(2,1)}, bf16[32,128,128]{2,1,0:T(8,128)(2,1)S(1)}, u32[]{:S(2)}) copy-start(bf16[32,128,128]{2,1,0:T(8,128)(2,1)S(1)} %constant_dynamic-update-slice_fusion.6.refs_1_.near) | copy-start | bytes 3145732
  50.0 7.2 %copy-start.18 = (f32[64,128]{1,0:T(8,128)S(1)}, f32[64,128]{1,0:T(8,128)}, u32[]{:S(2)}) copy-start(f32[64,128]{1,0:T(8,128)} %get-tuple-element.81) | copy-start | bytes 98308
  50.0 22.6 %collective-permute-start.11 = (bf16[32,128,128]{2,1,0:T(8,128)(2,1)S(1)}, bf16[32,128,128]{2,1,0:T(8,128)(2,1)S(1)}, u32[]{:S(2)}, u32[]{:S(2)}) collective-permute-start(bf16[32,128,128]{2,1,0:T(8,128)(2,1)S(1)} %constant_dynamic-update-slice_fusion.6.refs_1_.near), channel_id=1, source_target_pairs={{0,48},{1,17},{16,32},{17,1},{32,16},{33,49},{48,0},{49,33},{2,50}... | collective-permute-start | bytes 3145736 | tf_op jit(solution)/shard_map/gather_far_1/ppermute | solution.py:28
  52.3 19.4 %collective-permute-start.12 = (bf16[16,128,128]{2,1,0:T(8,128)(2,1)S(1)}, bf16[16,128,128]{2,1,0:T(8,128)(2,1)S(1)}, u32[]{:S(2)}, u32[]{:S(2)}) collective-permute-start(bf16[16,128,128]{2,1,0:T(8,128)(2,1)S(1)} %pad_maximum_fusion.3), channel_id=1, source_target_pairs={{0,16},{1,49},{16,0},{17,33},{32,48},{33,17},{48,32},{49,1},{2,18}... | collective-permute-start | bytes 1572872 | tf_op jit(solution)/shard_map/gather_near_2/ppermute | solution.py:28
  57.5 12.5 %copy-start.14 = (bf16[4,128,128]{2,1,0:T(8,128)(2,1)S(1)}, bf16[4,128,128]{2,1,0:T(8,128)(2,1)}, u32[]{:S(2)}) copy-start(bf16[4,128,128]{2,1,0:T(8,128)(2,1)} %copy-done.13) | copy-start | bytes 393220
  65.8 7.8 %copy-start.9 = (bf16[32,128,128]{2,1,0:T(8,128)(2,1)S(1)}, bf16[32,128,128]{2,1,0:T(8,128)(2,1)}, u32[]{:S(2)}) copy-start(bf16[32,128,128]{2,1,0:T(8,128)(2,1)} %copy-done.8) | copy-start | bytes 3145732
  65.8 23.3 %collective-permute-start.10 = (bf16[4224,128]{1,0:T(8,128)(2,1)}, bf16[4224,128]{1,0:T(8,128)(2,1)}, u32[]{:S(2)}, u32[]{:S(2)}) collective-permute-start(bf16[4224,128]{1,0:T(8,128)(2,1)} %get-tuple-element.55), channel_id=1, source_target_pairs={{0,4},{1,13},{4,0},{5,9},{8,12},{9,5},{12,8},{13,1},{2,6},{3,15},{... | collective-permute-start | bytes 3244040 | tf_op jit(solution)/shard_map/sum_near_0/ppermute | solution.py:28
  73.6 14.1 %collective-permute-start.14 = (bf16[16,128,128]{2,1,0:T(8,128)(2,1)}, bf16[16,128,128]{2,1,0:T(8,128)(2,1)}, u32[]{:S(2)}, u32[]{:S(2)}) collective-permute-start(bf16[16,128,128]{2,1,0:T(8,128)(2,1)} %pad_maximum_fusion.4), channel_id=1, source_target_pairs={{0,16},{1,49},{16,0},{17,33},{32,48},{33,17},{48,32},{49,1},{2,18}... | collective-permute-start | bytes 1572872 | tf_op jit(solution)/shard_map/gather_near_3/ppermute | solution.py:28
  73.6 24.1 %collective-permute-start.22 = (bf16[32,128,128]{2,1,0:T(8,128)(2,1)}, bf16[32,128,128]{2,1,0:T(8,128)(2,1)}, u32[]{:S(2)}, u32[]{:S(2)}) collective-permute-start(bf16[32,128,128]{2,1,0:T(8,128)(2,1)} %constant_dynamic-update-slice_fusion.8.refs_0_.near), channel_id=1, source_target_pairs={{0,48},{1,17},{16,32},{17,1},{32,16},{33,49},{48,0},{49,33},{2,50}... | collective-permute-start | bytes 3145736 | tf_op jit(solution)/shard_map/gather_far_2/ppermute | solution.py:28
  74.9 14.3 %copy-start.3 = (f32[2112,128]{1,0:T(8,128)S(1)}, f32[2112,128]{1,0:T(8,128)}, u32[]{:S(2)}) copy-start(f32[2112,128]{1,0:T(8,128)} %copy-done.2) | copy-start | bytes 3244036
  80.1 11.7 %copy-start.4 = (f32[2048,128]{1,0:T(8,128)}, f32[2048,128]{1,0:T(8,128)S(1)}, u32[]{:S(2)}) copy-start(f32[2048,128]{1,0:T(8,128)S(1)} %get-tuple-element.66) | copy-start | bytes 3145732
  80.1 11.7 %copy-start.6 = (f32[2048,128]{1,0:T(8,128)}, f32[2048,128]{1,0:T(8,128)S(1)}, u32[]{:S(2)}) copy-start(f32[2048,128]{1,0:T(8,128)S(1)} %get-tuple-element.67) | copy-start | bytes 3145732
  80.1 9.0 %copy-start.1 = (f32[2112,128]{1,0:T(8,128)S(1)}, f32[2112,128]{1,0:T(8,128)}, u32[]{:S(2)}) copy-start(f32[2112,128]{1,0:T(8,128)} %copy-done) | copy-start | bytes 3244036
  80.1 33.1 %collective-permute-start.18 = (bf16[4096,128]{1,0:T(8,128)(2,1)}, bf16[4096,128]{1,0:T(8,128)(2,1)}, u32[]{:S(2)}, u32[]{:S(2)}) collective-permute-start(bf16[4096,128]{1,0:T(8,128)(2,1)} %get-tuple-element.57), channel_id=1, source_target_pairs={{0,4},{1,13},{4,0},{5,9},{8,12},{9,5},{12,8},{13,1},{2,6},{3,15},{... | collective-permute-start | bytes 3145736 | tf_op jit(solution)/shard_map/sum_near_1/ppermute | solution.py:28
  88.8 15.9 %collective-permute-start.15 = (bf16[32,128,128]{2,1,0:T(8,128)(2,1)S(1)}, bf16[32,128,128]{2,1,0:T(8,128)(2,1)}, u32[]{:S(2)}, u32[]{:S(2)}) collective-permute-start(bf16[32,128,128]{2,1,0:T(8,128)(2,1)S(1)} %constant_dynamic-update-slice_fusion.10.near.refs_0_), channel_id=1, source_target_pairs={{0,48},{1,17},{16,32},{17,1},{32,16},{33,49},{48,0},{49,33},{2,50}... | collective-permute-start | bytes 3145736 | tf_op jit(solution)/shard_map/gather_far_3/ppermute | solution.py:28
  91.8 21.5 %collective-permute-start.13 = (bf16[2112,128]{1,0:T(8,128)(2,1)}, bf16[2112,128]{1,0:T(8,128)(2,1)}, u32[]{:S(2)}, u32[]{:S(2)}) collective-permute-start(bf16[2112,128]{1,0:T(8,128)(2,1)} %get-tuple-element.86.refs_0_.refs_1_), channel_id=1, source_target_pairs={{0,12},{1,5},{4,8},{5,1},{8,4},{9,13},{12,0},{13,9},{2,14},{3,7},{... | collective-permute-start | bytes 1622024 | tf_op jit(solution)/shard_map/sum_far_0/ppermute | solution.py:28
  102.9 10.3 %copy-start.12 = (f32[2112,128]{1,0:T(8,128)S(1)}, f32[2112,128]{1,0:T(8,128)}, u32[]{:S(2)}) copy-start(f32[2112,128]{1,0:T(8,128)} %get-tuple-element.85) | copy-start | bytes 3244036
  103.0 13.4 %copy-start.5 = (f32[2048,128]{1,0:T(8,128)S(1)}, f32[2048,128]{1,0:T(8,128)}, u32[]{:S(2)}) copy-start(f32[2048,128]{1,0:T(8,128)} %copy-done.4) | copy-start | bytes 3145732
  103.0 13.4 %copy-start.7 = (f32[2048,128]{1,0:T(8,128)S(1)}, f32[2048,128]{1,0:T(8,128)}, u32[]{:S(2)}) copy-start(f32[2048,128]{1,0:T(8,128)} %copy-done.6) | copy-start | bytes 3145732
  103.0 30.9 %collective-permute-start.23 = (bf16[4096,128]{1,0:T(8,128)(2,1)S(1)}, bf16[4096,128]{1,0:T(8,128)(2,1)S(1)}, u32[]{:S(2)}, u32[]{:S(2)}) collective-permute-start(bf16[4096,128]{1,0:T(8,128)(2,1)S(1)} %get-tuple-element.69), channel_id=1, source_target_pairs={{0,4},{1,13},{4,0},{5,9},{8,12},{9,5},{12,8},{13,1},{2,6},{3,15},{... | collective-permute-start | bytes 3145736 | tf_op jit(solution)/shard_map/sum_near_2/ppermute | solution.py:28
  109.7 37.3 %collective-permute-start.27 = (bf16[4096,128]{1,0:T(8,128)(2,1)S(1)}, bf16[4096,128]{1,0:T(8,128)(2,1)S(1)}, u32[]{:S(2)}, u32[]{:S(2)}) collective-permute-start(bf16[4096,128]{1,0:T(8,128)(2,1)S(1)} %get-tuple-element.61), channel_id=1, source_target_pairs={{0,4},{1,13},{4,0},{5,9},{8,12},{9,5},{12,8},{13,1},{2,6},{3,15},{... | collective-permute-start | bytes 3145736 | tf_op jit(solution)/shard_map/sum_near_3/ppermute | solution.py:28
  114.3 6.9 %collective-permute-start.16 = (bf16[1056,128]{1,0:T(8,128)(2,1)S(1)}, bf16[1056,128]{1,0:T(8,128)(2,1)S(1)}, u32[]{:S(2)}, u32[]{:S(2)}) collective-permute-start(bf16[1056,128]{1,0:T(8,128)(2,1)S(1)} %fusion.4), channel_id=1, source_target_pairs={{0,2},{2,0},{1,3},{3,1},{4,6},{6,4},{5,7},{7,5},{8,10},{10,8},{9,1... | collective-permute-start | bytes 811016 | tf_op jit(solution)/shard_map/sum_x_0/ppermute | solution.py:18
  117.8 14.1 %collective-permute-start.19 = (bf16[2048,128]{1,0:T(8,128)(2,1)S(1)}, bf16[2048,128]{1,0:T(8,128)(2,1)S(1)}, u32[]{:S(2)}, u32[]{:S(2)}) collective-permute-start(bf16[2048,128]{1,0:T(8,128)(2,1)S(1)} %get-tuple-element.91), channel_id=1, source_target_pairs={{0,12},{1,5},{4,8},{5,1},{8,4},{9,13},{12,0},{13,9},{2,14},{3,7},{... | collective-permute-start | bytes 1572872 | tf_op jit(solution)/shard_map/sum_far_1/ppermute | solution.py:28
  122.6 6.8 %collective-permute-start.17 = (bf16[512,128]{1,0:T(8,128)(2,1)S(1)}, bf16[512,128]{1,0:T(8,128)(2,1)S(1)}, u32[]{:S(2)}, u32[]{:S(2)}) collective-permute-start(bf16[512,128]{1,0:T(8,128)(2,1)S(1)} %bitcast.58), channel_id=1, source_target_pairs={{0,1},{1,0},{2,3},{3,2},{4,5},{5,4},{6,7},{7,6},{8,9},{9,8},{10,11... | collective-permute-start | bytes 393224 | tf_op jit(solution)/shard_map/mean_core_0/ppermute | solution.py:18
  131.9 6.8 %collective-permute-start.20 = (bf16[1024,128]{1,0:T(8,128)(2,1)S(1)}, bf16[1024,128]{1,0:T(8,128)(2,1)S(1)}, u32[]{:S(2)}, u32[]{:S(2)}) collective-permute-start(bf16[1024,128]{1,0:T(8,128)(2,1)S(1)} %fusion.10), channel_id=1, source_target_pairs={{0,2},{2,0},{1,3},{3,1},{4,6},{6,4},{5,7},{7,5},{8,10},{10,8},{9,1... | collective-permute-start | bytes 786440 | tf_op jit(solution)/shard_map/sum_x_1/ppermute | solution.py:18
  134.0 13.0 %collective-permute-start.24 = (bf16[2048,128]{1,0:T(8,128)(2,1)S(1)}, bf16[2048,128]{1,0:T(8,128)(2,1)S(1)}, u32[]{:S(2)}, u32[]{:S(2)}) collective-permute-start(bf16[2048,128]{1,0:T(8,128)(2,1)S(1)} %get-tuple-element.89), channel_id=1, source_target_pairs={{0,12},{1,5},{4,8},{5,1},{8,4},{9,13},{12,0},{13,9},{2,14},{3,7},{... | collective-permute-start | bytes 1572872 | tf_op jit(solution)/shard_map/sum_far_2/ppermute | solution.py:28
  139.1 6.2 %collective-permute-start.21 = (bf16[512,128]{1,0:T(8,128)(2,1)S(1)}, bf16[512,128]{1,0:T(8,128)(2,1)S(1)}, u32[]{:S(2)}, u32[]{:S(2)}) collective-permute-start(bf16[512,128]{1,0:T(8,128)(2,1)S(1)} %bitcast.59), channel_id=1, source_target_pairs={{0,1},{1,0},{2,3},{3,2},{4,5},{5,4},{6,7},{7,6},{8,9},{9,8},{10,11... | collective-permute-start | bytes 393224 | tf_op jit(solution)/shard_map/mean_core_1/ppermute | solution.py:18
  147.1 8.8 %collective-permute-start.25 = (bf16[1024,128]{1,0:T(8,128)(2,1)S(1)}, bf16[1024,128]{1,0:T(8,128)(2,1)S(1)}, u32[]{:S(2)}, u32[]{:S(2)}) collective-permute-start(bf16[1024,128]{1,0:T(8,128)(2,1)S(1)} %fusion.8), channel_id=1, source_target_pairs={{0,2},{2,0},{1,3},{3,1},{4,6},{6,4},{5,7},{7,5},{8,10},{10,8},{9,1... | collective-permute-start | bytes 786440 | tf_op jit(solution)/shard_map/sum_x_2/ppermute | solution.py:18
  150.6 8.4 %collective-permute-start.28 = (bf16[2048,128]{1,0:T(8,128)(2,1)S(1)}, bf16[2048,128]{1,0:T(8,128)(2,1)S(1)}, u32[]{:S(2)}, u32[]{:S(2)}) collective-permute-start(bf16[2048,128]{1,0:T(8,128)(2,1)S(1)} %get-tuple-element.87), channel_id=1, source_target_pairs={{0,12},{1,5},{4,8},{5,1},{8,4},{9,13},{12,0},{13,9},{2,14},{3,7},{... | collective-permute-start | bytes 1572872 | tf_op jit(solution)/shard_map/sum_far_3/ppermute | solution.py:28
  156.2 13.7 %collective-permute-start.26 = (bf16[512,128]{1,0:T(8,128)(2,1)S(1)}, bf16[512,128]{1,0:T(8,128)(2,1)S(1)}, u32[]{:S(2)}, u32[]{:S(2)}) collective-permute-start(bf16[512,128]{1,0:T(8,128)(2,1)S(1)} %bitcast.56), channel_id=1, source_target_pairs={{0,1},{1,0},{2,3},{3,2},{4,5},{5,4},{6,7},{7,6},{8,9},{9,8},{10,11... | collective-permute-start | bytes 393224 | tf_op jit(solution)/shard_map/mean_core_2/ppermute | solution.py:18
  159.1 6.8 %collective-permute-start.29 = (bf16[1024,128]{1,0:T(8,128)(2,1)S(1)}, bf16[1024,128]{1,0:T(8,128)(2,1)S(1)}, u32[]{:S(2)}, u32[]{:S(2)}) collective-permute-start(bf16[1024,128]{1,0:T(8,128)(2,1)S(1)} %fusion.6), channel_id=1, source_target_pairs={{0,2},{2,0},{1,3},{3,1},{4,6},{6,4},{5,7},{7,5},{8,10},{10,8},{9,1... | collective-permute-start | bytes 786440 | tf_op jit(solution)/shard_map/sum_x_3/ppermute | solution.py:18
  166.2 5.2 %collective-permute-start.30 = (bf16[512,128]{1,0:T(8,128)(2,1)S(1)}, bf16[512,128]{1,0:T(8,128)(2,1)S(1)}, u32[]{:S(2)}, u32[]{:S(2)}) collective-permute-start(bf16[512,128]{1,0:T(8,128)(2,1)S(1)} %bitcast.57), channel_id=1, source_target_pairs={{0,1},{1,0},{2,3},{3,2},{4,5},{5,4},{6,7},{7,6},{8,9},{9,8},{10,11... | collective-permute-start | bytes 393224 | tf_op jit(solution)/shard_map/mean_core_3/ppermute | solution.py:18
  (7 other events, 22.2 us)

commit v8 on v7

--- a/solution.py
+++ b/solution.py
@@ -41,7 +41,7 @@
 
 
 def tile_kernel(src_ref, dst_ref, live_ref, c_own, c_other, pieces_ref, near, far, *refs):
-    send, pass_on, stay, panel, acc, sems = refs[-6:]
+    send, pass_on, stay, panel, acc, sems = refs
     copies = [
         pltpu.make_async_copy(near, panel.at[pl.ds(0, 32)], sems.at[0]),
         pltpu.make_async_copy(far, panel.at[pl.ds(32, 32)], sems.at[1]),
@@ -94,7 +94,7 @@
             )
 
 
-def tile_sums(src, dst, live, c_own, c_other, pieces, with_pieces, near, far, earlier, cost):
+def tile_sums(src, dst, live, c_own, c_other, pieces, with_pieces, near, far, cost):
     tile, w = near.shape[-2:]
     any_spec = pl.BlockSpec(memory_space=pl.ANY)
     vmem = pl.BlockSpec(memory_space=pltpu.VMEM)
@@ -105,80 +105,75 @@
         tile_kernel,
         out_shape=(
             jax.ShapeDtypeStruct((4 * size, w), jnp.bfloat16),
-            jax.ShapeDtypeStruct((2 * size, w), jnp.float32),
-            jax.ShapeDtypeStruct((2 * size, w), jnp.float32),
+            jax.ShapeDtypeStruct((2 * size, w), jnp.bfloat16),
+            jax.ShapeDtypeStruct((2 * size, w), jnp.bfloat16),
         ),
-        in_specs=[smem] * 3 + [vmem] * 3 + [any_spec] * (2 + len(earlier)),
+        in_specs=[smem] * 3 + [vmem] * 3 + [any_spec] * 2,
         out_specs=(vmem,) * 3,
         scratch_shapes=[
             pltpu.VMEM((64, tile, w), jnp.bfloat16),
             pltpu.VMEM((64, tile, w), jnp.float32),
             pltpu.SemaphoreType.DMA((2,)),
         ],
-        compiler_params=pltpu.CompilerParams(vmem_limit_bytes=32 * 1024 * 1024),
+        compiler_params=pltpu.CompilerParams(vmem_limit_bytes=16 * 1024 * 1024),
         cost_estimate=pl.CostEstimate(
             flops=cost, bytes_accessed=64 * tile * w, transcendentals=0
         ),
-    )(src, dst, live, c_own, c_other, pieces, near, far, *earlier)
-
-
-def message_kernel(first, core_ref, x_hbm, weight, bias, theirs, mine, x, held, row, sems):
-    core = core_ref[0]
-    tile, w = mine.shape[1:]
-    blocks = x.shape[0] // tile
-    chunks = mine.shape[0] // blocks
+    )(src, dst, live, c_own, c_other, pieces, near, far)
+
+
+def message_kernel(first, core_ref, x_own, x_other, weight, bias, *refs):
+    outs, (x, held, row, sems) = refs[:-4], refs[-4:]
     half = weight.shape[1] // 2
-    size = chunks * w
-    starts = [
-        pl.multiple_of((1 - core) * half + first, 128),
-        pl.multiple_of(core * half + first, 128),
+    rows, size = x_own.shape[0], held.shape[1]
+    tile, w = outs[0].shape[1:]
+    at = pl.multiple_of(core_ref[0] * half + first, 128)
+    copies = [
+        pltpu.make_async_copy(x_own, x.at[pl.ds(0, rows)], sems.at[0]),
+        pltpu.make_async_copy(weight.at[:, pl.ds(at, size)], held, sems.at[1]),
+        pltpu.make_async_copy(bias, row, sems.at[2]),
+        pltpu.make_async_copy(x_other, x.at[pl.ds(rows, rows)], sems.at[3]),
     ]
-    copies = [
-        pltpu.make_async_copy(weight.at[:, pl.ds(starts[i], size)], held.at[i], sems.at[i])
-        for i in range(2)
-    ]
-    whole = [
-        pltpu.make_async_copy(x_hbm, x, sems.at[2]),
-        pltpu.make_async_copy(bias, row, sems.at[3]),
-    ]
-    copies[0].start()
-    whole[0].start()
-    whole[1].start()
-    copies[1].start()
-    whole[0].wait()
-    whole[1].wait()
-    for i, out in enumerate((theirs, mine)):
-        copies[i].wait()
-        for j in range(chunks):
+    for copy in copies:
+        copy.start()
+    for copy in copies:
+        copy.wait()
+    blocks = 2 * rows // tile
+    chunk = 0
+    for out in outs:
+        for j in range(out.shape[0] // blocks):
             total = jnp.dot(
-                x[...], held[i, :, j * w : (j + 1) * w], preferred_element_type=jnp.float32
+                x[...], held[:, chunk * w : (chunk + 1) * w], preferred_element_type=jnp.float32
             )
-            total = jnp.maximum(total + row[:, pl.ds(starts[i] + j * w, w)], 0.0)
-            out[j * blocks : (j + 1) * blocks] = total.astype(out.dtype).reshape(blocks, tile, w)
-
-
-def transform(core, features, weight, bias, first, chunks, tile, w):
-    vmem = pl.BlockSpec(memory_space=pltpu.VMEM)
+            total = jnp.maximum(total + row[:, pl.ds(at + chunk * w, w)], 0.0)
+            total = total.astype(out.dtype).reshape(blocks, tile, w)
+            out[j * blocks : (j + 1) * blocks] = total
+            chunk += 1
+
+
+def transform(core, x_own, x_other, weight, bias, first, sizes, tile, w, limit):
     any_spec = pl.BlockSpec(memory_space=pl.ANY)
-    out = jax.ShapeDtypeStruct((chunks * features.shape[0] // tile, tile, w), jnp.bfloat16)
+    rows, width = x_own.shape
+    blocks = 2 * rows // tile
+    chunks = sum(sizes)
     return pl.pallas_call(
         functools.partial(message_kernel, first),
-        out_shape=(out, out),
-        in_specs=[pl.BlockSpec(memory_space=pltpu.SMEM), any_spec, any_spec, any_spec],
-        out_specs=(vmem, vmem),
+        out_shape=tuple(jax.ShapeDtypeStruct((n * blocks, tile, w), jnp.bfloat16) for n in sizes),
+        in_specs=[pl.BlockSpec(memory_space=pltpu.SMEM)] + [any_spec] * 4,
+        out_specs=tuple(pl.BlockSpec(memory_space=pltpu.VMEM) for n in sizes),
         scratch_shapes=[
-            pltpu.VMEM(features.shape, jnp.bfloat16),
-            pltpu.VMEM((2, features.shape[1], chunks * w), jnp.bfloat16),
+            pltpu.VMEM((2 * rows, width), jnp.bfloat16),
+            pltpu.VMEM((width, chunks * w), jnp.bfloat16),
             pltpu.VMEM((1, bias.shape[0]), jnp.float32),
             pltpu.SemaphoreType.DMA((4,)),
         ],
-        compiler_params=pltpu.CompilerParams(vmem_limit_bytes=60 * 1024 * 1024),
+        compiler_params=pltpu.CompilerParams(vmem_limit_bytes=limit * 1024 * 1024),
         cost_estimate=pl.CostEstimate(
-            flops=32 * features.size * chunks * w,
-            bytes_accessed=2 * features.size + 4 * features.shape[1] * chunks * w,
+            flops=32 * rows * width * chunks * w,
+            bytes_accessed=4 * rows * width + 2 * width * chunks * w,
             transcendentals=0,
         ),
-    )(core.astype(jnp.int32).reshape(1), features, weight, bias.reshape(1, -1))
+    )(core.astype(jnp.int32).reshape(1), x_own, x_other, weight, bias.reshape(1, -1))
 
 
 def finish_kernel(hidden, near, got, weight, out):
@@ -206,7 +201,7 @@
             pl.BlockSpec(weight.shape, lambda i: (0, 0)),
         ],
         out_specs=by_row(width),
-        compiler_params=pltpu.CompilerParams(vmem_limit_bytes=32 * 1024 * 1024),
+        compiler_params=pltpu.CompilerParams(vmem_limit_bytes=8 * 1024 * 1024),
     )(hidden, near, got, weight)
 
 
@@ -229,29 +224,35 @@
     blocks = rows_dev // tile
     x_lo, y, z, x_hi, core = (lax.axis_index(a) for a in AXES)
 
-    make = functools.partial(transform, core)
-    theirs, mine = make(features, neigh_weight, neigh_bias, 0, 1, tile, cw)
-    own = [jnp.concatenate([mine, swap(theirs, "core", "other_core_0")])]
-    first = swap(own[0], "x_lo", "gather_x_0")
-    theirs, mine = make(
-        after(features, theirs), neigh_weight, neigh_bias, cw, CHUNKS - 1, tile, cw
-    )
-    theirs = swap(theirs, "core", "other_core_rest")
-    for j in range(CHUNKS - 1):
-        part = slice(j * blocks, (j + 1) * blocks)
-        own.append(jnp.concatenate([mine[part], theirs[part]]))
+    x_other = swap(features, "core", "other_features_0")
+    own0 = transform(
+        core, features, x_other, neigh_weight, neigh_bias, 0, (1,), tile, cw, 12
+    )[0]
+    first = swap(own0, "x_lo", "gather_x_0")
+    own1, own_rest = transform(
+        core,
+        after(features, own0),
+        x_other,
+        neigh_weight,
+        neigh_bias,
+        cw,
+        (1, CHUNKS - 2),
+        tile,
+        cw,
+        14,
+    )
 
     live = live_tiles[0, 0]
     used = jnp.arange(slots, dtype=jnp.int32) < live
-    counts = after(walk_counts, own[0])[0, 0]
+    counts = walk_counts[0, 0]
     c_own = jnp.where(used[:, None, None], counts, 0).astype(jnp.bfloat16)
-    pair0 = jnp.concatenate([own[0], after(first, c_own)])
+    pair0 = after(jnp.concatenate([own0, after(first, own1)]), own1)
     rows_own = jnp.where(used, tile_rows[0, 0], 0)
     meta = jnp.stack(
         [rows_own, jnp.where(used, tile_cols[0, 0], 0), jnp.full((slots,), live, jnp.int32)]
     )
-    c_other = swap(after(c_own, theirs), "core", "other_tiles")
-    metas = jnp.stack([meta, swap(after(meta, own[0]), "core", "other_meta")])
+    c_other = swap(after(c_own, own0), "core", "other_tiles")
+    metas = jnp.stack([meta, swap(after(meta, own0), "core", "other_meta")])
     k = metas[:, 1]
     src = (
         (ring_slot((k // 4) % 4, y, core) * 2 + ((k // 16) ^ x_lo)) * 8
@@ -283,7 +284,7 @@
     w_own = lax.dynamic_slice_in_dim(combine_weight, width + core * half, half, 0)
     w_other = lax.dynamic_slice_in_dim(combine_weight, width + (1 - core) * half, half, 0)
 
-    second = swap(after(own[1], first), "x_lo", "gather_x_1")
+    second = swap(after(own1, first), "x_lo", "gather_x_1")
     f32, bf16 = jnp.float32, jnp.bfloat16
     near_all, far_all, part_all, pass_all, hidden_all = [], [], [], [], []
     scale = None
@@ -294,8 +295,11 @@
 
     far(pair0, step(pair0, "y", 0, "gather_near_0"), 0)
     second = after(second, near_all[0])
-    rest = swap(after(jnp.stack(own[2:]), second), "x_lo", "gather_x_rest")
-    partner = [first, second] + [rest[j] for j in range(CHUNKS - 2)]
+    rest = swap(after(own_rest, second), "x_lo", "gather_x_rest")
+    size = own0.shape[0]
+    split = lambda x: [x[i * size : (i + 1) * size] for i in range(CHUNKS - 2)]
+    own = [own0, own1] + split(own_rest)
+    partner = [first, second] + split(rest)
     for j in range(1, CHUNKS):
         pair = jnp.concatenate([own[j], partner[j]])
         pair = after(pair, near_all[j - 1], *far_all[: j - 1])
@@ -310,7 +314,15 @@
         with jax.named_scope(f"tiles_{j}"):
             part_all.append(
                 tile_sums(
-                    src, dst, lives, c_own, c_other, parts, j == 0, near_all[j], far_all[j], earlier,
+                    after(src, *earlier) if earlier else src,
+                    dst,
+                    lives,
+                    c_own,
+                    c_other,
+                    parts,
+                    j == 0,
+                    near_all[j],
+                    far_all[j],
                     2**31 if j < 2 else 2**20,
                 )
             )
@@ -325,9 +337,9 @@
             got = after(got, part_all[1][0])
         else:
             got = after(got, part_all[-1][0])
-        passed = (got[: 2 * size].astype(f32) + pass_on).astype(bf16)
+        passed = (got[: 2 * size].astype(f32) + pass_on.astype(f32)).astype(bf16)
         pass_all.append(passed)
-        stay = got[2 * size :].astype(f32) + stay
+        stay = got[2 * size :].astype(f32) + stay.astype(f32)
         got = step(passed, "z", 1, f"sum_far_{j}")
         if j == 0:
             for i in range(2, CHUNKS):

time: 177 us -> 171 us (0.966)
  waiting for transfers between devices: 42.7 us -> 37.4 us
  Pallas kernels: 32.7 us -> 29.5 us
    ppermute x16, waiting for transfers between devices: 25.2 us -> 17.2 us  [step(): return lax.ppermute(x, (axis, 'core'), pairs)]
    pallas_call x2, Pallas kernels: 8.14 us -> 3.05 us  [transform(): pl.pallas_call(functools.partial(message_kernel, first), out_shape=tuple(...]
    ppermute x15 -> x14, waiting for transfers between devices: 17.5 us -> 20.2 us  [swap(): return lax.ppermute(x, axis, [(0, 1), (1, 0)])]
    pallas_call x4, Pallas kernels: 21.7 us -> 23.6 us  [tile_sums(): pl.pallas_call(tile_kernel, out_shape=(jax.ShapeDtypeStruct((4 * size, w)...]
    concatenate x3, other arithmetic: 0.94 us -> 2.83 us  [local(): pair = jnp.concatenate([own[j], partner[j]])]
    ppermute x15 -> x14, starting transfers between devices: 29 us -> 29.9 us  [swap(): return lax.ppermute(x, axis, [(0, 1), (1, 0)])]
    unnamed x54 -> x46, local copies, waits for them, and re-layouts: 8.48 us -> 9.17 us
  transfers between devices with their start and end apart: 31 -> 30, of which waited for: 13 -> 9; matrix products, arithmetic and copies ran while one was open for 25% -> 25% of each run, Pallas kernels for 15% -> 15%
where the time goes in v8:
time: 171 us; the launch traced here: 169 us
  starting transfers between devices  51.9 us (30%)
  waiting for transfers between devices  37.4 us (22%)
  Pallas kernels  29.5 us (17%)
  other arithmetic  18.7 us (11%)
  local copies, waits for them, and re-layouts  18.4 us (11%)
  matrix products  11.7 us (7%)
    ppermute x14, starting transfers between devices, swap(): return lax.ppermute(x, axis, [(0, 1), (1, 0)])  29.9 us
    pallas_call x4, Pallas kernels, tile_sums(): pl.pallas_call(tile_kernel, out_shape=(jax.ShapeDtypeStruct((4 * size, w)...  23.6 us
    ppermute x16, starting transfers between devices, step(): return lax.ppermute(x, (axis, 'core'), pairs)  22 us
    ppermute x14, waiting for transfers between devices, swap(): return lax.ppermute(x, axis, [(0, 1), (1, 0)])  20.2 us
    ppermute x16, waiting for transfers between devices, step(): return lax.ppermute(x, (axis, 'core'), pairs)  17.2 us
    unnamed x46, local copies, waits for them, and re-layouts  9.17 us
    concatenate x4, local copies, waits for them, and re-layouts, far(): near_all.append(jnp.concatenate([pair, got]))  5.02 us
    dot_general x3, matrix products, local(): hidden = hidden + jnp.dot(got, w_other[cols], preferred_element_type=f32)  4.28 us
  transfers between devices with their start and end apart: 30, of which 9 were waited for; matrix products, arithmetic and copies ran while one was open for 25% of the time, Pallas kernels for 15%

profile of v8, /device:TPU:3, one launch (start us, length us, event | category | flops | bytes accessed | tf_op | source)
XLA Modules:
  0.0 168.9 jit_solution(15060233248093024721)
XLA Ops:
  2.0 3.7 %convert_reduce_fusion.1 = (f32[64,128]{1,0:T(8,128)S(1)}, bf16[64,128,128]{2,1,0:T(8,128)(2,1)S(1)}) fusion(s32[1,1,64,128,128]{4,3,2,1,0:T(8,128)} %param.11, pred[64]{0:T(512)(128)(4,1)S(1)} %iota_compare_fusion.2), kind=kLoop, calls=%fused_computation.3 | loop fusion | flops 4186112 | bytes 6324288 | tf_op jit(solution)/shard_map/reduce_sum | solution.py:273
  7.3 1.2 copy-done.15
  8.6 2.1 %shard_map.101 = (bf16[8,128,128]{2,1,0:T(8,128)(2,1)S(1)}, bf16[16,128,128]{2,1,0:T(8,128)(2,1)S(1)}) custom-call(s32[1]{0:T(128)} %bitcast.4.core_ref, bf16[512,1024]{1,0:T(8,128)(2,1)S(1)} %copy-done.11, bf16[512,1024]{1,0:T(8,128)(2,1)S(1)} %copy-done.15, bf16[1024,1024]{1,0:T(8,128)(2,1)S(1)} %copy-done.10, f32[1,1024]{1,0:T(1,128)S(1)} %bitcast.41), custom_call_target="tpu_custom_call" | custom-call | flops 6442450944 | bytes 2883584 | tf_op jit(solution)/shard_map/pallas_call | solution.py:159
  10.6 4.2 %collective-permute-done.2 = bf16[8,128,128]{2,1,0:T(8,128)(2,1)S(1)} collective-permute-done((bf16[8,128,128]{2,1,0:T(8,128)(2,1)S(1)}, bf16[8,128,128]{2,1,0:T(8,128)(2,1)S(1)}, u32[]{:S(2)}, u32[]{:S(2)}) %collective-permute-start.2) | collective-permute-done | bytes 262176 | tf_op jit(solution)/shard_map/gather_x_0/ppermute | solution.py:18
  14.9 2.8 %collective-permute-start.4 = (bf16[16,128,128]{2,1,0:T(8,128)(2,1)S(1)}, bf16[16,128,128]{2,1,0:T(8,128)(2,1)}, u32[]{:S(2)}, u32[]{:S(2)}) collective-permute-start(bf16[16,128,128]{2,1,0:T(8,128)(2,1)S(1)} %pad_maximum_fusion), channel_id=1, source_target_pairs={{0,16},{1,49},{16,0},{17,33},{32,48},{33,17},{48,32},{49,1},{2,18}... | collective-permute-start | bytes 1572872 | tf_op jit(solution)/shard_map/gather_near_0/ppermute | solution.py:28
  20.2 4.2 %collective-permute-done.4 = bf16[16,128,128]{2,1,0:T(8,128)(2,1)} collective-permute-done((bf16[16,128,128]{2,1,0:T(8,128)(2,1)S(1)}, bf16[16,128,128]{2,1,0:T(8,128)(2,1)}, u32[]{:S(2)}, u32[]{:S(2)}) %collective-permute-start.4) | collective-permute-done | bytes 524320 | tf_op jit(solution)/shard_map/gather_near_0/ppermute | solution.py:28
  24.4 1.9 %constant_dynamic-update-slice_fusion.near = bf16[32,128,128]{2,1,0:T(8,128)(2,1)} fusion(bf16[32,128,128]{2,1,0:T(8,128)(2,1)} %constant_dynamic-update-slice_fusion.1, bf16[16,128,128]{2,1,0:T(8,128)(2,1)} %collective-permute-done.4), kind=kLoop, calls=%fused_computation.57 | loop fusion | bytes 1048576 | tf_op jit(solution)/shard_map/concatenate | solution.py:293
  27.6 2.4 %collective-permute-start.6 = (bf16[16,128,128]{2,1,0:T(8,128)(2,1)S(1)}, bf16[16,128,128]{2,1,0:T(8,128)(2,1)}, u32[]{:S(2)}, u32[]{:S(2)}) collective-permute-start(bf16[16,128,128]{2,1,0:T(8,128)(2,1)S(1)} %pad_maximum_fusion.1), channel_id=1, source_target_pairs={{0,16},{1,49},{16,0},{17,33},{32,48},{33,17},{48,32},{49,1},{2,18}... | collective-permute-start | bytes 1572872 | tf_op jit(solution)/shard_map/gather_near_1/ppermute | solution.py:28
  30.6 12.4 %collective-permute-done.6 = bf16[16,128,128]{2,1,0:T(8,128)(2,1)} collective-permute-done((bf16[16,128,128]{2,1,0:T(8,128)(2,1)S(1)}, bf16[16,128,128]{2,1,0:T(8,128)(2,1)}, u32[]{:S(2)}, u32[]{:S(2)}) %collective-permute-start.6) | collective-permute-done | bytes 524320 | tf_op jit(solution)/shard_map/gather_near_1/ppermute | solution.py:28
  42.9 1.1 constant_dynamic-update-slice_fusion.2.near
  46.7 2.2 %collective-permute-start.10 = (bf16[16,128,128]{2,1,0:T(8,128)(2,1)S(1)}, bf16[16,128,128]{2,1,0:T(8,128)(2,1)S(1)}, u32[]{:S(2)}, u32[]{:S(2)}) collective-permute-start(bf16[16,128,128]{2,1,0:T(8,128)(2,1)S(1)} %pad_maximum_fusion.2), channel_id=1, source_target_pairs={{0,16},{1,49},{16,0},{17,33},{32,48},{33,17},{48,32},{49,1},{2,18}... | collective-permute-start | bytes 1572872 | tf_op jit(solution)/shard_map/gather_near_2/ppermute | solution.py:28
  48.9 2.2 %convert_reduce_fusion = f32[64,128]{1,0:T(8,128)S(1)} fusion(bf16[64,128,128]{2,1,0:T(8,128)(2,1)} %collective-permute-done.7.c_other), kind=kLoop, calls=%fused_computation.2 | loop fusion | flops 2088960 | bytes 2129920 | tf_op jit(solution)/shard_map/reduce_sum | solution.py:273
  51.4 6.7 %tiles_0.1 = (bf16[4224,128]{1,0:T(8,128)(2,1)}, bf16[2112,128]{1,0:T(8,128)(2,1)S(1)}, bf16[2112,128]{1,0:T(8,128)(2,1)S(1)}) custom-call(s32[128]{0:T(128)S(1)} %fusion.32.src_ref, s32[128]{0:T(128)S(1)} %fusion.33.dst_ref, s32[2]{0:T(128)S(1)} %fusion.31.live_ref, bf16[64,128,128]{2,1,0:T(8,128)(2,1)S(1)} %get-tuple-element.55.c_own, ...), custom_call_target="tpu_custom_call" | custom-call | flops 2147483648 | bytes 1048576 | tf_op jit(solution)/shard_map/tiles_0/pallas_call | solution.py:104
  58.9 3.3 %collective-permute-start.9 = (bf16[4224,128]{1,0:T(8,128)(2,1)}, bf16[4224,128]{1,0:T(8,128)(2,1)}, u32[]{:S(2)}, u32[]{:S(2)}) collective-permute-start(bf16[4224,128]{1,0:T(8,128)(2,1)} %get-tuple-element.56), channel_id=1, source_target_pairs={{0,4},{1,13},{4,0},{5,9},{8,12},{9,5},{12,8},{13,1},{2,6},{3,15},{... | collective-permute-start | bytes 3244040 | tf_op jit(solution)/shard_map/sum_near_0/ppermute | solution.py:28
  64.3 1.4 collective-permute-start.13
  66.7 1.2 copy-done.9
  67.9 1.2 copy-done.13
  69.2 5.6 %tiles_1.1 = (bf16[4096,128]{1,0:T(8,128)(2,1)}, bf16[2048,128]{1,0:T(8,128)(2,1)S(1)}, bf16[2048,128]{1,0:T(8,128)(2,1)S(1)}) custom-call(s32[128]{0:T(128)S(1)} %fusion.32.src_ref, s32[128]{0:T(128)S(1)} %fusion.33.dst_ref, s32[2]{0:T(128)S(1)} %fusion.31.live_ref, bf16[64,128,128]{2,1,0:T(8,128)(2,1)S(1)} %get-tuple-element.55.c_own, ...), custom_call_target="tpu_custom_call" | custom-call | flops 2147483648 | bytes 1048576 | tf_op jit(solution)/shard_map/tiles_1/pallas_call | solution.py:104
  75.6 3.0 %collective-permute-start.17 = (bf16[4096,128]{1,0:T(8,128)(2,1)}, bf16[4096,128]{1,0:T(8,128)(2,1)}, u32[]{:S(2)}, u32[]{:S(2)}) collective-permute-start(bf16[4096,128]{1,0:T(8,128)(2,1)} %get-tuple-element.59), channel_id=1, source_target_pairs={{0,4},{1,13},{4,0},{5,9},{8,12},{9,5},{12,8},{13,1},{2,6},{3,15},{... | collective-permute-start | bytes 3145736 | tf_op jit(solution)/shard_map/sum_near_1/ppermute | solution.py:28
  78.6 1.9 %constant_dynamic-update-slice_fusion.7 = bf16[32,128,128]{2,1,0:T(8,128)(2,1)} fusion(bf16[16,128,128]{2,1,0:T(8,128)(2,1)} %pad_maximum_fusion.3), kind=kLoop, calls=%fused_computation.64 | loop fusion | bytes 1048576
  80.5 1.9 %constant_dynamic-update-slice_fusion.6.near = bf16[32,128,128]{2,1,0:T(8,128)(2,1)} fusion(bf16[32,128,128]{2,1,0:T(8,128)(2,1)} %constant_dynamic-update-slice_fusion.7, bf16[16,128,128]{2,1,0:T(8,128)(2,1)} %collective-permute-done.13), kind=kLoop, calls=%fused_computation.63 | loop fusion | bytes 1048576 | tf_op jit(solution)/shard_map/concatenate | solution.py:293
  82.5 2.0 %collective-permute-start.14 = (bf16[32,128,128]{2,1,0:T(8,128)(2,1)}, bf16[32,128,128]{2,1,0:T(8,128)(2,1)}, u32[]{:S(2)}, u32[]{:S(2)}) collective-permute-start(bf16[32,128,128]{2,1,0:T(8,128)(2,1)} %constant_dynamic-update-slice_fusion.6.near), channel_id=1, source_target_pairs={{0,48},{1,17},{16,32},{17,1},{32,16},{33,49},{48,0},{49,33},{2,50}... | collective-permute-start | bytes 3145736 | tf_op jit(solution)/shard_map/gather_far_3/ppermute | solution.py:28
  84.4 2.6 %convert_add_fusion = (f32[2112,128]{1,0:T(8,128)}, bf16[2112,128]{1,0:T(8,128)(2,1)}) fusion(bf16[2112,128]{1,0:T(8,128)(2,1)S(1)} %copy-done.3, bf16[4224,128]{1,0:T(8,128)(2,1)} %collective-permute-done.9, bf16[2112,128]{1,0:T(8,128)(2,1)S(1)} %copy-done.1), kind=kLoop, calls=%fused_computation.9 | loop fusion | flops 1892352 | bytes 3784704 | tf_op jit(solution)/shard_map/add | solution.py:342
  87.1 1.8 %constant_dynamic-slice_fusion.1 = (bf16[128,1024]{1,0:T(8,128)(2,1)S(1)}, bf16[128,1024]{1,0:T(8,128)(2,1)}) fusion(bf16[2048,1024]{1,0:T(8,128)(2,1)} %param.17, s32[]{:T(128)S(6)} %add.270, s32[]{:T(128)S(6)} %add.271), kind=kLoop, calls=%fused_computation.83 | loop fusion | bytes 1048584 | tf_op jit(solution)/shard_map/slice | solution.py:367
  89.8 3.2 %fusion.1 = f32[512,1024]{1,0:T(8,128)S(1)} fusion(bf16[512,1024]{1,0:T(8,128)(2,1)} %x_own.2, bf16[2048,1024]{1,0:T(8,128)(2,1)} %param.17), kind=kOutput, calls=%fused_computation.6 | convolution fusion | flops 1073741824 | bytes 5242880 | tf_op jit(solution)/shard_map/dot_general | solution.py:281
  93.0 5.5 %tiles_2.1 = (bf16[4096,128]{1,0:T(8,128)(2,1)S(1)}, bf16[2048,128]{1,0:T(8,128)(2,1)S(1)}, bf16[2048,128]{1,0:T(8,128)(2,1)S(1)}) custom-call(s32[128]{0:T(128)S(1)} %fusion.32.src_ref, s32[128]{0:T(128)S(1)} %fusion.33.dst_ref, s32[2]{0:T(128)S(1)} %fusion.31.live_ref, bf16[64,128,128]{2,1,0:T(8,128)(2,1)S(1)} %get-tuple-element.55.c_own, ...), custom_call_target="tpu_custom_call" | custom-call | flops 1048576 | bytes 1048576 | tf_op jit(solution)/shard_map/tiles_2/pallas_call | solution.py:104
  98.6 5.8 %tiles_3.1 = (bf16[4096,128]{1,0:T(8,128)(2,1)S(1)}, bf16[2048,128]{1,0:T(8,128)(2,1)S(1)}, bf16[2048,128]{1,0:T(8,128)(2,1)S(1)}) custom-call(s32[128]{0:T(128)S(1)} %fusion.32.src_ref, s32[128]{0:T(128)S(1)} %fusion.33.dst_ref, s32[2]{0:T(128)S(1)} %fusion.31.live_ref, bf16[64,128,128]{2,1,0:T(8,128)(2,1)S(1)} %get-tuple-element.55.c_own, ...), custom_call_target="tpu_custom_call" | custom-call | flops 1048576 | bytes 1048576 | tf_op jit(solution)/shard_map/tiles_3/pallas_call | solution.py:104
  104.4 2.1 %collective-permute-start.26 = (bf16[4096,128]{1,0:T(8,128)(2,1)S(1)}, bf16[4096,128]{1,0:T(8,128)(2,1)S(1)}, u32[]{:S(2)}, u32[]{:S(2)}) collective-permute-start(bf16[4096,128]{1,0:T(8,128)(2,1)S(1)} %get-tuple-element.64), channel_id=1, source_target_pairs={{0,4},{1,13},{4,0},{5,9},{8,12},{9,5},{12,8},{13,1},{2,6},{3,15},{... | collective-permute-start | bytes 3145736 | tf_op jit(solution)/shard_map/sum_near_3/ppermute | solution.py:28
  107.6 2.6 %collective-permute-start.15 = (bf16[1056,128]{1,0:T(8,128)(2,1)S(1)}, bf16[1056,128]{1,0:T(8,128)(2,1)S(1)}, u32[]{:S(2)}, u32[]{:S(2)}) collective-permute-start(bf16[1056,128]{1,0:T(8,128)(2,1)S(1)} %fusion.4), channel_id=1, source_target_pairs={{0,2},{2,0},{1,3},{3,1},{4,6},{6,4},{5,7},{7,5},{8,10},{10,8},{9,1... | collective-permute-start | bytes 811016 | tf_op jit(solution)/shard_map/sum_x_0/ppermute | solution.py:18
  110.2 1.4 add_convert_fusion.3
  111.7 2.7 %collective-permute-done.15 = bf16[1056,128]{1,0:T(8,128)(2,1)S(1)} collective-permute-done((bf16[1056,128]{1,0:T(8,128)(2,1)S(1)}, bf16[1056,128]{1,0:T(8,128)(2,1)S(1)}, u32[]{:S(2)}, u32[]{:S(2)}) %collective-permute-start.15) | collective-permute-done | bytes 270368 | tf_op jit(solution)/shard_map/sum_x_0/ppermute | solution.py:18
  115.9 8.7 %collective-permute-start.16 = (bf16[512,128]{1,0:T(8,128)(2,1)S(1)}, bf16[512,128]{1,0:T(8,128)(2,1)S(1)}, u32[]{:S(2)}, u32[]{:S(2)}) collective-permute-start(bf16[512,128]{1,0:T(8,128)(2,1)S(1)} %bitcast.52), channel_id=1, source_target_pairs={{0,1},{1,0},{2,3},{3,2},{4,5},{5,4},{6,7},{7,6},{8,9},{9,8},{10,11... | collective-permute-start | bytes 393224 | tf_op jit(solution)/shard_map/mean_core_0/ppermute | solution.py:18
  124.7 1.4 fusion.19
  126.0 1.4 fusion.17
  127.5 1.2 collective-permute-start.19
  129.6 4.7 %collective-permute-done.19 = bf16[1024,128]{1,0:T(8,128)(2,1)S(1)} collective-permute-done((bf16[1024,128]{1,0:T(8,128)(2,1)S(1)}, bf16[1024,128]{1,0:T(8,128)(2,1)S(1)}, u32[]{:S(2)}, u32[]{:S(2)}) %collective-permute-start.19) | collective-permute-done | bytes 262176 | tf_op jit(solution)/shard_map/sum_x_1/ppermute | solution.py:18
  134.7 4.8 %collective-permute-start.20 = (bf16[512,128]{1,0:T(8,128)(2,1)S(1)}, bf16[512,128]{1,0:T(8,128)(2,1)S(1)}, u32[]{:S(2)}, u32[]{:S(2)}) collective-permute-start(bf16[512,128]{1,0:T(8,128)(2,1)S(1)} %bitcast.53), channel_id=1, source_target_pairs={{0,1},{1,0},{2,3},{3,2},{4,5},{5,4},{6,7},{7,6},{8,9},{9,8},{10,11... | collective-permute-start | bytes 393224 | tf_op jit(solution)/shard_map/mean_core_1/ppermute | solution.py:18
  139.4 1.4 fusion.15
  140.8 1.5 add_add_fusion.1
  142.4 2.6 %collective-permute-start.24 = (bf16[1024,128]{1,0:T(8,128)(2,1)S(1)}, bf16[1024,128]{1,0:T(8,128)(2,1)S(1)}, u32[]{:S(2)}, u32[]{:S(2)}) collective-permute-start(bf16[1024,128]{1,0:T(8,128)(2,1)S(1)} %fusion.8), channel_id=1, source_target_pairs={{0,2},{2,0},{1,3},{3,1},{4,6},{6,4},{5,7},{7,5},{8,10},{10,8},{9,1... | collective-permute-start | bytes 786440 | tf_op jit(solution)/shard_map/sum_x_2/ppermute | solution.py:18
  145.4 5.2 %collective-permute-done.24 = bf16[1024,128]{1,0:T(8,128)(2,1)S(1)} collective-permute-done((bf16[1024,128]{1,0:T(8,128)(2,1)S(1)}, bf16[1024,128]{1,0:T(8,128)(2,1)S(1)}, u32[]{:S(2)}, u32[]{:S(2)}) %collective-permute-start.24) | collective-permute-done | bytes 262176 | tf_op jit(solution)/shard_map/sum_x_2/ppermute | solution.py:18
  150.8 2.3 %collective-permute-start.25 = (bf16[512,128]{1,0:T(8,128)(2,1)S(1)}, bf16[512,128]{1,0:T(8,128)(2,1)S(1)}, u32[]{:S(2)}, u32[]{:S(2)}) collective-permute-start(bf16[512,128]{1,0:T(8,128)(2,1)S(1)} %bitcast.50), channel_id=1, source_target_pairs={{0,1},{1,0},{2,3},{3,2},{4,5},{5,4},{6,7},{7,6},{8,9},{9,8},{10,11... | collective-permute-start | bytes 393224 | tf_op jit(solution)/shard_map/mean_core_2/ppermute | solution.py:18
  153.7 2.0 %collective-permute-start.28 = (bf16[1024,128]{1,0:T(8,128)(2,1)S(1)}, bf16[1024,128]{1,0:T(8,128)(2,1)S(1)}, u32[]{:S(2)}, u32[]{:S(2)}) collective-permute-start(bf16[1024,128]{1,0:T(8,128)(2,1)S(1)} %fusion.6), channel_id=1, source_target_pairs={{0,2},{2,0},{1,3},{3,1},{4,6},{6,4},{5,7},{7,5},{8,10},{10,8},{9,1... | collective-permute-start | bytes 786440 | tf_op jit(solution)/shard_map/sum_x_3/ppermute | solution.py:18
  155.8 1.4 fusion.12
  157.2 3.4 %collective-permute-done.28 = bf16[1024,128]{1,0:T(8,128)(2,1)S(1)} collective-permute-done((bf16[1024,128]{1,0:T(8,128)(2,1)S(1)}, bf16[1024,128]{1,0:T(8,128)(2,1)S(1)}, u32[]{:S(2)}, u32[]{:S(2)}) %collective-permute-start.28) | collective-permute-done | bytes 262176 | tf_op jit(solution)/shard_map/sum_x_3/ppermute | solution.py:18
  160.9 3.8 %collective-permute-start.29 = (bf16[512,128]{1,0:T(8,128)(2,1)S(1)}, bf16[512,128]{1,0:T(8,128)(2,1)S(1)}, u32[]{:S(2)}, u32[]{:S(2)}) collective-permute-start(bf16[512,128]{1,0:T(8,128)(2,1)S(1)} %bitcast.51), channel_id=1, source_target_pairs={{0,1},{1,0},{2,3},{3,2},{4,5},{5,4},{6,7},{7,6},{8,9},{9,8},{10,11... | collective-permute-start | bytes 393224 | tf_op jit(solution)/shard_map/mean_core_3/ppermute | solution.py:18
  164.7 1.4 add_add_fusion.hidden
  166.0 2.8 %shard_map.102 = f32[512,1024]{1,0:T(8,128)} custom-call(f32[512,1024]{1,0:T(8,128)S(1)} %add_add_fusion.hidden, bf16[512,128]{1,0:T(8,128)(2,1)S(1)} %bitcast.39, bf16[512,128]{1,0:T(8,128)(2,1)S(1)} %collective-permute-done.29.got, bf16[256,1024]{1,0:T(8,128)(2,1)S(1)} %pad_maximum_fusion.4.weight), custom_call_target="tpu_custom_call" | custom-call | tf_op jit(solution)/shard_map/pallas_call | solution.py:193
  (129 shorter events, 21.3 us)
Async XLA Ops:
  0.0 5.8 %collective-permute-start = (bf16[512,1024]{1,0:T(8,128)(2,1)}, bf16[512,1024]{1,0:T(8,128)(2,1)S(1)}, u32[]{:S(2)}, u32[]{:S(2)}) collective-permute-start(bf16[512,1024]{1,0:T(8,128)(2,1)} %x_own.2), channel_id=1, source_target_pairs={{0,1},{1,0},{2,3},{3,2},{4,5},{5,4},{6,7},{7,6},{8,9},{9,8},{10,11... | collective-permute-start | bytes 3145736 | tf_op jit(solution)/shard_map/other_features_0/ppermute | solution.py:18
  2.0 3.7 %copy-start.10 = (bf16[1024,1024]{1,0:T(8,128)(2,1)S(1)}, bf16[1024,1024]{1,0:T(8,128)(2,1)}, u32[]{:S(2)}) copy-start(bf16[1024,1024]{1,0:T(8,128)(2,1)} %weight.3) | copy-start | bytes 6291460
  2.0 3.8 %copy-start.11 = (bf16[512,1024]{1,0:T(8,128)(2,1)S(1)}, bf16[512,1024]{1,0:T(8,128)(2,1)}, u32[]{:S(2)}) copy-start(bf16[512,1024]{1,0:T(8,128)(2,1)} %x_own.2) | copy-start | bytes 3145732
  2.0 3.8 %copy-start.16 = (f32[1024]{0:T(1024)S(1)}, f32[1024]{0:T(1024)}, u32[]{:S(2)}) copy-start(f32[1024]{0:T(1024)} %param.16) | copy-start | bytes 12292
  5.8 1.0 copy-start.14
  6.8 8.0 %collective-permute-start.2 = (bf16[8,128,128]{2,1,0:T(8,128)(2,1)S(1)}, bf16[8,128,128]{2,1,0:T(8,128)(2,1)S(1)}, u32[]{:S(2)}, u32[]{:S(2)}) collective-permute-start(bf16[8,128,128]{2,1,0:T(8,128)(2,1)S(1)} %shard_map.100), channel_id=1, source_target_pairs={{0,64},{64,0},{1,65},{65,1},{2,66},{66,2},{3,67},{67,3},{4,68},{68... | collective-permute-start | bytes 786440 | tf_op jit(solution)/shard_map/gather_x_0/ppermute | solution.py:18
  7.0 41.8 %collective-permute-start.7 = (bf16[64,128,128]{2,1,0:T(8,128)(2,1)S(1)}, bf16[64,128,128]{2,1,0:T(8,128)(2,1)}, u32[]{:S(2)}, u32[]{:S(2)}) collective-permute-start(bf16[64,128,128]{2,1,0:T(8,128)(2,1)S(1)} %get-tuple-element.55.c_own), channel_id=1, source_target_pairs={{0,1},{1,0},{2,3},{3,2},{4,5},{5,4},{6,7},{7,6},{8,9},{9,8},{10,11... | collective-permute-start | bytes 6291464 | tf_op jit(solution)/shard_map/other_tiles/ppermute | solution.py:18
  7.3 1.2 copy-start.15
  14.9 9.5 %collective-permute-start.4 = (bf16[16,128,128]{2,1,0:T(8,128)(2,1)S(1)}, bf16[16,128,128]{2,1,0:T(8,128)(2,1)}, u32[]{:S(2)}, u32[]{:S(2)}) collective-permute-start(bf16[16,128,128]{2,1,0:T(8,128)(2,1)S(1)} %pad_maximum_fusion), channel_id=1, source_target_pairs={{0,16},{1,49},{16,0},{17,33},{32,48},{33,17},{48,32},{49,1},{2,18}... | collective-permute-start | bytes 1572872 | tf_op jit(solution)/shard_map/gather_near_0/ppermute | solution.py:28
  18.0 1.2 collective-permute-start.1
  18.1 8.5 %collective-permute-start.3 = (bf16[8,128,128]{2,1,0:T(8,128)(2,1)S(1)}, bf16[8,128,128]{2,1,0:T(8,128)(2,1)}, u32[]{:S(2)}, u32[]{:S(2)}) collective-permute-start(bf16[8,128,128]{2,1,0:T(8,128)(2,1)S(1)} %get-tuple-element.48), channel_id=1, source_target_pairs={{0,64},{64,0},{1,65},{65,1},{2,66},{66,2},{3,67},{67,3},{4,68},{68... | collective-permute-start | bytes 786440 | tf_op jit(solution)/shard_map/gather_x_1/ppermute | solution.py:18
  26.2 20.4 %collective-permute-start.8 = (bf16[32,128,128]{2,1,0:T(8,128)(2,1)}, bf16[32,128,128]{2,1,0:T(8,128)(2,1)}, u32[]{:S(2)}, u32[]{:S(2)}) collective-permute-start(bf16[32,128,128]{2,1,0:T(8,128)(2,1)} %constant_dynamic-update-slice_fusion.near), channel_id=1, source_target_pairs={{0,48},{1,17},{16,32},{17,1},{32,16},{33,49},{48,0},{49,33},{2,50}... | collective-permute-start | bytes 3145736 | tf_op jit(solution)/shard_map/gather_far_0/ppermute | solution.py:28
  27.6 15.3 %collective-permute-start.6 = (bf16[16,128,128]{2,1,0:T(8,128)(2,1)S(1)}, bf16[16,128,128]{2,1,0:T(8,128)(2,1)}, u32[]{:S(2)}, u32[]{:S(2)}) collective-permute-start(bf16[16,128,128]{2,1,0:T(8,128)(2,1)S(1)} %pad_maximum_fusion.1), channel_id=1, source_target_pairs={{0,16},{1,49},{16,0},{17,33},{32,48},{33,17},{48,32},{49,1},{2,18}... | collective-permute-start | bytes 1572872 | tf_op jit(solution)/shard_map/gather_near_1/ppermute | solution.py:28
  30.0 14.6 %collective-permute-start.5 = (bf16[16,128,128]{2,1,0:T(8,128)(2,1)S(1)}, bf16[16,128,128]{2,1,0:T(8,128)(2,1)}, u32[]{:S(2)}, u32[]{:S(2)}) collective-permute-start(bf16[16,128,128]{2,1,0:T(8,128)(2,1)S(1)} %get-tuple-element.52), channel_id=1, source_target_pairs={{0,64},{64,0},{1,65},{65,1},{2,66},{66,2},{3,67},{67,3},{4,68},{68... | collective-permute-start | bytes 1572872 | tf_op jit(solution)/shard_map/gather_x_rest/ppermute | solution.py:18
  44.0 7.0 %copy-start.8 = (bf16[32,128,128]{2,1,0:T(8,128)(2,1)}, bf16[32,128,128]{2,1,0:T(8,128)(2,1)S(1)}, u32[]{:S(2)}) copy-start(bf16[32,128,128]{2,1,0:T(8,128)(2,1)S(1)} %constant_dynamic-update-slice_fusion.2.near) | copy-start | bytes 3145732
  44.0 19.2 %collective-permute-start.11 = (bf16[32,128,128]{2,1,0:T(8,128)(2,1)S(1)}, bf16[32,128,128]{2,1,0:T(8,128)(2,1)S(1)}, u32[]{:S(2)}, u32[]{:S(2)}) collective-permute-start(bf16[32,128,128]{2,1,0:T(8,128)(2,1)S(1)} %constant_dynamic-update-slice_fusion.2.near), channel_id=1, source_target_pairs={{0,48},{1,17},{16,32},{17,1},{32,16},{33,49},{48,0},{49,33},{2,50}... | collective-permute-start | bytes 3145736 | tf_op jit(solution)/shard_map/gather_far_1/ppermute | solution.py:28
  46.7 16.4 %collective-permute-start.10 = (bf16[16,128,128]{2,1,0:T(8,128)(2,1)S(1)}, bf16[16,128,128]{2,1,0:T(8,128)(2,1)S(1)}, u32[]{:S(2)}, u32[]{:S(2)}) collective-permute-start(bf16[16,128,128]{2,1,0:T(8,128)(2,1)S(1)} %pad_maximum_fusion.2), channel_id=1, source_target_pairs={{0,16},{1,49},{16,0},{17,33},{32,48},{33,17},{48,32},{49,1},{2,18}... | collective-permute-start | bytes 1572872 | tf_op jit(solution)/shard_map/gather_near_2/ppermute | solution.py:28
  51.4 10.8 %copy-start.18 = (bf16[8,128,128]{2,1,0:T(8,128)(2,1)S(1)}, bf16[8,128,128]{2,1,0:T(8,128)(2,1)}, u32[]{:S(2)}) copy-start(bf16[8,128,128]{2,1,0:T(8,128)(2,1)} %get-tuple-element.97) | copy-start | bytes 786436
  58.9 4.3 %copy-start = (bf16[2112,128]{1,0:T(8,128)(2,1)}, bf16[2112,128]{1,0:T(8,128)(2,1)S(1)}, u32[]{:S(2)}) copy-start(bf16[2112,128]{1,0:T(8,128)(2,1)S(1)} %get-tuple-element.61) | copy-start | bytes 1622020
  58.9 25.5 %collective-permute-start.9 = (bf16[4224,128]{1,0:T(8,128)(2,1)}, bf16[4224,128]{1,0:T(8,128)(2,1)}, u32[]{:S(2)}, u32[]{:S(2)}) collective-permute-start(bf16[4224,128]{1,0:T(8,128)(2,1)} %get-tuple-element.56), channel_id=1, source_target_pairs={{0,4},{1,13},{4,0},{5,9},{8,12},{9,5},{12,8},{13,1},{2,6},{3,15},{... | collective-permute-start | bytes 3244040 | tf_op jit(solution)/shard_map/sum_near_0/ppermute | solution.py:28
  64.3 16.3 %collective-permute-start.13 = (bf16[16,128,128]{2,1,0:T(8,128)(2,1)}, bf16[16,128,128]{2,1,0:T(8,128)(2,1)}, u32[]{:S(2)}, u32[]{:S(2)}) collective-permute-start(bf16[16,128,128]{2,1,0:T(8,128)(2,1)} %pad_maximum_fusion.3), channel_id=1, source_target_pairs={{0,16},{1,49},{16,0},{17,33},{32,48},{33,17},{48,32},{49,1},{2,18}... | collective-permute-start | bytes 1572872 | tf_op jit(solution)/shard_map/gather_near_3/ppermute | solution.py:28
  65.7 27.3 %collective-permute-start.21 = (bf16[32,128,128]{2,1,0:T(8,128)(2,1)S(1)}, bf16[32,128,128]{2,1,0:T(8,128)(2,1)}, u32[]{:S(2)}, u32[]{:S(2)}) collective-permute-start(bf16[32,128,128]{2,1,0:T(8,128)(2,1)S(1)} %constant_dynamic-update-slice_fusion.4.near), channel_id=1, source_target_pairs={{0,48},{1,17},{16,32},{17,1},{32,16},{33,49},{48,0},{49,33},{2,50}... | collective-permute-start | bytes 3145736 | tf_op jit(solution)/shard_map/gather_far_2/ppermute | solution.py:28
  66.7 1.2 copy-start.9
  67.9 1.2 copy-start.13
  75.6 11.4 %copy-start.4 = (bf16[2048,128]{1,0:T(8,128)(2,1)}, bf16[2048,128]{1,0:T(8,128)(2,1)S(1)}, u32[]{:S(2)}) copy-start(bf16[2048,128]{1,0:T(8,128)(2,1)S(1)} %get-tuple-element.69) | copy-start | bytes 1572868
  75.6 8.8 %copy-start.1 = (bf16[2112,128]{1,0:T(8,128)(2,1)S(1)}, bf16[2112,128]{1,0:T(8,128)(2,1)}, u32[]{:S(2)}) copy-start(bf16[2112,128]{1,0:T(8,128)(2,1)} %copy-done) | copy-start | bytes 1622020
  75.6 8.8 %copy-start.3 = (bf16[2112,128]{1,0:T(8,128)(2,1)S(1)}, bf16[2112,128]{1,0:T(8,128)(2,1)}, u32[]{:S(2)}) copy-start(bf16[2112,128]{1,0:T(8,128)(2,1)} %copy-done.2) | copy-start | bytes 1622020
  75.6 30.9 %collective-permute-start.17 = (bf16[4096,128]{1,0:T(8,128)(2,1)}, bf16[4096,128]{1,0:T(8,128)(2,1)}, u32[]{:S(2)}, u32[]{:S(2)}) collective-permute-start(bf16[4096,128]{1,0:T(8,128)(2,1)} %get-tuple-element.59), channel_id=1, source_target_pairs={{0,4},{1,13},{4,0},{5,9},{8,12},{9,5},{12,8},{13,1},{2,6},{3,15},{... | collective-permute-start | bytes 3145736 | tf_op jit(solution)/shard_map/sum_near_1/ppermute | solution.py:28
  82.5 16.1 %collective-permute-start.14 = (bf16[32,128,128]{2,1,0:T(8,128)(2,1)}, bf16[32,128,128]{2,1,0:T(8,128)(2,1)}, u32[]{:S(2)}, u32[]{:S(2)}) collective-permute-start(bf16[32,128,128]{2,1,0:T(8,128)(2,1)} %constant_dynamic-update-slice_fusion.6.near), channel_id=1, source_target_pairs={{0,48},{1,17},{16,32},{17,1},{32,16},{33,49},{48,0},{49,33},{2,50}... | collective-permute-start | bytes 3145736 | tf_op jit(solution)/shard_map/gather_far_3/ppermute | solution.py:28
  87.1 19.5 %collective-permute-start.12 = (bf16[2112,128]{1,0:T(8,128)(2,1)}, bf16[2112,128]{1,0:T(8,128)(2,1)}, u32[]{:S(2)}, u32[]{:S(2)}) collective-permute-start(bf16[2112,128]{1,0:T(8,128)(2,1)} %get-tuple-element.90), channel_id=1, source_target_pairs={{0,12},{1,5},{4,8},{5,1},{8,4},{9,13},{12,0},{13,9},{2,14},{3,7},{... | collective-permute-start | bytes 1622024 | tf_op jit(solution)/shard_map/sum_far_0/ppermute | solution.py:28
  98.5 8.1 %copy-start.17 = (f32[2112,128]{1,0:T(8,128)S(1)}, f32[2112,128]{1,0:T(8,128)}, u32[]{:S(2)}) copy-start(f32[2112,128]{1,0:T(8,128)} %get-tuple-element.89) | copy-start | bytes 3244036
  98.5 11.7 %copy-start.5 = (bf16[2048,128]{1,0:T(8,128)(2,1)S(1)}, bf16[2048,128]{1,0:T(8,128)(2,1)}, u32[]{:S(2)}) copy-start(bf16[2048,128]{1,0:T(8,128)(2,1)} %copy-done.4) | copy-start | bytes 1572868
  98.5 11.7 %copy-start.7 = (bf16[2048,128]{1,0:T(8,128)(2,1)S(1)}, bf16[2048,128]{1,0:T(8,128)(2,1)}, u32[]{:S(2)}) copy-start(bf16[2048,128]{1,0:T(8,128)(2,1)} %copy-done.6) | copy-start | bytes 1572868
  98.5 30.3 %collective-permute-start.22 = (bf16[4096,128]{1,0:T(8,128)(2,1)S(1)}, bf16[4096,128]{1,0:T(8,128)(2,1)S(1)}, u32[]{:S(2)}, u32[]{:S(2)}) collective-permute-start(bf16[4096,128]{1,0:T(8,128)(2,1)S(1)} %get-tuple-element.73), channel_id=1, source_target_pairs={{0,4},{1,13},{4,0},{5,9},{8,12},{9,5},{12,8},{13,1},{2,6},{3,15},{... | collective-permute-start | bytes 3145736 | tf_op jit(solution)/shard_map/sum_near_2/ppermute | solution.py:28
  104.4 37.9 %collective-permute-start.26 = (bf16[4096,128]{1,0:T(8,128)(2,1)S(1)}, bf16[4096,128]{1,0:T(8,128)(2,1)S(1)}, u32[]{:S(2)}, u32[]{:S(2)}) collective-permute-start(bf16[4096,128]{1,0:T(8,128)(2,1)S(1)} %get-tuple-element.64), channel_id=1, source_target_pairs={{0,4},{1,13},{4,0},{5,9},{8,12},{9,5},{12,8},{13,1},{2,6},{3,15},{... | collective-permute-start | bytes 3145736 | tf_op jit(solution)/shard_map/sum_near_3/ppermute | solution.py:28
  107.6 6.9 %collective-permute-start.15 = (bf16[1056,128]{1,0:T(8,128)(2,1)S(1)}, bf16[1056,128]{1,0:T(8,128)(2,1)S(1)}, u32[]{:S(2)}, u32[]{:S(2)}) collective-permute-start(bf16[1056,128]{1,0:T(8,128)(2,1)S(1)} %fusion.4), channel_id=1, source_target_pairs={{0,2},{2,0},{1,3},{3,1},{4,6},{6,4},{5,7},{7,5},{8,10},{10,8},{9,1... | collective-permute-start | bytes 811016 | tf_op jit(solution)/shard_map/sum_x_0/ppermute | solution.py:18
  111.6 3.9 %copy-start.20 = (f32[4]{0:T(128)S(1)}, f32[4]{0:T(128)}, u32[]{:S(2)}) copy-start(f32[4]{0:T(128)} %constant.140.clone) | copy-start | bytes 52
  111.6 15.8 %collective-permute-start.18 = (bf16[2048,128]{1,0:T(8,128)(2,1)S(1)}, bf16[2048,128]{1,0:T(8,128)(2,1)S(1)}, u32[]{:S(2)}, u32[]{:S(2)}) collective-permute-start(bf16[2048,128]{1,0:T(8,128)(2,1)S(1)} %get-tuple-element.95), channel_id=1, source_target_pairs={{0,12},{1,5},{4,8},{5,1},{8,4},{9,13},{12,0},{13,9},{2,14},{3,7},{... | collective-permute-start | bytes 1572872 | tf_op jit(solution)/shard_map/sum_far_1/ppermute | solution.py:28
  115.9 10.1 %collective-permute-start.16 = (bf16[512,128]{1,0:T(8,128)(2,1)S(1)}, bf16[512,128]{1,0:T(8,128)(2,1)S(1)}, u32[]{:S(2)}, u32[]{:S(2)}) collective-permute-start(bf16[512,128]{1,0:T(8,128)(2,1)S(1)} %bitcast.52), channel_id=1, source_target_pairs={{0,1},{1,0},{2,3},{3,2},{4,5},{5,4},{6,7},{7,6},{8,9},{9,8},{10,11... | collective-permute-start | bytes 393224 | tf_op jit(solution)/shard_map/mean_core_0/ppermute | solution.py:18
  127.5 6.8 %collective-permute-start.19 = (bf16[1024,128]{1,0:T(8,128)(2,1)S(1)}, bf16[1024,128]{1,0:T(8,128)(2,1)S(1)}, u32[]{:S(2)}, u32[]{:S(2)}) collective-permute-start(bf16[1024,128]{1,0:T(8,128)(2,1)S(1)} %fusion.10), channel_id=1, source_target_pairs={{0,2},{2,0},{1,3},{3,1},{4,6},{6,4},{5,7},{7,5},{8,10},{10,8},{9,1... | collective-permute-start | bytes 786440 | tf_op jit(solution)/shard_map/sum_x_1/ppermute | solution.py:18
  129.0 13.4 %collective-permute-start.23 = (bf16[2048,128]{1,0:T(8,128)(2,1)S(1)}, bf16[2048,128]{1,0:T(8,128)(2,1)S(1)}, u32[]{:S(2)}, u32[]{:S(2)}) collective-permute-start(bf16[2048,128]{1,0:T(8,128)(2,1)S(1)} %get-tuple-element.93), channel_id=1, source_target_pairs={{0,12},{1,5},{4,8},{5,1},{8,4},{9,13},{12,0},{13,9},{2,14},{3,7},{... | collective-permute-start | bytes 1572872 | tf_op jit(solution)/shard_map/sum_far_2/ppermute | solution.py:28
  134.4 6.4 %copy-start.19 = (f32[1024]{0:T(1024)S(1)}, f32[1024]{0:T(1024)}, u32[]{:S(2)}) copy-start(f32[1024]{0:T(1024)} %param.18) | copy-start | bytes 12292
  134.7 6.1 %collective-permute-start.20 = (bf16[512,128]{1,0:T(8,128)(2,1)S(1)}, bf16[512,128]{1,0:T(8,128)(2,1)S(1)}, u32[]{:S(2)}, u32[]{:S(2)}) collective-permute-start(bf16[512,128]{1,0:T(8,128)(2,1)S(1)} %bitcast.53), channel_id=1, source_target_pairs={{0,1},{1,0},{2,3},{3,2},{4,5},{5,4},{6,7},{7,6},{8,9},{9,8},{10,11... | collective-permute-start | bytes 393224 | tf_op jit(solution)/shard_map/mean_core_1/ppermute | solution.py:18
  142.4 8.1 %collective-permute-start.24 = (bf16[1024,128]{1,0:T(8,128)(2,1)S(1)}, bf16[1024,128]{1,0:T(8,128)(2,1)S(1)}, u32[]{:S(2)}, u32[]{:S(2)}) collective-permute-start(bf16[1024,128]{1,0:T(8,128)(2,1)S(1)} %fusion.8), channel_id=1, source_target_pairs={{0,2},{2,0},{1,3},{3,1},{4,6},{6,4},{5,7},{7,5},{8,10},{10,8},{9,1... | collective-permute-start | bytes 786440 | tf_op jit(solution)/shard_map/sum_x_2/ppermute | solution.py:18
  145.3 8.4 %collective-permute-start.27 = (bf16[2048,128]{1,0:T(8,128)(2,1)S(1)}, bf16[2048,128]{1,0:T(8,128)(2,1)S(1)}, u32[]{:S(2)}, u32[]{:S(2)}) collective-permute-start(bf16[2048,128]{1,0:T(8,128)(2,1)S(1)} %get-tuple-element.91), channel_id=1, source_target_pairs={{0,12},{1,5},{4,8},{5,1},{8,4},{9,13},{12,0},{13,9},{2,14},{3,7},{... | collective-permute-start | bytes 1572872 | tf_op jit(solution)/shard_map/sum_far_3/ppermute | solution.py:28
  150.8 13.8 %collective-permute-start.25 = (bf16[512,128]{1,0:T(8,128)(2,1)S(1)}, bf16[512,128]{1,0:T(8,128)(2,1)S(1)}, u32[]{:S(2)}, u32[]{:S(2)}) collective-permute-start(bf16[512,128]{1,0:T(8,128)(2,1)S(1)} %bitcast.50), channel_id=1, source_target_pairs={{0,1},{1,0},{2,3},{3,2},{4,5},{5,4},{6,7},{7,6},{8,9},{9,8},{10,11... | collective-permute-start | bytes 393224 | tf_op jit(solution)/shard_map/mean_core_2/ppermute | solution.py:18
  153.7 6.8 %collective-permute-start.28 = (bf16[1024,128]{1,0:T(8,128)(2,1)S(1)}, bf16[1024,128]{1,0:T(8,128)(2,1)S(1)}, u32[]{:S(2)}, u32[]{:S(2)}) collective-permute-start(bf16[1024,128]{1,0:T(8,128)(2,1)S(1)} %fusion.6), channel_id=1, source_target_pairs={{0,2},{2,0},{1,3},{3,1},{4,6},{6,4},{5,7},{7,5},{8,10},{10,8},{9,1... | collective-permute-start | bytes 786440 | tf_op jit(solution)/shard_map/sum_x_3/ppermute | solution.py:18
  160.9 5.2 %collective-permute-start.29 = (bf16[512,128]{1,0:T(8,128)(2,1)S(1)}, bf16[512,128]{1,0:T(8,128)(2,1)S(1)}, u32[]{:S(2)}, u32[]{:S(2)}) collective-permute-start(bf16[512,128]{1,0:T(8,128)(2,1)S(1)} %bitcast.51), channel_id=1, source_target_pairs={{0,1},{1,0},{2,3},{3,2},{4,5},{5,4},{6,7},{7,6},{8,9},{9,8},{10,11... | collective-permute-start | bytes 393224 | tf_op jit(solution)/shard_map/mean_core_3/ppermute | solution.py:18
  (3 other events, 2.6 us)

commit v9 on v8

--- a/solution.py
+++ b/solution.py
@@ -41,20 +41,11 @@
 
 
 def tile_kernel(src_ref, dst_ref, live_ref, c_own, c_other, pieces_ref, near, far, *refs):
-    send, pass_on, stay, panel, acc, sems = refs
-    copies = [
-        pltpu.make_async_copy(near, panel.at[pl.ds(0, 32)], sems.at[0]),
-        pltpu.make_async_copy(far, panel.at[pl.ds(32, 32)], sems.at[1]),
-    ]
-    for copy in copies:
-        copy.start()
+    send, pass_on, stay, acc = refs
 
     @pl.loop(0, 64)
     def _(i):
         acc[i] = jnp.zeros(acc.shape[1:], jnp.float32)
-
-    for copy in copies:
-        copy.wait()
 
     slots, tile = c_own.shape[:2]
     for q, counts in enumerate((c_own, c_other)):
@@ -63,13 +54,9 @@
             terms = []
             for i in range(GROUP):
                 s = g * GROUP + i
-                terms.append(
-                    jnp.dot(
-                        counts[s],
-                        panel[src_ref[q * slots + s]],
-                        preferred_element_type=jnp.float32,
-                    )
-                )
+                at = src_ref[q * slots + s]
+                block = lax.select(at < 32, near[at & 31], far[at & 31])
+                terms.append(jnp.dot(counts[s], block, preferred_element_type=jnp.float32))
             for i in range(GROUP):
                 at = dst_ref[q * slots + g * GROUP + i]
                 acc[at] = acc[at] + terms[i]
@@ -96,7 +83,6 @@
 
 def tile_sums(src, dst, live, c_own, c_other, pieces, with_pieces, near, far, cost):
     tile, w = near.shape[-2:]
-    any_spec = pl.BlockSpec(memory_space=pl.ANY)
     vmem = pl.BlockSpec(memory_space=pltpu.VMEM)
     smem = pl.BlockSpec(memory_space=pltpu.SMEM)
     slots = c_own.shape[0]
@@ -108,14 +94,10 @@
             jax.ShapeDtypeStruct((2 * size, w), jnp.bfloat16),
             jax.ShapeDtypeStruct((2 * size, w), jnp.bfloat16),
         ),
-        in_specs=[smem] * 3 + [vmem] * 3 + [any_spec] * 2,
+        in_specs=[smem] * 3 + [vmem] * 5,
         out_specs=(vmem,) * 3,
-        scratch_shapes=[
-            pltpu.VMEM((64, tile, w), jnp.bfloat16),
-            pltpu.VMEM((64, tile, w), jnp.float32),
-            pltpu.SemaphoreType.DMA((2,)),
-        ],
-        compiler_params=pltpu.CompilerParams(vmem_limit_bytes=16 * 1024 * 1024),
+        scratch_shapes=[pltpu.VMEM((64, tile, w), jnp.float32)],
+        compiler_params=pltpu.CompilerParams(vmem_limit_bytes=48 * 1024 * 1024),
         cost_estimate=pl.CostEstimate(
             flops=cost, bytes_accessed=64 * tile * w, transcendentals=0
         ),
@@ -305,8 +287,11 @@
         pair = after(pair, near_all[j - 1], *far_all[: j - 1])
         far(pair, step(pair, "y", 0, f"gather_near_{j}"), j)
 
+    last = slice((CHUNKS - 1) * cw, CHUNKS * cw)
+    last_weight = jnp.concatenate([w_own[last], w_other[last]])
+
     def tiles(j):
-        earlier = (rest, near_all[1]) if j == 0 else ()
+        earlier = (rest, near_all[1], hidden, last_weight) if j == 0 else ()
         if 0 < j < CHUNKS - 1:
             earlier += (near_all[j + 1],)
         if j >= 2:
@@ -364,8 +349,7 @@
         got = swap(mean[1], "core", f"mean_core_{j}")
         cols = slice(j * cw, (j + 1) * cw)
         if j == CHUNKS - 1:
-            weight = jnp.concatenate([w_own[cols], w_other[cols]])
-            return finish(hidden, mean[0], got, weight)
+            return finish(hidden, mean[0], got, last_weight)
         hidden = hidden + jnp.dot(mean[0], w_own[cols], preferred_element_type=f32)
         hidden = hidden + jnp.dot(got, w_other[cols], preferred_element_type=f32)
         hidden_all.append(hidden)

time: 171 us -> 169 us (0.988)
  waiting for transfers between devices: 37.4 us -> 64.8 us
  starting transfers between devices: 51.9 us -> 37.9 us
  local copies, waits for them, and re-layouts: 18.4 us -> 5.81 us
  other arithmetic: 18.7 us -> 15.4 us
    ppermute x14, starting transfers between devices: 29.9 us -> 12.5 us  [swap(): return lax.ppermute(x, axis, [(0, 1), (1, 0)])]
    ppermute x16, waiting for transfers between devices: 17.2 us -> 32.6 us  [step(): return lax.ppermute(x, (axis, 'core'), pairs)]
    ppermute x14, waiting for transfers between devices: 20.2 us -> 32.2 us  [swap(): return lax.ppermute(x, axis, [(0, 1), (1, 0)])]
    unnamed x46 -> x24, local copies, waits for them, and re-layouts: 9.17 us -> 1 us
    ppermute x16, starting transfers between devices: 22 us -> 25.4 us  [step(): return lax.ppermute(x, (axis, 'core'), pairs)]
    concatenate x4, local copies, waits for them, and re-layouts: 5.02 us -> 2.39 us  [far(): near_all.append(jnp.concatenate([pair, got]))]
    concatenate x3, other arithmetic: 2.83 us -> 1.09 us  [local(): pair = jnp.concatenate([own[j], partner[j]])]
  transfers between devices with their start and end apart: 30 -> 30, of which waited for: 9 -> 14; matrix products, arithmetic and copies ran while one was open for 25% -> 19% of each run, Pallas kernels for 15% -> 16%
where the time goes in v9:
time: 169 us; the launch traced here: 168 us
  waiting for transfers between devices  64.8 us (38%)
  starting transfers between devices  37.9 us (22%)
  Pallas kernels  31.2 us (18%)
  other arithmetic  15.4 us (9%)
  matrix products  11.4 us (7%)
  local copies, waits for them, and re-layouts  5.81 us (3%)
    ppermute x16, waiting for transfers between devices, step(): return lax.ppermute(x, (axis, 'core'), pairs)  32.6 us
    ppermute x14, waiting for transfers between devices, swap(): return lax.ppermute(x, axis, [(0, 1), (1, 0)])  32.2 us
    ppermute x16, starting transfers between devices, step(): return lax.ppermute(x, (axis, 'core'), pairs)  25.4 us
    pallas_call x4, Pallas kernels, tile_sums(): pl.pallas_call(tile_kernel, out_shape=(jax.ShapeDtypeStruct((4 * size, w)...  25.3 us
    ppermute x14, starting transfers between devices, swap(): return lax.ppermute(x, axis, [(0, 1), (1, 0)])  12.5 us
    dot_general x3, matrix products, local(): hidden = hidden + jnp.dot(got, w_other[cols], preferred_element_type=f32)  4.35 us
    reduce_sum x1, other arithmetic, local(): jnp.sum(c_own.astype(jnp.float32), axis=2)  4.3 us
    dot_general x3, matrix products, local(): hidden = hidden + jnp.dot(mean[0], w_own[cols], preferred_element_type=f32)  4.27 us
  transfers between devices with their start and end apart: 30, of which 14 were waited for; matrix products, arithmetic and copies ran while one was open for 19% of the time, Pallas kernels for 16%

profile of v9, /device:TPU:3, one launch (start us, length us, event | category | flops | bytes accessed | tf_op | source)
XLA Modules:
  0.0 167.7 jit_solution(10679662720924798058)
XLA Ops:
  2.0 1.1 constant_dynamic-slice_fusion.1
  3.2 4.3 %convert_reduce_fusion.1 = (f32[64,128]{1,0:T(8,128)S(1)}, bf16[64,128,128]{2,1,0:T(8,128)(2,1)}) fusion(s32[1,1,64,128,128]{4,3,2,1,0:T(8,128)} %param.11, pred[64]{0:T(512)(128)(4,1)S(1)} %iota_compare_fusion.2), kind=kLoop, calls=%fused_computation.3 | loop fusion | flops 4186112 | bytes 6324288 | tf_op jit(solution)/shard_map/reduce_sum | solution.py:255
  7.5 2.6 %fusion.3 = f32[512,1024]{1,0:T(8,128)} fusion(bf16[512,1024]{1,0:T(8,128)(2,1)S(1)} %copy-done.3, bf16[2048,1024]{1,0:T(8,128)(2,1)S(1)} %copy-done.7, f32[1024]{0:T(1024)S(1)} %copy-done.9), kind=kOutput, calls=%fused_computation.8 | convolution fusion | flops 1074266112 | bytes 5246976 | tf_op jit(solution)/shard_map/dot_general | solution.py:263
  11.7 2.1 %shard_map.101 = (bf16[8,128,128]{2,1,0:T(8,128)(2,1)S(1)}, bf16[16,128,128]{2,1,0:T(8,128)(2,1)S(1)}) custom-call(s32[1]{0:T(128)} %bitcast.4.core_ref, bf16[512,1024]{1,0:T(8,128)(2,1)S(1)} %copy-done.3, bf16[512,1024]{1,0:T(8,128)(2,1)S(1)} %collective-permute-done.x_other, bf16[1024,1024]{1,0:T(8,128)(2,1)S(1)} %copy-done.2, f32[1,1024]{1,0:T(1,128)S(1)} %bitcast.41), custom_call_target="tpu_custom_call" | custom-call | flops 6442450944 | bytes 2883584 | tf_op jit(solution)/shard_map/pallas_call | solution.py:141
  13.7 5.4 %collective-permute-done.2 = bf16[8,128,128]{2,1,0:T(8,128)(2,1)S(1)} collective-permute-done((bf16[8,128,128]{2,1,0:T(8,128)(2,1)S(1)}, bf16[8,128,128]{2,1,0:T(8,128)(2,1)S(1)}, u32[]{:S(2)}, u32[]{:S(2)}) %collective-permute-start.2) | collective-permute-done | bytes 262176 | tf_op jit(solution)/shard_map/gather_x_0/ppermute | solution.py:18
  19.2 2.8 %collective-permute-start.4 = (bf16[16,128,128]{2,1,0:T(8,128)(2,1)S(1)}, bf16[16,128,128]{2,1,0:T(8,128)(2,1)}, u32[]{:S(2)}, u32[]{:S(2)}) collective-permute-start(bf16[16,128,128]{2,1,0:T(8,128)(2,1)S(1)} %pad_maximum_fusion), channel_id=1, source_target_pairs={{0,16},{1,49},{16,0},{17,33},{32,48},{33,17},{48,32},{49,1},{2,18}... | collective-permute-start | bytes 1572872 | tf_op jit(solution)/shard_map/gather_near_0/ppermute | solution.py:28
  23.7 5.0 %collective-permute-done.4 = bf16[16,128,128]{2,1,0:T(8,128)(2,1)} collective-permute-done((bf16[16,128,128]{2,1,0:T(8,128)(2,1)S(1)}, bf16[16,128,128]{2,1,0:T(8,128)(2,1)}, u32[]{:S(2)}, u32[]{:S(2)}) %collective-permute-start.4) | collective-permute-done | bytes 524320 | tf_op jit(solution)/shard_map/gather_near_0/ppermute | solution.py:28
  28.7 1.1 constant_dynamic-update-slice_fusion.near
  30.2 2.5 %collective-permute-start.6 = (bf16[16,128,128]{2,1,0:T(8,128)(2,1)S(1)}, bf16[16,128,128]{2,1,0:T(8,128)(2,1)}, u32[]{:S(2)}, u32[]{:S(2)}) collective-permute-start(bf16[16,128,128]{2,1,0:T(8,128)(2,1)S(1)} %pad_maximum_fusion.1), channel_id=1, source_target_pairs={{0,16},{1,49},{16,0},{17,33},{32,48},{33,17},{48,32},{49,1},{2,18}... | collective-permute-start | bytes 1572872 | tf_op jit(solution)/shard_map/gather_near_1/ppermute | solution.py:28
  33.3 11.7 %collective-permute-done.6 = bf16[16,128,128]{2,1,0:T(8,128)(2,1)} collective-permute-done((bf16[16,128,128]{2,1,0:T(8,128)(2,1)S(1)}, bf16[16,128,128]{2,1,0:T(8,128)(2,1)}, u32[]{:S(2)}, u32[]{:S(2)}) %collective-permute-start.6) | collective-permute-done | bytes 524320 | tf_op jit(solution)/shard_map/gather_near_1/ppermute | solution.py:28
  45.0 1.1 constant_dynamic-update-slice_fusion.2.near
  46.1 1.0 collective-permute-start.11
  48.2 1.4 collective-permute-done.8.far
  49.5 2.7 %collective-permute-start.10 = (bf16[16,128,128]{2,1,0:T(8,128)(2,1)S(1)}, bf16[16,128,128]{2,1,0:T(8,128)(2,1)S(1)}, u32[]{:S(2)}, u32[]{:S(2)}) collective-permute-start(bf16[16,128,128]{2,1,0:T(8,128)(2,1)S(1)} %pad_maximum_fusion.3), channel_id=1, source_target_pairs={{0,16},{1,49},{16,0},{17,33},{32,48},{33,17},{48,32},{49,1},{2,18}... | collective-permute-start | bytes 1572872 | tf_op jit(solution)/shard_map/gather_near_2/ppermute | solution.py:28
  52.2 2.2 %convert_reduce_fusion = f32[64,128]{1,0:T(8,128)S(1)} fusion(bf16[64,128,128]{2,1,0:T(8,128)(2,1)} %collective-permute-done.7.c_other), kind=kLoop, calls=%fused_computation.2 | loop fusion | flops 2088960 | bytes 2129920 | tf_op jit(solution)/shard_map/reduce_sum | solution.py:255
  54.7 6.1 %tiles_0.1 = (bf16[4224,128]{1,0:T(8,128)(2,1)S(1)}, bf16[2112,128]{1,0:T(8,128)(2,1)S(1)}, bf16[2112,128]{1,0:T(8,128)(2,1)S(1)}) custom-call(s32[128]{0:T(128)S(1)} %fusion.35.src_ref, s32[128]{0:T(128)S(1)} %fusion.36.dst_ref, s32[2]{0:T(128)S(1)} %fusion.34.live_ref, bf16[64,128,128]{2,1,0:T(8,128)(2,1)} %get-tuple-element.55.c_own, ...), custom_call_target="tpu_custom_call" | custom-call | flops 2147483648 | bytes 1048576 | tf_op jit(solution)/shard_map/tiles_0/pallas_call | solution.py:90
  60.9 2.4 %collective-permute-start.9 = (bf16[4224,128]{1,0:T(8,128)(2,1)S(1)}, bf16[4224,128]{1,0:T(8,128)(2,1)S(1)}, u32[]{:S(2)}, u32[]{:S(2)}) collective-permute-start(bf16[4224,128]{1,0:T(8,128)(2,1)S(1)} %get-tuple-element.56), channel_id=1, source_target_pairs={{0,4},{1,13},{4,0},{5,9},{8,12},{9,5},{12,8},{13,1},{2,6},{3,15},{... | collective-permute-start | bytes 3244040 | tf_op jit(solution)/shard_map/sum_near_0/ppermute | solution.py:28
  64.1 2.2 %collective-permute-done.11.far = bf16[32,128,128]{2,1,0:T(8,128)(2,1)S(1)} collective-permute-done((bf16[32,128,128]{2,1,0:T(8,128)(2,1)S(1)}, bf16[32,128,128]{2,1,0:T(8,128)(2,1)S(1)}, u32[]{:S(2)}, u32[]{:S(2)}) %collective-permute-start.11) | collective-permute-done | bytes 1048608 | tf_op jit(solution)/shard_map/gather_far_1/ppermute | solution.py:28
  66.3 2.7 %collective-permute-start.13 = (bf16[16,128,128]{2,1,0:T(8,128)(2,1)S(1)}, bf16[16,128,128]{2,1,0:T(8,128)(2,1)S(1)}, u32[]{:S(2)}, u32[]{:S(2)}) collective-permute-start(bf16[16,128,128]{2,1,0:T(8,128)(2,1)S(1)} %pad_maximum_fusion.4), channel_id=1, source_target_pairs={{0,16},{1,49},{16,0},{17,33},{32,48},{33,17},{48,32},{49,1},{2,18}... | collective-permute-start | bytes 1572872 | tf_op jit(solution)/shard_map/gather_near_3/ppermute | solution.py:28
  69.0 6.9 %tiles_1.1 = (bf16[4096,128]{1,0:T(8,128)(2,1)}, bf16[2048,128]{1,0:T(8,128)(2,1)S(1)}, bf16[2048,128]{1,0:T(8,128)(2,1)S(1)}) custom-call(s32[128]{0:T(128)S(1)} %fusion.35.src_ref, s32[128]{0:T(128)S(1)} %fusion.36.dst_ref, s32[2]{0:T(128)S(1)} %fusion.34.live_ref, bf16[64,128,128]{2,1,0:T(8,128)(2,1)} %get-tuple-element.55.c_own, ...), custom_call_target="tpu_custom_call" | custom-call | flops 2147483648 | bytes 1048576 | tf_op jit(solution)/shard_map/tiles_1/pallas_call | solution.py:90
  76.7 2.3 %collective-permute-start.17 = (bf16[4096,128]{1,0:T(8,128)(2,1)}, bf16[4096,128]{1,0:T(8,128)(2,1)}, u32[]{:S(2)}, u32[]{:S(2)}) collective-permute-start(bf16[4096,128]{1,0:T(8,128)(2,1)} %get-tuple-element.59), channel_id=1, source_target_pairs={{0,4},{1,13},{4,0},{5,9},{8,12},{9,5},{12,8},{13,1},{2,6},{3,15},{... | collective-permute-start | bytes 3145736 | tf_op jit(solution)/shard_map/sum_near_1/ppermute | solution.py:28
  79.1 2.8 %collective-permute-start.14 = (bf16[32,128,128]{2,1,0:T(8,128)(2,1)S(1)}, bf16[32,128,128]{2,1,0:T(8,128)(2,1)}, u32[]{:S(2)}, u32[]{:S(2)}) collective-permute-start(bf16[32,128,128]{2,1,0:T(8,128)(2,1)S(1)} %constant_dynamic-update-slice_fusion.6.near), channel_id=1, source_target_pairs={{0,48},{1,17},{16,32},{17,1},{32,16},{33,49},{48,0},{49,33},{2,50}... | collective-permute-start | bytes 3145736 | tf_op jit(solution)/shard_map/gather_far_3/ppermute | solution.py:28
  81.9 1.5 convert_add_fusion
  83.4 5.3 %collective-permute-done.21.far = bf16[32,128,128]{2,1,0:T(8,128)(2,1)} collective-permute-done((bf16[32,128,128]{2,1,0:T(8,128)(2,1)S(1)}, bf16[32,128,128]{2,1,0:T(8,128)(2,1)}, u32[]{:S(2)}, u32[]{:S(2)}) %collective-permute-start.21) | collective-permute-done | bytes 1048608 | tf_op jit(solution)/shard_map/gather_far_2/ppermute | solution.py:28
  88.6 6.1 %tiles_2.1 = (bf16[4096,128]{1,0:T(8,128)(2,1)S(1)}, bf16[2048,128]{1,0:T(8,128)(2,1)S(1)}, bf16[2048,128]{1,0:T(8,128)(2,1)S(1)}) custom-call(s32[128]{0:T(128)S(1)} %fusion.35.src_ref, s32[128]{0:T(128)S(1)} %fusion.36.dst_ref, s32[2]{0:T(128)S(1)} %fusion.34.live_ref, bf16[64,128,128]{2,1,0:T(8,128)(2,1)} %get-tuple-element.55.c_own, ...), custom_call_target="tpu_custom_call" | custom-call | flops 1048576 | bytes 1048576 | tf_op jit(solution)/shard_map/tiles_2/pallas_call | solution.py:90
  94.8 2.4 %collective-permute-start.22 = (bf16[4096,128]{1,0:T(8,128)(2,1)S(1)}, bf16[4096,128]{1,0:T(8,128)(2,1)S(1)}, u32[]{:S(2)}, u32[]{:S(2)}) collective-permute-start(bf16[4096,128]{1,0:T(8,128)(2,1)S(1)} %get-tuple-element.73), channel_id=1, source_target_pairs={{0,4},{1,13},{4,0},{5,9},{8,12},{9,5},{12,8},{13,1},{2,6},{3,15},{... | collective-permute-start | bytes 3145736 | tf_op jit(solution)/shard_map/sum_near_2/ppermute | solution.py:28
  97.2 2.7 %collective-permute-done.14.far = bf16[32,128,128]{2,1,0:T(8,128)(2,1)} collective-permute-done((bf16[32,128,128]{2,1,0:T(8,128)(2,1)S(1)}, bf16[32,128,128]{2,1,0:T(8,128)(2,1)}, u32[]{:S(2)}, u32[]{:S(2)}) %collective-permute-start.14) | collective-permute-done | bytes 1048608 | tf_op jit(solution)/shard_map/gather_far_3/ppermute | solution.py:28
  99.9 6.1 %tiles_3.1 = (bf16[4096,128]{1,0:T(8,128)(2,1)S(1)}, bf16[2048,128]{1,0:T(8,128)(2,1)S(1)}, bf16[2048,128]{1,0:T(8,128)(2,1)S(1)}) custom-call(s32[128]{0:T(128)S(1)} %fusion.35.src_ref, s32[128]{0:T(128)S(1)} %fusion.36.dst_ref, s32[2]{0:T(128)S(1)} %fusion.34.live_ref, bf16[64,128,128]{2,1,0:T(8,128)(2,1)} %get-tuple-element.55.c_own, ...), custom_call_target="tpu_custom_call" | custom-call | flops 1048576 | bytes 1048576 | tf_op jit(solution)/shard_map/tiles_3/pallas_call | solution.py:90
  106.0 2.4 %collective-permute-start.26 = (bf16[4096,128]{1,0:T(8,128)(2,1)S(1)}, bf16[4096,128]{1,0:T(8,128)(2,1)S(1)}, u32[]{:S(2)}, u32[]{:S(2)}) collective-permute-start(bf16[4096,128]{1,0:T(8,128)(2,1)S(1)} %get-tuple-element.64), channel_id=1, source_target_pairs={{0,4},{1,13},{4,0},{5,9},{8,12},{9,5},{12,8},{13,1},{2,6},{3,15},{... | collective-permute-start | bytes 3145736 | tf_op jit(solution)/shard_map/sum_near_3/ppermute | solution.py:28
  109.5 3.8 %collective-permute-start.15 = (bf16[1056,128]{1,0:T(8,128)(2,1)S(1)}, bf16[1056,128]{1,0:T(8,128)(2,1)S(1)}, u32[]{:S(2)}, u32[]{:S(2)}) collective-permute-start(bf16[1056,128]{1,0:T(8,128)(2,1)S(1)} %fusion.7), channel_id=1, source_target_pairs={{0,2},{2,0},{1,3},{3,1},{4,6},{6,4},{5,7},{7,5},{8,10},{10,8},{9,1... | collective-permute-start | bytes 811016 | tf_op jit(solution)/shard_map/sum_x_0/ppermute | solution.py:18
  113.3 1.4 add_convert_fusion.3
  114.8 4.7 %collective-permute-done.15 = bf16[1056,128]{1,0:T(8,128)(2,1)S(1)} collective-permute-done((bf16[1056,128]{1,0:T(8,128)(2,1)S(1)}, bf16[1056,128]{1,0:T(8,128)(2,1)S(1)}, u32[]{:S(2)}, u32[]{:S(2)}) %collective-permute-start.15) | collective-permute-done | bytes 270368 | tf_op jit(solution)/shard_map/sum_x_0/ppermute | solution.py:18
  119.5 1.0 fusion.6
  120.9 1.3 collective-permute-start.16
  122.2 1.4 fusion.22
  123.6 1.4 fusion.20
  125.0 3.8 %collective-permute-done.18 = bf16[2048,128]{1,0:T(8,128)(2,1)S(1)} collective-permute-done((bf16[2048,128]{1,0:T(8,128)(2,1)S(1)}, bf16[2048,128]{1,0:T(8,128)(2,1)S(1)}, u32[]{:S(2)}, u32[]{:S(2)}) %collective-permute-start.18) | collective-permute-done | bytes 524320 | tf_op jit(solution)/shard_map/sum_far_1/ppermute | solution.py:28
  129.7 8.6 %collective-permute-done.19 = bf16[1024,128]{1,0:T(8,128)(2,1)S(1)} collective-permute-done((bf16[1024,128]{1,0:T(8,128)(2,1)S(1)}, bf16[1024,128]{1,0:T(8,128)(2,1)S(1)}, u32[]{:S(2)}, u32[]{:S(2)}) %collective-permute-start.19) | collective-permute-done | bytes 262176 | tf_op jit(solution)/shard_map/sum_x_1/ppermute | solution.py:18
  138.7 1.5 fusion.18
  140.3 1.6 add_add_fusion.1
  143.5 7.7 %collective-permute-done.24 = bf16[1024,128]{1,0:T(8,128)(2,1)S(1)} collective-permute-done((bf16[1024,128]{1,0:T(8,128)(2,1)S(1)}, bf16[1024,128]{1,0:T(8,128)(2,1)S(1)}, u32[]{:S(2)}, u32[]{:S(2)}) %collective-permute-start.24) | collective-permute-done | bytes 262176 | tf_op jit(solution)/shard_map/sum_x_2/ppermute | solution.py:18
  151.5 1.2 collective-permute-start.25
  152.8 1.1 collective-permute-start.28
  153.9 1.4 fusion.15
  155.2 5.7 %collective-permute-done.28 = bf16[1024,128]{1,0:T(8,128)(2,1)S(1)} collective-permute-done((bf16[1024,128]{1,0:T(8,128)(2,1)S(1)}, bf16[1024,128]{1,0:T(8,128)(2,1)S(1)}, u32[]{:S(2)}, u32[]{:S(2)}) %collective-permute-start.28) | collective-permute-done | bytes 262176 | tf_op jit(solution)/shard_map/sum_x_3/ppermute | solution.py:18
  161.2 2.2 %collective-permute-start.29 = (bf16[512,128]{1,0:T(8,128)(2,1)S(1)}, bf16[512,128]{1,0:T(8,128)(2,1)S(1)}, u32[]{:S(2)}, u32[]{:S(2)}) collective-permute-start(bf16[512,128]{1,0:T(8,128)(2,1)S(1)} %bitcast.51), channel_id=1, source_target_pairs={{0,1},{1,0},{2,3},{3,2},{4,5},{5,4},{6,7},{7,6},{8,9},{9,8},{10,11... | collective-permute-start | bytes 393224 | tf_op jit(solution)/shard_map/mean_core_3/ppermute | solution.py:18
  163.5 1.4 add_add_fusion.hidden
  164.9 2.8 %shard_map.102 = f32[512,1024]{1,0:T(8,128)} custom-call(f32[512,1024]{1,0:T(8,128)S(1)} %add_add_fusion.hidden, bf16[512,128]{1,0:T(8,128)(2,1)S(1)} %bitcast.39, bf16[512,128]{1,0:T(8,128)(2,1)S(1)} %collective-permute-done.29.got, bf16[256,1024]{1,0:T(8,128)(2,1)S(1)} %pad_maximum_fusion.2.weight), custom_call_target="tpu_custom_call" | custom-call | tf_op jit(solution)/shard_map/pallas_call | solution.py:175
  (107 shorter events, 13.6 us)
Async XLA Ops:
  0.0 10.1 %collective-permute-start = (bf16[512,1024]{1,0:T(8,128)(2,1)}, bf16[512,1024]{1,0:T(8,128)(2,1)S(1)}, u32[]{:S(2)}, u32[]{:S(2)}) collective-permute-start(bf16[512,1024]{1,0:T(8,128)(2,1)} %x_own.2), channel_id=1, source_target_pairs={{0,1},{1,0},{2,3},{3,2},{4,5},{5,4},{6,7},{7,6},{8,9},{9,8},{10,11... | collective-permute-start | bytes 3145736 | tf_op jit(solution)/shard_map/other_features_0/ppermute | solution.py:18
  3.1 4.3 %copy-start.3 = (bf16[512,1024]{1,0:T(8,128)(2,1)S(1)}, bf16[512,1024]{1,0:T(8,128)(2,1)}, u32[]{:S(2)}) copy-start(bf16[512,1024]{1,0:T(8,128)(2,1)} %x_own.2) | copy-start | bytes 3145732
  3.1 4.3 %copy-start.7 = (bf16[2048,1024]{1,0:T(8,128)(2,1)S(1)}, bf16[2048,1024]{1,0:T(8,128)(2,1)}, u32[]{:S(2)}) copy-start(bf16[2048,1024]{1,0:T(8,128)(2,1)} %param.17) | copy-start | bytes 12582916
  3.1 4.3 %copy-start.9 = (f32[1024]{0:T(1024)S(1)}, f32[1024]{0:T(1024)}, u32[]{:S(2)}) copy-start(f32[1024]{0:T(1024)} %param.18) | copy-start | bytes 12292
  7.5 2.7 %copy-start.2 = (bf16[1024,1024]{1,0:T(8,128)(2,1)S(1)}, bf16[1024,1024]{1,0:T(8,128)(2,1)}, u32[]{:S(2)}) copy-start(bf16[1024,1024]{1,0:T(8,128)(2,1)} %weight.3) | copy-start | bytes 6291460
  7.5 2.6 %copy-start.4 = (f32[1024]{0:T(1024)S(1)}, f32[1024]{0:T(1024)}, u32[]{:S(2)}) copy-start(f32[1024]{0:T(1024)} %param.16) | copy-start | bytes 12292
  11.1 8.0 %collective-permute-start.2 = (bf16[8,128,128]{2,1,0:T(8,128)(2,1)S(1)}, bf16[8,128,128]{2,1,0:T(8,128)(2,1)S(1)}, u32[]{:S(2)}, u32[]{:S(2)}) collective-permute-start(bf16[8,128,128]{2,1,0:T(8,128)(2,1)S(1)} %shard_map.100), channel_id=1, source_target_pairs={{0,64},{64,0},{1,65},{65,1},{2,66},{66,2},{3,67},{67,3},{4,68},{68... | collective-permute-start | bytes 786440 | tf_op jit(solution)/shard_map/gather_x_0/ppermute | solution.py:18
  11.4 40.9 %collective-permute-start.7 = (bf16[64,128,128]{2,1,0:T(8,128)(2,1)}, bf16[64,128,128]{2,1,0:T(8,128)(2,1)}, u32[]{:S(2)}, u32[]{:S(2)}) collective-permute-start(bf16[64,128,128]{2,1,0:T(8,128)(2,1)} %get-tuple-element.55.c_own), channel_id=1, source_target_pairs={{0,1},{1,0},{2,3},{3,2},{4,5},{5,4},{6,7},{7,6},{8,9},{9,8},{10,11... | collective-permute-start | bytes 6291464 | tf_op jit(solution)/shard_map/other_tiles/ppermute | solution.py:18
  19.2 9.5 %collective-permute-start.4 = (bf16[16,128,128]{2,1,0:T(8,128)(2,1)S(1)}, bf16[16,128,128]{2,1,0:T(8,128)(2,1)}, u32[]{:S(2)}, u32[]{:S(2)}) collective-permute-start(bf16[16,128,128]{2,1,0:T(8,128)(2,1)S(1)} %pad_maximum_fusion), channel_id=1, source_target_pairs={{0,16},{1,49},{16,0},{17,33},{32,48},{33,17},{48,32},{49,1},{2,18}... | collective-permute-start | bytes 1572872 | tf_op jit(solution)/shard_map/gather_near_0/ppermute | solution.py:28
  22.3 1.2 collective-permute-start.1
  22.4 7.8 %collective-permute-start.3 = (bf16[8,128,128]{2,1,0:T(8,128)(2,1)S(1)}, bf16[8,128,128]{2,1,0:T(8,128)(2,1)S(1)}, u32[]{:S(2)}, u32[]{:S(2)}) collective-permute-start(bf16[8,128,128]{2,1,0:T(8,128)(2,1)S(1)} %get-tuple-element.48), channel_id=1, source_target_pairs={{0,64},{64,0},{1,65},{65,1},{2,66},{66,2},{3,67},{67,3},{4,68},{68... | collective-permute-start | bytes 786440 | tf_op jit(solution)/shard_map/gather_x_1/ppermute | solution.py:18
  29.8 19.7 %collective-permute-start.8 = (bf16[32,128,128]{2,1,0:T(8,128)(2,1)S(1)}, bf16[32,128,128]{2,1,0:T(8,128)(2,1)}, u32[]{:S(2)}, u32[]{:S(2)}) collective-permute-start(bf16[32,128,128]{2,1,0:T(8,128)(2,1)S(1)} %constant_dynamic-update-slice_fusion.near), channel_id=1, source_target_pairs={{0,48},{1,17},{16,32},{17,1},{32,16},{33,49},{48,0},{49,33},{2,50}... | collective-permute-start | bytes 3145736 | tf_op jit(solution)/shard_map/gather_far_0/ppermute | solution.py:28
  30.2 14.7 %collective-permute-start.6 = (bf16[16,128,128]{2,1,0:T(8,128)(2,1)S(1)}, bf16[16,128,128]{2,1,0:T(8,128)(2,1)}, u32[]{:S(2)}, u32[]{:S(2)}) collective-permute-start(bf16[16,128,128]{2,1,0:T(8,128)(2,1)S(1)} %pad_maximum_fusion.1), channel_id=1, source_target_pairs={{0,16},{1,49},{16,0},{17,33},{32,48},{33,17},{48,32},{49,1},{2,18}... | collective-permute-start | bytes 1572872 | tf_op jit(solution)/shard_map/gather_near_1/ppermute | solution.py:28
  32.7 14.4 %collective-permute-start.5 = (bf16[16,128,128]{2,1,0:T(8,128)(2,1)S(1)}, bf16[16,128,128]{2,1,0:T(8,128)(2,1)S(1)}, u32[]{:S(2)}, u32[]{:S(2)}) collective-permute-start(bf16[16,128,128]{2,1,0:T(8,128)(2,1)S(1)} %get-tuple-element.52), channel_id=1, source_target_pairs={{0,64},{64,0},{1,65},{65,1},{2,66},{66,2},{3,67},{67,3},{4,68},{68... | collective-permute-start | bytes 1572872 | tf_op jit(solution)/shard_map/gather_x_rest/ppermute | solution.py:18
  46.1 20.2 %collective-permute-start.11 = (bf16[32,128,128]{2,1,0:T(8,128)(2,1)S(1)}, bf16[32,128,128]{2,1,0:T(8,128)(2,1)S(1)}, u32[]{:S(2)}, u32[]{:S(2)}) collective-permute-start(bf16[32,128,128]{2,1,0:T(8,128)(2,1)S(1)} %constant_dynamic-update-slice_fusion.2.near), channel_id=1, source_target_pairs={{0,48},{1,17},{16,32},{17,1},{32,16},{33,49},{48,0},{49,33},{2,50}... | collective-permute-start | bytes 3145736 | tf_op jit(solution)/shard_map/gather_far_1/ppermute | solution.py:28
  49.5 14.5 %collective-permute-start.10 = (bf16[16,128,128]{2,1,0:T(8,128)(2,1)S(1)}, bf16[16,128,128]{2,1,0:T(8,128)(2,1)S(1)}, u32[]{:S(2)}, u32[]{:S(2)}) collective-permute-start(bf16[16,128,128]{2,1,0:T(8,128)(2,1)S(1)} %pad_maximum_fusion.3), channel_id=1, source_target_pairs={{0,16},{1,49},{16,0},{17,33},{32,48},{33,17},{48,32},{49,1},{2,18}... | collective-permute-start | bytes 1572872 | tf_op jit(solution)/shard_map/gather_near_2/ppermute | solution.py:28
  60.9 21.0 %collective-permute-start.9 = (bf16[4224,128]{1,0:T(8,128)(2,1)S(1)}, bf16[4224,128]{1,0:T(8,128)(2,1)S(1)}, u32[]{:S(2)}, u32[]{:S(2)}) collective-permute-start(bf16[4224,128]{1,0:T(8,128)(2,1)S(1)} %get-tuple-element.56), channel_id=1, source_target_pairs={{0,4},{1,13},{4,0},{5,9},{8,12},{9,5},{12,8},{13,1},{2,6},{3,15},{... | collective-permute-start | bytes 3244040 | tf_op jit(solution)/shard_map/sum_near_0/ppermute | solution.py:28
  66.3 12.7 %collective-permute-start.13 = (bf16[16,128,128]{2,1,0:T(8,128)(2,1)S(1)}, bf16[16,128,128]{2,1,0:T(8,128)(2,1)S(1)}, u32[]{:S(2)}, u32[]{:S(2)}) collective-permute-start(bf16[16,128,128]{2,1,0:T(8,128)(2,1)S(1)} %pad_maximum_fusion.4), channel_id=1, source_target_pairs={{0,16},{1,49},{16,0},{17,33},{32,48},{33,17},{48,32},{49,1},{2,18}... | collective-permute-start | bytes 1572872 | tf_op jit(solution)/shard_map/gather_near_3/ppermute | solution.py:28
  69.0 19.7 %collective-permute-start.21 = (bf16[32,128,128]{2,1,0:T(8,128)(2,1)S(1)}, bf16[32,128,128]{2,1,0:T(8,128)(2,1)}, u32[]{:S(2)}, u32[]{:S(2)}) collective-permute-start(bf16[32,128,128]{2,1,0:T(8,128)(2,1)S(1)} %constant_dynamic-update-slice_fusion.4.near), channel_id=1, source_target_pairs={{0,48},{1,17},{16,32},{17,1},{32,16},{33,49},{48,0},{49,33},{2,50}... | collective-permute-start | bytes 3145736 | tf_op jit(solution)/shard_map/gather_far_2/ppermute | solution.py:28
  75.9 0.8 copy-start
  76.7 31.7 %collective-permute-start.17 = (bf16[4096,128]{1,0:T(8,128)(2,1)}, bf16[4096,128]{1,0:T(8,128)(2,1)}, u32[]{:S(2)}, u32[]{:S(2)}) collective-permute-start(bf16[4096,128]{1,0:T(8,128)(2,1)} %get-tuple-element.59), channel_id=1, source_target_pairs={{0,4},{1,13},{4,0},{5,9},{8,12},{9,5},{12,8},{13,1},{2,6},{3,15},{... | collective-permute-start | bytes 3145736 | tf_op jit(solution)/shard_map/sum_near_1/ppermute | solution.py:28
  79.1 20.7 %collective-permute-start.14 = (bf16[32,128,128]{2,1,0:T(8,128)(2,1)S(1)}, bf16[32,128,128]{2,1,0:T(8,128)(2,1)}, u32[]{:S(2)}, u32[]{:S(2)}) collective-permute-start(bf16[32,128,128]{2,1,0:T(8,128)(2,1)S(1)} %constant_dynamic-update-slice_fusion.6.near), channel_id=1, source_target_pairs={{0,48},{1,17},{16,32},{17,1},{32,16},{33,49},{48,0},{49,33},{2,50}... | collective-permute-start | bytes 3145736 | tf_op jit(solution)/shard_map/gather_far_3/ppermute | solution.py:28
  83.4 25.1 %collective-permute-start.12 = (bf16[2112,128]{1,0:T(8,128)(2,1)}, bf16[2112,128]{1,0:T(8,128)(2,1)}, u32[]{:S(2)}, u32[]{:S(2)}) collective-permute-start(bf16[2112,128]{1,0:T(8,128)(2,1)} %get-tuple-element.90), channel_id=1, source_target_pairs={{0,12},{1,5},{4,8},{5,1},{8,4},{9,13},{12,0},{13,9},{2,14},{3,7},{... | collective-permute-start | bytes 1622024 | tf_op jit(solution)/shard_map/sum_far_0/ppermute | solution.py:28
  94.8 13.7 %copy-start.5 = (f32[2112,128]{1,0:T(8,128)S(1)}, f32[2112,128]{1,0:T(8,128)}, u32[]{:S(2)}) copy-start(f32[2112,128]{1,0:T(8,128)} %get-tuple-element.89) | copy-start | bytes 3244036
  94.8 18.5 %copy-start.1 = (bf16[2048,128]{1,0:T(8,128)(2,1)S(1)}, bf16[2048,128]{1,0:T(8,128)(2,1)}, u32[]{:S(2)}) copy-start(bf16[2048,128]{1,0:T(8,128)(2,1)} %copy-done) | copy-start | bytes 1572868
  94.8 34.2 %collective-permute-start.22 = (bf16[4096,128]{1,0:T(8,128)(2,1)S(1)}, bf16[4096,128]{1,0:T(8,128)(2,1)S(1)}, u32[]{:S(2)}, u32[]{:S(2)}) collective-permute-start(bf16[4096,128]{1,0:T(8,128)(2,1)S(1)} %get-tuple-element.73), channel_id=1, source_target_pairs={{0,4},{1,13},{4,0},{5,9},{8,12},{9,5},{12,8},{13,1},{2,6},{3,15},{... | collective-permute-start | bytes 3145736 | tf_op jit(solution)/shard_map/sum_near_2/ppermute | solution.py:28
  106.0 35.9 %collective-permute-start.26 = (bf16[4096,128]{1,0:T(8,128)(2,1)S(1)}, bf16[4096,128]{1,0:T(8,128)(2,1)S(1)}, u32[]{:S(2)}, u32[]{:S(2)}) collective-permute-start(bf16[4096,128]{1,0:T(8,128)(2,1)S(1)} %get-tuple-element.64), channel_id=1, source_target_pairs={{0,4},{1,13},{4,0},{5,9},{8,12},{9,5},{12,8},{13,1},{2,6},{3,15},{... | collective-permute-start | bytes 3145736 | tf_op jit(solution)/shard_map/sum_near_3/ppermute | solution.py:28
  109.5 10.0 %collective-permute-start.15 = (bf16[1056,128]{1,0:T(8,128)(2,1)S(1)}, bf16[1056,128]{1,0:T(8,128)(2,1)S(1)}, u32[]{:S(2)}, u32[]{:S(2)}) collective-permute-start(bf16[1056,128]{1,0:T(8,128)(2,1)S(1)} %fusion.7), channel_id=1, source_target_pairs={{0,2},{2,0},{1,3},{3,1},{4,6},{6,4},{5,7},{7,5},{8,10},{10,8},{9,1... | collective-permute-start | bytes 811016 | tf_op jit(solution)/shard_map/sum_x_0/ppermute | solution.py:18
  114.7 5.9 %copy-start.8 = (f32[4]{0:T(128)S(1)}, f32[4]{0:T(128)}, u32[]{:S(2)}) copy-start(f32[4]{0:T(128)} %constant.140.clone) | copy-start | bytes 52
  114.7 14.1 %collective-permute-start.18 = (bf16[2048,128]{1,0:T(8,128)(2,1)S(1)}, bf16[2048,128]{1,0:T(8,128)(2,1)S(1)}, u32[]{:S(2)}, u32[]{:S(2)}) collective-permute-start(bf16[2048,128]{1,0:T(8,128)(2,1)S(1)} %get-tuple-element.95), channel_id=1, source_target_pairs={{0,12},{1,5},{4,8},{5,1},{8,4},{9,13},{12,0},{13,9},{2,14},{3,7},{... | collective-permute-start | bytes 1572872 | tf_op jit(solution)/shard_map/sum_far_1/ppermute | solution.py:28
  120.9 2.7 %collective-permute-start.16 = (bf16[512,128]{1,0:T(8,128)(2,1)S(1)}, bf16[512,128]{1,0:T(8,128)(2,1)S(1)}, u32[]{:S(2)}, u32[]{:S(2)}) collective-permute-start(bf16[512,128]{1,0:T(8,128)(2,1)S(1)} %bitcast.52), channel_id=1, source_target_pairs={{0,1},{1,0},{2,3},{3,2},{4,5},{5,4},{6,7},{7,6},{8,9},{9,8},{10,11... | collective-permute-start | bytes 393224 | tf_op jit(solution)/shard_map/mean_core_0/ppermute | solution.py:18
  128.9 9.5 %collective-permute-start.19 = (bf16[1024,128]{1,0:T(8,128)(2,1)S(1)}, bf16[1024,128]{1,0:T(8,128)(2,1)S(1)}, u32[]{:S(2)}, u32[]{:S(2)}) collective-permute-start(bf16[1024,128]{1,0:T(8,128)(2,1)S(1)} %fusion.13), channel_id=1, source_target_pairs={{0,2},{2,0},{1,3},{3,1},{4,6},{6,4},{5,7},{7,5},{8,10},{10,8},{9,1... | collective-permute-start | bytes 786440 | tf_op jit(solution)/shard_map/sum_x_1/ppermute | solution.py:18
  129.2 12.7 %collective-permute-start.23 = (bf16[2048,128]{1,0:T(8,128)(2,1)S(1)}, bf16[2048,128]{1,0:T(8,128)(2,1)S(1)}, u32[]{:S(2)}, u32[]{:S(2)}) collective-permute-start(bf16[2048,128]{1,0:T(8,128)(2,1)S(1)} %get-tuple-element.93), channel_id=1, source_target_pairs={{0,12},{1,5},{4,8},{5,1},{8,4},{9,13},{12,0},{13,9},{2,14},{3,7},{... | collective-permute-start | bytes 1572872 | tf_op jit(solution)/shard_map/sum_far_2/ppermute | solution.py:28
  138.4 1.9 %copy-start.6 = (f32[512,1024]{1,0:T(8,128)S(1)}, f32[512,1024]{1,0:T(8,128)}, u32[]{:S(2)}) copy-start(f32[512,1024]{1,0:T(8,128)} %fusion.3) | copy-start | bytes 6291460
  138.6 1.6 collective-permute-start.20
  142.0 9.2 %collective-permute-start.24 = (bf16[1024,128]{1,0:T(8,128)(2,1)S(1)}, bf16[1024,128]{1,0:T(8,128)(2,1)S(1)}, u32[]{:S(2)}, u32[]{:S(2)}) collective-permute-start(bf16[1024,128]{1,0:T(8,128)(2,1)S(1)} %fusion.11), channel_id=1, source_target_pairs={{0,2},{2,0},{1,3},{3,1},{4,6},{6,4},{5,7},{7,5},{8,10},{10,8},{9,1... | collective-permute-start | bytes 786440 | tf_op jit(solution)/shard_map/sum_x_2/ppermute | solution.py:18
  143.0 9.7 %collective-permute-start.27 = (bf16[2048,128]{1,0:T(8,128)(2,1)S(1)}, bf16[2048,128]{1,0:T(8,128)(2,1)S(1)}, u32[]{:S(2)}, u32[]{:S(2)}) collective-permute-start(bf16[2048,128]{1,0:T(8,128)(2,1)S(1)} %get-tuple-element.91), channel_id=1, source_target_pairs={{0,12},{1,5},{4,8},{5,1},{8,4},{9,13},{12,0},{13,9},{2,14},{3,7},{... | collective-permute-start | bytes 1572872 | tf_op jit(solution)/shard_map/sum_far_3/ppermute | solution.py:28
  151.5 12.0 %collective-permute-start.25 = (bf16[512,128]{1,0:T(8,128)(2,1)S(1)}, bf16[512,128]{1,0:T(8,128)(2,1)S(1)}, u32[]{:S(2)}, u32[]{:S(2)}) collective-permute-start(bf16[512,128]{1,0:T(8,128)(2,1)S(1)} %bitcast.50), channel_id=1, source_target_pairs={{0,1},{1,0},{2,3},{3,2},{4,5},{5,4},{6,7},{7,6},{8,9},{9,8},{10,11... | collective-permute-start | bytes 393224 | tf_op jit(solution)/shard_map/mean_core_2/ppermute | solution.py:18
  152.8 8.1 %collective-permute-start.28 = (bf16[1024,128]{1,0:T(8,128)(2,1)S(1)}, bf16[1024,128]{1,0:T(8,128)(2,1)S(1)}, u32[]{:S(2)}, u32[]{:S(2)}) collective-permute-start(bf16[1024,128]{1,0:T(8,128)(2,1)S(1)} %fusion.9), channel_id=1, source_target_pairs={{0,2},{2,0},{1,3},{3,1},{4,6},{6,4},{5,7},{7,5},{8,10},{10,8},{9,1... | collective-permute-start | bytes 786440 | tf_op jit(solution)/shard_map/sum_x_3/ppermute | solution.py:18
  161.2 3.6 %collective-permute-start.29 = (bf16[512,128]{1,0:T(8,128)(2,1)S(1)}, bf16[512,128]{1,0:T(8,128)(2,1)S(1)}, u32[]{:S(2)}, u32[]{:S(2)}) collective-permute-start(bf16[512,128]{1,0:T(8,128)(2,1)S(1)} %bitcast.51), channel_id=1, source_target_pairs={{0,1},{1,0},{2,3},{3,2},{4,5},{5,4},{6,7},{7,6},{8,9},{9,8},{10,11... | collective-permute-start | bytes 393224 | tf_op jit(solution)/shard_map/mean_core_3/ppermute | solution.py:18

commit v10 on v9

--- a/solution.py
+++ b/solution.py
@@ -260,15 +260,16 @@
     parts = parts.astype(jnp.bfloat16).reshape(256, tile)
 
     hidden = (
-        jnp.dot(features, combine_weight[:width], preferred_element_type=jnp.float32)
+        jnp.dot(after(features, own0), combine_weight[:width], preferred_element_type=jnp.float32)
         + combine_bias
     )
-    w_own = lax.dynamic_slice_in_dim(combine_weight, width + core * half, half, 0)
-    w_other = lax.dynamic_slice_in_dim(combine_weight, width + (1 - core) * half, half, 0)
+    later_weight = after(combine_weight, own0)
+    w_own = lax.dynamic_slice_in_dim(later_weight, width + core * half, half, 0)
+    w_other = lax.dynamic_slice_in_dim(later_weight, width + (1 - core) * half, half, 0)
 
     second = swap(after(own1, first), "x_lo", "gather_x_1")
     f32, bf16 = jnp.float32, jnp.bfloat16
-    near_all, far_all, part_all, pass_all, hidden_all = [], [], [], [], []
+    near_all, far_all, part_all, pass_all = [], [], [], []
     scale = None
 
     def far(pair, got, j):
@@ -287,8 +288,8 @@
         pair = after(pair, near_all[j - 1], *far_all[: j - 1])
         far(pair, step(pair, "y", 0, f"gather_near_{j}"), j)
 
-    last = slice((CHUNKS - 1) * cw, CHUNKS * cw)
-    last_weight = jnp.concatenate([w_own[last], w_other[last]])
+    cut = (CHUNKS - 2) * cw
+    last_weight = jnp.concatenate([w_own[cut:], w_other[cut:]])
 
     def tiles(j):
         earlier = (rest, near_all[1], hidden, last_weight) if j == 0 else ()
@@ -313,28 +314,37 @@
             )
 
     tiles(0)
+    stays = []
     for j in range(CHUNKS):
         send, pass_on, stay = part_all[j]
         size = stay.shape[0] // 2
         got = step(send, "z", 0, f"sum_near_{j}")
         if j == 0:
             tiles(1)
-            got = after(got, part_all[1][0])
-        else:
-            got = after(got, part_all[-1][0])
+        if j + 1 < CHUNKS:
+            got = after(got, part_all[j + 1][0])
         passed = (got[: 2 * size].astype(f32) + pass_on.astype(f32)).astype(bf16)
         pass_all.append(passed)
-        stay = got[2 * size :].astype(f32) + stay.astype(f32)
-        got = step(passed, "z", 1, f"sum_far_{j}")
+        stays.append(got[2 * size :].astype(f32) + stay.astype(f32))
         if j == 0:
             for i in range(2, CHUNKS):
                 tiles(i)
+
+    means = []
+    for j in range(CHUNKS):
+        stay = stays[j]
+        size = stay.shape[0] // 2
+        got = step(pass_all[j], "z", 1, f"sum_far_{j}")
+        if j == 0:
             got = after(got, part_all[-1][0])
+        elif j + 1 < CHUNKS:
+            got = after(got, pass_all[j + 1])
         passed = (got[:size].astype(f32) + stay[:size]).astype(bf16)
         stay = got[size:].astype(f32) + stay[size:]
-        if j == CHUNKS - 1:
-            passed = after(passed, hidden_all[j - 2])
-        pooled = swap(passed, "x_hi", f"sum_x_{j}").astype(f32) + stay
+        got = swap(passed, "x_hi", f"sum_x_{j}")
+        if j + 2 < CHUNKS:
+            got = after(got, pass_all[j + 2])
+        pooled = got.astype(f32) + stay
         if j == 0:
             deg = jnp.sum(
                 pooled[8 * tile :].reshape(8, 4, tile)
@@ -345,14 +355,18 @@
             pooled = pooled[: 8 * tile]
         factor = after(scale, passed)[..., None]
         mean = (pooled.reshape(8, tile, cw) * factor).astype(bf16)
-        mean = mean.reshape(2, rows_dev, cw)
-        got = swap(mean[1], "core", f"mean_core_{j}")
-        cols = slice(j * cw, (j + 1) * cw)
-        if j == CHUNKS - 1:
-            return finish(hidden, mean[0], got, last_weight)
-        hidden = hidden + jnp.dot(mean[0], w_own[cols], preferred_element_type=f32)
-        hidden = hidden + jnp.dot(got, w_other[cols], preferred_element_type=f32)
-        hidden_all.append(hidden)
+        means.append(mean.reshape(2, rows_dev, cw))
+
+    def both_halves(chunks, name):
+        near = jnp.concatenate([means[j][0] for j in chunks], axis=1)
+        away = jnp.concatenate([means[j][1] for j in chunks], axis=1)
+        return near, swap(away, "core", name)
+
+    near, got = both_halves(range(CHUNKS - 2), "mean_core_0")
+    hidden = hidden + jnp.dot(near, w_own[:cut], preferred_element_type=f32)
+    hidden = hidden + jnp.dot(got, w_other[:cut], preferred_element_type=f32)
+    near, got = both_halves(range(CHUNKS - 2, CHUNKS), "mean_core_1")
+    return finish(hidden, near, got, last_weight)
 
 
 def solution(mesh):

time: 169 us -> 162 us (0.959)
  starting transfers between devices: 37.9 us -> 44.8 us
  matrix products: 11.4 us -> 5.73 us
  other arithmetic: 15.4 us -> 12.3 us
  waiting for transfers between devices: 64.8 us -> 61.7 us
  Pallas kernels: 31.2 us -> 28.4 us
    ppermute x14 -> x12, waiting for transfers between devices: 32.2 us -> 9.42 us  [swap(): return lax.ppermute(x, axis, [(0, 1), (1, 0)])]
    ppermute x16, waiting for transfers between devices: 32.6 us -> 52.3 us  [step(): return lax.ppermute(x, (axis, 'core'), pairs)]
    ppermute x14 -> x12, starting transfers between devices: 12.5 us -> 18.3 us  [swap(): return lax.ppermute(x, axis, [(0, 1), (1, 0)])]
    dot_general x7 -> x3, matrix products: 11.3 us -> 5.57 us  [the longest x1 2.59 us: local(): jnp.dot(after(features, own0), combine_weight[:width], preferred_element_...]
    pallas_call x4, Pallas kernels: 25.3 us -> 22.5 us  [tile_sums(): pl.pallas_call(tile_kernel, out_shape=(jax.ShapeDtypeStruct((4 * size, w)...]
  transfers between devices with their start and end apart: 30 -> 28, of which waited for: 14 -> 15; matrix products, arithmetic and copies ran while one was open for 19% -> 14% of each run, Pallas kernels for 16% -> 15%
where the time goes in v10:
time: 162 us; the launch traced here: 160 us
  waiting for transfers between devices  61.7 us (38%)
  starting transfers between devices  44.8 us (28%)
  Pallas kernels  28.4 us (18%)
  other arithmetic  12.3 us (8%)
  matrix products  5.73 us (4%)
  local copies, waits for them, and re-layouts  5.56 us (3%)
    ppermute x16, waiting for transfers between devices, step(): return lax.ppermute(x, (axis, 'core'), pairs)  52.3 us
    ppermute x16, starting transfers between devices, step(): return lax.ppermute(x, (axis, 'core'), pairs)  26.5 us
    pallas_call x4, Pallas kernels, tile_sums(): pl.pallas_call(tile_kernel, out_shape=(jax.ShapeDtypeStruct((4 * size, w)...  22.5 us
    ppermute x12, starting transfers between devices, swap(): return lax.ppermute(x, axis, [(0, 1), (1, 0)])  18.3 us
    ppermute x12, waiting for transfers between devices, swap(): return lax.ppermute(x, axis, [(0, 1), (1, 0)])  9.42 us
    reduce_sum x1, other arithmetic, local(): jnp.sum(c_own.astype(jnp.float32), axis=2)  4.35 us
  transfers between devices with their start and end apart: 28, of which 15 were waited for; matrix products, arithmetic and copies ran while one was open for 14% of the time, Pallas kernels for 15%

profile of v10, /device:TPU:3, one launch (start us, length us, event | category | flops | bytes accessed | tf_op | source)
XLA Modules:
  0.0 159.6 jit_solution(16298953402239223039)
XLA Ops:
  1.6 0.7 compare_select_fusion.14
  2.4 4.4 %convert_reduce_fusion.1 = (f32[64,128]{1,0:T(8,128)S(1)}, bf16[64,128,128]{2,1,0:T(8,128)(2,1)}) fusion(s32[1,1,64,128,128]{4,3,2,1,0:T(8,128)} %param.11, pred[64]{0:T(512)(128)(4,1)S(1)} %iota_compare_fusion.2), kind=kLoop, calls=%fused_computation.3 | loop fusion | flops 4186112 | bytes 6324288 | tf_op jit(solution)/shard_map/reduce_sum | solution.py:255
  6.8 1.0 shard_map.100
  8.9 2.6 %fusion.3 = f32[512,1024]{1,0:T(8,128)} fusion(bf16[512,1024]{1,0:T(8,128)(2,1)S(1)} %copy-done.1, bf16[2048,1024]{1,0:T(8,128)(2,1)S(1)} %copy-done.4, f32[1024]{0:T(1024)S(1)} %copy-done.7), kind=kOutput, calls=%fused_computation.7 | convolution fusion | flops 1074266112 | bytes 5246976 | tf_op jit(solution)/shard_map/dot_general | solution.py:263
  11.5 2.1 %shard_map.101 = (bf16[8,128,128]{2,1,0:T(8,128)(2,1)S(1)}, bf16[16,128,128]{2,1,0:T(8,128)(2,1)S(1)}) custom-call(s32[1]{0:T(128)} %bitcast.core_ref, bf16[512,1024]{1,0:T(8,128)(2,1)S(1)} %copy-done.1, bf16[512,1024]{1,0:T(8,128)(2,1)S(1)} %collective-permute-done.x_other, bf16[1024,1024]{1,0:T(8,128)(2,1)S(1)} %copy-done, f32[1,1024]{1,0:T(1,128)S(1)} %bitcast.35), custom_call_target="tpu_custom_call" | custom-call | flops 6442450944 | bytes 2883584 | tf_op jit(solution)/shard_map/pallas_call | solution.py:141
  13.6 2.2 %collective-permute-done.2 = bf16[8,128,128]{2,1,0:T(8,128)(2,1)S(1)} collective-permute-done((bf16[8,128,128]{2,1,0:T(8,128)(2,1)S(1)}, bf16[8,128,128]{2,1,0:T(8,128)(2,1)S(1)}, u32[]{:S(2)}, u32[]{:S(2)}) %collective-permute-start.2) | collective-permute-done | bytes 262176 | tf_op jit(solution)/shard_map/gather_x_0/ppermute | solution.py:18
  15.8 2.8 %collective-permute-start.4 = (bf16[16,128,128]{2,1,0:T(8,128)(2,1)S(1)}, bf16[16,128,128]{2,1,0:T(8,128)(2,1)}, u32[]{:S(2)}, u32[]{:S(2)}) collective-permute-start(bf16[16,128,128]{2,1,0:T(8,128)(2,1)S(1)} %pad_maximum_fusion.1), channel_id=1, source_target_pairs={{0,16},{1,49},{16,0},{17,33},{32,48},{33,17},{48,32},{49,1},{2,18}... | collective-permute-start | bytes 1572872 | tf_op jit(solution)/shard_map/gather_near_0/ppermute | solution.py:28
  18.7 0.9 fusion.44
  20.0 5.3 %collective-permute-done.4 = bf16[16,128,128]{2,1,0:T(8,128)(2,1)} collective-permute-done((bf16[16,128,128]{2,1,0:T(8,128)(2,1)S(1)}, bf16[16,128,128]{2,1,0:T(8,128)(2,1)}, u32[]{:S(2)}, u32[]{:S(2)}) %collective-permute-start.4) | collective-permute-done | bytes 524320 | tf_op jit(solution)/shard_map/gather_near_0/ppermute | solution.py:28
  25.3 1.1 constant_dynamic-update-slice_fusion.near
  26.8 1.1 collective-permute-done.3
  28.2 1.0 pad_maximum_fusion.2
  29.2 1.5 collective-permute-start.6
  30.9 13.6 %collective-permute-done.6 = bf16[16,128,128]{2,1,0:T(8,128)(2,1)} collective-permute-done((bf16[16,128,128]{2,1,0:T(8,128)(2,1)S(1)}, bf16[16,128,128]{2,1,0:T(8,128)(2,1)}, u32[]{:S(2)}, u32[]{:S(2)}) %collective-permute-start.6) | collective-permute-done | bytes 524320 | tf_op jit(solution)/shard_map/gather_near_1/ppermute | solution.py:28
  44.6 1.1 constant_dynamic-update-slice_fusion.2.near
  45.8 1.1 fusion.45
  46.9 1.0 pad_maximum_fusion.3
  47.9 1.6 collective-permute-start.10
  49.4 2.2 %convert_reduce_fusion = f32[64,128]{1,0:T(8,128)S(1)} fusion(bf16[64,128,128]{2,1,0:T(8,128)(2,1)} %collective-permute-done.7.c_other), kind=kLoop, calls=%fused_computation.2 | loop fusion | flops 2088960 | bytes 2129920 | tf_op jit(solution)/shard_map/reduce_sum | solution.py:255
  52.0 5.9 %tiles_0.1 = (bf16[4224,128]{1,0:T(8,128)(2,1)S(1)}, bf16[2112,128]{1,0:T(8,128)(2,1)S(1)}, bf16[2112,128]{1,0:T(8,128)(2,1)S(1)}) custom-call(s32[128]{0:T(128)S(1)} %fusion.27.src_ref, s32[128]{0:T(128)S(1)} %fusion.28.dst_ref, s32[2]{0:T(128)S(1)} %fusion.26.live_ref, bf16[64,128,128]{2,1,0:T(8,128)(2,1)} %get-tuple-element.59.c_own, ...), custom_call_target="tpu_custom_call" | custom-call | flops 2147483648 | bytes 1048576 | tf_op jit(solution)/shard_map/tiles_0/pallas_call | solution.py:90
  57.8 4.1 %collective-permute-start.9 = (bf16[4224,128]{1,0:T(8,128)(2,1)S(1)}, bf16[4224,128]{1,0:T(8,128)(2,1)S(1)}, u32[]{:S(2)}, u32[]{:S(2)}) collective-permute-start(bf16[4224,128]{1,0:T(8,128)(2,1)S(1)} %get-tuple-element.60), channel_id=1, source_target_pairs={{0,4},{1,13},{4,0},{5,9},{8,12},{9,5},{12,8},{13,1},{2,6},{3,15},{... | collective-permute-start | bytes 3244040 | tf_op jit(solution)/shard_map/sum_near_0/ppermute | solution.py:28
  62.0 0.8 collective-permute-done.10
  62.9 2.4 %collective-permute-done.11.far = bf16[32,128,128]{2,1,0:T(8,128)(2,1)S(1)} collective-permute-done((bf16[32,128,128]{2,1,0:T(8,128)(2,1)S(1)}, bf16[32,128,128]{2,1,0:T(8,128)(2,1)S(1)}, u32[]{:S(2)}, u32[]{:S(2)}) %collective-permute-start.11) | collective-permute-done | bytes 1048608 | tf_op jit(solution)/shard_map/gather_far_1/ppermute | solution.py:28
  66.0 5.5 %tiles_1.1 = (bf16[4096,128]{1,0:T(8,128)(2,1)S(1)}, bf16[2048,128]{1,0:T(8,128)(2,1)S(1)}, bf16[2048,128]{1,0:T(8,128)(2,1)S(1)}) custom-call(s32[128]{0:T(128)S(1)} %fusion.27.src_ref, s32[128]{0:T(128)S(1)} %fusion.28.dst_ref, s32[2]{0:T(128)S(1)} %fusion.26.live_ref, bf16[64,128,128]{2,1,0:T(8,128)(2,1)} %get-tuple-element.59.c_own, ...), custom_call_target="tpu_custom_call" | custom-call | flops 2147483648 | bytes 1048576 | tf_op jit(solution)/shard_map/tiles_1/pallas_call | solution.py:90
  71.4 4.0 %collective-permute-start.18 = (bf16[4096,128]{1,0:T(8,128)(2,1)S(1)}, bf16[4096,128]{1,0:T(8,128)(2,1)S(1)}, u32[]{:S(2)}, u32[]{:S(2)}) collective-permute-start(bf16[4096,128]{1,0:T(8,128)(2,1)S(1)} %get-tuple-element.63), channel_id=1, source_target_pairs={{0,4},{1,13},{4,0},{5,9},{8,12},{9,5},{12,8},{13,1},{2,6},{3,15},{... | collective-permute-start | bytes 3145736 | tf_op jit(solution)/shard_map/sum_near_1/ppermute | solution.py:28
  76.2 1.9 %collective-permute-start.14 = (bf16[32,128,128]{2,1,0:T(8,128)(2,1)S(1)}, bf16[32,128,128]{2,1,0:T(8,128)(2,1)S(1)}, u32[]{:S(2)}, u32[]{:S(2)}) collective-permute-start(bf16[32,128,128]{2,1,0:T(8,128)(2,1)S(1)} %constant_dynamic-update-slice_fusion.6.near), channel_id=1, source_target_pairs={{0,48},{1,17},{16,32},{17,1},{32,16},{33,49},{48,0},{49,33},{2,50}... | collective-permute-start | bytes 3145736 | tf_op jit(solution)/shard_map/gather_far_3/ppermute | solution.py:28
  78.4 7.1 %collective-permute-done.16.far = bf16[32,128,128]{2,1,0:T(8,128)(2,1)S(1)} collective-permute-done((bf16[32,128,128]{2,1,0:T(8,128)(2,1)S(1)}, bf16[32,128,128]{2,1,0:T(8,128)(2,1)S(1)}, u32[]{:S(2)}, u32[]{:S(2)}) %collective-permute-start.16) | collective-permute-done | bytes 1048608 | tf_op jit(solution)/shard_map/gather_far_2/ppermute | solution.py:28
  85.5 5.7 %tiles_2.1 = (bf16[4096,128]{1,0:T(8,128)(2,1)S(1)}, bf16[2048,128]{1,0:T(8,128)(2,1)S(1)}, bf16[2048,128]{1,0:T(8,128)(2,1)S(1)}) custom-call(s32[128]{0:T(128)S(1)} %fusion.27.src_ref, s32[128]{0:T(128)S(1)} %fusion.28.dst_ref, s32[2]{0:T(128)S(1)} %fusion.26.live_ref, bf16[64,128,128]{2,1,0:T(8,128)(2,1)} %get-tuple-element.59.c_own, ...), custom_call_target="tpu_custom_call" | custom-call | flops 1048576 | bytes 1048576 | tf_op jit(solution)/shard_map/tiles_2/pallas_call | solution.py:90
  91.2 4.1 %collective-permute-start.17 = (bf16[4096,128]{1,0:T(8,128)(2,1)S(1)}, bf16[4096,128]{1,0:T(8,128)(2,1)S(1)}, u32[]{:S(2)}, u32[]{:S(2)}) collective-permute-start(bf16[4096,128]{1,0:T(8,128)(2,1)S(1)} %get-tuple-element.72), channel_id=1, source_target_pairs={{0,4},{1,13},{4,0},{5,9},{8,12},{9,5},{12,8},{13,1},{2,6},{3,15},{... | collective-permute-start | bytes 3145736 | tf_op jit(solution)/shard_map/sum_near_2/ppermute | solution.py:28
  95.5 1.5 collective-permute-start.19
  97.0 5.5 %tiles_3.1 = (bf16[4096,128]{1,0:T(8,128)(2,1)S(1)}, bf16[2048,128]{1,0:T(8,128)(2,1)S(1)}, bf16[2048,128]{1,0:T(8,128)(2,1)S(1)}) custom-call(s32[128]{0:T(128)S(1)} %fusion.27.src_ref, s32[128]{0:T(128)S(1)} %fusion.28.dst_ref, s32[2]{0:T(128)S(1)} %fusion.26.live_ref, bf16[64,128,128]{2,1,0:T(8,128)(2,1)} %get-tuple-element.59.c_own, ...), custom_call_target="tpu_custom_call" | custom-call | flops 1048576 | bytes 1048576 | tf_op jit(solution)/shard_map/tiles_3/pallas_call | solution.py:90
  102.5 3.8 %collective-permute-start.21 = (bf16[4096,128]{1,0:T(8,128)(2,1)S(1)}, bf16[4096,128]{1,0:T(8,128)(2,1)S(1)}, u32[]{:S(2)}, u32[]{:S(2)}) collective-permute-start(bf16[4096,128]{1,0:T(8,128)(2,1)S(1)} %get-tuple-element.68), channel_id=1, source_target_pairs={{0,4},{1,13},{4,0},{5,9},{8,12},{9,5},{12,8},{13,1},{2,6},{3,15},{... | collective-permute-start | bytes 3145736 | tf_op jit(solution)/shard_map/sum_near_3/ppermute | solution.py:28
  106.3 3.3 %collective-permute-done.12 = bf16[2112,128]{1,0:T(8,128)(2,1)S(1)} collective-permute-done((bf16[2112,128]{1,0:T(8,128)(2,1)S(1)}, bf16[2112,128]{1,0:T(8,128)(2,1)S(1)}, u32[]{:S(2)}, u32[]{:S(2)}) %collective-permute-start.12) | collective-permute-done | bytes 540704 | tf_op jit(solution)/shard_map/sum_far_0/ppermute | solution.py:28
  109.6 1.9 %collective-permute-start.15 = (bf16[1056,128]{1,0:T(8,128)(2,1)S(1)}, bf16[1056,128]{1,0:T(8,128)(2,1)S(1)}, u32[]{:S(2)}, u32[]{:S(2)}) collective-permute-start(bf16[1056,128]{1,0:T(8,128)(2,1)S(1)} %fusion.7), channel_id=1, source_target_pairs={{0,2},{2,0},{1,3},{3,1},{4,6},{6,4},{5,7},{7,5},{8,10},{10,8},{9,1... | collective-permute-start | bytes 811016 | tf_op jit(solution)/shard_map/sum_x_0/ppermute | solution.py:18
  111.6 5.3 %collective-permute-done.17 = bf16[4096,128]{1,0:T(8,128)(2,1)S(1)} collective-permute-done((bf16[4096,128]{1,0:T(8,128)(2,1)S(1)}, bf16[4096,128]{1,0:T(8,128)(2,1)S(1)}, u32[]{:S(2)}, u32[]{:S(2)}) %collective-permute-start.17) | collective-permute-done | bytes 1048608 | tf_op jit(solution)/shard_map/sum_near_2/ppermute | solution.py:28
  117.1 1.1 collective-permute-done.15
  118.3 2.5 %collective-permute-done.19 = bf16[2048,128]{1,0:T(8,128)(2,1)S(1)} collective-permute-done((bf16[2048,128]{1,0:T(8,128)(2,1)S(1)}, bf16[2048,128]{1,0:T(8,128)(2,1)S(1)}, u32[]{:S(2)}, u32[]{:S(2)}) %collective-permute-start.19) | collective-permute-done | bytes 524320 | tf_op jit(solution)/shard_map/sum_far_1/ppermute | solution.py:28
  120.9 1.9 %collective-permute-start.20 = (bf16[1024,128]{1,0:T(8,128)(2,1)S(1)}, bf16[1024,128]{1,0:T(8,128)(2,1)S(1)}, u32[]{:S(2)}, u32[]{:S(2)}) collective-permute-start(bf16[1024,128]{1,0:T(8,128)(2,1)S(1)} %fusion.16), channel_id=1, source_target_pairs={{0,2},{2,0},{1,3},{3,1},{4,6},{6,4},{5,7},{7,5},{8,10},{10,8},{9,1... | collective-permute-start | bytes 786440 | tf_op jit(solution)/shard_map/sum_x_1/ppermute | solution.py:18
  123.2 9.0 %collective-permute-done.21 = bf16[4096,128]{1,0:T(8,128)(2,1)S(1)} collective-permute-done((bf16[4096,128]{1,0:T(8,128)(2,1)S(1)}, bf16[4096,128]{1,0:T(8,128)(2,1)S(1)}, u32[]{:S(2)}, u32[]{:S(2)}) %collective-permute-start.21) | collective-permute-done | bytes 1048608 | tf_op jit(solution)/shard_map/sum_near_3/ppermute | solution.py:28
  132.5 2.4 %collective-permute-done.23 = bf16[2048,128]{1,0:T(8,128)(2,1)S(1)} collective-permute-done((bf16[2048,128]{1,0:T(8,128)(2,1)S(1)}, bf16[2048,128]{1,0:T(8,128)(2,1)S(1)}, u32[]{:S(2)}, u32[]{:S(2)}) %collective-permute-start.23) | collective-permute-done | bytes 524320 | tf_op jit(solution)/shard_map/sum_far_2/ppermute | solution.py:28
  135.0 2.5 %collective-permute-start.24 = (bf16[1024,128]{1,0:T(8,128)(2,1)S(1)}, bf16[1024,128]{1,0:T(8,128)(2,1)S(1)}, u32[]{:S(2)}, u32[]{:S(2)}) collective-permute-start(bf16[1024,128]{1,0:T(8,128)(2,1)S(1)} %fusion.11), channel_id=1, source_target_pairs={{0,2},{2,0},{1,3},{3,1},{4,6},{6,4},{5,7},{7,5},{8,10},{10,8},{9,1... | collective-permute-start | bytes 786440 | tf_op jit(solution)/shard_map/sum_x_2/ppermute | solution.py:18
  137.8 3.4 %collective-permute-start.22 = (bf16[512,256]{1,0:T(8,128)(2,1)S(1)}, bf16[512,256]{1,0:T(8,128)(2,1)S(1)}, u32[]{:S(2)}, u32[]{:S(2)}) collective-permute-start(bf16[512,256]{1,0:T(8,128)(2,1)S(1)} %pad_maximum_fusion.5), channel_id=1, source_target_pairs={{0,1},{1,0},{2,3},{3,2},{4,5},{5,4},{6,7},{7,6},{8,9},{9,8},{10,11... | collective-permute-start | bytes 786440 | tf_op jit(solution)/shard_map/mean_core_0/ppermute | solution.py:18
  141.2 1.5 fusion.13
  142.9 1.5 collective-permute-start.26
  144.7 5.1 %collective-permute-done.26 = bf16[1024,128]{1,0:T(8,128)(2,1)S(1)} collective-permute-done((bf16[1024,128]{1,0:T(8,128)(2,1)S(1)}, bf16[1024,128]{1,0:T(8,128)(2,1)S(1)}, u32[]{:S(2)}, u32[]{:S(2)}) %collective-permute-start.26) | collective-permute-done | bytes 262176 | tf_op jit(solution)/shard_map/sum_x_3/ppermute | solution.py:18
  150.1 5.1 %collective-permute-start.27 = (bf16[512,256]{1,0:T(8,128)(2,1)S(1)}, bf16[512,256]{1,0:T(8,128)(2,1)S(1)}, u32[]{:S(2)}, u32[]{:S(2)}) collective-permute-start(bf16[512,256]{1,0:T(8,128)(2,1)S(1)} %pad_maximum_fusion.7), channel_id=1, source_target_pairs={{0,1},{1,0},{2,3},{3,2},{4,5},{5,4},{6,7},{7,6},{8,9},{9,8},{10,11... | collective-permute-start | bytes 786440 | tf_op jit(solution)/shard_map/mean_core_1/ppermute | solution.py:18
  155.2 1.5 add_add_fusion.hidden
  156.7 2.9 %shard_map.102 = f32[512,1024]{1,0:T(8,128)} custom-call(f32[512,1024]{1,0:T(8,128)S(1)} %add_add_fusion.hidden, bf16[512,256]{1,0:T(8,128)(2,1)S(1)} %pad_maximum_fusion.6.near, bf16[512,256]{1,0:T(8,128)(2,1)S(1)} %collective-permute-done.27.got, bf16[512,1024]{1,0:T(8,128)(2,1)S(1)} %pad_maximum_fusion.weight), custom_call_target="tpu_custom_call" | custom-call | tf_op jit(solution)/shard_map/pallas_call | solution.py:175
  (98 shorter events, 8.5 us)
Async XLA Ops:
  0.0 6.7 %collective-permute-start = (bf16[512,1024]{1,0:T(8,128)(2,1)}, bf16[512,1024]{1,0:T(8,128)(2,1)S(1)}, u32[]{:S(2)}, u32[]{:S(2)}) collective-permute-start(bf16[512,1024]{1,0:T(8,128)(2,1)} %x_own.2), channel_id=1, source_target_pairs={{0,1},{1,0},{2,3},{3,2},{4,5},{5,4},{6,7},{7,6},{8,9},{9,8},{10,11... | collective-permute-start | bytes 3145736 | tf_op jit(solution)/shard_map/other_features_0/ppermute | solution.py:18
  2.3 4.4 %copy-start = (bf16[1024,1024]{1,0:T(8,128)(2,1)S(1)}, bf16[1024,1024]{1,0:T(8,128)(2,1)}, u32[]{:S(2)}) copy-start(bf16[1024,1024]{1,0:T(8,128)(2,1)} %weight.3) | copy-start | bytes 6291460
  2.3 4.4 %copy-start.1 = (bf16[512,1024]{1,0:T(8,128)(2,1)S(1)}, bf16[512,1024]{1,0:T(8,128)(2,1)}, u32[]{:S(2)}) copy-start(bf16[512,1024]{1,0:T(8,128)(2,1)} %x_own.2) | copy-start | bytes 3145732
  2.4 4.4 %copy-start.2 = (f32[1024]{0:T(1024)S(1)}, f32[1024]{0:T(1024)}, u32[]{:S(2)}) copy-start(f32[1024]{0:T(1024)} %param.16) | copy-start | bytes 12292
  6.7 2.2 %copy-start.4 = (bf16[2048,1024]{1,0:T(8,128)(2,1)S(1)}, bf16[2048,1024]{1,0:T(8,128)(2,1)}, u32[]{:S(2)}) copy-start(bf16[2048,1024]{1,0:T(8,128)(2,1)} %param.17) | copy-start | bytes 12582916
  6.8 2.2 %copy-start.7 = (f32[1024]{0:T(1024)S(1)}, f32[1024]{0:T(1024)}, u32[]{:S(2)}) copy-start(f32[1024]{0:T(1024)} %param.18) | copy-start | bytes 12292
  7.7 8.0 %collective-permute-start.2 = (bf16[8,128,128]{2,1,0:T(8,128)(2,1)S(1)}, bf16[8,128,128]{2,1,0:T(8,128)(2,1)S(1)}, u32[]{:S(2)}, u32[]{:S(2)}) collective-permute-start(bf16[8,128,128]{2,1,0:T(8,128)(2,1)S(1)} %shard_map.100), channel_id=1, source_target_pairs={{0,64},{64,0},{1,65},{65,1},{2,66},{66,2},{3,67},{67,3},{4,68},{68... | collective-permute-start | bytes 786440 | tf_op jit(solution)/shard_map/gather_x_0/ppermute | solution.py:18
  8.0 11.9 %collective-permute-start.1 = (s32[3,64]{1,0:T(4,128)S(1)}, s32[3,64]{1,0:T(4,128)S(1)}, u32[]{:S(2)}, u32[]{:S(2)}) collective-permute-start(s32[3,64]{1,0:T(4,128)S(1)} %get-tuple-element.48), channel_id=1, source_target_pairs={{0,1},{1,0},{2,3},{3,2},{4,5},{5,4},{6,7},{7,6},{8,9},{9,8},{10,11... | collective-permute-start | bytes 2312 | tf_op jit(solution)/shard_map/other_meta/ppermute | solution.py:18
  8.3 41.2 %collective-permute-start.7 = (bf16[64,128,128]{2,1,0:T(8,128)(2,1)}, bf16[64,128,128]{2,1,0:T(8,128)(2,1)}, u32[]{:S(2)}, u32[]{:S(2)}) collective-permute-start(bf16[64,128,128]{2,1,0:T(8,128)(2,1)} %get-tuple-element.59.c_own), channel_id=1, source_target_pairs={{0,1},{1,0},{2,3},{3,2},{4,5},{5,4},{6,7},{7,6},{8,9},{9,8},{10,11... | collective-permute-start | bytes 6291464 | tf_op jit(solution)/shard_map/other_tiles/ppermute | solution.py:18
  15.8 9.5 %collective-permute-start.4 = (bf16[16,128,128]{2,1,0:T(8,128)(2,1)S(1)}, bf16[16,128,128]{2,1,0:T(8,128)(2,1)}, u32[]{:S(2)}, u32[]{:S(2)}) collective-permute-start(bf16[16,128,128]{2,1,0:T(8,128)(2,1)S(1)} %pad_maximum_fusion.1), channel_id=1, source_target_pairs={{0,16},{1,49},{16,0},{17,33},{32,48},{33,17},{48,32},{49,1},{2,18}... | collective-permute-start | bytes 1572872 | tf_op jit(solution)/shard_map/gather_near_0/ppermute | solution.py:28
  19.5 8.3 %collective-permute-start.3 = (bf16[8,128,128]{2,1,0:T(8,128)(2,1)S(1)}, bf16[8,128,128]{2,1,0:T(8,128)(2,1)}, u32[]{:S(2)}, u32[]{:S(2)}) collective-permute-start(bf16[8,128,128]{2,1,0:T(8,128)(2,1)S(1)} %get-tuple-element.51), channel_id=1, source_target_pairs={{0,64},{64,0},{1,65},{65,1},{2,66},{66,2},{3,67},{67,3},{4,68},{68... | collective-permute-start | bytes 786440 | tf_op jit(solution)/shard_map/gather_x_1/ppermute | solution.py:18
  26.4 21.4 %collective-permute-start.8 = (bf16[32,128,128]{2,1,0:T(8,128)(2,1)S(1)}, bf16[32,128,128]{2,1,0:T(8,128)(2,1)}, u32[]{:S(2)}, u32[]{:S(2)}) collective-permute-start(bf16[32,128,128]{2,1,0:T(8,128)(2,1)S(1)} %constant_dynamic-update-slice_fusion.near), channel_id=1, source_target_pairs={{0,48},{1,17},{16,32},{17,1},{32,16},{33,49},{48,0},{49,33},{2,50}... | collective-permute-start | bytes 3145736 | tf_op jit(solution)/shard_map/gather_far_0/ppermute | solution.py:28
  27.9 17.9 %collective-permute-start.5 = (bf16[16,128,128]{2,1,0:T(8,128)(2,1)S(1)}, bf16[16,128,128]{2,1,0:T(8,128)(2,1)}, u32[]{:S(2)}, u32[]{:S(2)}) collective-permute-start(bf16[16,128,128]{2,1,0:T(8,128)(2,1)S(1)} %get-tuple-element.55), channel_id=1, source_target_pairs={{0,64},{64,0},{1,65},{65,1},{2,66},{66,2},{3,67},{67,3},{4,68},{68... | collective-permute-start | bytes 1572872 | tf_op jit(solution)/shard_map/gather_x_rest/ppermute | solution.py:18
  29.2 15.4 %collective-permute-start.6 = (bf16[16,128,128]{2,1,0:T(8,128)(2,1)S(1)}, bf16[16,128,128]{2,1,0:T(8,128)(2,1)}, u32[]{:S(2)}, u32[]{:S(2)}) collective-permute-start(bf16[16,128,128]{2,1,0:T(8,128)(2,1)S(1)} %pad_maximum_fusion.2), channel_id=1, source_target_pairs={{0,16},{1,49},{16,0},{17,33},{32,48},{33,17},{48,32},{49,1},{2,18}... | collective-permute-start | bytes 1572872 | tf_op jit(solution)/shard_map/gather_near_1/ppermute | solution.py:28
  45.7 19.6 %collective-permute-start.11 = (bf16[32,128,128]{2,1,0:T(8,128)(2,1)S(1)}, bf16[32,128,128]{2,1,0:T(8,128)(2,1)S(1)}, u32[]{:S(2)}, u32[]{:S(2)}) collective-permute-start(bf16[32,128,128]{2,1,0:T(8,128)(2,1)S(1)} %constant_dynamic-update-slice_fusion.2.near), channel_id=1, source_target_pairs={{0,48},{1,17},{16,32},{17,1},{32,16},{33,49},{48,0},{49,33},{2,50}... | collective-permute-start | bytes 3145736 | tf_op jit(solution)/shard_map/gather_far_1/ppermute | solution.py:28
  47.9 14.9 %collective-permute-start.10 = (bf16[16,128,128]{2,1,0:T(8,128)(2,1)S(1)}, bf16[16,128,128]{2,1,0:T(8,128)(2,1)S(1)}, u32[]{:S(2)}, u32[]{:S(2)}) collective-permute-start(bf16[16,128,128]{2,1,0:T(8,128)(2,1)S(1)} %pad_maximum_fusion.3), channel_id=1, source_target_pairs={{0,16},{1,49},{16,0},{17,33},{32,48},{33,17},{48,32},{49,1},{2,18}... | collective-permute-start | bytes 1572872 | tf_op jit(solution)/shard_map/gather_near_2/ppermute | solution.py:28
  52.0 9.9 %copy-start.5 = (bf16[8,128,128]{2,1,0:T(8,128)(2,1)S(1)}, bf16[8,128,128]{2,1,0:T(8,128)(2,1)}, u32[]{:S(2)}) copy-start(bf16[8,128,128]{2,1,0:T(8,128)(2,1)} %get-tuple-element.103) | copy-start | bytes 786436
  57.8 20.3 %collective-permute-start.9 = (bf16[4224,128]{1,0:T(8,128)(2,1)S(1)}, bf16[4224,128]{1,0:T(8,128)(2,1)S(1)}, u32[]{:S(2)}, u32[]{:S(2)}) collective-permute-start(bf16[4224,128]{1,0:T(8,128)(2,1)S(1)} %get-tuple-element.60), channel_id=1, source_target_pairs={{0,4},{1,13},{4,0},{5,9},{8,12},{9,5},{12,8},{13,1},{2,6},{3,15},{... | collective-permute-start | bytes 3244040 | tf_op jit(solution)/shard_map/sum_near_0/ppermute | solution.py:28
  65.3 10.8 %collective-permute-start.13 = (bf16[16,128,128]{2,1,0:T(8,128)(2,1)S(1)}, bf16[16,128,128]{2,1,0:T(8,128)(2,1)S(1)}, u32[]{:S(2)}, u32[]{:S(2)}) collective-permute-start(bf16[16,128,128]{2,1,0:T(8,128)(2,1)S(1)} %pad_maximum_fusion.4), channel_id=1, source_target_pairs={{0,16},{1,49},{16,0},{17,33},{32,48},{33,17},{48,32},{49,1},{2,18}... | collective-permute-start | bytes 1572872 | tf_op jit(solution)/shard_map/gather_near_3/ppermute | solution.py:28
  65.9 19.6 %collective-permute-start.16 = (bf16[32,128,128]{2,1,0:T(8,128)(2,1)S(1)}, bf16[32,128,128]{2,1,0:T(8,128)(2,1)S(1)}, u32[]{:S(2)}, u32[]{:S(2)}) collective-permute-start(bf16[32,128,128]{2,1,0:T(8,128)(2,1)S(1)} %constant_dynamic-update-slice_fusion.4.near), channel_id=1, source_target_pairs={{0,48},{1,17},{16,32},{17,1},{32,16},{33,49},{48,0},{49,33},{2,50}... | collective-permute-start | bytes 3145736 | tf_op jit(solution)/shard_map/gather_far_2/ppermute | solution.py:28
  71.4 23.8 %collective-permute-start.18 = (bf16[4096,128]{1,0:T(8,128)(2,1)S(1)}, bf16[4096,128]{1,0:T(8,128)(2,1)S(1)}, u32[]{:S(2)}, u32[]{:S(2)}) collective-permute-start(bf16[4096,128]{1,0:T(8,128)(2,1)S(1)} %get-tuple-element.63), channel_id=1, source_target_pairs={{0,4},{1,13},{4,0},{5,9},{8,12},{9,5},{12,8},{13,1},{2,6},{3,15},{... | collective-permute-start | bytes 3145736 | tf_op jit(solution)/shard_map/sum_near_1/ppermute | solution.py:28
  76.2 20.8 %collective-permute-start.14 = (bf16[32,128,128]{2,1,0:T(8,128)(2,1)S(1)}, bf16[32,128,128]{2,1,0:T(8,128)(2,1)S(1)}, u32[]{:S(2)}, u32[]{:S(2)}) collective-permute-start(bf16[32,128,128]{2,1,0:T(8,128)(2,1)S(1)} %constant_dynamic-update-slice_fusion.6.near), channel_id=1, source_target_pairs={{0,48},{1,17},{16,32},{17,1},{32,16},{33,49},{48,0},{49,33},{2,50}... | collective-permute-start | bytes 3145736 | tf_op jit(solution)/shard_map/gather_far_3/ppermute | solution.py:28
  91.2 25.7 %collective-permute-start.17 = (bf16[4096,128]{1,0:T(8,128)(2,1)S(1)}, bf16[4096,128]{1,0:T(8,128)(2,1)S(1)}, u32[]{:S(2)}, u32[]{:S(2)}) collective-permute-start(bf16[4096,128]{1,0:T(8,128)(2,1)S(1)} %get-tuple-element.72), channel_id=1, source_target_pairs={{0,4},{1,13},{4,0},{5,9},{8,12},{9,5},{12,8},{13,1},{2,6},{3,15},{... | collective-permute-start | bytes 3145736 | tf_op jit(solution)/shard_map/sum_near_2/ppermute | solution.py:28
  95.2 14.4 %collective-permute-start.12 = (bf16[2112,128]{1,0:T(8,128)(2,1)S(1)}, bf16[2112,128]{1,0:T(8,128)(2,1)S(1)}, u32[]{:S(2)}, u32[]{:S(2)}) collective-permute-start(bf16[2112,128]{1,0:T(8,128)(2,1)S(1)} %get-tuple-element.96), channel_id=1, source_target_pairs={{0,12},{1,5},{4,8},{5,1},{8,4},{9,13},{12,0},{13,9},{2,14},{3,7},{... | collective-permute-start | bytes 1622024 | tf_op jit(solution)/shard_map/sum_far_0/ppermute | solution.py:28
  95.5 25.3 %collective-permute-start.19 = (bf16[2048,128]{1,0:T(8,128)(2,1)S(1)}, bf16[2048,128]{1,0:T(8,128)(2,1)S(1)}, u32[]{:S(2)}, u32[]{:S(2)}) collective-permute-start(bf16[2048,128]{1,0:T(8,128)(2,1)S(1)} %get-tuple-element.101), channel_id=1, source_target_pairs={{0,12},{1,5},{4,8},{5,1},{8,4},{9,13},{12,0},{13,9},{2,14},{3,7},{... | collective-permute-start | bytes 1572872 | tf_op jit(solution)/shard_map/sum_far_1/ppermute | solution.py:28
  102.5 29.7 %collective-permute-start.21 = (bf16[4096,128]{1,0:T(8,128)(2,1)S(1)}, bf16[4096,128]{1,0:T(8,128)(2,1)S(1)}, u32[]{:S(2)}, u32[]{:S(2)}) collective-permute-start(bf16[4096,128]{1,0:T(8,128)(2,1)S(1)} %get-tuple-element.68), channel_id=1, source_target_pairs={{0,4},{1,13},{4,0},{5,9},{8,12},{9,5},{12,8},{13,1},{2,6},{3,15},{... | collective-permute-start | bytes 3145736 | tf_op jit(solution)/shard_map/sum_near_3/ppermute | solution.py:28
  109.6 8.6 %collective-permute-start.15 = (bf16[1056,128]{1,0:T(8,128)(2,1)S(1)}, bf16[1056,128]{1,0:T(8,128)(2,1)S(1)}, u32[]{:S(2)}, u32[]{:S(2)}) collective-permute-start(bf16[1056,128]{1,0:T(8,128)(2,1)S(1)} %fusion.7), channel_id=1, source_target_pairs={{0,2},{2,0},{1,3},{3,1},{4,6},{6,4},{5,7},{7,5},{8,10},{10,8},{9,1... | collective-permute-start | bytes 811016 | tf_op jit(solution)/shard_map/sum_x_0/ppermute | solution.py:18
  117.1 5.7 %copy-start.6 = (f32[4]{0:T(128)S(1)}, f32[4]{0:T(128)}, u32[]{:S(2)}) copy-start(f32[4]{0:T(128)} %constant.140.clone) | copy-start | bytes 52
  120.9 16.6 %collective-permute-start.20 = (bf16[1024,128]{1,0:T(8,128)(2,1)S(1)}, bf16[1024,128]{1,0:T(8,128)(2,1)S(1)}, u32[]{:S(2)}, u32[]{:S(2)}) collective-permute-start(bf16[1024,128]{1,0:T(8,128)(2,1)S(1)} %fusion.16), channel_id=1, source_target_pairs={{0,2},{2,0},{1,3},{3,1},{4,6},{6,4},{5,7},{7,5},{8,10},{10,8},{9,1... | collective-permute-start | bytes 786440 | tf_op jit(solution)/shard_map/sum_x_1/ppermute | solution.py:18
  122.9 12.0 %collective-permute-start.23 = (bf16[2048,128]{1,0:T(8,128)(2,1)S(1)}, bf16[2048,128]{1,0:T(8,128)(2,1)S(1)}, u32[]{:S(2)}, u32[]{:S(2)}) collective-permute-start(bf16[2048,128]{1,0:T(8,128)(2,1)S(1)} %get-tuple-element.98), channel_id=1, source_target_pairs={{0,12},{1,5},{4,8},{5,1},{8,4},{9,13},{12,0},{13,9},{2,14},{3,7},{... | collective-permute-start | bytes 1572872 | tf_op jit(solution)/shard_map/sum_far_2/ppermute | solution.py:28
  132.4 10.4 %collective-permute-start.25 = (bf16[2048,128]{1,0:T(8,128)(2,1)S(1)}, bf16[2048,128]{1,0:T(8,128)(2,1)S(1)}, u32[]{:S(2)}, u32[]{:S(2)}) collective-permute-start(bf16[2048,128]{1,0:T(8,128)(2,1)S(1)} %get-tuple-element.100), channel_id=1, source_target_pairs={{0,12},{1,5},{4,8},{5,1},{8,4},{9,13},{12,0},{13,9},{2,14},{3,7},{... | collective-permute-start | bytes 1572872 | tf_op jit(solution)/shard_map/sum_far_3/ppermute | solution.py:28
  135.0 7.7 %collective-permute-start.24 = (bf16[1024,128]{1,0:T(8,128)(2,1)S(1)}, bf16[1024,128]{1,0:T(8,128)(2,1)S(1)}, u32[]{:S(2)}, u32[]{:S(2)}) collective-permute-start(bf16[1024,128]{1,0:T(8,128)(2,1)S(1)} %fusion.11), channel_id=1, source_target_pairs={{0,2},{2,0},{1,3},{3,1},{4,6},{6,4},{5,7},{7,5},{8,10},{10,8},{9,1... | collective-permute-start | bytes 786440 | tf_op jit(solution)/shard_map/sum_x_2/ppermute | solution.py:18
  137.8 17.4 %collective-permute-start.22 = (bf16[512,256]{1,0:T(8,128)(2,1)S(1)}, bf16[512,256]{1,0:T(8,128)(2,1)S(1)}, u32[]{:S(2)}, u32[]{:S(2)}) collective-permute-start(bf16[512,256]{1,0:T(8,128)(2,1)S(1)} %pad_maximum_fusion.5), channel_id=1, source_target_pairs={{0,1},{1,0},{2,3},{3,2},{4,5},{5,4},{6,7},{7,6},{8,9},{9,8},{10,11... | collective-permute-start | bytes 786440 | tf_op jit(solution)/shard_map/mean_core_0/ppermute | solution.py:18
  142.9 6.8 %collective-permute-start.26 = (bf16[1024,128]{1,0:T(8,128)(2,1)S(1)}, bf16[1024,128]{1,0:T(8,128)(2,1)S(1)}, u32[]{:S(2)}, u32[]{:S(2)}) collective-permute-start(bf16[1024,128]{1,0:T(8,128)(2,1)S(1)} %fusion.9), channel_id=1, source_target_pairs={{0,2},{2,0},{1,3},{3,1},{4,6},{6,4},{5,7},{7,5},{8,10},{10,8},{9,1... | collective-permute-start | bytes 786440 | tf_op jit(solution)/shard_map/sum_x_3/ppermute | solution.py:18
  144.6 10.5 %copy-start.3 = (f32[512,1024]{1,0:T(8,128)S(1)}, f32[512,1024]{1,0:T(8,128)}, u32[]{:S(2)}) copy-start(f32[512,1024]{1,0:T(8,128)} %fusion.3) | copy-start | bytes 6291460
  150.1 6.6 %collective-permute-start.27 = (bf16[512,256]{1,0:T(8,128)(2,1)S(1)}, bf16[512,256]{1,0:T(8,128)(2,1)S(1)}, u32[]{:S(2)}, u32[]{:S(2)}) collective-permute-start(bf16[512,256]{1,0:T(8,128)(2,1)S(1)} %pad_maximum_fusion.7), channel_id=1, source_target_pairs={{0,1},{1,0},{2,3},{3,2},{4,5},{5,4},{6,7},{7,6},{8,9},{9,8},{10,11... | collective-permute-start | bytes 786440 | tf_op jit(solution)/shard_map/mean_core_1/ppermute | solution.py:18

commit v11 on v10

--- a/solution.py
+++ b/solution.py
@@ -273,6 +273,8 @@
     scale = None
 
     def far(pair, got, j):
+        if j == 1:
+            got = after(got, parts)
         near_all.append(jnp.concatenate([pair, got]))
         far_all.append(step(near_all[j], "y", 1, f"gather_far_{j}"))
 
@@ -336,7 +338,7 @@
         size = stay.shape[0] // 2
         got = step(pass_all[j], "z", 1, f"sum_far_{j}")
         if j == 0:
-            got = after(got, part_all[-1][0])
+            got = after(got, part_all[2][0])
         elif j + 1 < CHUNKS:
             got = after(got, pass_all[j + 1])
         passed = (got[:size].astype(f32) + stay[:size]).astype(bf16)

time: 162 us -> 157 us (0.969)
  waiting for transfers between devices: 61.7 us -> 65.7 us
  local copies, waits for them, and re-layouts: 5.56 us -> 1.61 us
  starting transfers between devices: 44.8 us -> 42.3 us
  other arithmetic: 12.3 us -> 10.3 us
    ppermute x16, waiting for transfers between devices: 52.3 us -> 56.4 us  [step(): return lax.ppermute(x, (axis, 'core'), pairs)]
    concatenate x4, local copies, waits for them, and re-layouts: 2.38 us -> 0.29 us  [far(): near_all.append(jnp.concatenate([pair, got]))]
    ppermute x16, starting transfers between devices: 26.5 us -> 24.5 us  [step(): return lax.ppermute(x, (axis, 'core'), pairs)]
    concatenate x3, other arithmetic: 2.04 us -> 0.14 us  [local(): pair = jnp.concatenate([own[j], partner[j]])]
    slice x2, local copies, waits for them, and re-layouts: 1.92 us -> 0.08 us  [local(): split = lambda x: [x[i * size:(i + 1) * size] for i in range(CHUNKS - 2)]]
  transfers between devices with their start and end apart: 28 -> 28, of which waited for: 15 -> 11; matrix products, arithmetic and copies ran while one was open for 14% -> 11% of each run, Pallas kernels for 15% -> 16%
where the time goes in v11:
time: 157 us; the launch traced here: 156 us
  waiting for transfers between devices  65.7 us (42%)
  starting transfers between devices  42.3 us (27%)
  Pallas kernels  28.8 us (18%)
  other arithmetic  10.3 us (7%)
  matrix products  5.73 us (4%)
  local copies, waits for them, and re-layouts  1.61 us (1%)
    ppermute x16, waiting for transfers between devices, step(): return lax.ppermute(x, (axis, 'core'), pairs)  56.4 us
    ppermute x16, starting transfers between devices, step(): return lax.ppermute(x, (axis, 'core'), pairs)  24.5 us
    pallas_call x4, Pallas kernels, tile_sums(): pl.pallas_call(tile_kernel, out_shape=(jax.ShapeDtypeStruct((4 * size, w)...  22.8 us
    ppermute x12, starting transfers between devices, swap(): return lax.ppermute(x, axis, [(0, 1), (1, 0)])  17.7 us
    ppermute x12, waiting for transfers between devices, swap(): return lax.ppermute(x, axis, [(0, 1), (1, 0)])  9.35 us
    reduce_sum x1, other arithmetic, local(): jnp.sum(c_own.astype(jnp.float32), axis=2)  4.34 us
  transfers between devices with their start and end apart: 28, of which 11 were waited for; matrix products, arithmetic and copies ran while one was open for 11% of the time, Pallas kernels for 16%

profile of v11, /device:TPU:3, one launch (start us, length us, event | category | flops | bytes accessed | tf_op | source)
XLA Modules:
  0.0 155.7 jit_solution(7287060224401201358)
XLA Ops:
  0.0 0.7 collective-permute-start
  1.6 0.7 compare_select_fusion.14
  2.4 4.3 %convert_reduce_fusion.1 = (f32[64,128]{1,0:T(8,128)S(1)}, bf16[64,128,128]{2,1,0:T(8,128)(2,1)}) fusion(s32[1,1,64,128,128]{4,3,2,1,0:T(8,128)} %param.11, pred[64]{0:T(512)(128)(4,1)S(1)} %iota_compare_fusion.2), kind=kLoop, calls=%fused_computation.3 | loop fusion | flops 4186112 | bytes 6324288 | tf_op jit(solution)/shard_map/reduce_sum | solution.py:255
  6.8 1.0 shard_map.100
  7.7 0.3 collective-permute-start.2
  8.0 0.3 collective-permute-start.1
  8.5 0.4 copy-done.4
  8.9 2.6 %fusion.3 = f32[512,1024]{1,0:T(8,128)} fusion(bf16[512,1024]{1,0:T(8,128)(2,1)S(1)} %copy-done.1, bf16[2048,1024]{1,0:T(8,128)(2,1)S(1)} %copy-done.4, f32[1024]{0:T(1024)S(1)} %copy-done.6), kind=kOutput, calls=%fused_computation.7 | convolution fusion | flops 1074266112 | bytes 5246976 | tf_op jit(solution)/shard_map/dot_general | solution.py:263
  11.5 2.1 %shard_map.101 = (bf16[8,128,128]{2,1,0:T(8,128)(2,1)S(1)}, bf16[16,128,128]{2,1,0:T(8,128)(2,1)S(1)}) custom-call(s32[1]{0:T(128)} %bitcast.core_ref, bf16[512,1024]{1,0:T(8,128)(2,1)S(1)} %copy-done.1, bf16[512,1024]{1,0:T(8,128)(2,1)S(1)} %collective-permute-done.x_other, bf16[1024,1024]{1,0:T(8,128)(2,1)S(1)} %copy-done, f32[1,1024]{1,0:T(1,128)S(1)} %bitcast.35), custom_call_target="tpu_custom_call" | custom-call | flops 6442450944 | bytes 2883584 | tf_op jit(solution)/shard_map/pallas_call | solution.py:141
  13.7 2.1 %collective-permute-done.2 = bf16[8,128,128]{2,1,0:T(8,128)(2,1)S(1)} collective-permute-done((bf16[8,128,128]{2,1,0:T(8,128)(2,1)S(1)}, bf16[8,128,128]{2,1,0:T(8,128)(2,1)S(1)}, u32[]{:S(2)}, u32[]{:S(2)}) %collective-permute-start.2) | collective-permute-done | bytes 262176 | tf_op jit(solution)/shard_map/gather_x_0/ppermute | solution.py:18
  15.8 2.8 %collective-permute-start.4 = (bf16[16,128,128]{2,1,0:T(8,128)(2,1)S(1)}, bf16[16,128,128]{2,1,0:T(8,128)(2,1)S(1)}, u32[]{:S(2)}, u32[]{:S(2)}) collective-permute-start(bf16[16,128,128]{2,1,0:T(8,128)(2,1)S(1)} %pad_maximum_fusion.1), channel_id=1, source_target_pairs={{0,16},{1,49},{16,0},{17,33},{32,48},{33,17},{48,32},{49,1},{2,18}... | collective-permute-start | bytes 1572872 | tf_op jit(solution)/shard_map/gather_near_0/ppermute | solution.py:28
  19.0 0.3 collective-permute-start.3
  19.4 5.8 %collective-permute-done.4 = bf16[16,128,128]{2,1,0:T(8,128)(2,1)S(1)} collective-permute-done((bf16[16,128,128]{2,1,0:T(8,128)(2,1)S(1)}, bf16[16,128,128]{2,1,0:T(8,128)(2,1)S(1)}, u32[]{:S(2)}, u32[]{:S(2)}) %collective-permute-start.4) | collective-permute-done | bytes 524320 | tf_op jit(solution)/shard_map/gather_near_0/ppermute | solution.py:28
  25.3 0.4 collective-permute-start.8
  25.8 1.5 collective-permute-done.3
  27.6 1.1 collective-permute-start.6
  28.7 2.2 %convert_reduce_fusion = f32[64,128]{1,0:T(8,128)S(1)} fusion(bf16[64,128,128]{2,1,0:T(8,128)(2,1)} %collective-permute-done.7.c_other), kind=kLoop, calls=%fused_computation.2 | loop fusion | flops 2088960 | bytes 2129920 | tf_op jit(solution)/shard_map/reduce_sum | solution.py:255
  31.2 11.6 %collective-permute-done.6 = bf16[16,128,128]{2,1,0:T(8,128)(2,1)S(1)} collective-permute-done((bf16[16,128,128]{2,1,0:T(8,128)(2,1)S(1)}, bf16[16,128,128]{2,1,0:T(8,128)(2,1)S(1)}, u32[]{:S(2)}, u32[]{:S(2)}) %collective-permute-start.6) | collective-permute-done | bytes 524320 | tf_op jit(solution)/shard_map/gather_near_1/ppermute | solution.py:28
  43.0 1.9 %collective-permute-done.8.far = bf16[32,128,128]{2,1,0:T(8,128)(2,1)S(1)} collective-permute-done((bf16[32,128,128]{2,1,0:T(8,128)(2,1)S(1)}, bf16[32,128,128]{2,1,0:T(8,128)(2,1)S(1)}, u32[]{:S(2)}, u32[]{:S(2)}) %collective-permute-start.8) | collective-permute-done | bytes 1048608 | tf_op jit(solution)/shard_map/gather_far_0/ppermute | solution.py:28
  44.9 5.7 %tiles_0.1 = (bf16[4224,128]{1,0:T(8,128)(2,1)S(1)}, bf16[2112,128]{1,0:T(8,128)(2,1)S(1)}, bf16[2112,128]{1,0:T(8,128)(2,1)S(1)}) custom-call(s32[128]{0:T(128)S(1)} %fusion.27.src_ref, s32[128]{0:T(128)S(1)} %fusion.28.dst_ref, s32[2]{0:T(128)S(1)} %fusion.26.live_ref, bf16[64,128,128]{2,1,0:T(8,128)(2,1)} %get-tuple-element.58.c_own, ...), custom_call_target="tpu_custom_call" | custom-call | flops 2147483648 | bytes 1048576 | tf_op jit(solution)/shard_map/tiles_0/pallas_call | solution.py:90
  50.6 4.3 %collective-permute-start.9 = (bf16[4224,128]{1,0:T(8,128)(2,1)S(1)}, bf16[4224,128]{1,0:T(8,128)(2,1)S(1)}, u32[]{:S(2)}, u32[]{:S(2)}) collective-permute-start(bf16[4224,128]{1,0:T(8,128)(2,1)S(1)} %get-tuple-element.62), channel_id=1, source_target_pairs={{0,4},{1,13},{4,0},{5,9},{8,12},{9,5},{12,8},{13,1},{2,6},{3,15},{... | collective-permute-start | bytes 3244040 | tf_op jit(solution)/shard_map/sum_near_0/ppermute | solution.py:28
  55.0 3.0 %collective-permute-start.10 = (bf16[16,128,128]{2,1,0:T(8,128)(2,1)S(1)}, bf16[16,128,128]{2,1,0:T(8,128)(2,1)S(1)}, u32[]{:S(2)}, u32[]{:S(2)}) collective-permute-start(bf16[16,128,128]{2,1,0:T(8,128)(2,1)S(1)} %pad_maximum_fusion.3), channel_id=1, source_target_pairs={{0,16},{1,49},{16,0},{17,33},{32,48},{33,17},{48,32},{49,1},{2,18}... | collective-permute-start | bytes 1572872 | tf_op jit(solution)/shard_map/gather_near_2/ppermute | solution.py:28
  58.1 7.8 %collective-permute-done.10 = bf16[16,128,128]{2,1,0:T(8,128)(2,1)S(1)} collective-permute-done((bf16[16,128,128]{2,1,0:T(8,128)(2,1)S(1)}, bf16[16,128,128]{2,1,0:T(8,128)(2,1)S(1)}, u32[]{:S(2)}, u32[]{:S(2)}) %collective-permute-start.10) | collective-permute-done | bytes 524320 | tf_op jit(solution)/shard_map/gather_near_2/ppermute | solution.py:28
  66.1 5.7 %tiles_1.1 = (bf16[4096,128]{1,0:T(8,128)(2,1)S(1)}, bf16[2048,128]{1,0:T(8,128)(2,1)S(1)}, bf16[2048,128]{1,0:T(8,128)(2,1)S(1)}) custom-call(s32[128]{0:T(128)S(1)} %fusion.27.src_ref, s32[128]{0:T(128)S(1)} %fusion.28.dst_ref, s32[2]{0:T(128)S(1)} %fusion.26.live_ref, bf16[64,128,128]{2,1,0:T(8,128)(2,1)} %get-tuple-element.58.c_own, ...), custom_call_target="tpu_custom_call" | custom-call | flops 2147483648 | bytes 1048576 | tf_op jit(solution)/shard_map/tiles_1/pallas_call | solution.py:90
  71.8 4.3 %collective-permute-start.18 = (bf16[4096,128]{1,0:T(8,128)(2,1)S(1)}, bf16[4096,128]{1,0:T(8,128)(2,1)S(1)}, u32[]{:S(2)}, u32[]{:S(2)}) collective-permute-start(bf16[4096,128]{1,0:T(8,128)(2,1)S(1)} %get-tuple-element.65), channel_id=1, source_target_pairs={{0,4},{1,13},{4,0},{5,9},{8,12},{9,5},{12,8},{13,1},{2,6},{3,15},{... | collective-permute-start | bytes 3145736 | tf_op jit(solution)/shard_map/sum_near_1/ppermute | solution.py:28
  76.1 0.4 collective-permute-start.13
  76.5 0.2 convert_add_fusion
  76.9 8.7 %collective-permute-done.13 = bf16[16,128,128]{2,1,0:T(8,128)(2,1)S(1)} collective-permute-done((bf16[16,128,128]{2,1,0:T(8,128)(2,1)S(1)}, bf16[16,128,128]{2,1,0:T(8,128)(2,1)S(1)}, u32[]{:S(2)}, u32[]{:S(2)}) %collective-permute-start.13) | collective-permute-done | bytes 524320 | tf_op jit(solution)/shard_map/gather_near_3/ppermute | solution.py:28
  85.7 0.3 collective-permute-start.17
  86.0 5.7 %tiles_2.1 = (bf16[4096,128]{1,0:T(8,128)(2,1)S(1)}, bf16[2048,128]{1,0:T(8,128)(2,1)S(1)}, bf16[2048,128]{1,0:T(8,128)(2,1)S(1)}) custom-call(s32[128]{0:T(128)S(1)} %fusion.27.src_ref, s32[128]{0:T(128)S(1)} %fusion.28.dst_ref, s32[2]{0:T(128)S(1)} %fusion.26.live_ref, bf16[64,128,128]{2,1,0:T(8,128)(2,1)} %get-tuple-element.58.c_own, ...), custom_call_target="tpu_custom_call" | custom-call | flops 1048576 | bytes 1048576 | tf_op jit(solution)/shard_map/tiles_2/pallas_call | solution.py:90
  91.7 3.3 %collective-permute-start.16 = (bf16[4096,128]{1,0:T(8,128)(2,1)S(1)}, bf16[4096,128]{1,0:T(8,128)(2,1)S(1)}, u32[]{:S(2)}, u32[]{:S(2)}) collective-permute-start(bf16[4096,128]{1,0:T(8,128)(2,1)S(1)} %get-tuple-element.70), channel_id=1, source_target_pairs={{0,4},{1,13},{4,0},{5,9},{8,12},{9,5},{12,8},{13,1},{2,6},{3,15},{... | collective-permute-start | bytes 3145736 | tf_op jit(solution)/shard_map/sum_near_2/ppermute | solution.py:28
  95.1 0.7 collective-permute-start.15
  96.1 0.3 collective-permute-start.19
  96.4 3.5 %collective-permute-done.17.far = bf16[32,128,128]{2,1,0:T(8,128)(2,1)S(1)} collective-permute-done((bf16[32,128,128]{2,1,0:T(8,128)(2,1)S(1)}, bf16[32,128,128]{2,1,0:T(8,128)(2,1)S(1)}, u32[]{:S(2)}, u32[]{:S(2)}) %collective-permute-start.17) | collective-permute-done | bytes 1048608 | tf_op jit(solution)/shard_map/gather_far_3/ppermute | solution.py:28
  99.9 5.7 %tiles_3.1 = (bf16[4096,128]{1,0:T(8,128)(2,1)S(1)}, bf16[2048,128]{1,0:T(8,128)(2,1)S(1)}, bf16[2048,128]{1,0:T(8,128)(2,1)S(1)}) custom-call(s32[128]{0:T(128)S(1)} %fusion.27.src_ref, s32[128]{0:T(128)S(1)} %fusion.28.dst_ref, s32[2]{0:T(128)S(1)} %fusion.26.live_ref, bf16[64,128,128]{2,1,0:T(8,128)(2,1)} %get-tuple-element.58.c_own, ...), custom_call_target="tpu_custom_call" | custom-call | flops 1048576 | bytes 1048576 | tf_op jit(solution)/shard_map/tiles_3/pallas_call | solution.py:90
  105.6 3.3 %collective-permute-start.21 = (bf16[4096,128]{1,0:T(8,128)(2,1)S(1)}, bf16[4096,128]{1,0:T(8,128)(2,1)S(1)}, u32[]{:S(2)}, u32[]{:S(2)}) collective-permute-start(bf16[4096,128]{1,0:T(8,128)(2,1)S(1)} %get-tuple-element.74), channel_id=1, source_target_pairs={{0,4},{1,13},{4,0},{5,9},{8,12},{9,5},{12,8},{13,1},{2,6},{3,15},{... | collective-permute-start | bytes 3145736 | tf_op jit(solution)/shard_map/sum_near_3/ppermute | solution.py:28
  109.0 3.9 %collective-permute-done.16 = bf16[4096,128]{1,0:T(8,128)(2,1)S(1)} collective-permute-done((bf16[4096,128]{1,0:T(8,128)(2,1)S(1)}, bf16[4096,128]{1,0:T(8,128)(2,1)S(1)}, u32[]{:S(2)}, u32[]{:S(2)}) %collective-permute-start.16) | collective-permute-done | bytes 1048608 | tf_op jit(solution)/shard_map/sum_near_2/ppermute | solution.py:28
  113.4 1.3 collective-permute-start.20
  115.1 13.1 %collective-permute-done.21 = bf16[4096,128]{1,0:T(8,128)(2,1)S(1)} collective-permute-done((bf16[4096,128]{1,0:T(8,128)(2,1)S(1)}, bf16[4096,128]{1,0:T(8,128)(2,1)S(1)}, u32[]{:S(2)}, u32[]{:S(2)}) %collective-permute-start.21) | collective-permute-done | bytes 1048608 | tf_op jit(solution)/shard_map/sum_near_3/ppermute | solution.py:28
  128.4 0.7 collective-permute-start.25
  129.2 1.6 collective-permute-start.24
  131.1 6.6 %collective-permute-start.22 = (bf16[512,256]{1,0:T(8,128)(2,1)S(1)}, bf16[512,256]{1,0:T(8,128)(2,1)S(1)}, u32[]{:S(2)}, u32[]{:S(2)}) collective-permute-start(bf16[512,256]{1,0:T(8,128)(2,1)S(1)} %pad_maximum_fusion.5), channel_id=1, source_target_pairs={{0,1},{1,0},{2,3},{3,2},{4,5},{5,4},{6,7},{7,6},{8,9},{9,8},{10,11... | collective-permute-start | bytes 786440 | tf_op jit(solution)/shard_map/mean_core_0/ppermute | solution.py:18
  137.7 1.5 fusion.13
  139.4 0.8 collective-permute-start.26
  140.4 5.7 %collective-permute-done.26 = bf16[1024,128]{1,0:T(8,128)(2,1)S(1)} collective-permute-done((bf16[1024,128]{1,0:T(8,128)(2,1)S(1)}, bf16[1024,128]{1,0:T(8,128)(2,1)S(1)}, u32[]{:S(2)}, u32[]{:S(2)}) %collective-permute-start.26) | collective-permute-done | bytes 262176 | tf_op jit(solution)/shard_map/sum_x_3/ppermute | solution.py:18
  146.5 4.7 %collective-permute-start.27 = (bf16[512,256]{1,0:T(8,128)(2,1)S(1)}, bf16[512,256]{1,0:T(8,128)(2,1)S(1)}, u32[]{:S(2)}, u32[]{:S(2)}) collective-permute-start(bf16[512,256]{1,0:T(8,128)(2,1)S(1)} %pad_maximum_fusion.7), channel_id=1, source_target_pairs={{0,1},{1,0},{2,3},{3,2},{4,5},{5,4},{6,7},{7,6},{8,9},{9,8},{10,11... | collective-permute-start | bytes 786440 | tf_op jit(solution)/shard_map/mean_core_1/ppermute | solution.py:18
  151.2 1.5 add_add_fusion.hidden
  152.7 2.9 %shard_map.102 = f32[512,1024]{1,0:T(8,128)} custom-call(f32[512,1024]{1,0:T(8,128)S(1)} %add_add_fusion.hidden, bf16[512,256]{1,0:T(8,128)(2,1)S(1)} %pad_maximum_fusion.6.near, bf16[512,256]{1,0:T(8,128)(2,1)S(1)} %collective-permute-done.27.got, bf16[512,1024]{1,0:T(8,128)(2,1)S(1)} %pad_maximum_fusion.weight), custom_call_target="tpu_custom_call" | custom-call | tf_op jit(solution)/shard_map/pallas_call | solution.py:175
  (96 shorter events, 5.0 us)
Async XLA Ops:
  0.0 6.7 %collective-permute-start = (bf16[512,1024]{1,0:T(8,128)(2,1)}, bf16[512,1024]{1,0:T(8,128)(2,1)S(1)}, u32[]{:S(2)}, u32[]{:S(2)}) collective-permute-start(bf16[512,1024]{1,0:T(8,128)(2,1)} %x_own.2), channel_id=1, source_target_pairs={{0,1},{1,0},{2,3},{3,2},{4,5},{5,4},{6,7},{7,6},{8,9},{9,8},{10,11... | collective-permute-start | bytes 3145736 | tf_op jit(solution)/shard_map/other_features_0/ppermute | solution.py:18
  2.3 4.4 %copy-start = (bf16[1024,1024]{1,0:T(8,128)(2,1)S(1)}, bf16[1024,1024]{1,0:T(8,128)(2,1)}, u32[]{:S(2)}) copy-start(bf16[1024,1024]{1,0:T(8,128)(2,1)} %weight.3) | copy-start | bytes 6291460
  2.3 4.4 %copy-start.1 = (bf16[512,1024]{1,0:T(8,128)(2,1)S(1)}, bf16[512,1024]{1,0:T(8,128)(2,1)}, u32[]{:S(2)}) copy-start(bf16[512,1024]{1,0:T(8,128)(2,1)} %x_own.2) | copy-start | bytes 3145732
  2.4 4.4 %copy-start.2 = (f32[1024]{0:T(1024)S(1)}, f32[1024]{0:T(1024)}, u32[]{:S(2)}) copy-start(f32[1024]{0:T(1024)} %param.16) | copy-start | bytes 12292
  6.7 2.2 %copy-start.4 = (bf16[2048,1024]{1,0:T(8,128)(2,1)S(1)}, bf16[2048,1024]{1,0:T(8,128)(2,1)}, u32[]{:S(2)}) copy-start(bf16[2048,1024]{1,0:T(8,128)(2,1)} %param.17) | copy-start | bytes 12582916
  6.7 2.2 %copy-start.6 = (f32[1024]{0:T(1024)S(1)}, f32[1024]{0:T(1024)}, u32[]{:S(2)}) copy-start(f32[1024]{0:T(1024)} %param.18) | copy-start | bytes 12292
  7.7 8.0 %collective-permute-start.2 = (bf16[8,128,128]{2,1,0:T(8,128)(2,1)S(1)}, bf16[8,128,128]{2,1,0:T(8,128)(2,1)S(1)}, u32[]{:S(2)}, u32[]{:S(2)}) collective-permute-start(bf16[8,128,128]{2,1,0:T(8,128)(2,1)S(1)} %shard_map.100), channel_id=1, source_target_pairs={{0,64},{64,0},{1,65},{65,1},{2,66},{66,2},{3,67},{67,3},{4,68},{68... | collective-permute-start | bytes 786440 | tf_op jit(solution)/shard_map/gather_x_0/ppermute | solution.py:18
  8.0 10.8 %collective-permute-start.1 = (s32[3,64]{1,0:T(4,128)S(1)}, s32[3,64]{1,0:T(4,128)S(1)}, u32[]{:S(2)}, u32[]{:S(2)}) collective-permute-start(s32[3,64]{1,0:T(4,128)S(1)} %get-tuple-element.49), channel_id=1, source_target_pairs={{0,1},{1,0},{2,3},{3,2},{4,5},{5,4},{6,7},{7,6},{8,9},{9,8},{10,11... | collective-permute-start | bytes 2312 | tf_op jit(solution)/shard_map/other_meta/ppermute | solution.py:18
  8.3 20.4 %collective-permute-start.7 = (bf16[64,128,128]{2,1,0:T(8,128)(2,1)}, bf16[64,128,128]{2,1,0:T(8,128)(2,1)}, u32[]{:S(2)}, u32[]{:S(2)}) collective-permute-start(bf16[64,128,128]{2,1,0:T(8,128)(2,1)} %get-tuple-element.58.c_own), channel_id=1, source_target_pairs={{0,1},{1,0},{2,3},{3,2},{4,5},{5,4},{6,7},{7,6},{8,9},{9,8},{10,11... | collective-permute-start | bytes 6291464 | tf_op jit(solution)/shard_map/other_tiles/ppermute | solution.py:18
  15.8 9.4 %collective-permute-start.4 = (bf16[16,128,128]{2,1,0:T(8,128)(2,1)S(1)}, bf16[16,128,128]{2,1,0:T(8,128)(2,1)S(1)}, u32[]{:S(2)}, u32[]{:S(2)}) collective-permute-start(bf16[16,128,128]{2,1,0:T(8,128)(2,1)S(1)} %pad_maximum_fusion.1), channel_id=1, source_target_pairs={{0,16},{1,49},{16,0},{17,33},{32,48},{33,17},{48,32},{49,1},{2,18}... | collective-permute-start | bytes 1572872 | tf_op jit(solution)/shard_map/gather_near_0/ppermute | solution.py:28
  19.0 8.3 %collective-permute-start.3 = (bf16[8,128,128]{2,1,0:T(8,128)(2,1)S(1)}, bf16[8,128,128]{2,1,0:T(8,128)(2,1)S(1)}, u32[]{:S(2)}, u32[]{:S(2)}) collective-permute-start(bf16[8,128,128]{2,1,0:T(8,128)(2,1)S(1)} %get-tuple-element.52), channel_id=1, source_target_pairs={{0,64},{64,0},{1,65},{65,1},{2,66},{66,2},{3,67},{67,3},{4,68},{68... | collective-permute-start | bytes 786440 | tf_op jit(solution)/shard_map/gather_x_1/ppermute | solution.py:18
  25.3 19.6 %collective-permute-start.8 = (bf16[32,128,128]{2,1,0:T(8,128)(2,1)S(1)}, bf16[32,128,128]{2,1,0:T(8,128)(2,1)S(1)}, u32[]{:S(2)}, u32[]{:S(2)}) collective-permute-start(bf16[32,128,128]{2,1,0:T(8,128)(2,1)S(1)} %constant_dynamic-update-slice_fusion.near), channel_id=1, source_target_pairs={{0,48},{1,17},{16,32},{17,1},{32,16},{33,49},{48,0},{49,33},{2,50}... | collective-permute-start | bytes 3145736 | tf_op jit(solution)/shard_map/gather_far_0/ppermute | solution.py:28
  27.3 15.7 %collective-permute-start.5 = (bf16[16,128,128]{2,1,0:T(8,128)(2,1)S(1)}, bf16[16,128,128]{2,1,0:T(8,128)(2,1)S(1)}, u32[]{:S(2)}, u32[]{:S(2)}) collective-permute-start(bf16[16,128,128]{2,1,0:T(8,128)(2,1)S(1)} %get-tuple-element.56), channel_id=1, source_target_pairs={{0,64},{64,0},{1,65},{65,1},{2,66},{66,2},{3,67},{67,3},{4,68},{68... | collective-permute-start | bytes 1572872 | tf_op jit(solution)/shard_map/gather_x_rest/ppermute | solution.py:18
  27.6 15.3 %collective-permute-start.6 = (bf16[16,128,128]{2,1,0:T(8,128)(2,1)S(1)}, bf16[16,128,128]{2,1,0:T(8,128)(2,1)S(1)}, u32[]{:S(2)}, u32[]{:S(2)}) collective-permute-start(bf16[16,128,128]{2,1,0:T(8,128)(2,1)S(1)} %pad_maximum_fusion.2), channel_id=1, source_target_pairs={{0,16},{1,49},{16,0},{17,33},{32,48},{33,17},{48,32},{49,1},{2,18}... | collective-permute-start | bytes 1572872 | tf_op jit(solution)/shard_map/gather_near_1/ppermute | solution.py:28
  42.9 23.1 %collective-permute-start.11 = (bf16[32,128,128]{2,1,0:T(8,128)(2,1)S(1)}, bf16[32,128,128]{2,1,0:T(8,128)(2,1)S(1)}, u32[]{:S(2)}, u32[]{:S(2)}) collective-permute-start(bf16[32,128,128]{2,1,0:T(8,128)(2,1)S(1)} %constant_dynamic-update-slice_fusion.2.near), channel_id=1, source_target_pairs={{0,48},{1,17},{16,32},{17,1},{32,16},{33,49},{48,0},{49,33},{2,50}... | collective-permute-start | bytes 3145736 | tf_op jit(solution)/shard_map/gather_far_1/ppermute | solution.py:28
  50.6 25.9 %collective-permute-start.9 = (bf16[4224,128]{1,0:T(8,128)(2,1)S(1)}, bf16[4224,128]{1,0:T(8,128)(2,1)S(1)}, u32[]{:S(2)}, u32[]{:S(2)}) collective-permute-start(bf16[4224,128]{1,0:T(8,128)(2,1)S(1)} %get-tuple-element.62), channel_id=1, source_target_pairs={{0,4},{1,13},{4,0},{5,9},{8,12},{9,5},{12,8},{13,1},{2,6},{3,15},{... | collective-permute-start | bytes 3244040 | tf_op jit(solution)/shard_map/sum_near_0/ppermute | solution.py:28
  55.0 10.9 %collective-permute-start.10 = (bf16[16,128,128]{2,1,0:T(8,128)(2,1)S(1)}, bf16[16,128,128]{2,1,0:T(8,128)(2,1)S(1)}, u32[]{:S(2)}, u32[]{:S(2)}) collective-permute-start(bf16[16,128,128]{2,1,0:T(8,128)(2,1)S(1)} %pad_maximum_fusion.3), channel_id=1, source_target_pairs={{0,16},{1,49},{16,0},{17,33},{32,48},{33,17},{48,32},{49,1},{2,18}... | collective-permute-start | bytes 1572872 | tf_op jit(solution)/shard_map/gather_near_2/ppermute | solution.py:28
  66.0 20.0 %collective-permute-start.14 = (bf16[32,128,128]{2,1,0:T(8,128)(2,1)S(1)}, bf16[32,128,128]{2,1,0:T(8,128)(2,1)S(1)}, u32[]{:S(2)}, u32[]{:S(2)}) collective-permute-start(bf16[32,128,128]{2,1,0:T(8,128)(2,1)S(1)} %constant_dynamic-update-slice_fusion.4.near), channel_id=1, source_target_pairs={{0,48},{1,17},{16,32},{17,1},{32,16},{33,49},{48,0},{49,33},{2,50}... | collective-permute-start | bytes 3145736 | tf_op jit(solution)/shard_map/gather_far_2/ppermute | solution.py:28
  71.8 24.1 %collective-permute-start.18 = (bf16[4096,128]{1,0:T(8,128)(2,1)S(1)}, bf16[4096,128]{1,0:T(8,128)(2,1)S(1)}, u32[]{:S(2)}, u32[]{:S(2)}) collective-permute-start(bf16[4096,128]{1,0:T(8,128)(2,1)S(1)} %get-tuple-element.65), channel_id=1, source_target_pairs={{0,4},{1,13},{4,0},{5,9},{8,12},{9,5},{12,8},{13,1},{2,6},{3,15},{... | collective-permute-start | bytes 3145736 | tf_op jit(solution)/shard_map/sum_near_1/ppermute | solution.py:28
  76.1 9.5 %collective-permute-start.13 = (bf16[16,128,128]{2,1,0:T(8,128)(2,1)S(1)}, bf16[16,128,128]{2,1,0:T(8,128)(2,1)S(1)}, u32[]{:S(2)}, u32[]{:S(2)}) collective-permute-start(bf16[16,128,128]{2,1,0:T(8,128)(2,1)S(1)} %pad_maximum_fusion.4), channel_id=1, source_target_pairs={{0,16},{1,49},{16,0},{17,33},{32,48},{33,17},{48,32},{49,1},{2,18}... | collective-permute-start | bytes 1572872 | tf_op jit(solution)/shard_map/gather_near_3/ppermute | solution.py:28
  76.8 18.3 %collective-permute-start.12 = (bf16[2112,128]{1,0:T(8,128)(2,1)S(1)}, bf16[2112,128]{1,0:T(8,128)(2,1)S(1)}, u32[]{:S(2)}, u32[]{:S(2)}) collective-permute-start(bf16[2112,128]{1,0:T(8,128)(2,1)S(1)} %get-tuple-element.98), channel_id=1, source_target_pairs={{0,12},{1,5},{4,8},{5,1},{8,4},{9,13},{12,0},{13,9},{2,14},{3,7},{... | collective-permute-start | bytes 1622024 | tf_op jit(solution)/shard_map/sum_far_0/ppermute | solution.py:28
  85.7 14.2 %collective-permute-start.17 = (bf16[32,128,128]{2,1,0:T(8,128)(2,1)S(1)}, bf16[32,128,128]{2,1,0:T(8,128)(2,1)S(1)}, u32[]{:S(2)}, u32[]{:S(2)}) collective-permute-start(bf16[32,128,128]{2,1,0:T(8,128)(2,1)S(1)} %constant_dynamic-update-slice_fusion.6.near), channel_id=1, source_target_pairs={{0,48},{1,17},{16,32},{17,1},{32,16},{33,49},{48,0},{49,33},{2,50}... | collective-permute-start | bytes 3145736 | tf_op jit(solution)/shard_map/gather_far_3/ppermute | solution.py:28
  91.7 21.1 %collective-permute-start.16 = (bf16[4096,128]{1,0:T(8,128)(2,1)S(1)}, bf16[4096,128]{1,0:T(8,128)(2,1)S(1)}, u32[]{:S(2)}, u32[]{:S(2)}) collective-permute-start(bf16[4096,128]{1,0:T(8,128)(2,1)S(1)} %get-tuple-element.70), channel_id=1, source_target_pairs={{0,4},{1,13},{4,0},{5,9},{8,12},{9,5},{12,8},{13,1},{2,6},{3,15},{... | collective-permute-start | bytes 3145736 | tf_op jit(solution)/shard_map/sum_near_2/ppermute | solution.py:28
  95.1 18.0 %collective-permute-start.15 = (bf16[1056,128]{1,0:T(8,128)(2,1)S(1)}, bf16[1056,128]{1,0:T(8,128)(2,1)S(1)}, u32[]{:S(2)}, u32[]{:S(2)}) collective-permute-start(bf16[1056,128]{1,0:T(8,128)(2,1)S(1)} %fusion.7), channel_id=1, source_target_pairs={{0,2},{2,0},{1,3},{3,1},{4,6},{6,4},{5,7},{7,5},{8,10},{10,8},{9,1... | collective-permute-start | bytes 811016 | tf_op jit(solution)/shard_map/sum_x_0/ppermute | solution.py:18
  96.1 17.2 %collective-permute-start.19 = (bf16[2048,128]{1,0:T(8,128)(2,1)S(1)}, bf16[2048,128]{1,0:T(8,128)(2,1)S(1)}, u32[]{:S(2)}, u32[]{:S(2)}) collective-permute-start(bf16[2048,128]{1,0:T(8,128)(2,1)S(1)} %get-tuple-element.103), channel_id=1, source_target_pairs={{0,12},{1,5},{4,8},{5,1},{8,4},{9,13},{12,0},{13,9},{2,14},{3,7},{... | collective-permute-start | bytes 1572872 | tf_op jit(solution)/shard_map/sum_far_1/ppermute | solution.py:28
  105.6 22.6 %collective-permute-start.21 = (bf16[4096,128]{1,0:T(8,128)(2,1)S(1)}, bf16[4096,128]{1,0:T(8,128)(2,1)S(1)}, u32[]{:S(2)}, u32[]{:S(2)}) collective-permute-start(bf16[4096,128]{1,0:T(8,128)(2,1)S(1)} %get-tuple-element.74), channel_id=1, source_target_pairs={{0,4},{1,13},{4,0},{5,9},{8,12},{9,5},{12,8},{13,1},{2,6},{3,15},{... | collective-permute-start | bytes 3145736 | tf_op jit(solution)/shard_map/sum_near_3/ppermute | solution.py:28
  113.1 1.6 %copy-start.5 = (f32[4]{0:T(128)S(1)}, f32[4]{0:T(128)}, u32[]{:S(2)}) copy-start(f32[4]{0:T(128)} %constant.140.clone) | copy-start | bytes 52
  113.4 17.4 %collective-permute-start.20 = (bf16[1024,128]{1,0:T(8,128)(2,1)S(1)}, bf16[1024,128]{1,0:T(8,128)(2,1)S(1)}, u32[]{:S(2)}, u32[]{:S(2)}) collective-permute-start(bf16[1024,128]{1,0:T(8,128)(2,1)S(1)} %fusion.16), channel_id=1, source_target_pairs={{0,2},{2,0},{1,3},{3,1},{4,6},{6,4},{5,7},{7,5},{8,10},{10,8},{9,1... | collective-permute-start | bytes 786440 | tf_op jit(solution)/shard_map/sum_x_1/ppermute | solution.py:18
  114.8 14.3 %collective-permute-start.23 = (bf16[2048,128]{1,0:T(8,128)(2,1)S(1)}, bf16[2048,128]{1,0:T(8,128)(2,1)S(1)}, u32[]{:S(2)}, u32[]{:S(2)}) collective-permute-start(bf16[2048,128]{1,0:T(8,128)(2,1)S(1)} %get-tuple-element.100), channel_id=1, source_target_pairs={{0,12},{1,5},{4,8},{5,1},{8,4},{9,13},{12,0},{13,9},{2,14},{3,7},{... | collective-permute-start | bytes 1572872 | tf_op jit(solution)/shard_map/sum_far_2/ppermute | solution.py:28
  128.4 10.8 %collective-permute-start.25 = (bf16[2048,128]{1,0:T(8,128)(2,1)S(1)}, bf16[2048,128]{1,0:T(8,128)(2,1)S(1)}, u32[]{:S(2)}, u32[]{:S(2)}) collective-permute-start(bf16[2048,128]{1,0:T(8,128)(2,1)S(1)} %get-tuple-element.102), channel_id=1, source_target_pairs={{0,12},{1,5},{4,8},{5,1},{8,4},{9,13},{12,0},{13,9},{2,14},{3,7},{... | collective-permute-start | bytes 1572872 | tf_op jit(solution)/shard_map/sum_far_3/ppermute | solution.py:28
  129.2 10.0 %collective-permute-start.24 = (bf16[1024,128]{1,0:T(8,128)(2,1)S(1)}, bf16[1024,128]{1,0:T(8,128)(2,1)S(1)}, u32[]{:S(2)}, u32[]{:S(2)}) collective-permute-start(bf16[1024,128]{1,0:T(8,128)(2,1)S(1)} %fusion.11), channel_id=1, source_target_pairs={{0,2},{2,0},{1,3},{3,1},{4,6},{6,4},{5,7},{7,5},{8,10},{10,8},{9,1... | collective-permute-start | bytes 786440 | tf_op jit(solution)/shard_map/sum_x_2/ppermute | solution.py:18
  131.1 20.1 %collective-permute-start.22 = (bf16[512,256]{1,0:T(8,128)(2,1)S(1)}, bf16[512,256]{1,0:T(8,128)(2,1)S(1)}, u32[]{:S(2)}, u32[]{:S(2)}) collective-permute-start(bf16[512,256]{1,0:T(8,128)(2,1)S(1)} %pad_maximum_fusion.5), channel_id=1, source_target_pairs={{0,1},{1,0},{2,3},{3,2},{4,5},{5,4},{6,7},{7,6},{8,9},{9,8},{10,11... | collective-permute-start | bytes 786440 | tf_op jit(solution)/shard_map/mean_core_0/ppermute | solution.py:18
  139.4 6.8 %collective-permute-start.26 = (bf16[1024,128]{1,0:T(8,128)(2,1)S(1)}, bf16[1024,128]{1,0:T(8,128)(2,1)S(1)}, u32[]{:S(2)}, u32[]{:S(2)}) collective-permute-start(bf16[1024,128]{1,0:T(8,128)(2,1)S(1)} %fusion.9), channel_id=1, source_target_pairs={{0,2},{2,0},{1,3},{3,1},{4,6},{6,4},{5,7},{7,5},{8,10},{10,8},{9,1... | collective-permute-start | bytes 786440 | tf_op jit(solution)/shard_map/sum_x_3/ppermute | solution.py:18
  140.4 10.8 %copy-start.3 = (f32[512,1024]{1,0:T(8,128)S(1)}, f32[512,1024]{1,0:T(8,128)}, u32[]{:S(2)}) copy-start(f32[512,1024]{1,0:T(8,128)} %fusion.3) | copy-start | bytes 6291460
  146.5 6.2 %collective-permute-start.27 = (bf16[512,256]{1,0:T(8,128)(2,1)S(1)}, bf16[512,256]{1,0:T(8,128)(2,1)S(1)}, u32[]{:S(2)}, u32[]{:S(2)}) collective-permute-start(bf16[512,256]{1,0:T(8,128)(2,1)S(1)} %pad_maximum_fusion.7), channel_id=1, source_target_pairs={{0,1},{1,0},{2,3},{3,2},{4,5},{5,4},{6,7},{7,6},{8,9},{9,8},{10,11... | collective-permute-start | bytes 786440 | tf_op jit(solution)/shard_map/mean_core_1/ppermute | solution.py:18

commit v12 on v11

--- a/solution.py
+++ b/solution.py
@@ -295,7 +295,7 @@
 
     def tiles(j):
         earlier = (rest, near_all[1], hidden, last_weight) if j == 0 else ()
-        if 0 < j < CHUNKS - 1:
+        if j == 1:
             earlier += (near_all[j + 1],)
         if j >= 2:
             earlier += (pass_all[0],)
@@ -311,7 +311,7 @@
                     j == 0,
                     near_all[j],
                     far_all[j],
-                    2**31 if j < 2 else 2**20,
+                    2**34 if j == 1 else 2**31 if j == 0 else 2**20,
                 )
             )
 

time: 157 us -> 157 us (level)
  starting transfers between devices: 42.3 us -> 51.4 us
  waiting for transfers between devices: 65.7 us -> 56.9 us
  Pallas kernels: 28.8 us -> 26.9 us
    ppermute x16, waiting for transfers between devices: 56.4 us -> 47.4 us  [step(): return lax.ppermute(x, (axis, 'core'), pairs)]
    ppermute x12, starting transfers between devices: 17.7 us -> 23.9 us  [swap(): return lax.ppermute(x, axis, [(0, 1), (1, 0)])]
    ppermute x16, starting transfers between devices: 24.5 us -> 27.5 us  [step(): return lax.ppermute(x, (axis, 'core'), pairs)]
    pallas_call x4, Pallas kernels: 22.8 us -> 20.9 us  [tile_sums(): pl.pallas_call(tile_kernel, out_shape=(jax.ShapeDtypeStruct((4 * size, w)...]
  transfers between devices with their start and end apart: 28 -> 28, of which waited for: 11 -> 14; matrix products, arithmetic and copies ran while one was open for 11% -> 12% of each run, Pallas kernels for 16% -> 15%
where the time goes in v12:
time: 157 us; the launch traced here: 155 us
  waiting for transfers between devices  56.9 us (36%)
  starting transfers between devices  51.4 us (33%)
  Pallas kernels  26.9 us (17%)
  other arithmetic  11.2 us (7%)
  matrix products  5.74 us (4%)
    ppermute x16, waiting for transfers between devices, step(): return lax.ppermute(x, (axis, 'core'), pairs)  47.4 us
    ppermute x16, starting transfers between devices, step(): return lax.ppermute(x, (axis, 'core'), pairs)  27.5 us
    ppermute x12, starting transfers between devices, swap(): return lax.ppermute(x, axis, [(0, 1), (1, 0)])  23.9 us
    pallas_call x4, Pallas kernels, tile_sums(): pl.pallas_call(tile_kernel, out_shape=(jax.ShapeDtypeStruct((4 * size, w)...  20.9 us
    ppermute x12, waiting for transfers between devices, swap(): return lax.ppermute(x, axis, [(0, 1), (1, 0)])  9.55 us
    reduce_sum x1, other arithmetic, local(): jnp.sum(c_own.astype(jnp.float32), axis=2)  4.34 us
  transfers between devices with their start and end apart: 28, of which 14 were waited for; matrix products, arithmetic and copies ran while one was open for 12% of the time, Pallas kernels for 15%

profile of v12, /device:TPU:3, one launch (start us, length us, event | category | flops | bytes accessed | tf_op | source)
XLA Modules:
  0.0 154.6 jit_solution(3774388635797580152)
XLA Ops:
  0.0 0.7 collective-permute-start
  1.6 0.7 compare_select_fusion.14
  2.4 4.3 %convert_reduce_fusion.1 = (f32[64,128]{1,0:T(8,128)S(1)}, bf16[64,128,128]{2,1,0:T(8,128)(2,1)}) fusion(s32[1,1,64,128,128]{4,3,2,1,0:T(8,128)} %param.11, pred[64]{0:T(512)(128)(4,1)S(1)} %iota_compare_fusion.2), kind=kLoop, calls=%fused_computation.3 | loop fusion | flops 4186112 | bytes 6324288 | tf_op jit(solution)/shard_map/reduce_sum | solution.py:255
  6.7 1.0 shard_map.100
  8.0 0.3 collective-permute-start.1
  8.5 2.1 %shard_map.101 = (bf16[8,128,128]{2,1,0:T(8,128)(2,1)S(1)}, bf16[16,128,128]{2,1,0:T(8,128)(2,1)S(1)}) custom-call(s32[1]{0:T(128)} %bitcast.core_ref, bf16[512,1024]{1,0:T(8,128)(2,1)S(1)} %copy-done.1, bf16[512,1024]{1,0:T(8,128)(2,1)S(1)} %collective-permute-done.x_other, bf16[1024,1024]{1,0:T(8,128)(2,1)S(1)} %copy-done, f32[1,1024]{1,0:T(1,128)S(1)} %bitcast.35), custom_call_target="tpu_custom_call" | custom-call | flops 6442450944 | bytes 2883584 | tf_op jit(solution)/shard_map/pallas_call | solution.py:141
  10.6 2.6 %fusion.3 = f32[512,1024]{1,0:T(8,128)} fusion(bf16[512,1024]{1,0:T(8,128)(2,1)S(1)} %copy-done.1, bf16[2048,1024]{1,0:T(8,128)(2,1)S(1)} %copy-done.4, f32[1024]{0:T(1024)S(1)} %copy-done.6), kind=kOutput, calls=%fused_computation.7 | convolution fusion | flops 1074266112 | bytes 5246976 | tf_op jit(solution)/shard_map/dot_general | solution.py:263
  13.2 2.5 %collective-permute-done.2 = bf16[8,128,128]{2,1,0:T(8,128)(2,1)S(1)} collective-permute-done((bf16[8,128,128]{2,1,0:T(8,128)(2,1)S(1)}, bf16[8,128,128]{2,1,0:T(8,128)(2,1)S(1)}, u32[]{:S(2)}, u32[]{:S(2)}) %collective-permute-start.2) | collective-permute-done | bytes 262176 | tf_op jit(solution)/shard_map/gather_x_0/ppermute | solution.py:18
  15.8 2.8 %collective-permute-start.4 = (bf16[16,128,128]{2,1,0:T(8,128)(2,1)S(1)}, bf16[16,128,128]{2,1,0:T(8,128)(2,1)S(1)}, u32[]{:S(2)}, u32[]{:S(2)}) collective-permute-start(bf16[16,128,128]{2,1,0:T(8,128)(2,1)S(1)} %pad_maximum_fusion.1), channel_id=1, source_target_pairs={{0,16},{1,49},{16,0},{17,33},{32,48},{33,17},{48,32},{49,1},{2,18}... | collective-permute-start | bytes 1572872 | tf_op jit(solution)/shard_map/gather_near_0/ppermute | solution.py:28
  19.3 5.9 %collective-permute-done.4 = bf16[16,128,128]{2,1,0:T(8,128)(2,1)S(1)} collective-permute-done((bf16[16,128,128]{2,1,0:T(8,128)(2,1)S(1)}, bf16[16,128,128]{2,1,0:T(8,128)(2,1)S(1)}, u32[]{:S(2)}, u32[]{:S(2)}) %collective-permute-start.4) | collective-permute-done | bytes 524320 | tf_op jit(solution)/shard_map/gather_near_0/ppermute | solution.py:28
  25.2 0.5 collective-permute-start.8
  25.7 1.5 collective-permute-done.3
  27.2 1.0 pad_maximum_fusion.2
  28.2 0.9 collective-permute-start.6
  29.4 2.2 %convert_reduce_fusion = f32[64,128]{1,0:T(8,128)S(1)} fusion(bf16[64,128,128]{2,1,0:T(8,128)(2,1)} %collective-permute-done.7.c_other), kind=kLoop, calls=%fused_computation.2 | loop fusion | flops 2088960 | bytes 2129920 | tf_op jit(solution)/shard_map/reduce_sum | solution.py:255
  31.9 11.6 %collective-permute-done.6 = bf16[16,128,128]{2,1,0:T(8,128)(2,1)S(1)} collective-permute-done((bf16[16,128,128]{2,1,0:T(8,128)(2,1)S(1)}, bf16[16,128,128]{2,1,0:T(8,128)(2,1)S(1)}, u32[]{:S(2)}, u32[]{:S(2)}) %collective-permute-start.6) | collective-permute-done | bytes 524320 | tf_op jit(solution)/shard_map/gather_near_1/ppermute | solution.py:28
  43.8 1.1 collective-permute-done.8.far
  44.9 2.7 %collective-permute-start.10 = (bf16[16,128,128]{2,1,0:T(8,128)(2,1)S(1)}, bf16[16,128,128]{2,1,0:T(8,128)(2,1)S(1)}, u32[]{:S(2)}, u32[]{:S(2)}) collective-permute-start(bf16[16,128,128]{2,1,0:T(8,128)(2,1)S(1)} %pad_maximum_fusion.3), channel_id=1, source_target_pairs={{0,16},{1,49},{16,0},{17,33},{32,48},{33,17},{48,32},{49,1},{2,18}... | collective-permute-start | bytes 1572872 | tf_op jit(solution)/shard_map/gather_near_2/ppermute | solution.py:28
  47.8 5.2 %tiles_0.1 = (bf16[4224,128]{1,0:T(8,128)(2,1)S(1)}, bf16[2112,128]{1,0:T(8,128)(2,1)S(1)}, bf16[2112,128]{1,0:T(8,128)(2,1)S(1)}) custom-call(s32[128]{0:T(128)S(1)} %fusion.27.src_ref, s32[128]{0:T(128)S(1)} %fusion.28.dst_ref, s32[2]{0:T(128)S(1)} %fusion.26.live_ref, bf16[64,128,128]{2,1,0:T(8,128)(2,1)} %get-tuple-element.57.c_own, ...), custom_call_target="tpu_custom_call" | custom-call | flops 2147483648 | bytes 1048576 | tf_op jit(solution)/shard_map/tiles_0/pallas_call | solution.py:90
  53.0 4.1 %collective-permute-start.9 = (bf16[4224,128]{1,0:T(8,128)(2,1)S(1)}, bf16[4224,128]{1,0:T(8,128)(2,1)S(1)}, u32[]{:S(2)}, u32[]{:S(2)}) collective-permute-start(bf16[4224,128]{1,0:T(8,128)(2,1)S(1)} %get-tuple-element.61), channel_id=1, source_target_pairs={{0,4},{1,13},{4,0},{5,9},{8,12},{9,5},{12,8},{13,1},{2,6},{3,15},{... | collective-permute-start | bytes 3244040 | tf_op jit(solution)/shard_map/sum_near_0/ppermute | solution.py:28
  57.1 2.3 %collective-permute-done.10 = bf16[16,128,128]{2,1,0:T(8,128)(2,1)S(1)} collective-permute-done((bf16[16,128,128]{2,1,0:T(8,128)(2,1)S(1)}, bf16[16,128,128]{2,1,0:T(8,128)(2,1)S(1)}, u32[]{:S(2)}, u32[]{:S(2)}) %collective-permute-start.10) | collective-permute-done | bytes 524320 | tf_op jit(solution)/shard_map/gather_near_2/ppermute | solution.py:28
  59.6 3.7 %collective-permute-done.11.far = bf16[32,128,128]{2,1,0:T(8,128)(2,1)S(1)} collective-permute-done((bf16[32,128,128]{2,1,0:T(8,128)(2,1)S(1)}, bf16[32,128,128]{2,1,0:T(8,128)(2,1)S(1)}, u32[]{:S(2)}, u32[]{:S(2)}) %collective-permute-start.11) | collective-permute-done | bytes 1048608 | tf_op jit(solution)/shard_map/gather_far_1/ppermute | solution.py:28
  63.2 0.8 collective-permute-start.16
  64.1 5.2 %tiles_1.1 = (bf16[4096,128]{1,0:T(8,128)(2,1)S(1)}, bf16[2048,128]{1,0:T(8,128)(2,1)S(1)}, bf16[2048,128]{1,0:T(8,128)(2,1)S(1)}) custom-call(s32[128]{0:T(128)S(1)} %fusion.27.src_ref, s32[128]{0:T(128)S(1)} %fusion.28.dst_ref, s32[2]{0:T(128)S(1)} %fusion.26.live_ref, bf16[64,128,128]{2,1,0:T(8,128)(2,1)} %get-tuple-element.57.c_own, ...), custom_call_target="tpu_custom_call" | custom-call | flops 17179869184 | bytes 1048576 | tf_op jit(solution)/shard_map/tiles_1/pallas_call | solution.py:90
  69.3 4.1 %collective-permute-start.18 = (bf16[4096,128]{1,0:T(8,128)(2,1)S(1)}, bf16[4096,128]{1,0:T(8,128)(2,1)S(1)}, u32[]{:S(2)}, u32[]{:S(2)}) collective-permute-start(bf16[4096,128]{1,0:T(8,128)(2,1)S(1)} %get-tuple-element.64), channel_id=1, source_target_pairs={{0,4},{1,13},{4,0},{5,9},{8,12},{9,5},{12,8},{13,1},{2,6},{3,15},{... | collective-permute-start | bytes 3145736 | tf_op jit(solution)/shard_map/sum_near_1/ppermute | solution.py:28
  73.6 0.6 collective-permute-start.12
  74.2 4.1 %collective-permute-done.16 = bf16[16,128,128]{2,1,0:T(8,128)(2,1)S(1)} collective-permute-done((bf16[16,128,128]{2,1,0:T(8,128)(2,1)S(1)}, bf16[16,128,128]{2,1,0:T(8,128)(2,1)S(1)}, u32[]{:S(2)}, u32[]{:S(2)}) %collective-permute-start.16) | collective-permute-done | bytes 524320 | tf_op jit(solution)/shard_map/gather_near_3/ppermute | solution.py:28
  78.7 0.9 collective-permute-done.13.far
  79.7 5.2 %tiles_2.1 = (bf16[4096,128]{1,0:T(8,128)(2,1)S(1)}, bf16[2048,128]{1,0:T(8,128)(2,1)S(1)}, bf16[2048,128]{1,0:T(8,128)(2,1)S(1)}) custom-call(s32[128]{0:T(128)S(1)} %fusion.27.src_ref, s32[128]{0:T(128)S(1)} %fusion.28.dst_ref, s32[2]{0:T(128)S(1)} %fusion.26.live_ref, bf16[64,128,128]{2,1,0:T(8,128)(2,1)} %get-tuple-element.57.c_own, ...), custom_call_target="tpu_custom_call" | custom-call | flops 1048576 | bytes 1048576 | tf_op jit(solution)/shard_map/tiles_2/pallas_call | solution.py:90
  84.9 4.1 %collective-permute-start.15 = (bf16[4096,128]{1,0:T(8,128)(2,1)S(1)}, bf16[4096,128]{1,0:T(8,128)(2,1)S(1)}, u32[]{:S(2)}, u32[]{:S(2)}) collective-permute-start(bf16[4096,128]{1,0:T(8,128)(2,1)S(1)} %get-tuple-element.68), channel_id=1, source_target_pairs={{0,4},{1,13},{4,0},{5,9},{8,12},{9,5},{12,8},{13,1},{2,6},{3,15},{... | collective-permute-start | bytes 3145736 | tf_op jit(solution)/shard_map/sum_near_2/ppermute | solution.py:28
  89.0 1.7 %collective-permute-start.14 = (bf16[1056,128]{1,0:T(8,128)(2,1)S(1)}, bf16[1056,128]{1,0:T(8,128)(2,1)S(1)}, u32[]{:S(2)}, u32[]{:S(2)}) collective-permute-start(bf16[1056,128]{1,0:T(8,128)(2,1)S(1)} %fusion.7), channel_id=1, source_target_pairs={{0,2},{2,0},{1,3},{3,1},{4,6},{6,4},{5,7},{7,5},{8,10},{10,8},{9,1... | collective-permute-start | bytes 811016 | tf_op jit(solution)/shard_map/sum_x_0/ppermute | solution.py:18
  90.7 1.0 collective-permute-done.18
  91.9 0.6 collective-permute-start.19
  92.7 5.2 %tiles_3.1 = (bf16[4096,128]{1,0:T(8,128)(2,1)S(1)}, bf16[2048,128]{1,0:T(8,128)(2,1)S(1)}, bf16[2048,128]{1,0:T(8,128)(2,1)S(1)}) custom-call(s32[128]{0:T(128)S(1)} %fusion.27.src_ref, s32[128]{0:T(128)S(1)} %fusion.28.dst_ref, s32[2]{0:T(128)S(1)} %fusion.26.live_ref, bf16[64,128,128]{2,1,0:T(8,128)(2,1)} %get-tuple-element.57.c_own, ...), custom_call_target="tpu_custom_call" | custom-call | flops 1048576 | bytes 1048576 | tf_op jit(solution)/shard_map/tiles_3/pallas_call | solution.py:90
  97.9 4.1 %collective-permute-start.21 = (bf16[4096,128]{1,0:T(8,128)(2,1)S(1)}, bf16[4096,128]{1,0:T(8,128)(2,1)S(1)}, u32[]{:S(2)}, u32[]{:S(2)}) collective-permute-start(bf16[4096,128]{1,0:T(8,128)(2,1)S(1)} %get-tuple-element.72), channel_id=1, source_target_pairs={{0,4},{1,13},{4,0},{5,9},{8,12},{9,5},{12,8},{13,1},{2,6},{3,15},{... | collective-permute-start | bytes 3145736 | tf_op jit(solution)/shard_map/sum_near_3/ppermute | solution.py:28
  102.0 5.0 %collective-permute-done.15 = bf16[4096,128]{1,0:T(8,128)(2,1)S(1)} collective-permute-done((bf16[4096,128]{1,0:T(8,128)(2,1)S(1)}, bf16[4096,128]{1,0:T(8,128)(2,1)S(1)}, u32[]{:S(2)}, u32[]{:S(2)}) %collective-permute-start.15) | collective-permute-done | bytes 1048608 | tf_op jit(solution)/shard_map/sum_near_2/ppermute | solution.py:28
  107.2 1.3 collective-permute-start.23
  108.9 1.9 %collective-permute-start.20 = (bf16[1024,128]{1,0:T(8,128)(2,1)S(1)}, bf16[1024,128]{1,0:T(8,128)(2,1)S(1)}, u32[]{:S(2)}, u32[]{:S(2)}) collective-permute-start(bf16[1024,128]{1,0:T(8,128)(2,1)S(1)} %fusion.16), channel_id=1, source_target_pairs={{0,2},{2,0},{1,3},{3,1},{4,6},{6,4},{5,7},{7,5},{8,10},{10,8},{9,1... | collective-permute-start | bytes 786440 | tf_op jit(solution)/shard_map/sum_x_1/ppermute | solution.py:18
  111.0 11.6 %collective-permute-done.21 = bf16[4096,128]{1,0:T(8,128)(2,1)S(1)} collective-permute-done((bf16[4096,128]{1,0:T(8,128)(2,1)S(1)}, bf16[4096,128]{1,0:T(8,128)(2,1)S(1)}, u32[]{:S(2)}, u32[]{:S(2)}) %collective-permute-start.21) | collective-permute-done | bytes 1048608 | tf_op jit(solution)/shard_map/sum_near_3/ppermute | solution.py:28
  122.9 2.1 %collective-permute-start.24 = (bf16[1024,128]{1,0:T(8,128)(2,1)S(1)}, bf16[1024,128]{1,0:T(8,128)(2,1)S(1)}, u32[]{:S(2)}, u32[]{:S(2)}) collective-permute-start(bf16[1024,128]{1,0:T(8,128)(2,1)S(1)} %fusion.11), channel_id=1, source_target_pairs={{0,2},{2,0},{1,3},{3,1},{4,6},{6,4},{5,7},{7,5},{8,10},{10,8},{9,1... | collective-permute-start | bytes 786440 | tf_op jit(solution)/shard_map/sum_x_2/ppermute | solution.py:18
  125.1 0.6 collective-permute-start.25
  126.0 8.6 %collective-permute-start.22 = (bf16[512,256]{1,0:T(8,128)(2,1)S(1)}, bf16[512,256]{1,0:T(8,128)(2,1)S(1)}, u32[]{:S(2)}, u32[]{:S(2)}) collective-permute-start(bf16[512,256]{1,0:T(8,128)(2,1)S(1)} %pad_maximum_fusion.5), channel_id=1, source_target_pairs={{0,1},{1,0},{2,3},{3,2},{4,5},{5,4},{6,7},{7,6},{8,9},{9,8},{10,11... | collective-permute-start | bytes 786440 | tf_op jit(solution)/shard_map/mean_core_0/ppermute | solution.py:18
  134.7 1.5 fusion.13
  136.3 1.0 collective-permute-start.26
  137.6 5.5 %collective-permute-done.26 = bf16[1024,128]{1,0:T(8,128)(2,1)S(1)} collective-permute-done((bf16[1024,128]{1,0:T(8,128)(2,1)S(1)}, bf16[1024,128]{1,0:T(8,128)(2,1)S(1)}, u32[]{:S(2)}, u32[]{:S(2)}) %collective-permute-start.26) | collective-permute-done | bytes 262176 | tf_op jit(solution)/shard_map/sum_x_3/ppermute | solution.py:18
  143.5 6.6 %collective-permute-start.27 = (bf16[512,256]{1,0:T(8,128)(2,1)S(1)}, bf16[512,256]{1,0:T(8,128)(2,1)S(1)}, u32[]{:S(2)}, u32[]{:S(2)}) collective-permute-start(bf16[512,256]{1,0:T(8,128)(2,1)S(1)} %pad_maximum_fusion.7), channel_id=1, source_target_pairs={{0,1},{1,0},{2,3},{3,2},{4,5},{5,4},{6,7},{7,6},{8,9},{9,8},{10,11... | collective-permute-start | bytes 786440 | tf_op jit(solution)/shard_map/mean_core_1/ppermute | solution.py:18
  150.1 1.5 add_add_fusion.hidden
  151.6 2.9 %shard_map.102 = f32[512,1024]{1,0:T(8,128)} custom-call(f32[512,1024]{1,0:T(8,128)S(1)} %add_add_fusion.hidden, bf16[512,256]{1,0:T(8,128)(2,1)S(1)} %pad_maximum_fusion.6.near, bf16[512,256]{1,0:T(8,128)(2,1)S(1)} %collective-permute-done.27.got, bf16[512,1024]{1,0:T(8,128)(2,1)S(1)} %pad_maximum_fusion.weight), custom_call_target="tpu_custom_call" | custom-call | tf_op jit(solution)/shard_map/pallas_call | solution.py:175
  (96 shorter events, 6.1 us)
Async XLA Ops:
  0.0 6.7 %collective-permute-start = (bf16[512,1024]{1,0:T(8,128)(2,1)}, bf16[512,1024]{1,0:T(8,128)(2,1)S(1)}, u32[]{:S(2)}, u32[]{:S(2)}) collective-permute-start(bf16[512,1024]{1,0:T(8,128)(2,1)} %x_own.2), channel_id=1, source_target_pairs={{0,1},{1,0},{2,3},{3,2},{4,5},{5,4},{6,7},{7,6},{8,9},{9,8},{10,11... | collective-permute-start | bytes 3145736 | tf_op jit(solution)/shard_map/other_features_0/ppermute | solution.py:18
  2.3 4.4 %copy-start = (bf16[1024,1024]{1,0:T(8,128)(2,1)S(1)}, bf16[1024,1024]{1,0:T(8,128)(2,1)}, u32[]{:S(2)}) copy-start(bf16[1024,1024]{1,0:T(8,128)(2,1)} %weight.3) | copy-start | bytes 6291460
  2.3 4.4 %copy-start.1 = (bf16[512,1024]{1,0:T(8,128)(2,1)S(1)}, bf16[512,1024]{1,0:T(8,128)(2,1)}, u32[]{:S(2)}) copy-start(bf16[512,1024]{1,0:T(8,128)(2,1)} %x_own.2) | copy-start | bytes 3145732
  2.4 4.4 %copy-start.2 = (f32[1024]{0:T(1024)S(1)}, f32[1024]{0:T(1024)}, u32[]{:S(2)}) copy-start(f32[1024]{0:T(1024)} %param.16) | copy-start | bytes 12292
  7.7 8.0 %collective-permute-start.2 = (bf16[8,128,128]{2,1,0:T(8,128)(2,1)S(1)}, bf16[8,128,128]{2,1,0:T(8,128)(2,1)S(1)}, u32[]{:S(2)}, u32[]{:S(2)}) collective-permute-start(bf16[8,128,128]{2,1,0:T(8,128)(2,1)S(1)} %shard_map.100), channel_id=1, source_target_pairs={{0,64},{64,0},{1,65},{65,1},{2,66},{66,2},{3,67},{67,3},{4,68},{68... | collective-permute-start | bytes 786440 | tf_op jit(solution)/shard_map/gather_x_0/ppermute | solution.py:18
  8.0 10.8 %collective-permute-start.1 = (s32[3,64]{1,0:T(4,128)S(1)}, s32[3,64]{1,0:T(4,128)S(1)}, u32[]{:S(2)}, u32[]{:S(2)}) collective-permute-start(s32[3,64]{1,0:T(4,128)S(1)} %get-tuple-element.48), channel_id=1, source_target_pairs={{0,1},{1,0},{2,3},{3,2},{4,5},{5,4},{6,7},{7,6},{8,9},{9,8},{10,11... | collective-permute-start | bytes 2312 | tf_op jit(solution)/shard_map/other_meta/ppermute | solution.py:18
  8.2 2.3 %copy-start.4 = (bf16[2048,1024]{1,0:T(8,128)(2,1)S(1)}, bf16[2048,1024]{1,0:T(8,128)(2,1)}, u32[]{:S(2)}) copy-start(bf16[2048,1024]{1,0:T(8,128)(2,1)} %param.17) | copy-start | bytes 12582916
  8.2 2.3 %copy-start.6 = (f32[1024]{0:T(1024)S(1)}, f32[1024]{0:T(1024)}, u32[]{:S(2)}) copy-start(f32[1024]{0:T(1024)} %param.18) | copy-start | bytes 12292
  8.2 21.1 %collective-permute-start.7 = (bf16[64,128,128]{2,1,0:T(8,128)(2,1)}, bf16[64,128,128]{2,1,0:T(8,128)(2,1)}, u32[]{:S(2)}, u32[]{:S(2)}) collective-permute-start(bf16[64,128,128]{2,1,0:T(8,128)(2,1)} %get-tuple-element.57.c_own), channel_id=1, source_target_pairs={{0,1},{1,0},{2,3},{3,2},{4,5},{5,4},{6,7},{7,6},{8,9},{9,8},{10,11... | collective-permute-start | bytes 6291464 | tf_op jit(solution)/shard_map/other_tiles/ppermute | solution.py:18
  15.8 9.4 %collective-permute-start.4 = (bf16[16,128,128]{2,1,0:T(8,128)(2,1)S(1)}, bf16[16,128,128]{2,1,0:T(8,128)(2,1)S(1)}, u32[]{:S(2)}, u32[]{:S(2)}) collective-permute-start(bf16[16,128,128]{2,1,0:T(8,128)(2,1)S(1)} %pad_maximum_fusion.1), channel_id=1, source_target_pairs={{0,16},{1,49},{16,0},{17,33},{32,48},{33,17},{48,32},{49,1},{2,18}... | collective-permute-start | bytes 1572872 | tf_op jit(solution)/shard_map/gather_near_0/ppermute | solution.py:28
  18.9 8.4 %collective-permute-start.3 = (bf16[8,128,128]{2,1,0:T(8,128)(2,1)S(1)}, bf16[8,128,128]{2,1,0:T(8,128)(2,1)}, u32[]{:S(2)}, u32[]{:S(2)}) collective-permute-start(bf16[8,128,128]{2,1,0:T(8,128)(2,1)S(1)} %get-tuple-element.51), channel_id=1, source_target_pairs={{0,64},{64,0},{1,65},{65,1},{2,66},{66,2},{3,67},{67,3},{4,68},{68... | collective-permute-start | bytes 786440 | tf_op jit(solution)/shard_map/gather_x_1/ppermute | solution.py:18
  25.2 19.6 %collective-permute-start.8 = (bf16[32,128,128]{2,1,0:T(8,128)(2,1)S(1)}, bf16[32,128,128]{2,1,0:T(8,128)(2,1)S(1)}, u32[]{:S(2)}, u32[]{:S(2)}) collective-permute-start(bf16[32,128,128]{2,1,0:T(8,128)(2,1)S(1)} %constant_dynamic-update-slice_fusion.near), channel_id=1, source_target_pairs={{0,48},{1,17},{16,32},{17,1},{32,16},{33,49},{48,0},{49,33},{2,50}... | collective-permute-start | bytes 3145736 | tf_op jit(solution)/shard_map/gather_far_0/ppermute | solution.py:28
  28.2 15.3 %collective-permute-start.6 = (bf16[16,128,128]{2,1,0:T(8,128)(2,1)S(1)}, bf16[16,128,128]{2,1,0:T(8,128)(2,1)S(1)}, u32[]{:S(2)}, u32[]{:S(2)}) collective-permute-start(bf16[16,128,128]{2,1,0:T(8,128)(2,1)S(1)} %pad_maximum_fusion.2), channel_id=1, source_target_pairs={{0,16},{1,49},{16,0},{17,33},{32,48},{33,17},{48,32},{49,1},{2,18}... | collective-permute-start | bytes 1572872 | tf_op jit(solution)/shard_map/gather_near_1/ppermute | solution.py:28
  29.1 14.6 %collective-permute-start.5 = (bf16[16,128,128]{2,1,0:T(8,128)(2,1)S(1)}, bf16[16,128,128]{2,1,0:T(8,128)(2,1)S(1)}, u32[]{:S(2)}, u32[]{:S(2)}) collective-permute-start(bf16[16,128,128]{2,1,0:T(8,128)(2,1)S(1)} %get-tuple-element.55), channel_id=1, source_target_pairs={{0,64},{64,0},{1,65},{65,1},{2,66},{66,2},{3,67},{67,3},{4,68},{68... | collective-permute-start | bytes 1572872 | tf_op jit(solution)/shard_map/gather_x_rest/ppermute | solution.py:18
  43.6 19.6 %collective-permute-start.11 = (bf16[32,128,128]{2,1,0:T(8,128)(2,1)S(1)}, bf16[32,128,128]{2,1,0:T(8,128)(2,1)S(1)}, u32[]{:S(2)}, u32[]{:S(2)}) collective-permute-start(bf16[32,128,128]{2,1,0:T(8,128)(2,1)S(1)} %constant_dynamic-update-slice_fusion.2.near), channel_id=1, source_target_pairs={{0,48},{1,17},{16,32},{17,1},{32,16},{33,49},{48,0},{49,33},{2,50}... | collective-permute-start | bytes 3145736 | tf_op jit(solution)/shard_map/gather_far_1/ppermute | solution.py:28
  44.9 14.5 %collective-permute-start.10 = (bf16[16,128,128]{2,1,0:T(8,128)(2,1)S(1)}, bf16[16,128,128]{2,1,0:T(8,128)(2,1)S(1)}, u32[]{:S(2)}, u32[]{:S(2)}) collective-permute-start(bf16[16,128,128]{2,1,0:T(8,128)(2,1)S(1)} %pad_maximum_fusion.3), channel_id=1, source_target_pairs={{0,16},{1,49},{16,0},{17,33},{32,48},{33,17},{48,32},{49,1},{2,18}... | collective-permute-start | bytes 1572872 | tf_op jit(solution)/shard_map/gather_near_2/ppermute | solution.py:28
  53.0 20.4 %collective-permute-start.9 = (bf16[4224,128]{1,0:T(8,128)(2,1)S(1)}, bf16[4224,128]{1,0:T(8,128)(2,1)S(1)}, u32[]{:S(2)}, u32[]{:S(2)}) collective-permute-start(bf16[4224,128]{1,0:T(8,128)(2,1)S(1)} %get-tuple-element.61), channel_id=1, source_target_pairs={{0,4},{1,13},{4,0},{5,9},{8,12},{9,5},{12,8},{13,1},{2,6},{3,15},{... | collective-permute-start | bytes 3244040 | tf_op jit(solution)/shard_map/sum_near_0/ppermute | solution.py:28
  59.5 20.2 %collective-permute-start.13 = (bf16[32,128,128]{2,1,0:T(8,128)(2,1)S(1)}, bf16[32,128,128]{2,1,0:T(8,128)(2,1)S(1)}, u32[]{:S(2)}, u32[]{:S(2)}) collective-permute-start(bf16[32,128,128]{2,1,0:T(8,128)(2,1)S(1)} %constant_dynamic-update-slice_fusion.4.near), channel_id=1, source_target_pairs={{0,48},{1,17},{16,32},{17,1},{32,16},{33,49},{48,0},{49,33},{2,50}... | collective-permute-start | bytes 3145736 | tf_op jit(solution)/shard_map/gather_far_2/ppermute | solution.py:28
  63.2 15.2 %collective-permute-start.16 = (bf16[16,128,128]{2,1,0:T(8,128)(2,1)S(1)}, bf16[16,128,128]{2,1,0:T(8,128)(2,1)S(1)}, u32[]{:S(2)}, u32[]{:S(2)}) collective-permute-start(bf16[16,128,128]{2,1,0:T(8,128)(2,1)S(1)} %pad_maximum_fusion.4), channel_id=1, source_target_pairs={{0,16},{1,49},{16,0},{17,33},{32,48},{33,17},{48,32},{49,1},{2,18}... | collective-permute-start | bytes 1572872 | tf_op jit(solution)/shard_map/gather_near_3/ppermute | solution.py:28
  69.3 22.4 %collective-permute-start.18 = (bf16[4096,128]{1,0:T(8,128)(2,1)S(1)}, bf16[4096,128]{1,0:T(8,128)(2,1)S(1)}, u32[]{:S(2)}, u32[]{:S(2)}) collective-permute-start(bf16[4096,128]{1,0:T(8,128)(2,1)S(1)} %get-tuple-element.64), channel_id=1, source_target_pairs={{0,4},{1,13},{4,0},{5,9},{8,12},{9,5},{12,8},{13,1},{2,6},{3,15},{... | collective-permute-start | bytes 3145736 | tf_op jit(solution)/shard_map/sum_near_1/ppermute | solution.py:28
  73.6 15.3 %collective-permute-start.12 = (bf16[2112,128]{1,0:T(8,128)(2,1)S(1)}, bf16[2112,128]{1,0:T(8,128)(2,1)S(1)}, u32[]{:S(2)}, u32[]{:S(2)}) collective-permute-start(bf16[2112,128]{1,0:T(8,128)(2,1)S(1)} %get-tuple-element.96), channel_id=1, source_target_pairs={{0,12},{1,5},{4,8},{5,1},{8,4},{9,13},{12,0},{13,9},{2,14},{3,7},{... | collective-permute-start | bytes 1622024 | tf_op jit(solution)/shard_map/sum_far_0/ppermute | solution.py:28
  78.5 14.2 %collective-permute-start.17 = (bf16[32,128,128]{2,1,0:T(8,128)(2,1)S(1)}, bf16[32,128,128]{2,1,0:T(8,128)(2,1)S(1)}, u32[]{:S(2)}, u32[]{:S(2)}) collective-permute-start(bf16[32,128,128]{2,1,0:T(8,128)(2,1)S(1)} %constant_dynamic-update-slice_fusion.6.near), channel_id=1, source_target_pairs={{0,48},{1,17},{16,32},{17,1},{32,16},{33,49},{48,0},{49,33},{2,50}... | collective-permute-start | bytes 3145736 | tf_op jit(solution)/shard_map/gather_far_3/ppermute | solution.py:28
  84.9 22.1 %collective-permute-start.15 = (bf16[4096,128]{1,0:T(8,128)(2,1)S(1)}, bf16[4096,128]{1,0:T(8,128)(2,1)S(1)}, u32[]{:S(2)}, u32[]{:S(2)}) collective-permute-start(bf16[4096,128]{1,0:T(8,128)(2,1)S(1)} %get-tuple-element.68), channel_id=1, source_target_pairs={{0,4},{1,13},{4,0},{5,9},{8,12},{9,5},{12,8},{13,1},{2,6},{3,15},{... | collective-permute-start | bytes 3145736 | tf_op jit(solution)/shard_map/sum_near_2/ppermute | solution.py:28
  89.0 19.5 %collective-permute-start.14 = (bf16[1056,128]{1,0:T(8,128)(2,1)S(1)}, bf16[1056,128]{1,0:T(8,128)(2,1)S(1)}, u32[]{:S(2)}, u32[]{:S(2)}) collective-permute-start(bf16[1056,128]{1,0:T(8,128)(2,1)S(1)} %fusion.7), channel_id=1, source_target_pairs={{0,2},{2,0},{1,3},{3,1},{4,6},{6,4},{5,7},{7,5},{8,10},{10,8},{9,1... | collective-permute-start | bytes 811016 | tf_op jit(solution)/shard_map/sum_x_0/ppermute | solution.py:18
  91.9 16.9 %collective-permute-start.19 = (bf16[2048,128]{1,0:T(8,128)(2,1)S(1)}, bf16[2048,128]{1,0:T(8,128)(2,1)S(1)}, u32[]{:S(2)}, u32[]{:S(2)}) collective-permute-start(bf16[2048,128]{1,0:T(8,128)(2,1)S(1)} %get-tuple-element.101), channel_id=1, source_target_pairs={{0,12},{1,5},{4,8},{5,1},{8,4},{9,13},{12,0},{13,9},{2,14},{3,7},{... | collective-permute-start | bytes 1572872 | tf_op jit(solution)/shard_map/sum_far_1/ppermute | solution.py:28
  97.9 24.7 %collective-permute-start.21 = (bf16[4096,128]{1,0:T(8,128)(2,1)S(1)}, bf16[4096,128]{1,0:T(8,128)(2,1)S(1)}, u32[]{:S(2)}, u32[]{:S(2)}) collective-permute-start(bf16[4096,128]{1,0:T(8,128)(2,1)S(1)} %get-tuple-element.72), channel_id=1, source_target_pairs={{0,4},{1,13},{4,0},{5,9},{8,12},{9,5},{12,8},{13,1},{2,6},{3,15},{... | collective-permute-start | bytes 3145736 | tf_op jit(solution)/shard_map/sum_near_3/ppermute | solution.py:28
  107.2 1.5 copy-start.5
  107.2 15.6 %collective-permute-start.23 = (bf16[2048,128]{1,0:T(8,128)(2,1)S(1)}, bf16[2048,128]{1,0:T(8,128)(2,1)S(1)}, u32[]{:S(2)}, u32[]{:S(2)}) collective-permute-start(bf16[2048,128]{1,0:T(8,128)(2,1)S(1)} %get-tuple-element.98), channel_id=1, source_target_pairs={{0,12},{1,5},{4,8},{5,1},{8,4},{9,13},{12,0},{13,9},{2,14},{3,7},{... | collective-permute-start | bytes 1572872 | tf_op jit(solution)/shard_map/sum_far_2/ppermute | solution.py:28
  108.9 16.8 %collective-permute-start.20 = (bf16[1024,128]{1,0:T(8,128)(2,1)S(1)}, bf16[1024,128]{1,0:T(8,128)(2,1)S(1)}, u32[]{:S(2)}, u32[]{:S(2)}) collective-permute-start(bf16[1024,128]{1,0:T(8,128)(2,1)S(1)} %fusion.16), channel_id=1, source_target_pairs={{0,2},{2,0},{1,3},{3,1},{4,6},{6,4},{5,7},{7,5},{8,10},{10,8},{9,1... | collective-permute-start | bytes 786440 | tf_op jit(solution)/shard_map/sum_x_1/ppermute | solution.py:18
  122.9 13.2 %collective-permute-start.24 = (bf16[1024,128]{1,0:T(8,128)(2,1)S(1)}, bf16[1024,128]{1,0:T(8,128)(2,1)S(1)}, u32[]{:S(2)}, u32[]{:S(2)}) collective-permute-start(bf16[1024,128]{1,0:T(8,128)(2,1)S(1)} %fusion.11), channel_id=1, source_target_pairs={{0,2},{2,0},{1,3},{3,1},{4,6},{6,4},{5,7},{7,5},{8,10},{10,8},{9,1... | collective-permute-start | bytes 786440 | tf_op jit(solution)/shard_map/sum_x_2/ppermute | solution.py:18
  125.1 11.2 %collective-permute-start.25 = (bf16[2048,128]{1,0:T(8,128)(2,1)S(1)}, bf16[2048,128]{1,0:T(8,128)(2,1)S(1)}, u32[]{:S(2)}, u32[]{:S(2)}) collective-permute-start(bf16[2048,128]{1,0:T(8,128)(2,1)S(1)} %get-tuple-element.100), channel_id=1, source_target_pairs={{0,12},{1,5},{4,8},{5,1},{8,4},{9,13},{12,0},{13,9},{2,14},{3,7},{... | collective-permute-start | bytes 1572872 | tf_op jit(solution)/shard_map/sum_far_3/ppermute | solution.py:28
  126.0 24.0 %collective-permute-start.22 = (bf16[512,256]{1,0:T(8,128)(2,1)S(1)}, bf16[512,256]{1,0:T(8,128)(2,1)S(1)}, u32[]{:S(2)}, u32[]{:S(2)}) collective-permute-start(bf16[512,256]{1,0:T(8,128)(2,1)S(1)} %pad_maximum_fusion.5), channel_id=1, source_target_pairs={{0,1},{1,0},{2,3},{3,2},{4,5},{5,4},{6,7},{7,6},{8,9},{9,8},{10,11... | collective-permute-start | bytes 786440 | tf_op jit(solution)/shard_map/mean_core_0/ppermute | solution.py:18
  136.3 6.8 %collective-permute-start.26 = (bf16[1024,128]{1,0:T(8,128)(2,1)S(1)}, bf16[1024,128]{1,0:T(8,128)(2,1)S(1)}, u32[]{:S(2)}, u32[]{:S(2)}) collective-permute-start(bf16[1024,128]{1,0:T(8,128)(2,1)S(1)} %fusion.9), channel_id=1, source_target_pairs={{0,2},{2,0},{1,3},{3,1},{4,6},{6,4},{5,7},{7,5},{8,10},{10,8},{9,1... | collective-permute-start | bytes 786440 | tf_op jit(solution)/shard_map/sum_x_3/ppermute | solution.py:18
  137.5 12.6 %copy-start.3 = (f32[512,1024]{1,0:T(8,128)S(1)}, f32[512,1024]{1,0:T(8,128)}, u32[]{:S(2)}) copy-start(f32[512,1024]{1,0:T(8,128)} %fusion.3) | copy-start | bytes 6291460
  143.5 8.2 %collective-permute-start.27 = (bf16[512,256]{1,0:T(8,128)(2,1)S(1)}, bf16[512,256]{1,0:T(8,128)(2,1)S(1)}, u32[]{:S(2)}, u32[]{:S(2)}) collective-permute-start(bf16[512,256]{1,0:T(8,128)(2,1)S(1)} %pad_maximum_fusion.7), channel_id=1, source_target_pairs={{0,1},{1,0},{2,3},{3,2},{4,5},{5,4},{6,7},{7,6},{8,9},{9,8},{10,11... | collective-permute-start | bytes 786440 | tf_op jit(solution)/shard_map/mean_core_1/ppermute | solution.py:18

commit v13 on v12

--- a/solution.py
+++ b/solution.py
@@ -332,7 +332,7 @@
             for i in range(2, CHUNKS):
                 tiles(i)
 
-    means = []
+    means, ready = [], []
     for j in range(CHUNKS):
         stay = stays[j]
         size = stay.shape[0] // 2
@@ -342,10 +342,14 @@
         elif j + 1 < CHUNKS:
             got = after(got, pass_all[j + 1])
         passed = (got[:size].astype(f32) + stay[:size]).astype(bf16)
-        stay = got[size:].astype(f32) + stay[size:]
+        ready.append((passed, got[size:].astype(f32) + stay[size:]))
+
+    for j, (passed, stay) in enumerate(ready):
         got = swap(passed, "x_hi", f"sum_x_{j}")
         if j + 2 < CHUNKS:
             got = after(got, pass_all[j + 2])
+        elif j + 1 < CHUNKS:
+            got = after(got, ready[j + 1][0])
         pooled = got.astype(f32) + stay
         if j == 0:
             deg = jnp.sum(

time: 157 us -> 155 us (0.987)
  waiting for transfers between devices: 56.9 us -> 54.9 us
  Pallas kernels: 26.9 us -> 28.8 us
    ppermute x16, starting transfers between devices: 27.5 us -> 23.9 us  [step(): return lax.ppermute(x, (axis, 'core'), pairs)]
    ppermute x12, starting transfers between devices: 23.9 us -> 26.4 us  [swap(): return lax.ppermute(x, axis, [(0, 1), (1, 0)])]
    pallas_call x4, Pallas kernels: 20.9 us -> 22.8 us  [tile_sums(): pl.pallas_call(tile_kernel, out_shape=(jax.ShapeDtypeStruct((4 * size, w)...]
    ppermute x16, waiting for transfers between devices: 47.4 us -> 45.6 us  [step(): return lax.ppermute(x, (axis, 'core'), pairs)]
  transfers between devices with their start and end apart: 28 -> 28, of which waited for: 14 -> 13; matrix products, arithmetic and copies ran while one was open for 12% -> 12% of each run, Pallas kernels for 15% -> 16%
where the time goes in v13:
time: 155 us; the launch traced here: 154 us
  waiting for transfers between devices  54.9 us (35%)
  starting transfers between devices  50.3 us (32%)
  Pallas kernels  28.8 us (19%)
  other arithmetic  11.2 us (7%)
  matrix products  5.73 us (4%)
  local copies, waits for them, and re-layouts  1.58 us (1%)
    ppermute x16, waiting for transfers between devices, step(): return lax.ppermute(x, (axis, 'core'), pairs)  45.6 us
    ppermute x12, starting transfers between devices, swap(): return lax.ppermute(x, axis, [(0, 1), (1, 0)])  26.4 us
    ppermute x16, starting transfers between devices, step(): return lax.ppermute(x, (axis, 'core'), pairs)  23.9 us
    pallas_call x4, Pallas kernels, tile_sums(): pl.pallas_call(tile_kernel, out_shape=(jax.ShapeDtypeStruct((4 * size, w)...  22.8 us
    ppermute x12, waiting for transfers between devices, swap(): return lax.ppermute(x, axis, [(0, 1), (1, 0)])  9.29 us
    reduce_sum x1, other arithmetic, local(): jnp.sum(c_own.astype(jnp.float32), axis=2)  4.34 us
  transfers between devices with their start and end apart: 28, of which 13 were waited for; matrix products, arithmetic and copies ran while one was open for 12% of the time, Pallas kernels for 16%

profile of v13, /device:TPU:3, one launch (start us, length us, event | category | flops | bytes accessed | tf_op | source)
XLA Modules:
  0.0 153.7 jit_solution(8641007154349158352)
XLA Ops:
  0.0 0.7 collective-permute-start
  1.6 0.7 compare_select_fusion.14
  2.4 4.3 %convert_reduce_fusion.1 = (f32[64,128]{1,0:T(8,128)S(1)}, bf16[64,128,128]{2,1,0:T(8,128)(2,1)}) fusion(s32[1,1,64,128,128]{4,3,2,1,0:T(8,128)} %param.11, pred[64]{0:T(512)(128)(4,1)S(1)} %iota_compare_fusion.2), kind=kLoop, calls=%fused_computation.3 | loop fusion | flops 4186112 | bytes 6324288 | tf_op jit(solution)/shard_map/reduce_sum | solution.py:255
  6.7 1.0 shard_map.100
  8.0 0.3 collective-permute-start.1
  8.5 2.1 %shard_map.101 = (bf16[8,128,128]{2,1,0:T(8,128)(2,1)S(1)}, bf16[16,128,128]{2,1,0:T(8,128)(2,1)S(1)}) custom-call(s32[1]{0:T(128)} %bitcast.core_ref, bf16[512,1024]{1,0:T(8,128)(2,1)S(1)} %copy-done.1, bf16[512,1024]{1,0:T(8,128)(2,1)S(1)} %collective-permute-done.x_other, bf16[1024,1024]{1,0:T(8,128)(2,1)S(1)} %copy-done, f32[1,1024]{1,0:T(1,128)S(1)} %bitcast.35), custom_call_target="tpu_custom_call" | custom-call | flops 6442450944 | bytes 2883584 | tf_op jit(solution)/shard_map/pallas_call | solution.py:141
  10.6 2.6 %fusion.3 = f32[512,1024]{1,0:T(8,128)} fusion(bf16[512,1024]{1,0:T(8,128)(2,1)S(1)} %copy-done.1, bf16[2048,1024]{1,0:T(8,128)(2,1)S(1)} %copy-done.4, f32[1024]{0:T(1024)S(1)} %copy-done.6), kind=kOutput, calls=%fused_computation.7 | convolution fusion | flops 1074266112 | bytes 5246976 | tf_op jit(solution)/shard_map/dot_general | solution.py:263
  13.2 2.5 %collective-permute-done.2 = bf16[8,128,128]{2,1,0:T(8,128)(2,1)S(1)} collective-permute-done((bf16[8,128,128]{2,1,0:T(8,128)(2,1)S(1)}, bf16[8,128,128]{2,1,0:T(8,128)(2,1)S(1)}, u32[]{:S(2)}, u32[]{:S(2)}) %collective-permute-start.2) | collective-permute-done | bytes 262176 | tf_op jit(solution)/shard_map/gather_x_0/ppermute | solution.py:18
  15.8 2.8 %collective-permute-start.4 = (bf16[16,128,128]{2,1,0:T(8,128)(2,1)S(1)}, bf16[16,128,128]{2,1,0:T(8,128)(2,1)S(1)}, u32[]{:S(2)}, u32[]{:S(2)}) collective-permute-start(bf16[16,128,128]{2,1,0:T(8,128)(2,1)S(1)} %pad_maximum_fusion.1), channel_id=1, source_target_pairs={{0,16},{1,49},{16,0},{17,33},{32,48},{33,17},{48,32},{49,1},{2,18}... | collective-permute-start | bytes 1572872 | tf_op jit(solution)/shard_map/gather_near_0/ppermute | solution.py:28
  18.9 0.3 collective-permute-start.3
  19.3 5.9 %collective-permute-done.4 = bf16[16,128,128]{2,1,0:T(8,128)(2,1)S(1)} collective-permute-done((bf16[16,128,128]{2,1,0:T(8,128)(2,1)S(1)}, bf16[16,128,128]{2,1,0:T(8,128)(2,1)S(1)}, u32[]{:S(2)}, u32[]{:S(2)}) %collective-permute-start.4) | collective-permute-done | bytes 524320 | tf_op jit(solution)/shard_map/gather_near_0/ppermute | solution.py:28
  25.2 0.5 collective-permute-start.8
  25.7 1.5 collective-permute-done.3
  27.2 1.0 pad_maximum_fusion.2
  28.2 0.9 collective-permute-start.6
  29.1 0.3 collective-permute-start.5
  29.4 2.2 %convert_reduce_fusion = f32[64,128]{1,0:T(8,128)S(1)} fusion(bf16[64,128,128]{2,1,0:T(8,128)(2,1)} %collective-permute-done.7.c_other), kind=kLoop, calls=%fused_computation.2 | loop fusion | flops 2088960 | bytes 2129920 | tf_op jit(solution)/shard_map/reduce_sum | solution.py:255
  31.9 11.6 %collective-permute-done.6 = bf16[16,128,128]{2,1,0:T(8,128)(2,1)S(1)} collective-permute-done((bf16[16,128,128]{2,1,0:T(8,128)(2,1)S(1)}, bf16[16,128,128]{2,1,0:T(8,128)(2,1)S(1)}, u32[]{:S(2)}, u32[]{:S(2)}) %collective-permute-start.6) | collective-permute-done | bytes 524320 | tf_op jit(solution)/shard_map/gather_near_1/ppermute | solution.py:28
  43.8 1.1 collective-permute-done.8.far
  44.9 2.7 %collective-permute-start.10 = (bf16[16,128,128]{2,1,0:T(8,128)(2,1)S(1)}, bf16[16,128,128]{2,1,0:T(8,128)(2,1)S(1)}, u32[]{:S(2)}, u32[]{:S(2)}) collective-permute-start(bf16[16,128,128]{2,1,0:T(8,128)(2,1)S(1)} %pad_maximum_fusion.3), channel_id=1, source_target_pairs={{0,16},{1,49},{16,0},{17,33},{32,48},{33,17},{48,32},{49,1},{2,18}... | collective-permute-start | bytes 1572872 | tf_op jit(solution)/shard_map/gather_near_2/ppermute | solution.py:28
  47.8 5.7 %tiles_0.1 = (bf16[4224,128]{1,0:T(8,128)(2,1)S(1)}, bf16[2112,128]{1,0:T(8,128)(2,1)S(1)}, bf16[2112,128]{1,0:T(8,128)(2,1)S(1)}) custom-call(s32[128]{0:T(128)S(1)} %fusion.27.src_ref, s32[128]{0:T(128)S(1)} %fusion.28.dst_ref, s32[2]{0:T(128)S(1)} %fusion.26.live_ref, bf16[64,128,128]{2,1,0:T(8,128)(2,1)} %get-tuple-element.58.c_own, ...), custom_call_target="tpu_custom_call" | custom-call | flops 2147483648 | bytes 1048576 | tf_op jit(solution)/shard_map/tiles_0/pallas_call | solution.py:90
  53.5 3.8 %collective-permute-start.9 = (bf16[4224,128]{1,0:T(8,128)(2,1)S(1)}, bf16[4224,128]{1,0:T(8,128)(2,1)S(1)}, u32[]{:S(2)}, u32[]{:S(2)}) collective-permute-start(bf16[4224,128]{1,0:T(8,128)(2,1)S(1)} %get-tuple-element.62), channel_id=1, source_target_pairs={{0,4},{1,13},{4,0},{5,9},{8,12},{9,5},{12,8},{13,1},{2,6},{3,15},{... | collective-permute-start | bytes 3244040 | tf_op jit(solution)/shard_map/sum_near_0/ppermute | solution.py:28
  57.3 2.0 %collective-permute-done.10 = bf16[16,128,128]{2,1,0:T(8,128)(2,1)S(1)} collective-permute-done((bf16[16,128,128]{2,1,0:T(8,128)(2,1)S(1)}, bf16[16,128,128]{2,1,0:T(8,128)(2,1)S(1)}, u32[]{:S(2)}, u32[]{:S(2)}) %collective-permute-start.10) | collective-permute-done | bytes 524320 | tf_op jit(solution)/shard_map/gather_near_2/ppermute | solution.py:28
  59.6 3.7 %collective-permute-done.11.far = bf16[32,128,128]{2,1,0:T(8,128)(2,1)S(1)} collective-permute-done((bf16[32,128,128]{2,1,0:T(8,128)(2,1)S(1)}, bf16[32,128,128]{2,1,0:T(8,128)(2,1)S(1)}, u32[]{:S(2)}, u32[]{:S(2)}) %collective-permute-start.11) | collective-permute-done | bytes 1048608 | tf_op jit(solution)/shard_map/gather_far_1/ppermute | solution.py:28
  63.2 0.8 collective-permute-start.16
  64.1 5.7 %tiles_1.1 = (bf16[4096,128]{1,0:T(8,128)(2,1)S(1)}, bf16[2048,128]{1,0:T(8,128)(2,1)S(1)}, bf16[2048,128]{1,0:T(8,128)(2,1)S(1)}) custom-call(s32[128]{0:T(128)S(1)} %fusion.27.src_ref, s32[128]{0:T(128)S(1)} %fusion.28.dst_ref, s32[2]{0:T(128)S(1)} %fusion.26.live_ref, bf16[64,128,128]{2,1,0:T(8,128)(2,1)} %get-tuple-element.58.c_own, ...), custom_call_target="tpu_custom_call" | custom-call | flops 17179869184 | bytes 1048576 | tf_op jit(solution)/shard_map/tiles_1/pallas_call | solution.py:90
  69.8 3.8 %collective-permute-start.18 = (bf16[4096,128]{1,0:T(8,128)(2,1)S(1)}, bf16[4096,128]{1,0:T(8,128)(2,1)S(1)}, u32[]{:S(2)}, u32[]{:S(2)}) collective-permute-start(bf16[4096,128]{1,0:T(8,128)(2,1)S(1)} %get-tuple-element.65), channel_id=1, source_target_pairs={{0,4},{1,13},{4,0},{5,9},{8,12},{9,5},{12,8},{13,1},{2,6},{3,15},{... | collective-permute-start | bytes 3145736 | tf_op jit(solution)/shard_map/sum_near_1/ppermute | solution.py:28
  74.0 4.4 %collective-permute-done.16 = bf16[16,128,128]{2,1,0:T(8,128)(2,1)S(1)} collective-permute-done((bf16[16,128,128]{2,1,0:T(8,128)(2,1)S(1)}, bf16[16,128,128]{2,1,0:T(8,128)(2,1)S(1)}, u32[]{:S(2)}, u32[]{:S(2)}) %collective-permute-start.16) | collective-permute-done | bytes 524320 | tf_op jit(solution)/shard_map/gather_near_3/ppermute | solution.py:28
  78.5 0.3 collective-permute-start.17
  78.7 0.9 collective-permute-done.13.far
  79.7 5.7 %tiles_2.1 = (bf16[4096,128]{1,0:T(8,128)(2,1)S(1)}, bf16[2048,128]{1,0:T(8,128)(2,1)S(1)}, bf16[2048,128]{1,0:T(8,128)(2,1)S(1)}) custom-call(s32[128]{0:T(128)S(1)} %fusion.27.src_ref, s32[128]{0:T(128)S(1)} %fusion.28.dst_ref, s32[2]{0:T(128)S(1)} %fusion.26.live_ref, bf16[64,128,128]{2,1,0:T(8,128)(2,1)} %get-tuple-element.58.c_own, ...), custom_call_target="tpu_custom_call" | custom-call | flops 1048576 | bytes 1048576 | tf_op jit(solution)/shard_map/tiles_2/pallas_call | solution.py:90
  85.4 3.8 %collective-permute-start.15 = (bf16[4096,128]{1,0:T(8,128)(2,1)S(1)}, bf16[4096,128]{1,0:T(8,128)(2,1)S(1)}, u32[]{:S(2)}, u32[]{:S(2)}) collective-permute-start(bf16[4096,128]{1,0:T(8,128)(2,1)S(1)} %get-tuple-element.69), channel_id=1, source_target_pairs={{0,4},{1,13},{4,0},{5,9},{8,12},{9,5},{12,8},{13,1},{2,6},{3,15},{... | collective-permute-start | bytes 3145736 | tf_op jit(solution)/shard_map/sum_near_2/ppermute | solution.py:28
  89.3 2.7 %collective-permute-start.14 = (bf16[1056,128]{1,0:T(8,128)(2,1)S(1)}, bf16[1056,128]{1,0:T(8,128)(2,1)S(1)}, u32[]{:S(2)}, u32[]{:S(2)}) collective-permute-start(bf16[1056,128]{1,0:T(8,128)(2,1)S(1)} %fusion.7), channel_id=1, source_target_pairs={{0,2},{2,0},{1,3},{3,1},{4,6},{6,4},{5,7},{7,5},{8,10},{10,8},{9,1... | collective-permute-start | bytes 811016 | tf_op jit(solution)/shard_map/sum_x_0/ppermute | solution.py:18
  92.3 0.4 collective-permute-done.17.far
  92.7 5.7 %tiles_3.1 = (bf16[4096,128]{1,0:T(8,128)(2,1)S(1)}, bf16[2048,128]{1,0:T(8,128)(2,1)S(1)}, bf16[2048,128]{1,0:T(8,128)(2,1)S(1)}) custom-call(s32[128]{0:T(128)S(1)} %fusion.27.src_ref, s32[128]{0:T(128)S(1)} %fusion.28.dst_ref, s32[2]{0:T(128)S(1)} %fusion.26.live_ref, bf16[64,128,128]{2,1,0:T(8,128)(2,1)} %get-tuple-element.58.c_own, ...), custom_call_target="tpu_custom_call" | custom-call | flops 1048576 | bytes 1048576 | tf_op jit(solution)/shard_map/tiles_3/pallas_call | solution.py:90
  98.4 3.8 %collective-permute-start.21 = (bf16[4096,128]{1,0:T(8,128)(2,1)S(1)}, bf16[4096,128]{1,0:T(8,128)(2,1)S(1)}, u32[]{:S(2)}, u32[]{:S(2)}) collective-permute-start(bf16[4096,128]{1,0:T(8,128)(2,1)S(1)} %get-tuple-element.73), channel_id=1, source_target_pairs={{0,4},{1,13},{4,0},{5,9},{8,12},{9,5},{12,8},{13,1},{2,6},{3,15},{... | collective-permute-start | bytes 3145736 | tf_op jit(solution)/shard_map/sum_near_3/ppermute | solution.py:28
  102.2 4.8 %collective-permute-done.15 = bf16[4096,128]{1,0:T(8,128)(2,1)S(1)} collective-permute-done((bf16[4096,128]{1,0:T(8,128)(2,1)S(1)}, bf16[4096,128]{1,0:T(8,128)(2,1)S(1)}, u32[]{:S(2)}, u32[]{:S(2)}) %collective-permute-start.15) | collective-permute-done | bytes 1048608 | tf_op jit(solution)/shard_map/sum_near_2/ppermute | solution.py:28
  107.5 0.4 copy-done.5
  108.1 4.1 %collective-permute-start.20 = (bf16[1024,128]{1,0:T(8,128)(2,1)S(1)}, bf16[1024,128]{1,0:T(8,128)(2,1)S(1)}, u32[]{:S(2)}, u32[]{:S(2)}) collective-permute-start(bf16[1024,128]{1,0:T(8,128)(2,1)S(1)} %fusion.16), channel_id=1, source_target_pairs={{0,2},{2,0},{1,3},{3,1},{4,6},{6,4},{5,7},{7,5},{8,10},{10,8},{9,1... | collective-permute-start | bytes 786440 | tf_op jit(solution)/shard_map/sum_x_1/ppermute | solution.py:18
  112.4 10.8 %collective-permute-done.21 = bf16[4096,128]{1,0:T(8,128)(2,1)S(1)} collective-permute-done((bf16[4096,128]{1,0:T(8,128)(2,1)S(1)}, bf16[4096,128]{1,0:T(8,128)(2,1)S(1)}, u32[]{:S(2)}, u32[]{:S(2)}) %collective-permute-start.21) | collective-permute-done | bytes 1048608 | tf_op jit(solution)/shard_map/sum_near_3/ppermute | solution.py:28
  123.7 3.3 %collective-permute-start.24 = (bf16[1024,128]{1,0:T(8,128)(2,1)S(1)}, bf16[1024,128]{1,0:T(8,128)(2,1)S(1)}, u32[]{:S(2)}, u32[]{:S(2)}) collective-permute-start(bf16[1024,128]{1,0:T(8,128)(2,1)S(1)} %fusion.11), channel_id=1, source_target_pairs={{0,2},{2,0},{1,3},{3,1},{4,6},{6,4},{5,7},{7,5},{8,10},{10,8},{9,1... | collective-permute-start | bytes 786440 | tf_op jit(solution)/shard_map/sum_x_2/ppermute | solution.py:18
  127.4 8.9 %collective-permute-start.22 = (bf16[512,256]{1,0:T(8,128)(2,1)S(1)}, bf16[512,256]{1,0:T(8,128)(2,1)S(1)}, u32[]{:S(2)}, u32[]{:S(2)}) collective-permute-start(bf16[512,256]{1,0:T(8,128)(2,1)S(1)} %pad_maximum_fusion.5), channel_id=1, source_target_pairs={{0,1},{1,0},{2,3},{3,2},{4,5},{5,4},{6,7},{7,6},{8,9},{9,8},{10,11... | collective-permute-start | bytes 786440 | tf_op jit(solution)/shard_map/mean_core_0/ppermute | solution.py:18
  136.3 1.5 fusion.13
  137.8 1.2 collective-permute-start.26
  139.4 5.3 %collective-permute-done.26 = bf16[1024,128]{1,0:T(8,128)(2,1)S(1)} collective-permute-done((bf16[1024,128]{1,0:T(8,128)(2,1)S(1)}, bf16[1024,128]{1,0:T(8,128)(2,1)S(1)}, u32[]{:S(2)}, u32[]{:S(2)}) %collective-permute-start.26) | collective-permute-done | bytes 262176 | tf_op jit(solution)/shard_map/sum_x_3/ppermute | solution.py:18
  145.0 4.2 %collective-permute-start.27 = (bf16[512,256]{1,0:T(8,128)(2,1)S(1)}, bf16[512,256]{1,0:T(8,128)(2,1)S(1)}, u32[]{:S(2)}, u32[]{:S(2)}) collective-permute-start(bf16[512,256]{1,0:T(8,128)(2,1)S(1)} %pad_maximum_fusion.7), channel_id=1, source_target_pairs={{0,1},{1,0},{2,3},{3,2},{4,5},{5,4},{6,7},{7,6},{8,9},{9,8},{10,11... | collective-permute-start | bytes 786440 | tf_op jit(solution)/shard_map/mean_core_1/ppermute | solution.py:18
  149.2 1.5 add_add_fusion.hidden
  150.7 2.9 %shard_map.102 = f32[512,1024]{1,0:T(8,128)} custom-call(f32[512,1024]{1,0:T(8,128)S(1)} %add_add_fusion.hidden, bf16[512,256]{1,0:T(8,128)(2,1)S(1)} %pad_maximum_fusion.6.near, bf16[512,256]{1,0:T(8,128)(2,1)S(1)} %collective-permute-done.27.got, bf16[512,1024]{1,0:T(8,128)(2,1)S(1)} %pad_maximum_fusion.weight), custom_call_target="tpu_custom_call" | custom-call | tf_op jit(solution)/shard_map/pallas_call | solution.py:175
  (96 shorter events, 5.4 us)
Async XLA Ops:
  0.0 6.7 %collective-permute-start = (bf16[512,1024]{1,0:T(8,128)(2,1)}, bf16[512,1024]{1,0:T(8,128)(2,1)S(1)}, u32[]{:S(2)}, u32[]{:S(2)}) collective-permute-start(bf16[512,1024]{1,0:T(8,128)(2,1)} %x_own.2), channel_id=1, source_target_pairs={{0,1},{1,0},{2,3},{3,2},{4,5},{5,4},{6,7},{7,6},{8,9},{9,8},{10,11... | collective-permute-start | bytes 3145736 | tf_op jit(solution)/shard_map/other_features_0/ppermute | solution.py:18
  2.3 4.4 %copy-start = (bf16[1024,1024]{1,0:T(8,128)(2,1)S(1)}, bf16[1024,1024]{1,0:T(8,128)(2,1)}, u32[]{:S(2)}) copy-start(bf16[1024,1024]{1,0:T(8,128)(2,1)} %weight.3) | copy-start | bytes 6291460
  2.3 4.4 %copy-start.1 = (bf16[512,1024]{1,0:T(8,128)(2,1)S(1)}, bf16[512,1024]{1,0:T(8,128)(2,1)}, u32[]{:S(2)}) copy-start(bf16[512,1024]{1,0:T(8,128)(2,1)} %x_own.2) | copy-start | bytes 3145732
  2.4 4.4 %copy-start.2 = (f32[1024]{0:T(1024)S(1)}, f32[1024]{0:T(1024)}, u32[]{:S(2)}) copy-start(f32[1024]{0:T(1024)} %param.16) | copy-start | bytes 12292
  7.7 8.0 %collective-permute-start.2 = (bf16[8,128,128]{2,1,0:T(8,128)(2,1)S(1)}, bf16[8,128,128]{2,1,0:T(8,128)(2,1)S(1)}, u32[]{:S(2)}, u32[]{:S(2)}) collective-permute-start(bf16[8,128,128]{2,1,0:T(8,128)(2,1)S(1)} %shard_map.100), channel_id=1, source_target_pairs={{0,64},{64,0},{1,65},{65,1},{2,66},{66,2},{3,67},{67,3},{4,68},{68... | collective-permute-start | bytes 786440 | tf_op jit(solution)/shard_map/gather_x_0/ppermute | solution.py:18
  8.0 10.8 %collective-permute-start.1 = (s32[3,64]{1,0:T(4,128)S(1)}, s32[3,64]{1,0:T(4,128)S(1)}, u32[]{:S(2)}, u32[]{:S(2)}) collective-permute-start(s32[3,64]{1,0:T(4,128)S(1)} %get-tuple-element.49), channel_id=1, source_target_pairs={{0,1},{1,0},{2,3},{3,2},{4,5},{5,4},{6,7},{7,6},{8,9},{9,8},{10,11... | collective-permute-start | bytes 2312 | tf_op jit(solution)/shard_map/other_meta/ppermute | solution.py:18
  8.2 2.3 %copy-start.4 = (bf16[2048,1024]{1,0:T(8,128)(2,1)S(1)}, bf16[2048,1024]{1,0:T(8,128)(2,1)}, u32[]{:S(2)}) copy-start(bf16[2048,1024]{1,0:T(8,128)(2,1)} %param.17) | copy-start | bytes 12582916
  8.2 2.3 %copy-start.6 = (f32[1024]{0:T(1024)S(1)}, f32[1024]{0:T(1024)}, u32[]{:S(2)}) copy-start(f32[1024]{0:T(1024)} %param.18) | copy-start | bytes 12292
  8.2 21.1 %collective-permute-start.7 = (bf16[64,128,128]{2,1,0:T(8,128)(2,1)}, bf16[64,128,128]{2,1,0:T(8,128)(2,1)}, u32[]{:S(2)}, u32[]{:S(2)}) collective-permute-start(bf16[64,128,128]{2,1,0:T(8,128)(2,1)} %get-tuple-element.58.c_own), channel_id=1, source_target_pairs={{0,1},{1,0},{2,3},{3,2},{4,5},{5,4},{6,7},{7,6},{8,9},{9,8},{10,11... | collective-permute-start | bytes 6291464 | tf_op jit(solution)/shard_map/other_tiles/ppermute | solution.py:18
  15.8 9.4 %collective-permute-start.4 = (bf16[16,128,128]{2,1,0:T(8,128)(2,1)S(1)}, bf16[16,128,128]{2,1,0:T(8,128)(2,1)S(1)}, u32[]{:S(2)}, u32[]{:S(2)}) collective-permute-start(bf16[16,128,128]{2,1,0:T(8,128)(2,1)S(1)} %pad_maximum_fusion.1), channel_id=1, source_target_pairs={{0,16},{1,49},{16,0},{17,33},{32,48},{33,17},{48,32},{49,1},{2,18}... | collective-permute-start | bytes 1572872 | tf_op jit(solution)/shard_map/gather_near_0/ppermute | solution.py:28
  18.9 8.4 %collective-permute-start.3 = (bf16[8,128,128]{2,1,0:T(8,128)(2,1)S(1)}, bf16[8,128,128]{2,1,0:T(8,128)(2,1)}, u32[]{:S(2)}, u32[]{:S(2)}) collective-permute-start(bf16[8,128,128]{2,1,0:T(8,128)(2,1)S(1)} %get-tuple-element.52), channel_id=1, source_target_pairs={{0,64},{64,0},{1,65},{65,1},{2,66},{66,2},{3,67},{67,3},{4,68},{68... | collective-permute-start | bytes 786440 | tf_op jit(solution)/shard_map/gather_x_1/ppermute | solution.py:18
  25.2 19.6 %collective-permute-start.8 = (bf16[32,128,128]{2,1,0:T(8,128)(2,1)S(1)}, bf16[32,128,128]{2,1,0:T(8,128)(2,1)S(1)}, u32[]{:S(2)}, u32[]{:S(2)}) collective-permute-start(bf16[32,128,128]{2,1,0:T(8,128)(2,1)S(1)} %constant_dynamic-update-slice_fusion.near), channel_id=1, source_target_pairs={{0,48},{1,17},{16,32},{17,1},{32,16},{33,49},{48,0},{49,33},{2,50}... | collective-permute-start | bytes 3145736 | tf_op jit(solution)/shard_map/gather_far_0/ppermute | solution.py:28
  28.2 15.3 %collective-permute-start.6 = (bf16[16,128,128]{2,1,0:T(8,128)(2,1)S(1)}, bf16[16,128,128]{2,1,0:T(8,128)(2,1)S(1)}, u32[]{:S(2)}, u32[]{:S(2)}) collective-permute-start(bf16[16,128,128]{2,1,0:T(8,128)(2,1)S(1)} %pad_maximum_fusion.2), channel_id=1, source_target_pairs={{0,16},{1,49},{16,0},{17,33},{32,48},{33,17},{48,32},{49,1},{2,18}... | collective-permute-start | bytes 1572872 | tf_op jit(solution)/shard_map/gather_near_1/ppermute | solution.py:28
  29.1 14.6 %collective-permute-start.5 = (bf16[16,128,128]{2,1,0:T(8,128)(2,1)S(1)}, bf16[16,128,128]{2,1,0:T(8,128)(2,1)S(1)}, u32[]{:S(2)}, u32[]{:S(2)}) collective-permute-start(bf16[16,128,128]{2,1,0:T(8,128)(2,1)S(1)} %get-tuple-element.56), channel_id=1, source_target_pairs={{0,64},{64,0},{1,65},{65,1},{2,66},{66,2},{3,67},{67,3},{4,68},{68... | collective-permute-start | bytes 1572872 | tf_op jit(solution)/shard_map/gather_x_rest/ppermute | solution.py:18
  43.6 19.6 %collective-permute-start.11 = (bf16[32,128,128]{2,1,0:T(8,128)(2,1)S(1)}, bf16[32,128,128]{2,1,0:T(8,128)(2,1)S(1)}, u32[]{:S(2)}, u32[]{:S(2)}) collective-permute-start(bf16[32,128,128]{2,1,0:T(8,128)(2,1)S(1)} %constant_dynamic-update-slice_fusion.2.near), channel_id=1, source_target_pairs={{0,48},{1,17},{16,32},{17,1},{32,16},{33,49},{48,0},{49,33},{2,50}... | collective-permute-start | bytes 3145736 | tf_op jit(solution)/shard_map/gather_far_1/ppermute | solution.py:28
  44.9 14.5 %collective-permute-start.10 = (bf16[16,128,128]{2,1,0:T(8,128)(2,1)S(1)}, bf16[16,128,128]{2,1,0:T(8,128)(2,1)S(1)}, u32[]{:S(2)}, u32[]{:S(2)}) collective-permute-start(bf16[16,128,128]{2,1,0:T(8,128)(2,1)S(1)} %pad_maximum_fusion.3), channel_id=1, source_target_pairs={{0,16},{1,49},{16,0},{17,33},{32,48},{33,17},{48,32},{49,1},{2,18}... | collective-permute-start | bytes 1572872 | tf_op jit(solution)/shard_map/gather_near_2/ppermute | solution.py:28
  53.5 20.1 %collective-permute-start.9 = (bf16[4224,128]{1,0:T(8,128)(2,1)S(1)}, bf16[4224,128]{1,0:T(8,128)(2,1)S(1)}, u32[]{:S(2)}, u32[]{:S(2)}) collective-permute-start(bf16[4224,128]{1,0:T(8,128)(2,1)S(1)} %get-tuple-element.62), channel_id=1, source_target_pairs={{0,4},{1,13},{4,0},{5,9},{8,12},{9,5},{12,8},{13,1},{2,6},{3,15},{... | collective-permute-start | bytes 3244040 | tf_op jit(solution)/shard_map/sum_near_0/ppermute | solution.py:28
  59.5 20.2 %collective-permute-start.13 = (bf16[32,128,128]{2,1,0:T(8,128)(2,1)S(1)}, bf16[32,128,128]{2,1,0:T(8,128)(2,1)S(1)}, u32[]{:S(2)}, u32[]{:S(2)}) collective-permute-start(bf16[32,128,128]{2,1,0:T(8,128)(2,1)S(1)} %constant_dynamic-update-slice_fusion.4.near), channel_id=1, source_target_pairs={{0,48},{1,17},{16,32},{17,1},{32,16},{33,49},{48,0},{49,33},{2,50}... | collective-permute-start | bytes 3145736 | tf_op jit(solution)/shard_map/gather_far_2/ppermute | solution.py:28
  63.2 15.2 %collective-permute-start.16 = (bf16[16,128,128]{2,1,0:T(8,128)(2,1)S(1)}, bf16[16,128,128]{2,1,0:T(8,128)(2,1)S(1)}, u32[]{:S(2)}, u32[]{:S(2)}) collective-permute-start(bf16[16,128,128]{2,1,0:T(8,128)(2,1)S(1)} %pad_maximum_fusion.4), channel_id=1, source_target_pairs={{0,16},{1,49},{16,0},{17,33},{32,48},{33,17},{48,32},{49,1},{2,18}... | collective-permute-start | bytes 1572872 | tf_op jit(solution)/shard_map/gather_near_3/ppermute | solution.py:28
  69.8 22.1 %collective-permute-start.18 = (bf16[4096,128]{1,0:T(8,128)(2,1)S(1)}, bf16[4096,128]{1,0:T(8,128)(2,1)S(1)}, u32[]{:S(2)}, u32[]{:S(2)}) collective-permute-start(bf16[4096,128]{1,0:T(8,128)(2,1)S(1)} %get-tuple-element.65), channel_id=1, source_target_pairs={{0,4},{1,13},{4,0},{5,9},{8,12},{9,5},{12,8},{13,1},{2,6},{3,15},{... | collective-permute-start | bytes 3145736 | tf_op jit(solution)/shard_map/sum_near_1/ppermute | solution.py:28
  73.9 15.3 %collective-permute-start.12 = (bf16[2112,128]{1,0:T(8,128)(2,1)S(1)}, bf16[2112,128]{1,0:T(8,128)(2,1)S(1)}, u32[]{:S(2)}, u32[]{:S(2)}) collective-permute-start(bf16[2112,128]{1,0:T(8,128)(2,1)S(1)} %get-tuple-element.98), channel_id=1, source_target_pairs={{0,12},{1,5},{4,8},{5,1},{8,4},{9,13},{12,0},{13,9},{2,14},{3,7},{... | collective-permute-start | bytes 1622024 | tf_op jit(solution)/shard_map/sum_far_0/ppermute | solution.py:28
  78.5 14.2 %collective-permute-start.17 = (bf16[32,128,128]{2,1,0:T(8,128)(2,1)S(1)}, bf16[32,128,128]{2,1,0:T(8,128)(2,1)S(1)}, u32[]{:S(2)}, u32[]{:S(2)}) collective-permute-start(bf16[32,128,128]{2,1,0:T(8,128)(2,1)S(1)} %constant_dynamic-update-slice_fusion.6.near), channel_id=1, source_target_pairs={{0,48},{1,17},{16,32},{17,1},{32,16},{33,49},{48,0},{49,33},{2,50}... | collective-permute-start | bytes 3145736 | tf_op jit(solution)/shard_map/gather_far_3/ppermute | solution.py:28
  85.4 21.6 %collective-permute-start.15 = (bf16[4096,128]{1,0:T(8,128)(2,1)S(1)}, bf16[4096,128]{1,0:T(8,128)(2,1)S(1)}, u32[]{:S(2)}, u32[]{:S(2)}) collective-permute-start(bf16[4096,128]{1,0:T(8,128)(2,1)S(1)} %get-tuple-element.69), channel_id=1, source_target_pairs={{0,4},{1,13},{4,0},{5,9},{8,12},{9,5},{12,8},{13,1},{2,6},{3,15},{... | collective-permute-start | bytes 3145736 | tf_op jit(solution)/shard_map/sum_near_2/ppermute | solution.py:28
  89.3 18.1 %collective-permute-start.14 = (bf16[1056,128]{1,0:T(8,128)(2,1)S(1)}, bf16[1056,128]{1,0:T(8,128)(2,1)S(1)}, u32[]{:S(2)}, u32[]{:S(2)}) collective-permute-start(bf16[1056,128]{1,0:T(8,128)(2,1)S(1)} %fusion.7), channel_id=1, source_target_pairs={{0,2},{2,0},{1,3},{3,1},{4,6},{6,4},{5,7},{7,5},{8,10},{10,8},{9,1... | collective-permute-start | bytes 811016 | tf_op jit(solution)/shard_map/sum_x_0/ppermute | solution.py:18
  92.2 15.8 %collective-permute-start.19 = (bf16[2048,128]{1,0:T(8,128)(2,1)S(1)}, bf16[2048,128]{1,0:T(8,128)(2,1)S(1)}, u32[]{:S(2)}, u32[]{:S(2)}) collective-permute-start(bf16[2048,128]{1,0:T(8,128)(2,1)S(1)} %get-tuple-element.103), channel_id=1, source_target_pairs={{0,12},{1,5},{4,8},{5,1},{8,4},{9,13},{12,0},{13,9},{2,14},{3,7},{... | collective-permute-start | bytes 1572872 | tf_op jit(solution)/shard_map/sum_far_1/ppermute | solution.py:28
  98.4 24.9 %collective-permute-start.21 = (bf16[4096,128]{1,0:T(8,128)(2,1)S(1)}, bf16[4096,128]{1,0:T(8,128)(2,1)S(1)}, u32[]{:S(2)}, u32[]{:S(2)}) collective-permute-start(bf16[4096,128]{1,0:T(8,128)(2,1)S(1)} %get-tuple-element.73), channel_id=1, source_target_pairs={{0,4},{1,13},{4,0},{5,9},{8,12},{9,5},{12,8},{13,1},{2,6},{3,15},{... | collective-permute-start | bytes 3145736 | tf_op jit(solution)/shard_map/sum_near_3/ppermute | solution.py:28
  107.2 0.7 copy-start.5
  107.2 16.3 %collective-permute-start.23 = (bf16[2048,128]{1,0:T(8,128)(2,1)S(1)}, bf16[2048,128]{1,0:T(8,128)(2,1)S(1)}, u32[]{:S(2)}, u32[]{:S(2)}) collective-permute-start(bf16[2048,128]{1,0:T(8,128)(2,1)S(1)} %get-tuple-element.100), channel_id=1, source_target_pairs={{0,12},{1,5},{4,8},{5,1},{8,4},{9,13},{12,0},{13,9},{2,14},{3,7},{... | collective-permute-start | bytes 1572872 | tf_op jit(solution)/shard_map/sum_far_2/ppermute | solution.py:28
  108.1 18.9 %collective-permute-start.20 = (bf16[1024,128]{1,0:T(8,128)(2,1)S(1)}, bf16[1024,128]{1,0:T(8,128)(2,1)S(1)}, u32[]{:S(2)}, u32[]{:S(2)}) collective-permute-start(bf16[1024,128]{1,0:T(8,128)(2,1)S(1)} %fusion.16), channel_id=1, source_target_pairs={{0,2},{2,0},{1,3},{3,1},{4,6},{6,4},{5,7},{7,5},{8,10},{10,8},{9,1... | collective-permute-start | bytes 786440 | tf_op jit(solution)/shard_map/sum_x_1/ppermute | solution.py:18
  123.5 14.3 %collective-permute-start.25 = (bf16[2048,128]{1,0:T(8,128)(2,1)S(1)}, bf16[2048,128]{1,0:T(8,128)(2,1)S(1)}, u32[]{:S(2)}, u32[]{:S(2)}) collective-permute-start(bf16[2048,128]{1,0:T(8,128)(2,1)S(1)} %get-tuple-element.102), channel_id=1, source_target_pairs={{0,12},{1,5},{4,8},{5,1},{8,4},{9,13},{12,0},{13,9},{2,14},{3,7},{... | collective-permute-start | bytes 1572872 | tf_op jit(solution)/shard_map/sum_far_3/ppermute | solution.py:28
  123.7 15.4 %collective-permute-start.24 = (bf16[1024,128]{1,0:T(8,128)(2,1)S(1)}, bf16[1024,128]{1,0:T(8,128)(2,1)S(1)}, u32[]{:S(2)}, u32[]{:S(2)}) collective-permute-start(bf16[1024,128]{1,0:T(8,128)(2,1)S(1)} %fusion.11), channel_id=1, source_target_pairs={{0,2},{2,0},{1,3},{3,1},{4,6},{6,4},{5,7},{7,5},{8,10},{10,8},{9,1... | collective-permute-start | bytes 786440 | tf_op jit(solution)/shard_map/sum_x_2/ppermute | solution.py:18
  127.4 21.8 %collective-permute-start.22 = (bf16[512,256]{1,0:T(8,128)(2,1)S(1)}, bf16[512,256]{1,0:T(8,128)(2,1)S(1)}, u32[]{:S(2)}, u32[]{:S(2)}) collective-permute-start(bf16[512,256]{1,0:T(8,128)(2,1)S(1)} %pad_maximum_fusion.5), channel_id=1, source_target_pairs={{0,1},{1,0},{2,3},{3,2},{4,5},{5,4},{6,7},{7,6},{8,9},{9,8},{10,11... | collective-permute-start | bytes 786440 | tf_op jit(solution)/shard_map/mean_core_0/ppermute | solution.py:18
  137.8 6.8 %collective-permute-start.26 = (bf16[1024,128]{1,0:T(8,128)(2,1)S(1)}, bf16[1024,128]{1,0:T(8,128)(2,1)S(1)}, u32[]{:S(2)}, u32[]{:S(2)}) collective-permute-start(bf16[1024,128]{1,0:T(8,128)(2,1)S(1)} %fusion.10), channel_id=1, source_target_pairs={{0,2},{2,0},{1,3},{3,1},{4,6},{6,4},{5,7},{7,5},{8,10},{10,8},{9,1... | collective-permute-start | bytes 786440 | tf_op jit(solution)/shard_map/sum_x_3/ppermute | solution.py:18
  139.3 9.9 %copy-start.3 = (f32[512,1024]{1,0:T(8,128)S(1)}, f32[512,1024]{1,0:T(8,128)}, u32[]{:S(2)}) copy-start(f32[512,1024]{1,0:T(8,128)} %fusion.3) | copy-start | bytes 6291460
  145.0 5.7 %collective-permute-start.27 = (bf16[512,256]{1,0:T(8,128)(2,1)S(1)}, bf16[512,256]{1,0:T(8,128)(2,1)S(1)}, u32[]{:S(2)}, u32[]{:S(2)}) collective-permute-start(bf16[512,256]{1,0:T(8,128)(2,1)S(1)} %pad_maximum_fusion.7), channel_id=1, source_target_pairs={{0,1},{1,0},{2,3},{3,2},{4,5},{5,4},{6,7},{7,6},{8,9},{9,8},{10,11... | collective-permute-start | bytes 786440 | tf_op jit(solution)/shard_map/mean_core_1/ppermute | solution.py:18

commit v14 on v13

--- a/solution.py
+++ b/solution.py
@@ -10,7 +10,7 @@
 AXES = ("x_lo", "y", "z", "x_hi", "core")
 SIZES = (2, 4, 4, 2, 2)
 CHUNKS = 4
-GROUP = 8
+GROUP = 4
 
 
 def swap(x, axis, name):

time: 155 us -> 157 us (1.013)
  Pallas kernels: 28.8 us -> 38.9 us
  starting transfers between devices: 50.3 us -> 41.7 us
    pallas_call x4, Pallas kernels: 22.8 us -> 32.9 us  [tile_sums(): pl.pallas_call(tile_kernel, out_shape=(jax.ShapeDtypeStruct((4 * size, w)...]
    ppermute x12, starting transfers between devices: 26.4 us -> 21.1 us  [swap(): return lax.ppermute(x, axis, [(0, 1), (1, 0)])]
    ppermute x16, starting transfers between devices: 23.9 us -> 20.6 us  [step(): return lax.ppermute(x, (axis, 'core'), pairs)]
  transfers between devices with their start and end apart: 28 -> 28, of which waited for: 13 -> 13; matrix products, arithmetic and copies ran while one was open for 12% -> 12% of each run, Pallas kernels for 16% -> 22%
where the time goes in v14:
time: 157 us; the launch traced here: 156 us
  waiting for transfers between devices  55.9 us (36%)
  starting transfers between devices  41.7 us (27%)
  Pallas kernels  38.9 us (25%)
  other arithmetic  11.2 us (7%)
  matrix products  5.73 us (4%)
    ppermute x16, waiting for transfers between devices, step(): return lax.ppermute(x, (axis, 'core'), pairs)  46.4 us
    pallas_call x4, Pallas kernels, tile_sums(): pl.pallas_call(tile_kernel, out_shape=(jax.ShapeDtypeStruct((4 * size, w)...  32.9 us
    ppermute x12, starting transfers between devices, swap(): return lax.ppermute(x, axis, [(0, 1), (1, 0)])  21.1 us
    ppermute x16, starting transfers between devices, step(): return lax.ppermute(x, (axis, 'core'), pairs)  20.6 us
    ppermute x12, waiting for transfers between devices, swap(): return lax.ppermute(x, axis, [(0, 1), (1, 0)])  9.47 us
    reduce_sum x1, other arithmetic, local(): jnp.sum(c_own.astype(jnp.float32), axis=2)  4.34 us
  transfers between devices with their start and end apart: 28, of which 13 were waited for; matrix products, arithmetic and copies ran while one was open for 12% of the time, Pallas kernels for 22%

profile of v14, /device:TPU:3, one launch (start us, length us, event | category | flops | bytes accessed | tf_op | source)
XLA Modules:
  0.0 155.8 jit_solution(8947566163706213375)
XLA Ops:
  0.0 0.7 collective-permute-start
  1.6 0.7 compare_select_fusion.14
  2.4 4.3 %convert_reduce_fusion.1 = (f32[64,128]{1,0:T(8,128)S(1)}, bf16[64,128,128]{2,1,0:T(8,128)(2,1)}) fusion(s32[1,1,64,128,128]{4,3,2,1,0:T(8,128)} %param.11, pred[64]{0:T(512)(128)(4,1)S(1)} %iota_compare_fusion.2), kind=kLoop, calls=%fused_computation.3 | loop fusion | flops 4186112 | bytes 6324288 | tf_op jit(solution)/shard_map/reduce_sum | solution.py:255
  6.7 1.0 shard_map.100
  8.0 0.3 collective-permute-start.1
  8.5 2.1 %shard_map.101 = (bf16[8,128,128]{2,1,0:T(8,128)(2,1)S(1)}, bf16[16,128,128]{2,1,0:T(8,128)(2,1)S(1)}) custom-call(s32[1]{0:T(128)} %bitcast.core_ref, bf16[512,1024]{1,0:T(8,128)(2,1)S(1)} %copy-done.1, bf16[512,1024]{1,0:T(8,128)(2,1)S(1)} %collective-permute-done.x_other, bf16[1024,1024]{1,0:T(8,128)(2,1)S(1)} %copy-done, f32[1,1024]{1,0:T(1,128)S(1)} %bitcast.35), custom_call_target="tpu_custom_call" | custom-call | flops 6442450944 | bytes 2883584 | tf_op jit(solution)/shard_map/pallas_call | solution.py:141
  10.6 2.6 %fusion.3 = f32[512,1024]{1,0:T(8,128)} fusion(bf16[512,1024]{1,0:T(8,128)(2,1)S(1)} %copy-done.1, bf16[2048,1024]{1,0:T(8,128)(2,1)S(1)} %copy-done.4, f32[1024]{0:T(1024)S(1)} %copy-done.6), kind=kOutput, calls=%fused_computation.7 | convolution fusion | flops 1074266112 | bytes 5246976 | tf_op jit(solution)/shard_map/dot_general | solution.py:263
  13.2 2.5 %collective-permute-done.2 = bf16[8,128,128]{2,1,0:T(8,128)(2,1)S(1)} collective-permute-done((bf16[8,128,128]{2,1,0:T(8,128)(2,1)S(1)}, bf16[8,128,128]{2,1,0:T(8,128)(2,1)S(1)}, u32[]{:S(2)}, u32[]{:S(2)}) %collective-permute-start.2) | collective-permute-done | bytes 262176 | tf_op jit(solution)/shard_map/gather_x_0/ppermute | solution.py:18
  15.8 2.8 %collective-permute-start.4 = (bf16[16,128,128]{2,1,0:T(8,128)(2,1)S(1)}, bf16[16,128,128]{2,1,0:T(8,128)(2,1)S(1)}, u32[]{:S(2)}, u32[]{:S(2)}) collective-permute-start(bf16[16,128,128]{2,1,0:T(8,128)(2,1)S(1)} %pad_maximum_fusion.1), channel_id=1, source_target_pairs={{0,16},{1,49},{16,0},{17,33},{32,48},{33,17},{48,32},{49,1},{2,18}... | collective-permute-start | bytes 1572872 | tf_op jit(solution)/shard_map/gather_near_0/ppermute | solution.py:28
  18.9 0.3 collective-permute-start.3
  19.3 5.9 %collective-permute-done.4 = bf16[16,128,128]{2,1,0:T(8,128)(2,1)S(1)} collective-permute-done((bf16[16,128,128]{2,1,0:T(8,128)(2,1)S(1)}, bf16[16,128,128]{2,1,0:T(8,128)(2,1)S(1)}, u32[]{:S(2)}, u32[]{:S(2)}) %collective-permute-start.4) | collective-permute-done | bytes 524320 | tf_op jit(solution)/shard_map/gather_near_0/ppermute | solution.py:28
  25.2 0.5 collective-permute-start.8
  25.7 1.5 collective-permute-done.3
  27.2 1.0 pad_maximum_fusion.2
  28.2 0.9 collective-permute-start.6
  29.4 2.2 %convert_reduce_fusion = f32[64,128]{1,0:T(8,128)S(1)} fusion(bf16[64,128,128]{2,1,0:T(8,128)(2,1)} %collective-permute-done.7.c_other), kind=kLoop, calls=%fused_computation.2 | loop fusion | flops 2088960 | bytes 2129920 | tf_op jit(solution)/shard_map/reduce_sum | solution.py:255
  31.9 11.6 %collective-permute-done.6 = bf16[16,128,128]{2,1,0:T(8,128)(2,1)S(1)} collective-permute-done((bf16[16,128,128]{2,1,0:T(8,128)(2,1)S(1)}, bf16[16,128,128]{2,1,0:T(8,128)(2,1)S(1)}, u32[]{:S(2)}, u32[]{:S(2)}) %collective-permute-start.6) | collective-permute-done | bytes 524320 | tf_op jit(solution)/shard_map/gather_near_1/ppermute | solution.py:28
  43.8 1.1 collective-permute-done.8.far
  44.9 2.7 %collective-permute-start.10 = (bf16[16,128,128]{2,1,0:T(8,128)(2,1)S(1)}, bf16[16,128,128]{2,1,0:T(8,128)(2,1)S(1)}, u32[]{:S(2)}, u32[]{:S(2)}) collective-permute-start(bf16[16,128,128]{2,1,0:T(8,128)(2,1)S(1)} %pad_maximum_fusion.3), channel_id=1, source_target_pairs={{0,16},{1,49},{16,0},{17,33},{32,48},{33,17},{48,32},{49,1},{2,18}... | collective-permute-start | bytes 1572872 | tf_op jit(solution)/shard_map/gather_near_2/ppermute | solution.py:28
  47.8 8.2 %tiles_0.1 = (bf16[4224,128]{1,0:T(8,128)(2,1)S(1)}, bf16[2112,128]{1,0:T(8,128)(2,1)S(1)}, bf16[2112,128]{1,0:T(8,128)(2,1)S(1)}) custom-call(s32[128]{0:T(128)S(1)} %fusion.27.src_ref, s32[128]{0:T(128)S(1)} %fusion.28.dst_ref, s32[2]{0:T(128)S(1)} %fusion.26.live_ref, bf16[64,128,128]{2,1,0:T(8,128)(2,1)} %get-tuple-element.58.c_own, ...), custom_call_target="tpu_custom_call" | custom-call | flops 2147483648 | bytes 1048576 | tf_op jit(solution)/shard_map/tiles_0/pallas_call | solution.py:90
  56.0 3.1 %collective-permute-start.9 = (bf16[4224,128]{1,0:T(8,128)(2,1)S(1)}, bf16[4224,128]{1,0:T(8,128)(2,1)S(1)}, u32[]{:S(2)}, u32[]{:S(2)}) collective-permute-start(bf16[4224,128]{1,0:T(8,128)(2,1)S(1)} %get-tuple-element.62), channel_id=1, source_target_pairs={{0,4},{1,13},{4,0},{5,9},{8,12},{9,5},{12,8},{13,1},{2,6},{3,15},{... | collective-permute-start | bytes 3244040 | tf_op jit(solution)/shard_map/sum_near_0/ppermute | solution.py:28
  59.1 0.3 collective-permute-done.10
  59.6 3.7 %collective-permute-done.11.far = bf16[32,128,128]{2,1,0:T(8,128)(2,1)S(1)} collective-permute-done((bf16[32,128,128]{2,1,0:T(8,128)(2,1)S(1)}, bf16[32,128,128]{2,1,0:T(8,128)(2,1)S(1)}, u32[]{:S(2)}, u32[]{:S(2)}) %collective-permute-start.11) | collective-permute-done | bytes 1048608 | tf_op jit(solution)/shard_map/gather_far_1/ppermute | solution.py:28
  63.2 0.8 collective-permute-start.16
  64.1 8.2 %tiles_1.1 = (bf16[4096,128]{1,0:T(8,128)(2,1)S(1)}, bf16[2048,128]{1,0:T(8,128)(2,1)S(1)}, bf16[2048,128]{1,0:T(8,128)(2,1)S(1)}) custom-call(s32[128]{0:T(128)S(1)} %fusion.27.src_ref, s32[128]{0:T(128)S(1)} %fusion.28.dst_ref, s32[2]{0:T(128)S(1)} %fusion.26.live_ref, bf16[64,128,128]{2,1,0:T(8,128)(2,1)} %get-tuple-element.58.c_own, ...), custom_call_target="tpu_custom_call" | custom-call | flops 17179869184 | bytes 1048576 | tf_op jit(solution)/shard_map/tiles_1/pallas_call | solution.py:90
  72.3 3.1 %collective-permute-start.18 = (bf16[4096,128]{1,0:T(8,128)(2,1)S(1)}, bf16[4096,128]{1,0:T(8,128)(2,1)S(1)}, u32[]{:S(2)}, u32[]{:S(2)}) collective-permute-start(bf16[4096,128]{1,0:T(8,128)(2,1)S(1)} %get-tuple-element.65), channel_id=1, source_target_pairs={{0,4},{1,13},{4,0},{5,9},{8,12},{9,5},{12,8},{13,1},{2,6},{3,15},{... | collective-permute-start | bytes 3145736 | tf_op jit(solution)/shard_map/sum_near_1/ppermute | solution.py:28
  75.6 0.4 collective-permute-start.12
  76.0 2.4 %collective-permute-done.16 = bf16[16,128,128]{2,1,0:T(8,128)(2,1)S(1)} collective-permute-done((bf16[16,128,128]{2,1,0:T(8,128)(2,1)S(1)}, bf16[16,128,128]{2,1,0:T(8,128)(2,1)S(1)}, u32[]{:S(2)}, u32[]{:S(2)}) %collective-permute-start.16) | collective-permute-done | bytes 524320 | tf_op jit(solution)/shard_map/gather_near_3/ppermute | solution.py:28
  78.6 1.1 collective-permute-done.13.far
  79.7 8.4 %tiles_2.1 = (bf16[4096,128]{1,0:T(8,128)(2,1)S(1)}, bf16[2048,128]{1,0:T(8,128)(2,1)S(1)}, bf16[2048,128]{1,0:T(8,128)(2,1)S(1)}) custom-call(s32[128]{0:T(128)S(1)} %fusion.27.src_ref, s32[128]{0:T(128)S(1)} %fusion.28.dst_ref, s32[2]{0:T(128)S(1)} %fusion.26.live_ref, bf16[64,128,128]{2,1,0:T(8,128)(2,1)} %get-tuple-element.58.c_own, ...), custom_call_target="tpu_custom_call" | custom-call | flops 1048576 | bytes 1048576 | tf_op jit(solution)/shard_map/tiles_2/pallas_call | solution.py:90
  88.0 3.1 %collective-permute-start.15 = (bf16[4096,128]{1,0:T(8,128)(2,1)S(1)}, bf16[4096,128]{1,0:T(8,128)(2,1)S(1)}, u32[]{:S(2)}, u32[]{:S(2)}) collective-permute-start(bf16[4096,128]{1,0:T(8,128)(2,1)S(1)} %get-tuple-element.69), channel_id=1, source_target_pairs={{0,4},{1,13},{4,0},{5,9},{8,12},{9,5},{12,8},{13,1},{2,6},{3,15},{... | collective-permute-start | bytes 3145736 | tf_op jit(solution)/shard_map/sum_near_2/ppermute | solution.py:28
  91.2 1.2 collective-permute-start.14
  92.3 1.3 collective-permute-done.18
  93.8 0.4 collective-permute-start.19
  94.2 8.2 %tiles_3.1 = (bf16[4096,128]{1,0:T(8,128)(2,1)S(1)}, bf16[2048,128]{1,0:T(8,128)(2,1)S(1)}, bf16[2048,128]{1,0:T(8,128)(2,1)S(1)}) custom-call(s32[128]{0:T(128)S(1)} %fusion.27.src_ref, s32[128]{0:T(128)S(1)} %fusion.28.dst_ref, s32[2]{0:T(128)S(1)} %fusion.26.live_ref, bf16[64,128,128]{2,1,0:T(8,128)(2,1)} %get-tuple-element.58.c_own, ...), custom_call_target="tpu_custom_call" | custom-call | flops 1048576 | bytes 1048576 | tf_op jit(solution)/shard_map/tiles_3/pallas_call | solution.py:90
  102.4 1.7 %collective-permute-start.21 = (bf16[4096,128]{1,0:T(8,128)(2,1)S(1)}, bf16[4096,128]{1,0:T(8,128)(2,1)S(1)}, u32[]{:S(2)}, u32[]{:S(2)}) collective-permute-start(bf16[4096,128]{1,0:T(8,128)(2,1)S(1)} %get-tuple-element.73), channel_id=1, source_target_pairs={{0,4},{1,13},{4,0},{5,9},{8,12},{9,5},{12,8},{13,1},{2,6},{3,15},{... | collective-permute-start | bytes 3145736 | tf_op jit(solution)/shard_map/sum_near_3/ppermute | solution.py:28
  104.1 5.5 %collective-permute-done.15 = bf16[4096,128]{1,0:T(8,128)(2,1)S(1)} collective-permute-done((bf16[4096,128]{1,0:T(8,128)(2,1)S(1)}, bf16[4096,128]{1,0:T(8,128)(2,1)S(1)}, u32[]{:S(2)}, u32[]{:S(2)}) %collective-permute-start.15) | collective-permute-done | bytes 1048608 | tf_op jit(solution)/shard_map/sum_near_2/ppermute | solution.py:28
  109.9 0.5 collective-permute-start.23
  110.8 0.3 collective-permute-start.20
  111.3 13.6 %collective-permute-done.21 = bf16[4096,128]{1,0:T(8,128)(2,1)S(1)} collective-permute-done((bf16[4096,128]{1,0:T(8,128)(2,1)S(1)}, bf16[4096,128]{1,0:T(8,128)(2,1)S(1)}, u32[]{:S(2)}, u32[]{:S(2)}) %collective-permute-start.21) | collective-permute-done | bytes 1048608 | tf_op jit(solution)/shard_map/sum_near_3/ppermute | solution.py:28
  125.2 0.4 collective-permute-start.25
  126.1 12.6 %collective-permute-start.22 = (bf16[512,256]{1,0:T(8,128)(2,1)S(1)}, bf16[512,256]{1,0:T(8,128)(2,1)S(1)}, u32[]{:S(2)}, u32[]{:S(2)}) collective-permute-start(bf16[512,256]{1,0:T(8,128)(2,1)S(1)} %pad_maximum_fusion.5), channel_id=1, source_target_pairs={{0,1},{1,0},{2,3},{3,2},{4,5},{5,4},{6,7},{7,6},{8,9},{9,8},{10,11... | collective-permute-start | bytes 786440 | tf_op jit(solution)/shard_map/mean_core_0/ppermute | solution.py:18
  138.6 1.5 fusion.13
  140.2 1.0 collective-permute-start.26
  141.5 5.5 %collective-permute-done.26 = bf16[1024,128]{1,0:T(8,128)(2,1)S(1)} collective-permute-done((bf16[1024,128]{1,0:T(8,128)(2,1)S(1)}, bf16[1024,128]{1,0:T(8,128)(2,1)S(1)}, u32[]{:S(2)}, u32[]{:S(2)}) %collective-permute-start.26) | collective-permute-done | bytes 262176 | tf_op jit(solution)/shard_map/sum_x_3/ppermute | solution.py:18
  147.4 4.0 %collective-permute-start.27 = (bf16[512,256]{1,0:T(8,128)(2,1)S(1)}, bf16[512,256]{1,0:T(8,128)(2,1)S(1)}, u32[]{:S(2)}, u32[]{:S(2)}) collective-permute-start(bf16[512,256]{1,0:T(8,128)(2,1)S(1)} %pad_maximum_fusion.7), channel_id=1, source_target_pairs={{0,1},{1,0},{2,3},{3,2},{4,5},{5,4},{6,7},{7,6},{8,9},{9,8},{10,11... | collective-permute-start | bytes 786440 | tf_op jit(solution)/shard_map/mean_core_1/ppermute | solution.py:18
  151.4 1.5 add_add_fusion.hidden
  152.9 2.9 %shard_map.102 = f32[512,1024]{1,0:T(8,128)} custom-call(f32[512,1024]{1,0:T(8,128)S(1)} %add_add_fusion.hidden, bf16[512,256]{1,0:T(8,128)(2,1)S(1)} %pad_maximum_fusion.6.near, bf16[512,256]{1,0:T(8,128)(2,1)S(1)} %collective-permute-done.27.got, bf16[512,1024]{1,0:T(8,128)(2,1)S(1)} %pad_maximum_fusion.weight), custom_call_target="tpu_custom_call" | custom-call | tf_op jit(solution)/shard_map/pallas_call | solution.py:175
  (96 shorter events, 5.5 us)
Async XLA Ops:
  0.0 6.7 %collective-permute-start = (bf16[512,1024]{1,0:T(8,128)(2,1)}, bf16[512,1024]{1,0:T(8,128)(2,1)S(1)}, u32[]{:S(2)}, u32[]{:S(2)}) collective-permute-start(bf16[512,1024]{1,0:T(8,128)(2,1)} %x_own.2), channel_id=1, source_target_pairs={{0,1},{1,0},{2,3},{3,2},{4,5},{5,4},{6,7},{7,6},{8,9},{9,8},{10,11... | collective-permute-start | bytes 3145736 | tf_op jit(solution)/shard_map/other_features_0/ppermute | solution.py:18
  2.3 4.4 %copy-start = (bf16[1024,1024]{1,0:T(8,128)(2,1)S(1)}, bf16[1024,1024]{1,0:T(8,128)(2,1)}, u32[]{:S(2)}) copy-start(bf16[1024,1024]{1,0:T(8,128)(2,1)} %weight.3) | copy-start | bytes 6291460
  2.3 4.4 %copy-start.1 = (bf16[512,1024]{1,0:T(8,128)(2,1)S(1)}, bf16[512,1024]{1,0:T(8,128)(2,1)}, u32[]{:S(2)}) copy-start(bf16[512,1024]{1,0:T(8,128)(2,1)} %x_own.2) | copy-start | bytes 3145732
  2.4 4.4 %copy-start.2 = (f32[1024]{0:T(1024)S(1)}, f32[1024]{0:T(1024)}, u32[]{:S(2)}) copy-start(f32[1024]{0:T(1024)} %param.16) | copy-start | bytes 12292
  7.7 8.0 %collective-permute-start.2 = (bf16[8,128,128]{2,1,0:T(8,128)(2,1)S(1)}, bf16[8,128,128]{2,1,0:T(8,128)(2,1)S(1)}, u32[]{:S(2)}, u32[]{:S(2)}) collective-permute-start(bf16[8,128,128]{2,1,0:T(8,128)(2,1)S(1)} %shard_map.100), channel_id=1, source_target_pairs={{0,64},{64,0},{1,65},{65,1},{2,66},{66,2},{3,67},{67,3},{4,68},{68... | collective-permute-start | bytes 786440 | tf_op jit(solution)/shard_map/gather_x_0/ppermute | solution.py:18
  8.0 10.8 %collective-permute-start.1 = (s32[3,64]{1,0:T(4,128)S(1)}, s32[3,64]{1,0:T(4,128)S(1)}, u32[]{:S(2)}, u32[]{:S(2)}) collective-permute-start(s32[3,64]{1,0:T(4,128)S(1)} %get-tuple-element.49), channel_id=1, source_target_pairs={{0,1},{1,0},{2,3},{3,2},{4,5},{5,4},{6,7},{7,6},{8,9},{9,8},{10,11... | collective-permute-start | bytes 2312 | tf_op jit(solution)/shard_map/other_meta/ppermute | solution.py:18
  8.2 2.3 %copy-start.4 = (bf16[2048,1024]{1,0:T(8,128)(2,1)S(1)}, bf16[2048,1024]{1,0:T(8,128)(2,1)}, u32[]{:S(2)}) copy-start(bf16[2048,1024]{1,0:T(8,128)(2,1)} %param.17) | copy-start | bytes 12582916
  8.2 2.3 %copy-start.6 = (f32[1024]{0:T(1024)S(1)}, f32[1024]{0:T(1024)}, u32[]{:S(2)}) copy-start(f32[1024]{0:T(1024)} %param.18) | copy-start | bytes 12292
  8.2 21.1 %collective-permute-start.7 = (bf16[64,128,128]{2,1,0:T(8,128)(2,1)}, bf16[64,128,128]{2,1,0:T(8,128)(2,1)}, u32[]{:S(2)}, u32[]{:S(2)}) collective-permute-start(bf16[64,128,128]{2,1,0:T(8,128)(2,1)} %get-tuple-element.58.c_own), channel_id=1, source_target_pairs={{0,1},{1,0},{2,3},{3,2},{4,5},{5,4},{6,7},{7,6},{8,9},{9,8},{10,11... | collective-permute-start | bytes 6291464 | tf_op jit(solution)/shard_map/other_tiles/ppermute | solution.py:18
  15.8 9.4 %collective-permute-start.4 = (bf16[16,128,128]{2,1,0:T(8,128)(2,1)S(1)}, bf16[16,128,128]{2,1,0:T(8,128)(2,1)S(1)}, u32[]{:S(2)}, u32[]{:S(2)}) collective-permute-start(bf16[16,128,128]{2,1,0:T(8,128)(2,1)S(1)} %pad_maximum_fusion.1), channel_id=1, source_target_pairs={{0,16},{1,49},{16,0},{17,33},{32,48},{33,17},{48,32},{49,1},{2,18}... | collective-permute-start | bytes 1572872 | tf_op jit(solution)/shard_map/gather_near_0/ppermute | solution.py:28
  18.9 8.4 %collective-permute-start.3 = (bf16[8,128,128]{2,1,0:T(8,128)(2,1)S(1)}, bf16[8,128,128]{2,1,0:T(8,128)(2,1)}, u32[]{:S(2)}, u32[]{:S(2)}) collective-permute-start(bf16[8,128,128]{2,1,0:T(8,128)(2,1)S(1)} %get-tuple-element.52), channel_id=1, source_target_pairs={{0,64},{64,0},{1,65},{65,1},{2,66},{66,2},{3,67},{67,3},{4,68},{68... | collective-permute-start | bytes 786440 | tf_op jit(solution)/shard_map/gather_x_1/ppermute | solution.py:18
  25.2 19.6 %collective-permute-start.8 = (bf16[32,128,128]{2,1,0:T(8,128)(2,1)S(1)}, bf16[32,128,128]{2,1,0:T(8,128)(2,1)S(1)}, u32[]{:S(2)}, u32[]{:S(2)}) collective-permute-start(bf16[32,128,128]{2,1,0:T(8,128)(2,1)S(1)} %constant_dynamic-update-slice_fusion.near), channel_id=1, source_target_pairs={{0,48},{1,17},{16,32},{17,1},{32,16},{33,49},{48,0},{49,33},{2,50}... | collective-permute-start | bytes 3145736 | tf_op jit(solution)/shard_map/gather_far_0/ppermute | solution.py:28
  28.2 15.3 %collective-permute-start.6 = (bf16[16,128,128]{2,1,0:T(8,128)(2,1)S(1)}, bf16[16,128,128]{2,1,0:T(8,128)(2,1)S(1)}, u32[]{:S(2)}, u32[]{:S(2)}) collective-permute-start(bf16[16,128,128]{2,1,0:T(8,128)(2,1)S(1)} %pad_maximum_fusion.2), channel_id=1, source_target_pairs={{0,16},{1,49},{16,0},{17,33},{32,48},{33,17},{48,32},{49,1},{2,18}... | collective-permute-start | bytes 1572872 | tf_op jit(solution)/shard_map/gather_near_1/ppermute | solution.py:28
  29.1 14.6 %collective-permute-start.5 = (bf16[16,128,128]{2,1,0:T(8,128)(2,1)S(1)}, bf16[16,128,128]{2,1,0:T(8,128)(2,1)S(1)}, u32[]{:S(2)}, u32[]{:S(2)}) collective-permute-start(bf16[16,128,128]{2,1,0:T(8,128)(2,1)S(1)} %get-tuple-element.56), channel_id=1, source_target_pairs={{0,64},{64,0},{1,65},{65,1},{2,66},{66,2},{3,67},{67,3},{4,68},{68... | collective-permute-start | bytes 1572872 | tf_op jit(solution)/shard_map/gather_x_rest/ppermute | solution.py:18
  43.6 19.6 %collective-permute-start.11 = (bf16[32,128,128]{2,1,0:T(8,128)(2,1)S(1)}, bf16[32,128,128]{2,1,0:T(8,128)(2,1)S(1)}, u32[]{:S(2)}, u32[]{:S(2)}) collective-permute-start(bf16[32,128,128]{2,1,0:T(8,128)(2,1)S(1)} %constant_dynamic-update-slice_fusion.2.near), channel_id=1, source_target_pairs={{0,48},{1,17},{16,32},{17,1},{32,16},{33,49},{48,0},{49,33},{2,50}... | collective-permute-start | bytes 3145736 | tf_op jit(solution)/shard_map/gather_far_1/ppermute | solution.py:28
  44.9 14.5 %collective-permute-start.10 = (bf16[16,128,128]{2,1,0:T(8,128)(2,1)S(1)}, bf16[16,128,128]{2,1,0:T(8,128)(2,1)S(1)}, u32[]{:S(2)}, u32[]{:S(2)}) collective-permute-start(bf16[16,128,128]{2,1,0:T(8,128)(2,1)S(1)} %pad_maximum_fusion.3), channel_id=1, source_target_pairs={{0,16},{1,49},{16,0},{17,33},{32,48},{33,17},{48,32},{49,1},{2,18}... | collective-permute-start | bytes 1572872 | tf_op jit(solution)/shard_map/gather_near_2/ppermute | solution.py:28
  56.0 19.4 %collective-permute-start.9 = (bf16[4224,128]{1,0:T(8,128)(2,1)S(1)}, bf16[4224,128]{1,0:T(8,128)(2,1)S(1)}, u32[]{:S(2)}, u32[]{:S(2)}) collective-permute-start(bf16[4224,128]{1,0:T(8,128)(2,1)S(1)} %get-tuple-element.62), channel_id=1, source_target_pairs={{0,4},{1,13},{4,0},{5,9},{8,12},{9,5},{12,8},{13,1},{2,6},{3,15},{... | collective-permute-start | bytes 3244040 | tf_op jit(solution)/shard_map/sum_near_0/ppermute | solution.py:28
  59.5 20.2 %collective-permute-start.13 = (bf16[32,128,128]{2,1,0:T(8,128)(2,1)S(1)}, bf16[32,128,128]{2,1,0:T(8,128)(2,1)S(1)}, u32[]{:S(2)}, u32[]{:S(2)}) collective-permute-start(bf16[32,128,128]{2,1,0:T(8,128)(2,1)S(1)} %constant_dynamic-update-slice_fusion.4.near), channel_id=1, source_target_pairs={{0,48},{1,17},{16,32},{17,1},{32,16},{33,49},{48,0},{49,33},{2,50}... | collective-permute-start | bytes 3145736 | tf_op jit(solution)/shard_map/gather_far_2/ppermute | solution.py:28
  63.2 15.2 %collective-permute-start.16 = (bf16[16,128,128]{2,1,0:T(8,128)(2,1)S(1)}, bf16[16,128,128]{2,1,0:T(8,128)(2,1)S(1)}, u32[]{:S(2)}, u32[]{:S(2)}) collective-permute-start(bf16[16,128,128]{2,1,0:T(8,128)(2,1)S(1)} %pad_maximum_fusion.4), channel_id=1, source_target_pairs={{0,16},{1,49},{16,0},{17,33},{32,48},{33,17},{48,32},{49,1},{2,18}... | collective-permute-start | bytes 1572872 | tf_op jit(solution)/shard_map/gather_near_3/ppermute | solution.py:28
  72.3 21.3 %collective-permute-start.18 = (bf16[4096,128]{1,0:T(8,128)(2,1)S(1)}, bf16[4096,128]{1,0:T(8,128)(2,1)S(1)}, u32[]{:S(2)}, u32[]{:S(2)}) collective-permute-start(bf16[4096,128]{1,0:T(8,128)(2,1)S(1)} %get-tuple-element.65), channel_id=1, source_target_pairs={{0,4},{1,13},{4,0},{5,9},{8,12},{9,5},{12,8},{13,1},{2,6},{3,15},{... | collective-permute-start | bytes 3145736 | tf_op jit(solution)/shard_map/sum_near_1/ppermute | solution.py:28
  75.6 15.5 %collective-permute-start.12 = (bf16[2112,128]{1,0:T(8,128)(2,1)S(1)}, bf16[2112,128]{1,0:T(8,128)(2,1)S(1)}, u32[]{:S(2)}, u32[]{:S(2)}) collective-permute-start(bf16[2112,128]{1,0:T(8,128)(2,1)S(1)} %get-tuple-element.98), channel_id=1, source_target_pairs={{0,12},{1,5},{4,8},{5,1},{8,4},{9,13},{12,0},{13,9},{2,14},{3,7},{... | collective-permute-start | bytes 1622024 | tf_op jit(solution)/shard_map/sum_far_0/ppermute | solution.py:28
  78.5 15.8 %collective-permute-start.17 = (bf16[32,128,128]{2,1,0:T(8,128)(2,1)S(1)}, bf16[32,128,128]{2,1,0:T(8,128)(2,1)S(1)}, u32[]{:S(2)}, u32[]{:S(2)}) collective-permute-start(bf16[32,128,128]{2,1,0:T(8,128)(2,1)S(1)} %constant_dynamic-update-slice_fusion.6.near), channel_id=1, source_target_pairs={{0,48},{1,17},{16,32},{17,1},{32,16},{33,49},{48,0},{49,33},{2,50}... | collective-permute-start | bytes 3145736 | tf_op jit(solution)/shard_map/gather_far_3/ppermute | solution.py:28
  88.0 21.7 %collective-permute-start.15 = (bf16[4096,128]{1,0:T(8,128)(2,1)S(1)}, bf16[4096,128]{1,0:T(8,128)(2,1)S(1)}, u32[]{:S(2)}, u32[]{:S(2)}) collective-permute-start(bf16[4096,128]{1,0:T(8,128)(2,1)S(1)} %get-tuple-element.69), channel_id=1, source_target_pairs={{0,4},{1,13},{4,0},{5,9},{8,12},{9,5},{12,8},{13,1},{2,6},{3,15},{... | collective-permute-start | bytes 3145736 | tf_op jit(solution)/shard_map/sum_near_2/ppermute | solution.py:28
  91.2 19.3 %collective-permute-start.14 = (bf16[1056,128]{1,0:T(8,128)(2,1)S(1)}, bf16[1056,128]{1,0:T(8,128)(2,1)S(1)}, u32[]{:S(2)}, u32[]{:S(2)}) collective-permute-start(bf16[1056,128]{1,0:T(8,128)(2,1)S(1)} %fusion.7), channel_id=1, source_target_pairs={{0,2},{2,0},{1,3},{3,1},{4,6},{6,4},{5,7},{7,5},{8,10},{10,8},{9,1... | collective-permute-start | bytes 811016 | tf_op jit(solution)/shard_map/sum_x_0/ppermute | solution.py:18
  93.8 16.8 %collective-permute-start.19 = (bf16[2048,128]{1,0:T(8,128)(2,1)S(1)}, bf16[2048,128]{1,0:T(8,128)(2,1)S(1)}, u32[]{:S(2)}, u32[]{:S(2)}) collective-permute-start(bf16[2048,128]{1,0:T(8,128)(2,1)S(1)} %get-tuple-element.103), channel_id=1, source_target_pairs={{0,12},{1,5},{4,8},{5,1},{8,4},{9,13},{12,0},{13,9},{2,14},{3,7},{... | collective-permute-start | bytes 1572872 | tf_op jit(solution)/shard_map/sum_far_1/ppermute | solution.py:28
  102.4 22.5 %collective-permute-start.21 = (bf16[4096,128]{1,0:T(8,128)(2,1)S(1)}, bf16[4096,128]{1,0:T(8,128)(2,1)S(1)}, u32[]{:S(2)}, u32[]{:S(2)}) collective-permute-start(bf16[4096,128]{1,0:T(8,128)(2,1)S(1)} %get-tuple-element.73), channel_id=1, source_target_pairs={{0,4},{1,13},{4,0},{5,9},{8,12},{9,5},{12,8},{13,1},{2,6},{3,15},{... | collective-permute-start | bytes 3145736 | tf_op jit(solution)/shard_map/sum_near_3/ppermute | solution.py:28
  109.9 0.7 copy-start.5
  109.9 15.6 %collective-permute-start.23 = (bf16[2048,128]{1,0:T(8,128)(2,1)S(1)}, bf16[2048,128]{1,0:T(8,128)(2,1)S(1)}, u32[]{:S(2)}, u32[]{:S(2)}) collective-permute-start(bf16[2048,128]{1,0:T(8,128)(2,1)S(1)} %get-tuple-element.100), channel_id=1, source_target_pairs={{0,12},{1,5},{4,8},{5,1},{8,4},{9,13},{12,0},{13,9},{2,14},{3,7},{... | collective-permute-start | bytes 1572872 | tf_op jit(solution)/shard_map/sum_far_2/ppermute | solution.py:28
  110.8 14.9 %collective-permute-start.20 = (bf16[1024,128]{1,0:T(8,128)(2,1)S(1)}, bf16[1024,128]{1,0:T(8,128)(2,1)S(1)}, u32[]{:S(2)}, u32[]{:S(2)}) collective-permute-start(bf16[1024,128]{1,0:T(8,128)(2,1)S(1)} %fusion.16), channel_id=1, source_target_pairs={{0,2},{2,0},{1,3},{3,1},{4,6},{6,4},{5,7},{7,5},{8,10},{10,8},{9,1... | collective-permute-start | bytes 786440 | tf_op jit(solution)/shard_map/sum_x_1/ppermute | solution.py:18
  125.2 15.0 %collective-permute-start.25 = (bf16[2048,128]{1,0:T(8,128)(2,1)S(1)}, bf16[2048,128]{1,0:T(8,128)(2,1)S(1)}, u32[]{:S(2)}, u32[]{:S(2)}) collective-permute-start(bf16[2048,128]{1,0:T(8,128)(2,1)S(1)} %get-tuple-element.102), channel_id=1, source_target_pairs={{0,12},{1,5},{4,8},{5,1},{8,4},{9,13},{12,0},{13,9},{2,14},{3,7},{... | collective-permute-start | bytes 1572872 | tf_op jit(solution)/shard_map/sum_far_3/ppermute | solution.py:28
  125.6 15.6 %collective-permute-start.24 = (bf16[1024,128]{1,0:T(8,128)(2,1)S(1)}, bf16[1024,128]{1,0:T(8,128)(2,1)S(1)}, u32[]{:S(2)}, u32[]{:S(2)}) collective-permute-start(bf16[1024,128]{1,0:T(8,128)(2,1)S(1)} %fusion.11), channel_id=1, source_target_pairs={{0,2},{2,0},{1,3},{3,1},{4,6},{6,4},{5,7},{7,5},{8,10},{10,8},{9,1... | collective-permute-start | bytes 786440 | tf_op jit(solution)/shard_map/sum_x_2/ppermute | solution.py:18
  126.1 25.3 %collective-permute-start.22 = (bf16[512,256]{1,0:T(8,128)(2,1)S(1)}, bf16[512,256]{1,0:T(8,128)(2,1)S(1)}, u32[]{:S(2)}, u32[]{:S(2)}) collective-permute-start(bf16[512,256]{1,0:T(8,128)(2,1)S(1)} %pad_maximum_fusion.5), channel_id=1, source_target_pairs={{0,1},{1,0},{2,3},{3,2},{4,5},{5,4},{6,7},{7,6},{8,9},{9,8},{10,11... | collective-permute-start | bytes 786440 | tf_op jit(solution)/shard_map/mean_core_0/ppermute | solution.py:18
  140.2 6.8 %collective-permute-start.26 = (bf16[1024,128]{1,0:T(8,128)(2,1)S(1)}, bf16[1024,128]{1,0:T(8,128)(2,1)S(1)}, u32[]{:S(2)}, u32[]{:S(2)}) collective-permute-start(bf16[1024,128]{1,0:T(8,128)(2,1)S(1)} %fusion.10), channel_id=1, source_target_pairs={{0,2},{2,0},{1,3},{3,1},{4,6},{6,4},{5,7},{7,5},{8,10},{10,8},{9,1... | collective-permute-start | bytes 786440 | tf_op jit(solution)/shard_map/sum_x_3/ppermute | solution.py:18
  141.5 9.9 %copy-start.3 = (f32[512,1024]{1,0:T(8,128)S(1)}, f32[512,1024]{1,0:T(8,128)}, u32[]{:S(2)}) copy-start(f32[512,1024]{1,0:T(8,128)} %fusion.3) | copy-start | bytes 6291460
  147.4 5.5 %collective-permute-start.27 = (bf16[512,256]{1,0:T(8,128)(2,1)S(1)}, bf16[512,256]{1,0:T(8,128)(2,1)S(1)}, u32[]{:S(2)}, u32[]{:S(2)}) collective-permute-start(bf16[512,256]{1,0:T(8,128)(2,1)S(1)} %pad_maximum_fusion.7), channel_id=1, source_target_pairs={{0,1},{1,0},{2,3},{3,2},{4,5},{5,4},{6,7},{7,6},{8,9},{9,8},{10,11... | collective-permute-start | bytes 786440 | tf_op jit(solution)/shard_map/mean_core_1/ppermute | solution.py:18
